TPU v7x, 32 devices: a whole 2x2x4 slice. The times are simulated.
32 devices in a mesh: groups: 2 (over x), zslab: 16 (over z, y, core).
Axes of the slice: x: 2, y: 2, z: 4, core: 2. Of those that a mesh axis runs over, the one named last changes fastest.
Arguments:
- feats: bfloat16 [64, 8, 64, 256], P(('groups', 'zslab')), parts along dimension 0, may hold values from -6 to 6
- voxmask: int32 [64, 512], P(('groups', 'zslab')), parts along dimension 0, may hold values 0 or 1
- links: int32 [64, 2], P(('groups', 'zslab')), parts along dimension 0, may hold values from -1 to 31, as said below
- weight: bfloat16 [27, 256, 256], replicated, may hold values from -0.078125 to 0.078125
- bias: float32 [256], replicated, may hold values from -3 to 3
- cotangent: bfloat16 [64, 8, 64, 256], P(('groups', 'zslab')), parts along dimension 0, may hold values from -6 to 6
Outputs:
- output: bfloat16 [64, 8, 64, 256], P(('groups', 'zslab')), parts along dimension 0
- grad_feats: bfloat16 [64, 8, 64, 256], P(('groups', 'zslab')), parts along dimension 0
- grad_weight: bfloat16 [54, 256, 256], P('groups'), parts along dimension 0
- grad_bias: float32 [512], P('groups'), parts along dimension 0
There are 2 independent parts, one for each index of `groups`. A program takes and returns all parts, laid end to end along the dimension named above; an argument that names none is the same for every part. Nothing has to cross between parts.
Inputs may be any that keep to these rules, and one draw needn't show every extreme that they name: links[b, 0] == i >= 0 exactly when links[i, 1] == b; no brick is linked to itself; the bricks of one device (rows d * 2 to d * 2 + 1) have their upper links on pairwise different devices other than d, and their lower links too.
All inputs are finite; a program needn't handle non-finite values. No bound on the sum of `voxmask` on one device may be relied on, other than what follows from the above.
Results may differ from a plain program's by a relative error of at most 0.0055.
Values may be sent and summed in bfloat16 or wider, within the bound.
No kernel may reach another device: no remote copies, remote signals or barrier semaphores. Data moves between devices by JAX's collectives and lax.ppermute only.
A program may use at most 128 MiB of HBM per device.

v0:
```python
import jax
import jax.numpy as jnp
from jax import lax
from jax.sharding import PartitionSpec as P


def extend_with(planes, below, above):
    count = planes.shape[0]
    width = planes.shape[3]
    stacked = jnp.concatenate([below[:, None], planes, above[:, None]], axis=1)
    stacked = stacked.reshape(count, 10, 8, 8, width)
    return jnp.pad(stacked, ((0, 0), (0, 0), (1, 1), (1, 1), (0, 0)))


def extend_gathered(planes, bottoms, tops, links):
    lower = links[:, 0]
    upper = links[:, 1]
    below = jnp.take(tops, jnp.maximum(lower, 0), axis=0)
    above = jnp.take(bottoms, jnp.maximum(upper, 0), axis=0)
    below = jnp.where((lower >= 0)[:, None, None], below, jnp.zeros_like(below))
    above = jnp.where((upper >= 0)[:, None, None], above, jnp.zeros_like(above))
    return extend_with(planes, below, above)


def forward_conv(extended, weight):
    count = extended.shape[0]
    width = extended.shape[4]
    total = jnp.zeros((count * 512, weight.shape[2]), jnp.float32)
    for depth in range(3):
        for row in range(3):
            for col in range(3):
                piece = extended[:, depth : depth + 8, row : row + 8, col : col + 8].reshape(
                    count * 512, width
                )
                total = total + jnp.dot(
                    piece, weight[9 * depth + 3 * row + col], preferred_element_type=jnp.float32
                )
    return total


def transpose_conv(grad_ext, weight):
    count = grad_ext.shape[0]
    width = grad_ext.shape[4]
    total = jnp.zeros((count * 512, weight.shape[1]), jnp.float32)
    for depth in range(3):
        for row in range(3):
            for col in range(3):
                piece = grad_ext[
                    :, 2 - depth : 10 - depth, 2 - row : 10 - row, 2 - col : 10 - col
                ].reshape(count * 512, width)
                total = total + lax.dot_general(
                    piece,
                    weight[9 * depth + 3 * row + col],
                    (((1,), (1,)), ((), ())),
                    preferred_element_type=jnp.float32,
                )
    return total


def weight_terms(extended, grad_rows):
    count = extended.shape[0]
    width = extended.shape[4]
    terms = []
    for depth in range(3):
        for row in range(3):
            for col in range(3):
                piece = extended[:, depth : depth + 8, row : row + 8, col : col + 8].reshape(
                    count * 512, width
                )
                terms.append(
                    lax.dot_general(
                        piece,
                        grad_rows,
                        (((0,), (0,)), ((), ())),
                        preferred_element_type=jnp.float32,
                    )
                )
    return jnp.stack(terms, axis=0)


def per_device(feats, voxmask, links, weight, bias, cotangent):
    count = feats.shape[0]
    width = feats.shape[3]
    keep = (voxmask == 1).reshape(count, 8, 64, 1)
    masked = jnp.where(keep, feats, jnp.zeros_like(feats))
    rims = jnp.stack([masked[:, 0], masked[:, 7]], axis=1)
    all_rims = lax.all_gather(rims, "zslab", axis=0, tiled=True)
    extended = extend_gathered(masked, all_rims[:, 0], all_rims[:, 1], links)
    pre = forward_conv(extended, weight) + bias[None, :]
    keep_rows = keep.reshape(count * 512, 1)
    sigma = jax.nn.sigmoid(pre)
    output = jnp.where(keep_rows, pre * sigma, 0.0).astype(jnp.bfloat16)
    grad_pre = jnp.where(
        keep_rows,
        cotangent.reshape(count * 512, width).astype(jnp.float32)
        * sigma
        * (1.0 + pre * (1.0 - sigma)),
        0.0,
    ).astype(jnp.bfloat16)
    grad_planes = grad_pre.reshape(count, 8, 64, width)
    grad_edges = jnp.stack([grad_planes[:, 0], grad_planes[:, 7]], axis=1)
    all_grad_edges = lax.all_gather(grad_edges, "zslab", axis=0, tiled=True)
    grad_ext = extend_gathered(grad_planes, all_grad_edges[:, 0], all_grad_edges[:, 1], links)
    grad_feats = jnp.where(keep_rows, transpose_conv(grad_ext, weight), 0.0).astype(jnp.bfloat16)
    weight_local = weight_terms(extended, grad_pre)
    bias_local = jnp.sum(grad_pre.astype(jnp.float32), axis=0)
    weight_sum, bias_sum = lax.psum((weight_local, bias_local), "zslab")
    grad_weight = weight_sum.astype(jnp.bfloat16)
    return (
        output.reshape(count, 8, 64, width),
        grad_feats.reshape(count, 8, 64, width),
        grad_weight,
        bias_sum,
    )


def solution(mesh):
    return jax.shard_map(
        per_device,
        mesh=mesh,
        in_specs=(
            P(("groups", "zslab"), None, None, None),
            P(("groups", "zslab"), None),
            P(("groups", "zslab"), None),
            P(),
            P(),
            P(("groups", "zslab"), None, None, None),
        ),
        out_specs=(
            P(("groups", "zslab"), None, None, None),
            P(("groups", "zslab"), None, None, None),
            P("groups", None, None),
            P("groups"),
        ),
        check_vma=False,
    )
```

profile of v0, /device:TPU:0, one launch (start us, length us, event | category | flops | bytes accessed | tf_op | source)
XLA Modules:
  0.0 296.6 jit_solution(10011183112644567827)
XLA Ops:
  8.0 1.2 broadcast_select_fusion
  12.7 1.2 fusion.266
  13.9 41.0 %all-gather.3.cloned.1.call-done = bf16[32,2,64,256]{3,2,1,0:T(8,128)(2,1)} async-done(((bf16[2,2,64,256]{3,2,1,0:T(8,128)(2,1)}), bf16[32,2,64,256]{3,2,1,0:T(8,128)(2,1)}) %all-gather.3.cloned.1.call-update) | async-done | bytes 2097168 | tf_op jit(solution)/shard_map/all_gather | solution.py:87
  54.9 1.8 slice_bitcast_fusion.3
  59.3 2.5 fusion.154
  69.9 2.2 convert_reduce_fusion
  75.2 1.1 fusion.30
  76.2 1.1 fusion.29
  79.4 1.1 fusion.26
  82.5 1.1 fusion.23
  92.9 1.1 fusion.13
  95.1 1.1 fusion.11
  97.2 1.3 fusion.9
  99.1 2.3 fusion.8
  101.4 2.3 fusion.7
  103.7 160.2 %all-reduce.4 = (bf16[27,256,256]{2,1,0:T(8,128)(2,1)}, f32[256]{0:T(256)}) all-reduce(f32[27,256,256]{2,1,0:T(8,128)} %fusion.7, f32[256]{0:T(256)} %get-tuple-element.11), channel_id=1, replica_groups=mesh['groups'=2,'zslab'=16] {'zslab'}, use_global_device_ids=true, to_apply=%region_0.2 | all-reduce | flops 1769728 | bytes 10618880 | tf_op jit(solution)/shard_map/psum | solution.py:107
  263.8 3.1 %slice_bitcast_fusion.1 = (bf16[32,64,256]{2,1,0:T(8,128)(2,1)}, bf16[32,64,256]{2,1,0:T(8,128)(2,1)}) fusion(bf16[32,2,64,256]{3,2,1,0:T(8,128)(2,1)} %all-gather.5.cloned.1.call-done), kind=kLoop, calls=%fused_computation.126 | loop fusion | bytes 4194304 | tf_op jit(solution)/shard_map/squeeze | solution.py:103
  266.9 2.4 gather_fusion.2
  269.3 1.5 fusion.148
  270.9 2.4 gather_fusion.3
  274.2 1.6 select_maximum_fusion
  275.8 1.3 pad_maximum_fusion
  277.1 2.3 fusion.152
  288.6 1.1 fusion.6
  (123 shorter events, 44.0 us)
Async XLA Ops:
  7.2 47.7 %all-gather.3.cloned.1.call-start = ((), (), s32[]{:S(2)}) async-start(), calls=%async_computation | async-start | bytes 2228224 | tf_op jit(solution)/shard_map/all_gather | solution.py:87
  9.2 3.4 %copy-start.3 = (bf16[2,8,64,256]{3,2,1,0:T(8,128)(2,1)}, bf16[2,8,64,256]{3,2,1,0:T(8,128)(2,1)S(1)}, u32[]{:S(2)}) copy-start(bf16[2,8,64,256]{3,2,1,0:T(8,128)(2,1)S(1)} %broadcast_select_fusion) | copy-start | bytes 1572868
  10.0 253.8 %all-gather.5.cloned.1.call-start = ((), (), s32[]{:S(2)}) async-start(), calls=%async_computation.1 | async-start | bytes 2228224 | tf_op jit(solution)/shard_map/all_gather | solution.py:102
  12.6 46.0 %copy-start.7 = (pred[2]{0:T(512)(128)(4,1)}, pred[2]{0:T(512)(128)(4,1)S(1)}, u32[]{:S(2)}) copy-start(pred[2]{0:T(512)(128)(4,1)S(1)} %get-tuple-element.5) | copy-start | bytes 10
  12.6 46.0 %copy-start.8 = (pred[2]{0:T(512)(128)(4,1)}, pred[2]{0:T(512)(128)(4,1)S(1)}, u32[]{:S(2)}) copy-start(pred[2]{0:T(512)(128)(4,1)S(1)} %get-tuple-element.77) | copy-start | bytes 10
  59.2 2.5 copy-start
  61.7 7.8 %copy-start.5 = (bf16[2,8,8,8,256]{4,3,2,1,0:T(8,128)(2,1)}, bf16[2,8,8,8,256]{4,3,2,1,0:T(8,128)(2,1)S(1)}, u32[]{:S(2)}) copy-start(bf16[2,8,8,8,256]{4,3,2,1,0:T(8,128)(2,1)S(1)} %get-tuple-element.42) | copy-start | bytes 1572868
  61.7 8.1 %copy-start.6 = (bf16[2,8,8,8,256]{4,3,2,1,0:T(8,128)(2,1)}, bf16[2,8,8,8,256]{4,3,2,1,0:T(8,128)(2,1)S(1)}, u32[]{:S(2)}) copy-start(bf16[2,8,8,8,256]{4,3,2,1,0:T(8,128)(2,1)S(1)} %get-tuple-element.41) | copy-start | bytes 1572868
  64.8 1.0 copy-start.4
  68.9 1.0 copy-start.9
  68.9 1.0 copy-start.11
  68.9 1.0 copy-start.12
  72.1 26.4 %copy-start.1 = (bf16[1024,256]{1,0:T(8,128)(2,1)}, bf16[1024,256]{1,0:T(8,128)(2,1)S(1)}, u32[]{:S(2)}) copy-start(bf16[1024,256]{1,0:T(8,128)(2,1)S(1)} %get-tuple-element.12) | copy-start | bytes 1572868
  283.2 1.0 copy-start.2
  287.6 1.0 copy-start.10
Sparse Core Ops, SparseCore 0:
  10.7 44.0 all-gather.2
  99.3 53.8 all-gather.4
where the time goes:
time: 300 us; the launch traced here: 297 us
  blocking collectives  160 us (53%)
  matrix products  50.5 us (17%)
  waiting for transfers between devices  41 us (14%)
  local copies, waits for them, and re-layouts  17.4 us (6%)
  between operations  14.7 us (5%)
  other arithmetic  12.8 us (4%)
    psum x1, blocking collectives, per_device(): weight_sum, bias_sum = lax.psum((weight_local, bias_local), 'zslab')  160 us
    all_gather x1, waiting for transfers between devices, per_device(): all_rims = lax.all_gather(rims, 'zslab', axis=0, tiled=True)  41 us
    dot_general x27, matrix products, weight_terms(): lax.dot_general(piece, grad_rows, (((0,), (0,)), ((), ())), preferred_ele...  30.9 us
    dot_general x27, matrix products, forward_conv(): jnp.dot(piece, weight[9 * depth + 3 * row + col], preferred_element_type=...  9.86 us
    dot_general x27, matrix products, transpose_conv(): lax.dot_general(piece, weight[9 * depth + 3 * row + col], (((1,), (1,)),...  9.72 us
    concatenate x9, other arithmetic, extend_with(): stacked = jnp.concatenate([below[:, None], planes, above[:, None]], axis=1)  7.52 us
  transfers between devices with their start and end apart: 2, of which 1 were waited for; matrix products, arithmetic and copies ran while one was open for 3% of the time, Pallas kernels for 0%

commit v1 on v0

--- a/solution.py
+++ b/solution.py
@@ -1,3 +1,5 @@
+import functools
+
 import jax
 import jax.numpy as jnp
 from jax import lax
@@ -12,14 +14,103 @@
     return jnp.pad(stacked, ((0, 0), (0, 0), (1, 1), (1, 1), (0, 0)))
 
 
-def extend_gathered(planes, bottoms, tops, links):
-    lower = links[:, 0]
-    upper = links[:, 1]
-    below = jnp.take(tops, jnp.maximum(lower, 0), axis=0)
-    above = jnp.take(bottoms, jnp.maximum(upper, 0), axis=0)
-    below = jnp.where((lower >= 0)[:, None, None], below, jnp.zeros_like(below))
-    above = jnp.where((upper >= 0)[:, None, None], above, jnp.zeros_like(above))
-    return extend_with(planes, below, above)
+def partners(size, bit):
+    return [(i, i ^ bit) for i in range(size)]
+
+
+def swap(x, size, bit):
+    return lax.ppermute(x, "zslab", partners(size, bit))
+
+
+def rotate(x, size, steps):
+    return lax.ppermute(x, "zslab", [(i, (i + 4 * steps) % size) for i in range(size)])
+
+
+def outer_gather(x, size):
+    return [x] + [rotate(x, size, k) for k in range(1, size // 4)]
+
+
+def gather_rims(rims, size):
+    rows = jnp.concatenate([rims[None], swap(rims, size, 2)[None]], axis=0)
+    return jnp.stack(outer_gather(rows, size), axis=0)
+
+
+def rim_index(link, size, me):
+    owner = jnp.maximum(link, 0) // 2
+    steps = (me // 4 - owner // 4) % (size // 4)
+    other = ((me // 2) ^ (owner // 2)) % 2
+    return (steps * 2 + other) * 2 + link % 2, (link >= 0) & (owner % 2 == me % 2)
+
+
+def pick_halos(rims, links, size):
+    me = lax.axis_index("zslab")
+    gathered = gather_rims(rims, size)
+    count = gathered.shape[0] * gathered.shape[1] * gathered.shape[2]
+    planes = gathered.reshape(count * 2, 64, gathered.shape[-1])
+
+    def pick(wanted):
+        flat = wanted.T.reshape(4)
+        place, here = rim_index(flat, size, me)
+        side = jnp.array([1, 1, 0, 0], jnp.int32)
+        taken = jnp.take(planes, jnp.where(here, place * 2 + side, 0), axis=0)
+        return jnp.where(here[:, None, None], taken, jnp.zeros_like(taken))
+
+    mine = pick(links)
+    theirs = pick(swap(links, size, 1))
+    return mine + swap(theirs, size, 1)
+
+
+def take_rows(x, place, rows):
+    return lax.dynamic_slice_in_dim(x, place * rows, rows, axis=0)
+
+
+def scatter_inner(x, size, bit):
+    me = lax.axis_index("zslab")
+    mine = (me // bit) % 2
+    half = x.shape[0] // 2
+    got = swap(take_rows(x, 1 - mine, half), size, bit)
+    return (take_rows(x, mine, half).astype(jnp.float32) + got.astype(jnp.float32)).astype(jnp.bfloat16)
+
+
+def scatter_outer(x, size):
+    me = lax.axis_index("zslab")
+    outer = size // 4
+    place = me // 4
+    rows = x.shape[0] // outer
+    total = take_rows(x, place, rows).astype(jnp.float32)
+    for k in range(1, outer):
+        got = rotate(take_rows(x, (place + k) % outer, rows), size, k)
+        total = total + got.astype(jnp.float32)
+    return total.astype(jnp.bfloat16)
+
+
+def gather_inner(x, size, bit):
+    me = lax.axis_index("zslab")
+    mine = (me // bit) % 2
+    got = swap(x, size, bit)
+    return jnp.where(mine == 0, jnp.concatenate([x, got]), jnp.concatenate([got, x]))
+
+
+def gather_outer(x, size):
+    me = lax.axis_index("zslab")
+    outer = size // 4
+    place = me // 4
+    rows = x.shape[0]
+    whole = jnp.zeros((outer * rows, x.shape[1]), x.dtype)
+    for k, block in enumerate(outer_gather(x, size)):
+        whole = lax.dynamic_update_slice_in_dim(whole, block, ((place - k) % outer) * rows, axis=0)
+    return whole
+
+
+def sum_terms(terms, size):
+    part = scatter_inner(terms, size, 1)
+    split = part.shape[0] * 16 // 27
+    first, second = part[:split], part[split:]
+    first = scatter_outer(scatter_inner(first, size, 2), size)
+    second = scatter_inner(scatter_outer(second, size), size, 2)
+    first = gather_inner(gather_outer(first, size), size, 2)
+    second = gather_outer(gather_inner(second, size, 2), size)
+    return gather_inner(jnp.concatenate([first, second]), size, 1)
 
 
 def forward_conv(extended, weight):
@@ -78,14 +169,14 @@
     return jnp.stack(terms, axis=0)
 
 
-def per_device(feats, voxmask, links, weight, bias, cotangent):
+def per_device(size, feats, voxmask, links, weight, bias, cotangent):
     count = feats.shape[0]
     width = feats.shape[3]
     keep = (voxmask == 1).reshape(count, 8, 64, 1)
     masked = jnp.where(keep, feats, jnp.zeros_like(feats))
     rims = jnp.stack([masked[:, 0], masked[:, 7]], axis=1)
-    all_rims = lax.all_gather(rims, "zslab", axis=0, tiled=True)
-    extended = extend_gathered(masked, all_rims[:, 0], all_rims[:, 1], links)
+    halos = pick_halos(rims, links, size)
+    extended = extend_with(masked, halos[:2], halos[2:])
     pre = forward_conv(extended, weight) + bias[None, :]
     keep_rows = keep.reshape(count * 512, 1)
     sigma = jax.nn.sigmoid(pre)
@@ -99,13 +190,14 @@
     ).astype(jnp.bfloat16)
     grad_planes = grad_pre.reshape(count, 8, 64, width)
     grad_edges = jnp.stack([grad_planes[:, 0], grad_planes[:, 7]], axis=1)
-    all_grad_edges = lax.all_gather(grad_edges, "zslab", axis=0, tiled=True)
-    grad_ext = extend_gathered(grad_planes, all_grad_edges[:, 0], all_grad_edges[:, 1], links)
+    grad_halos = pick_halos(grad_edges, links, size)
+    grad_ext = extend_with(grad_planes, grad_halos[:2], grad_halos[2:])
     grad_feats = jnp.where(keep_rows, transpose_conv(grad_ext, weight), 0.0).astype(jnp.bfloat16)
     weight_local = weight_terms(extended, grad_pre)
     bias_local = jnp.sum(grad_pre.astype(jnp.float32), axis=0)
-    weight_sum, bias_sum = lax.psum((weight_local, bias_local), "zslab")
-    grad_weight = weight_sum.astype(jnp.bfloat16)
+    bias_sum = lax.psum(bias_local, "zslab")
+    terms = weight_local.reshape(-1, width).astype(jnp.bfloat16)
+    grad_weight = sum_terms(terms, size).reshape(weight_local.shape)
     return (
         output.reshape(count, 8, 64, width),
         grad_feats.reshape(count, 8, 64, width),
@@ -116,7 +208,7 @@
 
 def solution(mesh):
     return jax.shard_map(
-        per_device,
+        functools.partial(per_device, mesh.shape["zslab"]),
         mesh=mesh,
         in_specs=(
             P(("groups", "zslab"), None, None, None),

time: 300 us -> 227 us (0.76)
  the two profiles are of different devices: /device:TPU:0 before, /device:TPU:13 now
where the time goes in v1:
time: 227 us; the launch traced here: 226 us
  waiting for transfers between devices  103 us (45%)
  starting transfers between devices  32.3 us (14%)
  matrix products  29.1 us (13%)
  blocking collectives  22.4 us (10%)
  local copies, waits for them, and re-layouts  22.2 us (10%)
  other arithmetic  15.8 us (7%)
    ppermute x18, waiting for transfers between devices, rotate(): lax.ppermute(x, 'zslab', [(i, (i + 4 * steps) % size) for i in range(size)])  88.7 us
    ppermute x18, starting transfers between devices, rotate(): lax.ppermute(x, 'zslab', [(i, (i + 4 * steps) % size) for i in range(size)])  23.2 us
    psum x1, blocking collectives, per_device(): bias_sum = lax.psum(bias_local, 'zslab')  22.4 us
    ppermute x11, waiting for transfers between devices, swap(): return lax.ppermute(x, 'zslab', partners(size, bit))  13.8 us
    dot_general x27, matrix products, forward_conv(): jnp.dot(piece, weight[9 * depth + 3 * row + col], preferred_element_type=...  9.83 us
    dot_general x27, matrix products, transpose_conv(): lax.dot_general(piece, weight[9 * depth + 3 * row + col], (((1,), (1,)),...  9.72 us
    dot_general x27, matrix products, weight_terms(): lax.dot_general(piece, grad_rows, (((0,), (0,)), ((), ())), preferred_ele...  9.57 us
    ppermute x11, starting transfers between devices, swap(): return lax.ppermute(x, 'zslab', partners(size, bit))  9.14 us
  transfers between devices with their start and end apart: 29, of which 21 were waited for; matrix products, arithmetic and copies ran while one was open for 12% of the time, Pallas kernels for 0%

profile of v1, /device:TPU:13, one launch (start us, length us, event | category | flops | bytes accessed | tf_op | source)
XLA Modules:
  0.0 226.0 jit_solution(14437247794703850152)
XLA Ops:
  6.0 2.0 collective-permute-done
  14.3 15.9 %collective-permute-done.2 = bf16[2,2,2,64,256]{4,3,2,1,0:T(8,128)(2,1)S(1)} collective-permute-done((bf16[2,2,2,64,256]{4,3,2,1,0:T(8,128)(2,1)S(1)}, bf16[2,2,2,64,256]{4,3,2,1,0:T(8,128)(2,1)S(1)}, u32[]{:S(2)}, u32[]{:S(2)}) %collective-permute-start.2) | collective-permute-done | bytes 262176 | tf_op jit(solution)/shard_map/ppermute | solution.py:26
  30.3 3.8 %collective-permute-done.3 = bf16[2,2,2,64,256]{4,3,2,1,0:T(8,128)(2,1)S(1)} collective-permute-done((bf16[2,2,2,64,256]{4,3,2,1,0:T(8,128)(2,1)S(1)}, bf16[2,2,2,64,256]{4,3,2,1,0:T(8,128)(2,1)S(1)}, u32[]{:S(2)}, u32[]{:S(2)}) %collective-permute-start.3) | collective-permute-done | bytes 262176 | tf_op jit(solution)/shard_map/ppermute | solution.py:26
  37.7 2.5 %fusion.195 = (bf16[2,8,8,8,256]{4,3,2,1,0:T(8,128)(2,1)S(1)}, bf16[2,8,8,8,256]{4,3,2,1,0:T(8,128)(2,1)S(1)}, bf16[2,8,8,8,256]{4,3,2,1,0:T(8,128)(2,1)S(1)}, b...) fusion(bf16[2,10,10,10,256]{4,3,2,1,0:T(8,128)(2,1)S(1)} %selec, ...), kind=kLoop, calls=%fused_computation.379 | loop fusion | bytes 19922944 | tf_op jit(solution)/shard_map/slice | solution.py:123
  50.5 2.1 convert_reduce_fusion
  62.0 4.5 %collective-permute-done.6 = bf16[2,2,64,256]{3,2,1,0:T(8,128)(2,1)S(1)} collective-permute-done((bf16[2,2,64,256]{3,2,1,0:T(8,128)(2,1)S(1)}, bf16[2,2,64,256]{3,2,1,0:T(8,128)(2,1)S(1)}, u32[]{:S(2)}, u32[]{:S(2)}) %collective-permute-start.6) | collective-permute-done | bytes 131104 | tf_op jit(solution)/shard_map/ppermute | solution.py:22
  73.6 15.0 %collective-permute-done.8 = bf16[2,2,2,64,256]{4,3,2,1,0:T(8,128)(2,1)S(1)} collective-permute-done((bf16[2,2,2,64,256]{4,3,2,1,0:T(8,128)(2,1)S(1)}, bf16[2,2,2,64,256]{4,3,2,1,0:T(8,128)(2,1)S(1)}, u32[]{:S(2)}, u32[]{:S(2)}) %collective-permute-start.8) | collective-permute-done | bytes 262176 | tf_op jit(solution)/shard_map/ppermute | solution.py:26
  88.6 3.0 %collective-permute-done.9 = bf16[2,2,2,64,256]{4,3,2,1,0:T(8,128)(2,1)S(1)} collective-permute-done((bf16[2,2,2,64,256]{4,3,2,1,0:T(8,128)(2,1)S(1)}, bf16[2,2,2,64,256]{4,3,2,1,0:T(8,128)(2,1)S(1)}, u32[]{:S(2)}, u32[]{:S(2)}) %collective-permute-start.9) | collective-permute-done | bytes 262176 | tf_op jit(solution)/shard_map/ppermute | solution.py:26
  92.7 2.4 %gather_fusion.3 = bf16[4,64,256]{2,1,0:T(8,128)(2,1)} fusion(bf16[32,64,256]{2,1,0:T(8,128)(2,1)} %bitcast.532, s32[1024]{0:T(1024)S(1)} %pad_clamp_fusion), kind=kCustom, calls=%fused_computation.3.clone | custom fusion | bytes 262160 | tf_op jit(solution)/shard_map/jit(_take)/gather | solution.py:55
  97.3 2.9 %constant_dynamic-slice_fusion.8 = bf16[3456,256]{1,0:T(8,128)(2,1)} fusion(bf16[6912,256]{1,0:T(8,128)(2,1)} %bitcast.450, s32[]{:T(128)S(6)} %select_n.357), kind=kLoop, calls=%fused_computation.315 | loop fusion | bytes 3538948 | tf_op jit(solution)/shard_map/dynamic_slice | solution.py:64
  100.2 22.4 %psum.7 = f32[256]{0:T(256)} all-reduce(f32[256]{0:T(256)} %get-tuple-element.5), channel_id=1, replica_groups=mesh['groups'=2,'zslab'=16] {'zslab'}, use_global_device_ids=true, to_apply=%region_1.3 | all-reduce | flops 256 | bytes 2048 | tf_op jit(solution)/shard_map/psum | solution.py:198
  122.6 2.4 %gather_fusion.2 = bf16[4,64,256]{2,1,0:T(8,128)(2,1)} fusion(bf16[32,64,256]{2,1,0:T(8,128)(2,1)} %bitcast.533, s32[1024]{0:T(1024)S(1)} %pad_clamp_fusion.1), kind=kCustom, calls=%fused_computation.2.clone | custom fusion | bytes 262160 | tf_op jit(solution)/shard_map/jit(_take)/gather | solution.py:55
  129.0 2.3 %fusion.193 = (bf16[2,8,8,8,256]{4,3,2,1,0:T(8,128)(2,1)S(1)}, bf16[2,8,8,8,256]{4,3,2,1,0:T(8,128)(2,1)S(1)}, bf16[2,8,8,8,256]{4,3,2,1,0:T(8,128)(2,1)S(1)}, b...) fusion(bf16[2,10,10,10,256]{4,3,2,1,0:T(8,128)(2,1)S(1)} %selec, ...), kind=kLoop, calls=%fused_computation.377 | loop fusion | bytes 19922944 | tf_op jit(solution)/shard_map/slice | solution.py:139
  138.5 2.0 add_convert_fusion
  141.6 8.2 %collective-permute-start.21 = (bf16[352,256]{1,0:T(8,128)(2,1)S(1)}, bf16[352,256]{1,0:T(8,128)(2,1)S(1)}, u32[]{:S(2)}, u32[]{:S(2)}) collective-permute-start(bf16[352,256]{1,0:T(8,128)(2,1)S(1)} %get-tuple-element.68), channel_id=1, source_target_pairs={{0,8},{1,9},{2,10},{3,11},{4,12},{5,13},{6,14},{7,15},{8,0},{9,1},... | collective-permute-start | bytes 540680 | tf_op jit(solution)/shard_map/ppermute | solution.py:26
  150.9 5.0 %collective-permute-done.21 = bf16[352,256]{1,0:T(8,128)(2,1)S(1)} collective-permute-done((bf16[352,256]{1,0:T(8,128)(2,1)S(1)}, bf16[352,256]{1,0:T(8,128)(2,1)S(1)}, u32[]{:S(2)}, u32[]{:S(2)}) %collective-permute-start.21) | collective-permute-done | bytes 180256 | tf_op jit(solution)/shard_map/ppermute | solution.py:26
  155.8 8.9 %collective-permute-done.22 = bf16[352,256]{1,0:T(8,128)(2,1)S(1)} collective-permute-done((bf16[352,256]{1,0:T(8,128)(2,1)S(1)}, bf16[352,256]{1,0:T(8,128)(2,1)S(1)}, u32[]{:S(2)}, u32[]{:S(2)}) %collective-permute-start.22) | collective-permute-done | bytes 180256 | tf_op jit(solution)/shard_map/ppermute | solution.py:26
  164.9 2.3 %collective-permute-start.23 = (bf16[176,256]{1,0:T(8,128)(2,1)S(1)}, bf16[176,256]{1,0:T(8,128)(2,1)S(1)}, u32[]{:S(2)}, u32[]{:S(2)}) collective-permute-start(bf16[176,256]{1,0:T(8,128)(2,1)S(1)} %constant_dynamic-slice_fusion), channel_id=1, source_target_pairs={{0,2},{1,3},{2,0},{3,1},{4,6},{5,7},{6,4},{7,5},{8,10},{9,11},{10,... | collective-permute-start | bytes 270344 | tf_op jit(solution)/shard_map/ppermute | solution.py:22
  171.8 6.4 %collective-permute-done.14 = bf16[256,256]{1,0:T(8,128)(2,1)S(1)} collective-permute-done((bf16[256,256]{1,0:T(8,128)(2,1)S(1)}, bf16[256,256]{1,0:T(8,128)(2,1)S(1)}, u32[]{:S(2)}, u32[]{:S(2)}) %collective-permute-start.14) | collective-permute-done | bytes 131104 | tf_op jit(solution)/shard_map/ppermute | solution.py:26
  182.9 2.8 %collective-permute-start.26 = (bf16[352,256]{1,0:T(8,128)(2,1)S(1)}, bf16[352,256]{1,0:T(8,128)(2,1)S(1)}, u32[]{:S(2)}, u32[]{:S(2)}) collective-permute-start(bf16[352,256]{1,0:T(8,128)(2,1)S(1)} %get-tuple-element.10), channel_id=1, source_target_pairs={{0,8},{1,9},{2,10},{3,11},{4,12},{5,13},{6,14},{7,15},{8,0},{9,1},... | collective-permute-start | bytes 540680 | tf_op jit(solution)/shard_map/ppermute | solution.py:26
  186.7 18.9 %collective-permute-done.18 = bf16[256,256]{1,0:T(8,128)(2,1)S(1)} collective-permute-done((bf16[256,256]{1,0:T(8,128)(2,1)S(1)}, bf16[256,256]{1,0:T(8,128)(2,1)S(1)}, u32[]{:S(2)}, u32[]{:S(2)}) %collective-permute-start.18) | collective-permute-done | bytes 131104 | tf_op jit(solution)/shard_map/ppermute | solution.py:26
  206.5 5.2 %collective-permute-done.27 = bf16[352,256]{1,0:T(8,128)(2,1)S(1)} collective-permute-done((bf16[352,256]{1,0:T(8,128)(2,1)S(1)}, bf16[352,256]{1,0:T(8,128)(2,1)S(1)}, u32[]{:S(2)}, u32[]{:S(2)}) %collective-permute-start.27) | collective-permute-done | bytes 180256 | tf_op jit(solution)/shard_map/ppermute | solution.py:26
  211.8 6.9 %collective-permute-done.19 = bf16[1024,256]{1,0:T(8,128)(2,1)S(1)} collective-permute-done((bf16[1024,256]{1,0:T(8,128)(2,1)S(1)}, bf16[1024,256]{1,0:T(8,128)(2,1)S(1)}, u32[]{:S(2)}, u32[]{:S(2)}) %collective-permute-start.19) | collective-permute-done | bytes 524320 | tf_op jit(solution)/shard_map/ppermute | solution.py:22
  223.8 2.2 maximum_select_fusion
  (210 shorter events, 74.3 us)
Async XLA Ops:
  8.0 6.3 %collective-permute-start.1 = (bf16[2,2,2,64,256]{4,3,2,1,0:T(8,128)(2,1)S(1)}, bf16[2,2,2,64,256]{4,3,2,1,0:T(8,128)(2,1)S(1)}, u32[]{:S(2)}, u32[]{:S(2)}) collective-permute-start(bf16[2,2,2,64,256]{4,3,2,1,0:T(8,128)(2,1)S(1)} %get-tuple-element.83), channel_id=1, source_target_pairs={{0,4},{1,5},{2,6},{3,7},{4,8},{5,9},{6,10},{7,11},{8,12},{9,13},{1... | collective-permute-start | bytes 786440 | tf_op jit(solution)/shard_map/ppermute | solution.py:26
  9.4 20.9 %collective-permute-start.2 = (bf16[2,2,2,64,256]{4,3,2,1,0:T(8,128)(2,1)S(1)}, bf16[2,2,2,64,256]{4,3,2,1,0:T(8,128)(2,1)S(1)}, u32[]{:S(2)}, u32[]{:S(2)}) collective-permute-start(bf16[2,2,2,64,256]{4,3,2,1,0:T(8,128)(2,1)S(1)} %get-tuple-element.83), channel_id=1, source_target_pairs={{0,8},{1,9},{2,10},{3,11},{4,12},{5,13},{6,14},{7,15},{8,0},{9,1},... | collective-permute-start | bytes 786440 | tf_op jit(solution)/shard_map/ppermute | solution.py:26
  10.5 23.6 %collective-permute-start.3 = (bf16[2,2,2,64,256]{4,3,2,1,0:T(8,128)(2,1)S(1)}, bf16[2,2,2,64,256]{4,3,2,1,0:T(8,128)(2,1)S(1)}, u32[]{:S(2)}, u32[]{:S(2)}) collective-permute-start(bf16[2,2,2,64,256]{4,3,2,1,0:T(8,128)(2,1)S(1)} %get-tuple-element.83), channel_id=1, source_target_pairs={{0,12},{1,13},{2,14},{3,15},{4,0},{5,1},{6,2},{7,3},{8,4},{9,5},{1... | collective-permute-start | bytes 786440 | tf_op jit(solution)/shard_map/ppermute | solution.py:26
  61.4 5.2 %collective-permute-start.6 = (bf16[2,2,64,256]{3,2,1,0:T(8,128)(2,1)S(1)}, bf16[2,2,64,256]{3,2,1,0:T(8,128)(2,1)S(1)}, u32[]{:S(2)}, u32[]{:S(2)}) collective-permute-start(bf16[2,2,64,256]{3,2,1,0:T(8,128)(2,1)S(1)} %get-tuple-element.87), channel_id=1, source_target_pairs={{0,2},{1,3},{2,0},{3,1},{4,6},{5,7},{6,4},{7,5},{8,10},{9,11},{10,... | collective-permute-start | bytes 393224 | tf_op jit(solution)/shard_map/ppermute | solution.py:22
  66.6 7.1 %collective-permute-start.7 = (bf16[2,2,2,64,256]{4,3,2,1,0:T(8,128)(2,1)S(1)}, bf16[2,2,2,64,256]{4,3,2,1,0:T(8,128)(2,1)S(1)}, u32[]{:S(2)}, u32[]{:S(2)}) collective-permute-start(bf16[2,2,2,64,256]{4,3,2,1,0:T(8,128)(2,1)S(1)} %get-tuple-element.81), channel_id=1, source_target_pairs={{0,4},{1,5},{2,6},{3,7},{4,8},{5,9},{6,10},{7,11},{8,12},{9,13},{1... | collective-permute-start | bytes 786440 | tf_op jit(solution)/shard_map/ppermute | solution.py:26
  66.6 22.0 %collective-permute-start.8 = (bf16[2,2,2,64,256]{4,3,2,1,0:T(8,128)(2,1)S(1)}, bf16[2,2,2,64,256]{4,3,2,1,0:T(8,128)(2,1)S(1)}, u32[]{:S(2)}, u32[]{:S(2)}) collective-permute-start(bf16[2,2,2,64,256]{4,3,2,1,0:T(8,128)(2,1)S(1)} %get-tuple-element.81), channel_id=1, source_target_pairs={{0,8},{1,9},{2,10},{3,11},{4,12},{5,13},{6,14},{7,15},{8,0},{9,1},... | collective-permute-start | bytes 786440 | tf_op jit(solution)/shard_map/ppermute | solution.py:26
  68.0 23.6 %collective-permute-start.9 = (bf16[2,2,2,64,256]{4,3,2,1,0:T(8,128)(2,1)S(1)}, bf16[2,2,2,64,256]{4,3,2,1,0:T(8,128)(2,1)S(1)}, u32[]{:S(2)}, u32[]{:S(2)}) collective-permute-start(bf16[2,2,2,64,256]{4,3,2,1,0:T(8,128)(2,1)S(1)} %get-tuple-element.81), channel_id=1, source_target_pairs={{0,12},{1,13},{2,14},{3,15},{4,0},{5,1},{6,2},{7,3},{8,4},{9,5},{1... | collective-permute-start | bytes 786440 | tf_op jit(solution)/shard_map/ppermute | solution.py:26
  96.8 28.2 %collective-permute-start.10 = (bf16[4,64,256]{2,1,0:T(8,128)(2,1)}, bf16[4,64,256]{2,1,0:T(8,128)(2,1)}, u32[]{:S(2)}, u32[]{:S(2)}) collective-permute-start(bf16[4,64,256]{2,1,0:T(8,128)(2,1)} %select_select_fusion), channel_id=1, source_target_pairs={{0,1},{1,0},{2,3},{3,2},{4,5},{5,4},{6,7},{7,6},{8,9},{9,8},{10,11... | collective-permute-start | bytes 393224 | tf_op jit(solution)/shard_map/ppermute | solution.py:22
  100.2 37.3 %collective-permute-start.11 = (bf16[3456,256]{1,0:T(8,128)(2,1)}, bf16[3456,256]{1,0:T(8,128)(2,1)}, u32[]{:S(2)}, u32[]{:S(2)}) collective-permute-start(bf16[3456,256]{1,0:T(8,128)(2,1)} %constant_dynamic-slice_fusion.8), channel_id=1, source_target_pairs={{0,1},{1,0},{2,3},{3,2},{4,5},{5,4},{6,7},{7,6},{8,9},{9,8},{10,11... | collective-permute-start | bytes 5308424 | tf_op jit(solution)/shard_map/ppermute | solution.py:22
  140.6 26.6 %collective-permute-start.12 = (bf16[1024,256]{1,0:T(8,128)(2,1)S(1)}, bf16[1024,256]{1,0:T(8,128)(2,1)S(1)}, u32[]{:S(2)}, u32[]{:S(2)}) collective-permute-start(bf16[1024,256]{1,0:T(8,128)(2,1)S(1)} %constant_dynamic-slice_fusion.7), channel_id=1, source_target_pairs={{0,2},{1,3},{2,0},{3,1},{4,6},{5,7},{6,4},{7,5},{8,10},{9,11},{10,... | collective-permute-start | bytes 1572872 | tf_op jit(solution)/shard_map/ppermute | solution.py:22
  141.4 9.5 %collective-permute-start.20 = (bf16[352,256]{1,0:T(8,128)(2,1)S(1)}, bf16[352,256]{1,0:T(8,128)(2,1)S(1)}, u32[]{:S(2)}, u32[]{:S(2)}) collective-permute-start(bf16[352,256]{1,0:T(8,128)(2,1)S(1)} %get-tuple-element.66), channel_id=1, source_target_pairs={{0,4},{1,5},{2,6},{3,7},{4,8},{5,9},{6,10},{7,11},{8,12},{9,13},{1... | collective-permute-start | bytes 540680 | tf_op jit(solution)/shard_map/ppermute | solution.py:26
  141.6 14.3 %collective-permute-start.21 = (bf16[352,256]{1,0:T(8,128)(2,1)S(1)}, bf16[352,256]{1,0:T(8,128)(2,1)S(1)}, u32[]{:S(2)}, u32[]{:S(2)}) collective-permute-start(bf16[352,256]{1,0:T(8,128)(2,1)S(1)} %get-tuple-element.68), channel_id=1, source_target_pairs={{0,8},{1,9},{2,10},{3,11},{4,12},{5,13},{6,14},{7,15},{8,0},{9,1},... | collective-permute-start | bytes 540680 | tf_op jit(solution)/shard_map/ppermute | solution.py:26
  149.8 15.0 %collective-permute-start.22 = (bf16[352,256]{1,0:T(8,128)(2,1)S(1)}, bf16[352,256]{1,0:T(8,128)(2,1)S(1)}, u32[]{:S(2)}, u32[]{:S(2)}) collective-permute-start(bf16[352,256]{1,0:T(8,128)(2,1)S(1)} %get-tuple-element.67), channel_id=1, source_target_pairs={{0,12},{1,13},{2,14},{3,15},{4,0},{5,1},{6,2},{7,3},{8,4},{9,5},{1... | collective-permute-start | bytes 540680 | tf_op jit(solution)/shard_map/ppermute | solution.py:26
  167.5 10.7 %collective-permute-start.14 = (bf16[256,256]{1,0:T(8,128)(2,1)S(1)}, bf16[256,256]{1,0:T(8,128)(2,1)S(1)}, u32[]{:S(2)}, u32[]{:S(2)}) collective-permute-start(bf16[256,256]{1,0:T(8,128)(2,1)S(1)} %get-tuple-element.71), channel_id=1, source_target_pairs={{0,8},{1,9},{2,10},{3,11},{4,12},{5,13},{6,14},{7,15},{8,0},{9,1},... | collective-permute-start | bytes 393224 | tf_op jit(solution)/shard_map/ppermute | solution.py:26
  167.6 11.9 %collective-permute-start.15 = (bf16[256,256]{1,0:T(8,128)(2,1)S(1)}, bf16[256,256]{1,0:T(8,128)(2,1)S(1)}, u32[]{:S(2)}, u32[]{:S(2)}) collective-permute-start(bf16[256,256]{1,0:T(8,128)(2,1)S(1)} %get-tuple-element.70), channel_id=1, source_target_pairs={{0,12},{1,13},{2,14},{3,15},{4,0},{5,1},{6,2},{7,3},{8,4},{9,5},{1... | collective-permute-start | bytes 393224 | tf_op jit(solution)/shard_map/ppermute | solution.py:26
  169.2 12.8 %collective-permute-start.24 = (bf16[176,256]{1,0:T(8,128)(2,1)S(1)}, bf16[176,256]{1,0:T(8,128)(2,1)S(1)}, u32[]{:S(2)}, u32[]{:S(2)}) collective-permute-start(bf16[176,256]{1,0:T(8,128)(2,1)S(1)} %add_convert_fusion.4), channel_id=1, source_target_pairs={{0,2},{1,3},{2,0},{3,1},{4,6},{5,7},{6,4},{7,5},{8,10},{9,11},{10,... | collective-permute-start | bytes 270344 | tf_op jit(solution)/shard_map/ppermute | solution.py:22
  179.6 6.1 %collective-permute-start.16 = (bf16[256,256]{1,0:T(8,128)(2,1)S(1)}, bf16[256,256]{1,0:T(8,128)(2,1)S(1)}, u32[]{:S(2)}, u32[]{:S(2)}) collective-permute-start(bf16[256,256]{1,0:T(8,128)(2,1)S(1)} %get-tuple-element.8), channel_id=1, source_target_pairs={{0,4},{1,5},{2,6},{3,7},{4,8},{5,9},{6,10},{7,11},{8,12},{9,13},{1... | collective-permute-start | bytes 393224 | tf_op jit(solution)/shard_map/ppermute | solution.py:26
  180.0 6.6 %collective-permute-start.17 = (bf16[256,256]{1,0:T(8,128)(2,1)S(1)}, bf16[256,256]{1,0:T(8,128)(2,1)S(1)}, u32[]{:S(2)}, u32[]{:S(2)}) collective-permute-start(bf16[256,256]{1,0:T(8,128)(2,1)S(1)} %get-tuple-element.8), channel_id=1, source_target_pairs={{0,8},{1,9},{2,10},{3,11},{4,12},{5,13},{6,14},{7,15},{8,0},{9,1},... | collective-permute-start | bytes 393224 | tf_op jit(solution)/shard_map/ppermute | solution.py:26
  182.1 24.3 %collective-permute-start.25 = (bf16[352,256]{1,0:T(8,128)(2,1)S(1)}, bf16[352,256]{1,0:T(8,128)(2,1)S(1)}, u32[]{:S(2)}, u32[]{:S(2)}) collective-permute-start(bf16[352,256]{1,0:T(8,128)(2,1)S(1)} %get-tuple-element.10), channel_id=1, source_target_pairs={{0,4},{1,5},{2,6},{3,7},{4,8},{5,9},{6,10},{7,11},{8,12},{9,13},{1... | collective-permute-start | bytes 540680 | tf_op jit(solution)/shard_map/ppermute | solution.py:26
  182.9 23.6 %collective-permute-start.26 = (bf16[352,256]{1,0:T(8,128)(2,1)S(1)}, bf16[352,256]{1,0:T(8,128)(2,1)S(1)}, u32[]{:S(2)}, u32[]{:S(2)}) collective-permute-start(bf16[352,256]{1,0:T(8,128)(2,1)S(1)} %get-tuple-element.10), channel_id=1, source_target_pairs={{0,8},{1,9},{2,10},{3,11},{4,12},{5,13},{6,14},{7,15},{8,0},{9,1},... | collective-permute-start | bytes 540680 | tf_op jit(solution)/shard_map/ppermute | solution.py:26
  185.7 19.8 %collective-permute-start.18 = (bf16[256,256]{1,0:T(8,128)(2,1)S(1)}, bf16[256,256]{1,0:T(8,128)(2,1)S(1)}, u32[]{:S(2)}, u32[]{:S(2)}) collective-permute-start(bf16[256,256]{1,0:T(8,128)(2,1)S(1)} %get-tuple-element.8), channel_id=1, source_target_pairs={{0,12},{1,13},{2,14},{3,15},{4,0},{5,1},{6,2},{7,3},{8,4},{9,5},{1... | collective-permute-start | bytes 393224 | tf_op jit(solution)/shard_map/ppermute | solution.py:26
  205.6 13.1 %collective-permute-start.19 = (bf16[1024,256]{1,0:T(8,128)(2,1)S(1)}, bf16[1024,256]{1,0:T(8,128)(2,1)S(1)}, u32[]{:S(2)}, u32[]{:S(2)}) collective-permute-start(bf16[1024,256]{1,0:T(8,128)(2,1)S(1)} %constant_dynamic-update-slice_fusion.4), channel_id=1, source_target_pairs={{0,2},{1,3},{2,0},{3,1},{4,6},{5,7},{6,4},{7,5},{8,10},{9,11},{10,... | collective-permute-start | bytes 1572872 | tf_op jit(solution)/shard_map/ppermute | solution.py:22
  206.1 5.6 %collective-permute-start.27 = (bf16[352,256]{1,0:T(8,128)(2,1)S(1)}, bf16[352,256]{1,0:T(8,128)(2,1)S(1)}, u32[]{:S(2)}, u32[]{:S(2)}) collective-permute-start(bf16[352,256]{1,0:T(8,128)(2,1)S(1)} %get-tuple-element.10), channel_id=1, source_target_pairs={{0,12},{1,13},{2,14},{3,15},{4,0},{5,1},{6,2},{7,3},{8,4},{9,5},{1... | collective-permute-start | bytes 540680 | tf_op jit(solution)/shard_map/ppermute | solution.py:26
  219.0 4.7 %collective-permute-start.28 = (bf16[3456,256]{1,0:T(8,128)(2,1)S(1)}, bf16[3456,256]{1,0:T(8,128)(2,1)S(1)}, u32[]{:S(2)}, u32[]{:S(2)}) collective-permute-start(bf16[3456,256]{1,0:T(8,128)(2,1)S(1)} %pad_maximum_fusion), channel_id=1, source_target_pairs={{0,1},{1,0},{2,3},{3,2},{4,5},{5,4},{6,7},{7,6},{8,9},{9,8},{10,11... | collective-permute-start | bytes 5308424 | tf_op jit(solution)/shard_map/ppermute | solution.py:22
  (21 other events, 130.9 us)

commit v2 on v0

v2 whole, which is shorter than its diff:
```python
import functools

import jax
import jax.numpy as jnp
from jax import lax
from jax.experimental import pallas as pl
from jax.experimental.pallas import tpu as pltpu
from jax.sharding import PartitionSpec as P

VMEM_LIMIT = 56 * 1024 * 1024
SIDES = (1, 1, 0, 0)


def params():
    return pltpu.CompilerParams(vmem_limit_bytes=VMEM_LIMIT)


def cost(flops, bytes_accessed):
    return pl.CostEstimate(flops=flops, bytes_accessed=bytes_accessed, transcendentals=0)


def swap(x, size, bit):
    return lax.ppermute(x, "zslab", [(i, i ^ bit) for i in range(size)])


def rotate(x, size, steps):
    return lax.ppermute(x, "zslab", [(i, (i + 4 * steps) % size) for i in range(size)])


def wanted(links):
    return links.T.reshape(4)


def route(links, size):
    me = lax.axis_index("zslab")
    side = jnp.array(SIDES, jnp.int32)
    places = []
    for steps in range(size // 4):
        want = wanted(links if steps == 0 else rotate(links, size, -steps))
        owner = jnp.maximum(want, 0) // 2
        group = ((owner % 2) ^ (me % 2)) * 2 + (((owner // 2) % 2) ^ ((me // 2) % 2))
        places.append((group * 2 + jnp.maximum(want, 0) % 2) * 2 + side)
    return places


def fetch_halos(rims, links, places, size):
    me = lax.axis_index("zslab")
    pair = jnp.concatenate([rims, swap(rims, size, 2)], axis=0)
    group = jnp.concatenate([pair, swap(pair, size, 1)], axis=0)
    planes = group.reshape(16, 64, rims.shape[-1])
    outer = size // 4
    want = wanted(links)
    step = (me // 4 - jnp.maximum(want, 0) // 8) % outer
    halos = jnp.zeros((4, 64, rims.shape[-1]), rims.dtype)
    for steps in range(outer):
        got = jnp.take(planes, places[steps], axis=0)
        if steps:
            got = rotate(got, size, steps)
        here = (step == steps) & (want >= 0)
        halos = jnp.where(here[:, None, None], got, halos)
    return halos


def take_rows(x, place, rows):
    return lax.dynamic_slice_in_dim(x, place * rows, rows, axis=0)


def scatter_inner(x, size):
    me = lax.axis_index("zslab")
    mine = (me // 2) % 2
    half = x.shape[0] // 2
    got = swap(take_rows(x, 1 - mine, half), size, 2)
    return (take_rows(x, mine, half).astype(jnp.float32) + got.astype(jnp.float32)).astype(jnp.bfloat16)


def scatter_outer(x, size):
    place = lax.axis_index("zslab") // 4
    outer = size // 4
    rows = x.shape[0] // outer
    total = take_rows(x, place, rows).astype(jnp.float32)
    for steps in range(1, outer):
        got = rotate(take_rows(x, (place + steps) % outer, rows), size, steps)
        total = total + got.astype(jnp.float32)
    return total.astype(jnp.bfloat16)


def gather_outer(x, size):
    place = lax.axis_index("zslab") // 4
    outer = size // 4
    rows = x.shape[0]
    whole = jnp.zeros((outer * rows, x.shape[1]), x.dtype)
    for steps in range(outer):
        block = x if steps == 0 else rotate(x, size, steps)
        whole = lax.dynamic_update_slice_in_dim(whole, block, ((place - steps) % outer) * rows, axis=0)
    return whole


def gather_inner(x, size):
    mine = (lax.axis_index("zslab") // 2) % 2
    got = swap(x, size, 2)
    return jnp.where(mine == 0, jnp.concatenate([x, got]), jnp.concatenate([got, x]))


def shifted(x, rows, cols):
    count = x.shape[0]
    index = lax.broadcasted_iota(jnp.int32, x.shape, 0)
    row = (index // 8) % 8 + rows
    col = index % 8 + cols
    move = 8 * rows + cols
    if move:
        x = pltpu.roll(x, (-move) % count, 0)
    inside = (row >= 0) & (row < 8) & (col >= 0) & (col < 8)
    return jnp.where(inside, x, 0.0)


def shifted_lanes(x, rows, cols):
    index = lax.broadcasted_iota(jnp.int32, x.shape, 1)
    row = (index // 8) % 8 + rows
    col = index % 8 + cols
    move = 8 * rows + cols
    if move:
        x = pltpu.roll(x, (-move) % x.shape[1], 1)
    inside = (row >= 0) & (row < 8) & (col >= 0) & (col < 8)
    return jnp.where(inside, x, 0.0)


def both(ref, z):
    return jnp.concatenate([ref[0, z], ref[1, z]], axis=0)


def wide(mask):
    return jnp.concatenate([mask, mask], axis=1) > 0


def activate(pre, cotangent, keep):
    sigma = 1.0 / (1.0 + jnp.exp(-pre))
    out = jnp.where(keep, pre * sigma, 0.0)
    grad = jnp.where(keep, cotangent * sigma * (1.0 + pre * (1.0 - sigma)), 0.0)
    return out, grad


def forward_kernel(feats, mask, weight, bias, cotangent, out, grad, edge, bias_sum, cols, pre):
    width = feats.shape[3]

    def fill(z, carry):
        keep = wide(mask[pl.ds(pl.multiple_of(z * 128, 128), 128), :])
        plane = jnp.where(keep, both(feats, z).astype(jnp.float32), 0.0)
        for p in range(3):
            for q in range(3):
                at = (3 * p + q) * width
                cols[pl.ds(pl.multiple_of(z * 128, 128), 128), at : at + width] = shifted(
                    plane, p - 1, q - 1
                ).astype(jnp.bfloat16)
        return carry

    lax.fori_loop(0, 8, fill, 0)
    taps = [weight[9 * a : 9 * a + 9].reshape(9 * width, width) for a in range(3)]
    pre[...] = jnp.dot(cols[...], taps[1], preferred_element_type=jnp.float32) + bias[...]
    pre[128:, :] += jnp.dot(cols[:896, :], taps[0], preferred_element_type=jnp.float32)
    pre[:896, :] += jnp.dot(cols[128:, :], taps[2], preferred_element_type=jnp.float32)
    edge[0] = pre[:128, :]
    edge[1] = pre[896:, :]
    bias_sum[...] = jnp.zeros_like(bias_sum)

    def finish(z, carry):
        rows = pl.ds(pl.multiple_of(z * 128, 128), 128)
        keep = wide(mask[rows, :])
        act, slope = activate(pre[rows, :], both(cotangent, z).astype(jnp.float32), keep)
        act = act.astype(jnp.bfloat16)
        slope = slope.astype(jnp.bfloat16)
        for b in range(2):
            out[b, z] = act[64 * b : 64 * b + 64]
            grad[b, z] = slope[64 * b : 64 * b + 64]
        bias_sum[...] += jnp.sum(slope.astype(jnp.float32), axis=0, keepdims=True)
        return carry

    lax.fori_loop(1, 7, finish, 0)


def forward_inside(feats, mask, weight, bias, cotangent):
    width = feats.shape[3]
    shape = jax.ShapeDtypeStruct(feats.shape, jnp.bfloat16)
    return pl.pallas_call(
        forward_kernel,
        out_shape=(
            shape,
            shape,
            jax.ShapeDtypeStruct((2, 128, width), jnp.float32),
            jax.ShapeDtypeStruct((1, width), jnp.float32),
        ),
        scratch_shapes=[
            pltpu.VMEM((1024, 9 * width), jnp.bfloat16),
            pltpu.VMEM((1024, width), jnp.float32),
        ],
        compiler_params=params(),
        cost_estimate=cost(2 * 1024 * 27 * width * width, 6 * 1024 * 1024),
        name="forward_inside",
    )(feats, mask, weight, bias, cotangent)


def edge_kernel(halos, mask, weight, edge, cotangent, inside, out_in, grad_in, out, grad, rims, bias_sum):
    width = halos.shape[3]
    side = pl.program_id(0)
    halo = jnp.concatenate([halos[0, 0], halos[0, 1]], axis=0).astype(jnp.float32)
    cols = jnp.concatenate(
        [shifted(halo, p - 1, q - 1).astype(jnp.bfloat16) for p in range(3) for q in range(3)], axis=1
    )
    taps = weight[...].reshape(9 * width, width)
    pre = edge[0] + jnp.dot(cols, taps, preferred_element_type=jnp.float32)
    act, slope = activate(pre, both(cotangent, 0).astype(jnp.float32), wide(mask[...]))
    act = act.astype(jnp.bfloat16)
    slope = slope.astype(jnp.bfloat16)
    for b in range(2):
        out[b, 0] = act[64 * b : 64 * b + 64]
        grad[b, 0] = slope[64 * b : 64 * b + 64]
        rims[b, 0] = slope[64 * b : 64 * b + 64]

    @pl.when(side == 0)
    def _():
        bias_sum[...] = inside[...]

    bias_sum[...] += jnp.sum(slope.astype(jnp.float32), axis=0, keepdims=True)


def forward_edges(halos, mask, weight, edge, cotangent, inside, out, grad):
    width = halos.shape[2]
    plane = pl.BlockSpec((2, 1, 64, width), lambda i: (0, 7 * i, 0, 0))
    once = pl.BlockSpec((1, width), lambda i: (0, 0))
    return pl.pallas_call(
        edge_kernel,
        grid=(2,),
        in_specs=[
            pl.BlockSpec((1, 2, 64, width), lambda i: (i, 0, 0, 0)),
            pl.BlockSpec((128, 128), lambda i: (7 * i, 0)),
            pl.BlockSpec((9, width, width), lambda i: (2 * i, 0, 0)),
            pl.BlockSpec((1, 128, width), lambda i: (i, 0, 0)),
            plane,
            once,
            pl.BlockSpec(memory_space=pl.ANY),
            pl.BlockSpec(memory_space=pl.ANY),
        ],
        out_specs=(
            plane,
            plane,
            pl.BlockSpec((2, 1, 64, width), lambda i: (0, i, 0, 0)),
            once,
        ),
        out_shape=(
            jax.ShapeDtypeStruct(out.shape, out.dtype),
            jax.ShapeDtypeStruct(grad.shape, grad.dtype),
            jax.ShapeDtypeStruct((2, 2, 64, width), jnp.bfloat16),
            jax.ShapeDtypeStruct((1, width), jnp.float32),
        ),
        input_output_aliases={6: 0, 7: 1},
        compiler_params=params(),
        cost_estimate=cost(2 * 256 * 9 * width * width, 3 * 1024 * 1024),
        name="forward_edges",
    )(halos.reshape(2, 2, 64, width), mask, weight, edge, cotangent, inside, out, grad)


def turned_kernel(mine, theirs, turned):
    half = mine.shape[3]

    def fill(z, carry):
        for who, ref in ((0, mine), (1, theirs)):
            plane = both(ref, z).astype(jnp.float32).T
            for p in range(3):
                for q in range(3):
                    at = (3 * p + q) * half
                    turned[at : at + half, pl.ds(pl.multiple_of(who * 1024 + z * 128, 128), 128)] = shifted_lanes(
                        plane, p - 1, q - 1
                    ).astype(jnp.bfloat16)
        return carry

    lax.fori_loop(0, 8, fill, 0)


def turn_features(mine, theirs):
    half = mine.shape[3]
    return pl.pallas_call(
        turned_kernel,
        out_shape=jax.ShapeDtypeStruct((9 * half, 2048), jnp.bfloat16),
        compiler_params=params(),
        cost_estimate=cost(0, 16 * 1024 * 1024),
        name="turn_features",
    )(mine, theirs)


def weight_kernel(turned, halos, their_halos, grad, their_grad, terms, rows, ends):
    half = halos.shape[2]

    def order(z, carry):
        for who, ref in ((0, grad), (1, their_grad)):
            rows[pl.ds(pl.multiple_of(who * 1024 + z * 128, 128), 128), :] = both(ref, z)
        return carry

    lax.fori_loop(0, 8, order, 0)
    for who, ref in ((0, halos), (1, their_halos)):
        for side in range(2):
            plane = jnp.concatenate([ref[2 * side], ref[2 * side + 1]], axis=0).astype(jnp.float32).T
            for p in range(3):
                for q in range(3):
                    at = (3 * p + q) * half
                    ends[side, at : at + half, who * 128 : who * 128 + 128] = shifted_lanes(
                        plane, p - 1, q - 1
                    ).astype(jnp.bfloat16)
    terms[1] = jnp.dot(turned[...], rows[...], preferred_element_type=jnp.float32).astype(jnp.bfloat16)
    for a, side in ((0, 0), (2, 1)):
        first = 0 if a == 0 else 128
        other = 128 - first
        total = jnp.dot(
            turned[:, first : first + 896], rows[other : other + 896, :], preferred_element_type=jnp.float32
        )
        total += jnp.dot(
            turned[:, 1024 + first : 1920 + first],
            rows[1024 + other : 1920 + other, :],
            preferred_element_type=jnp.float32,
        )
        rim = 0 if a == 0 else 896
        facing = jnp.concatenate([rows[rim : rim + 128, :], rows[1024 + rim : 1152 + rim, :]], axis=0)
        total += jnp.dot(ends[side], facing, preferred_element_type=jnp.float32)
        terms[a] = total.astype(jnp.bfloat16)


def weight_terms(turned, halos, their_halos, grad, their_grad):
    half = halos.shape[2]
    width = grad.shape[3]
    return pl.pallas_call(
        weight_kernel,
        out_shape=jax.ShapeDtypeStruct((3, 9 * half, width), jnp.bfloat16),
        scratch_shapes=[
            pltpu.VMEM((2048, width), jnp.bfloat16),
            pltpu.VMEM((2, 9 * half, 256), jnp.bfloat16),
        ],
        compiler_params=params(),
        cost_estimate=cost(2 * 2048 * 27 * half * width, 8 * 1024 * 1024),
        name="weight_terms",
    )(turned, halos, their_halos, grad, their_grad)


def backward_kernel(grad, halos, mask, weight, grad_feats, cols, total):
    width = grad.shape[3]

    def spread(plane, place):
        for p in range(3):
            for q in range(3):
                at = (3 * p + q) * width
                cols[pl.ds(pl.multiple_of(place, 128), 128), at : at + width] = shifted(
                    plane.astype(jnp.float32), 1 - p, 1 - q
                ).astype(jnp.bfloat16)

    def fill(z, carry):
        spread(both(grad, z), (z + 1) * 128)
        return carry

    spread(jnp.concatenate([halos[0], halos[1]], axis=0), 0)
    spread(jnp.concatenate([halos[2], halos[3]], axis=0), 1152)
    lax.fori_loop(0, 8, fill, 0)
    total[...] = jnp.zeros_like(total)

    def add(tap, carry):
        a, pq = tap // 9, tap % 9
        piece = cols[pl.ds(pl.multiple_of((2 - a) * 128, 128), 1024), pl.ds(pl.multiple_of(pq * width, 128), width)]
        total[...] += lax.dot_general(
            piece, weight[tap], (((1,), (1,)), ((), ())), preferred_element_type=jnp.float32
        )
        return carry

    lax.fori_loop(0, 27, add, 0)

    def finish(z, carry):
        rows = pl.ds(pl.multiple_of(z * 128, 128), 128)
        done = jnp.where(wide(mask[rows, :]), total[rows, :], 0.0).astype(jnp.bfloat16)
        for b in range(2):
            grad_feats[b, z] = done[64 * b : 64 * b + 64]
        return carry

    lax.fori_loop(0, 8, finish, 0)


def backward(grad, halos, mask, weight):
    width = grad.shape[3]
    return pl.pallas_call(
        backward_kernel,
        out_shape=jax.ShapeDtypeStruct(grad.shape, jnp.bfloat16),
        scratch_shapes=[
            pltpu.VMEM((1280, 9 * width), jnp.bfloat16),
            pltpu.VMEM((1024, width), jnp.float32),
        ],
        compiler_params=params(),
        cost_estimate=cost(2 * 1024 * 27 * width * width, 6 * 1024 * 1024),
        name="backward",
    )(grad, halos, mask, weight)


def per_device(size, feats, voxmask, links, weight, bias, cotangent):
    width = feats.shape[3]
    half = width // 2
    core = lax.axis_index("zslab") % 2
    keep = (voxmask == 1).reshape(2, 8, 64, 1)
    rims = jnp.stack([feats[:, 0], feats[:, 7]], axis=1)
    rims = jnp.where(jnp.stack([keep[:, 0], keep[:, 7]], axis=1), rims, jnp.zeros_like(rims))
    places = route(links, size)
    halos = fetch_halos(rims, links, places, size)

    mask = jnp.broadcast_to(keep.transpose(1, 0, 2, 3).astype(jnp.float32).reshape(1024, 1), (1024, 128))
    halves = jnp.where(keep, feats, jnp.zeros_like(feats)).reshape(2, 8, 64, 2, half)
    own = jnp.where(core == 0, halves[..., 0, :], halves[..., 1, :])
    give = jnp.where(core == 0, halves[..., 1, :], halves[..., 0, :])
    turned = turn_features(own, swap(give, size, 1))

    out, grad, edge, inside = forward_inside(feats, mask, weight, bias.reshape(1, width), cotangent)
    out, grad, grad_rims, bias_local = forward_edges(halos, mask, weight, edge, cotangent, inside, out, grad)
    grad_bias = jnp.sum(lax.all_gather(bias_local, "zslab", axis=0, tiled=True), axis=0)

    halves = halos.reshape(4, 64, 2, half)
    own_halos = jnp.where(core == 0, halves[..., 0, :], halves[..., 1, :])
    their_halos = swap(jnp.where(core == 0, halves[..., 1, :], halves[..., 0, :]), size, 1)
    terms = weight_terms(turned, own_halos, their_halos, grad, swap(grad, size, 1))

    grad_halos = fetch_halos(grad_rims, links, places, size)
    grad_feats = backward(grad, grad_halos, mask, weight)

    parts = []
    for a in range(3):
        part = scatter_outer(scatter_inner(terms[a], size), size)
        part = gather_inner(gather_outer(part, size), size)
        other = swap(part, size, 1)
        part = part.reshape(9, 1, half, width)
        other = other.reshape(9, 1, half, width)
        parts.append(
            jnp.where(
                core == 0, jnp.concatenate([part, other], axis=1), jnp.concatenate([other, part], axis=1)
            ).reshape(9, width, width)
        )
    grad_weight = jnp.concatenate(parts, axis=0)
    return out, grad_feats, grad_weight, grad_bias


def solution(mesh):
    return jax.shard_map(
        functools.partial(per_device, mesh.shape["zslab"]),
        mesh=mesh,
        in_specs=(
            P(("groups", "zslab"), None, None, None),
            P(("groups", "zslab"), None),
            P(("groups", "zslab"), None),
            P(),
            P(),
            P(("groups", "zslab"), None, None, None),
        ),
        out_specs=(
            P(("groups", "zslab"), None, None, None),
            P(("groups", "zslab"), None, None, None),
            P("groups", None, None),
            P("groups"),
        ),
        check_vma=False,
    )
```

time: 300 us -> 179 us (0.60); the launches traced: 297 us -> 179 us
  blocking collectives: 160 us -> 21.1 us
  starting transfers between devices: 0.08 us -> 53.1 us
  matrix products: 50.5 us -> 0 us
  Pallas kernels: 0 us -> 39.4 us
  between operations: 14.7 us -> 1.26 us
  local copies, waits for them, and re-layouts: 17.4 us -> 14.2 us
    psum x1 -> x0, blocking collectives: 160 us -> none  [per_device(): weight_sum, bias_sum = lax.psum((weight_local, bias_local), 'zslab')]
    ppermute x0 -> x43, starting transfers between devices: none -> 53.1 us  [the longest x27 44.6 us: rotate(): lax.ppermute(x, 'zslab', [(i, (i + 4 * steps) % size) for i in range(size)])]
    dot_general x81 -> x0, matrix products: 50.5 us -> none  [the longest x27 30.9 us: weight_terms(): lax.dot_general(piece, grad_rows, (((0,), (0,)), ((), ())), preferred_ele...]
    all_gather x2 -> x0, waiting for transfers between devices: 41 us -> none  [the longest x1 41 us: per_device(): all_rims = lax.all_gather(rims, 'zslab', axis=0, tiled=True)]
    ppermute x0 -> x43, waiting for transfers between devices: none -> 39.8 us  [the longest x16 27.4 us: swap(): return lax.ppermute(x, 'zslab', [(i, i ^ bit) for i in range(size)])]
    pallas_call x0 -> x5, Pallas kernels: none -> 39.4 us  [the longest x1 13.5 us: backward(): pl.pallas_call(backward_kernel, out_shape=jax.ShapeDtypeStruct(grad.shape...]
    all_gather x0 -> x1, blocking collectives: none -> 21.1 us  [per_device(): lax.all_gather(bias_local, 'zslab', axis=0, tiled=True)]
    concatenate x9 -> x5, other arithmetic: 7.52 us -> 2.16 us  [the longest x1 2 us: per_device(): grad_weight = jnp.concatenate(parts, axis=0)]
  transfers between devices with their start and end apart: 2 -> 43, of which waited for: 1 -> 13; matrix products, arithmetic and copies ran while one was open for 3% -> 11% of each run, Pallas kernels for 0% -> 22%
where the time goes in v2:
time: 179 us
  starting transfers between devices  53.1 us (30%)
  waiting for transfers between devices  39.8 us (22%)
  Pallas kernels  39.4 us (22%)
  blocking collectives  21.1 us (12%)
  local copies, waits for them, and re-layouts  14.2 us (8%)
  other arithmetic  9.93 us (6%)
    ppermute x27, starting transfers between devices, rotate(): lax.ppermute(x, 'zslab', [(i, (i + 4 * steps) % size) for i in range(size)])  44.6 us
    ppermute x16, waiting for transfers between devices, swap(): return lax.ppermute(x, 'zslab', [(i, i ^ bit) for i in range(size)])  27.4 us
    all_gather x1, blocking collectives, per_device(): lax.all_gather(bias_local, 'zslab', axis=0, tiled=True)  21.1 us
    pallas_call x1, Pallas kernels, backward(): pl.pallas_call(backward_kernel, out_shape=jax.ShapeDtypeStruct(grad.shape...  13.5 us
    ppermute x27, waiting for transfers between devices, rotate(): lax.ppermute(x, 'zslab', [(i, (i + 4 * steps) % size) for i in range(size)])  12.5 us
    pallas_call x1, Pallas kernels, forward_inside(): pl.pallas_call(forward_kernel, out_shape=(shape, shape, jax.ShapeDtypeStr...  8.78 us
    ppermute x16, starting transfers between devices, swap(): return lax.ppermute(x, 'zslab', [(i, i ^ bit) for i in range(size)])  8.49 us
    pallas_call x1, Pallas kernels, weight_terms(): pl.pallas_call(weight_kernel, out_shape=jax.ShapeDtypeStruct((3, 9 * half...  8.09 us
  transfers between devices with their start and end apart: 43, of which 13 were waited for; matrix products, arithmetic and copies ran while one was open for 11% of the time, Pallas kernels for 22%

profile of v2, /device:TPU:0, one launch (start us, length us, event | category | flops | bytes accessed | tf_op | source)
XLA Modules:
  0.0 178.8 jit_solution(8713675570617059727)
XLA Ops:
  0.6 3.1 %collective-permute-start.2 = (s32[2,2]{1,0:T(2,128)}, s32[2,2]{1,0:T(2,128)S(1)}, u32[]{:S(2)}, u32[]{:S(2)}) collective-permute-start(s32[2,2]{1,0:T(2,128)} %param.11), channel_id=1, source_target_pairs={{0,4},{1,5},{2,6},{3,7},{4,8},{5,9},{6,10},{7,11},{8,12},{9,13},{1... | collective-permute-start | bytes 56 | tf_op jit(solution)/shard_map/ppermute | solution.py:27
  3.7 2.6 %collective-permute-start.4 = (s32[2,2]{1,0:T(2,128)}, s32[2,2]{1,0:T(2,128)S(1)}, u32[]{:S(2)}, u32[]{:S(2)}) collective-permute-start(s32[2,2]{1,0:T(2,128)} %param.11), channel_id=1, source_target_pairs={{0,8},{1,9},{2,10},{3,11},{4,12},{5,13},{6,14},{7,15},{8,0},{9,1},... | collective-permute-start | bytes 56 | tf_op jit(solution)/shard_map/ppermute | solution.py:27
  16.6 8.8 %forward_inside.1 = (bf16[2,8,64,256]{3,2,1,0:T(8,128)(2,1)}, bf16[2,8,64,256]{3,2,1,0:T(8,128)(2,1)}, f32[2,128,256]{2,1,0:T(8,128)}, f32[1,256]{1,0:T(1,128)}) custom-call(bf16[2,8,64,256]{3,2,1,0:T(8,128)(2,1)} %feats.1, f32[1024,128]{1,0:T(8,128)} %broadcast_in_dim.97.mask, bf16[27,256,256]{2,1,0:T(8,128)(2,1)} %weight.5, f32[1,256]{1,0:T(1,128)} %bitcast.98, ...), custom_call_target="tpu_custom_call" | custom-call | flops 3623878656 | bytes 6291456 | tf_op jit(solution)/shard_map/forward_inside/pallas_call | solution.py:183
  32.2 2.9 %collective-permute-start.3 = (bf16[4,64,256]{2,1,0:T(8,128)(2,1)S(1)}, bf16[4,64,256]{2,1,0:T(8,128)(2,1)S(1)}, u32[]{:S(2)}, u32[]{:S(2)}) collective-permute-start(bf16[4,64,256]{2,1,0:T(8,128)(2,1)S(1)} %broadcast_select_fusion.6), channel_id=1, source_target_pairs={{0,12},{1,13},{2,14},{3,15},{4,0},{5,1},{6,2},{7,3},{8,4},{9,5},{1... | collective-permute-start | bytes 393224 | tf_op jit(solution)/shard_map/ppermute | solution.py:27
  35.6 2.4 %collective-permute-done.7 = bf16[4,64,256]{2,1,0:T(8,128)(2,1)S(1)} collective-permute-done((bf16[4,64,256]{2,1,0:T(8,128)(2,1)S(1)}, bf16[4,64,256]{2,1,0:T(8,128)(2,1)S(1)}, u32[]{:S(2)}, u32[]{:S(2)}) %collective-permute-start.7) | collective-permute-done | bytes 131104 | tf_op jit(solution)/shard_map/ppermute | solution.py:27
  38.0 5.0 %collective-permute-done.5 = bf16[4,64,256]{2,1,0:T(8,128)(2,1)S(1)} collective-permute-done((bf16[4,64,256]{2,1,0:T(8,128)(2,1)S(1)}, bf16[4,64,256]{2,1,0:T(8,128)(2,1)S(1)}, u32[]{:S(2)}, u32[]{:S(2)}) %collective-permute-start.5) | collective-permute-done | bytes 131104 | tf_op jit(solution)/shard_map/ppermute | solution.py:27
  43.8 3.0 %forward_edges.1 = (bf16[2,8,64,256]{3,2,1,0:T(8,128)(2,1)}, bf16[2,8,64,256]{3,2,1,0:T(8,128)(2,1)}, bf16[2,2,64,256]{3,2,1,0:T(8,128)(2,1)}, f32[1,256]{1,0:T(1,128)}) custom-call(bf16[2,2,64,256]{3,2,1,0:T(8,128)(2,1)} %bitcast.93, f32[1024,128]{1,0:T(8,128)} %broadcast_in_dim.97.mask, ...), custom_call_target="tpu_custom_call", output_to_operand_aliasing={{0}: (6, {}), {1}: (7, {})} | custom-call | flops 301989888 | bytes 3145728 | tf_op jit(solution)/shard_map/forward_edges/pallas_call | solution.py:229
  48.1 6.0 %turn_features.1.turned = bf16[1152,2048]{1,0:T(8,128)(2,1)} custom-call(bf16[2,8,64,128]{3,2,1,0:T(8,128)(2,1)} %get-tuple-element.41.mine, bf16[2,8,64,128]{3,2,1,0:T(8,128)(2,1)} %copy-done.3), custom_call_target="tpu_custom_call" | custom-call | bytes 16777216 | tf_op jit(solution)/shard_map/turn_features/pallas_call | solution.py:280
  55.6 21.1 %all-gather = f32[16,1,256]{2,1,0:T(1,128)S(1)} all-gather(f32[1,1,256]{2,1,0:T(1,128)S(1)} %bitcast.97), channel_id=1, replica_groups=mesh['groups'=2,'zslab'=16] {'zslab'}, dimensions={0}, use_global_device_ids=true | all-gather | bytes 17408 | tf_op jit(solution)/shard_map/all_gather | solution.py:414
  80.1 3.9 %collective-permute-start.10 = (bf16[4,64,256]{2,1,0:T(8,128)(2,1)S(1)}, bf16[4,64,256]{2,1,0:T(8,128)(2,1)S(1)}, u32[]{:S(2)}, u32[]{:S(2)}) collective-permute-start(bf16[4,64,256]{2,1,0:T(8,128)(2,1)S(1)} %broadcast_select_fusion.5), channel_id=1, source_target_pairs={{0,12},{1,13},{2,14},{3,15},{4,0},{5,1},{6,2},{7,3},{8,4},{9,5},{1... | collective-permute-start | bytes 393224 | tf_op jit(solution)/shard_map/ppermute | solution.py:27
  84.7 8.1 %weight_terms.1 = bf16[3,1152,256]{2,1,0:T(8,128)(2,1)} custom-call(bf16[1152,2048]{1,0:T(8,128)(2,1)} %turn_features.1.turned, bf16[4,64,128]{2,1,0:T(8,128)(2,1)} %get-tuple-element.56.halos, bf16[4,64,128]{2,1,0:T(8,128)(2,1)} %copy-done.8, bf16[2,8,64,256]{3,2,1,0:T(8,128)(2,1)} %get-tuple-element.18.grad, bf16[2,8,64,256]{3,2,1,0:T(8,128)(2,1)} %copy-done.7), custom_call_target="tpu_custom_call" | custom-call | flops 3623878656 | bytes 8388608 | tf_op jit(solution)/shard_map/weight_terms/pallas_call | solution.py:328
  94.5 2.1 %collective-permute-start.25 = (bf16[576,256]{1,0:T(8,128)(2,1)S(1)}, bf16[576,256]{1,0:T(8,128)(2,1)S(1)}, u32[]{:S(2)}, u32[]{:S(2)}) collective-permute-start(bf16[576,256]{1,0:T(8,128)(2,1)S(1)} %dynamic-slice_bitcast_fusion.1), channel_id=1, source_target_pairs={{0,2},{1,3},{2,0},{3,1},{4,6},{5,7},{6,4},{7,5},{8,10},{9,11},{10,... | collective-permute-start | bytes 884744 | tf_op jit(solution)/shard_map/ppermute | solution.py:23
  97.5 6.9 %collective-permute-done.16 = bf16[576,256]{1,0:T(8,128)(2,1)S(1)} collective-permute-done((bf16[576,256]{1,0:T(8,128)(2,1)S(1)}, bf16[576,256]{1,0:T(8,128)(2,1)S(1)}, u32[]{:S(2)}, u32[]{:S(2)}) %collective-permute-start.16) | collective-permute-done | bytes 294944 | tf_op jit(solution)/shard_map/ppermute | solution.py:23
  106.7 2.8 %collective-permute-start.19 = (bf16[144,256]{1,0:T(8,128)(2,1)S(1)}, bf16[144,256]{1,0:T(8,128)(2,1)S(1)}, u32[]{:S(2)}, u32[]{:S(2)}) collective-permute-start(bf16[144,256]{1,0:T(8,128)(2,1)S(1)} %get-tuple-element.47), channel_id=1, source_target_pairs={{0,12},{1,13},{2,14},{3,15},{4,0},{5,1},{6,2},{7,3},{8,4},{9,5},{1... | collective-permute-start | bytes 221192 | tf_op jit(solution)/shard_map/ppermute | solution.py:27
  111.4 4.3 %collective-permute-done.34 = bf16[576,256]{1,0:T(8,128)(2,1)S(1)} collective-permute-done((bf16[576,256]{1,0:T(8,128)(2,1)S(1)}, bf16[576,256]{1,0:T(8,128)(2,1)S(1)}, u32[]{:S(2)}, u32[]{:S(2)}) %collective-permute-start.34) | collective-permute-done | bytes 294944 | tf_op jit(solution)/shard_map/ppermute | solution.py:23
  126.1 2.3 %collective-permute-start.21 = (bf16[144,256]{1,0:T(8,128)(2,1)S(1)}, bf16[144,256]{1,0:T(8,128)(2,1)S(1)}, u32[]{:S(2)}, u32[]{:S(2)}) collective-permute-start(bf16[144,256]{1,0:T(8,128)(2,1)S(1)} %get-tuple-element.22), channel_id=1, source_target_pairs={{0,8},{1,9},{2,10},{3,11},{4,12},{5,13},{6,14},{7,15},{8,0},{9,1},... | collective-permute-start | bytes 221192 | tf_op jit(solution)/shard_map/ppermute | solution.py:27
  128.5 3.6 %collective-permute-start.22 = (bf16[144,256]{1,0:T(8,128)(2,1)S(1)}, bf16[144,256]{1,0:T(8,128)(2,1)S(1)}, u32[]{:S(2)}, u32[]{:S(2)}) collective-permute-start(bf16[144,256]{1,0:T(8,128)(2,1)S(1)} %get-tuple-element.22), channel_id=1, source_target_pairs={{0,12},{1,13},{2,14},{3,15},{4,0},{5,1},{6,2},{7,3},{8,4},{9,5},{1... | collective-permute-start | bytes 221192 | tf_op jit(solution)/shard_map/ppermute | solution.py:27
  132.1 2.6 %collective-permute-start.30 = (bf16[144,256]{1,0:T(8,128)(2,1)S(1)}, bf16[144,256]{1,0:T(8,128)(2,1)S(1)}, u32[]{:S(2)}, u32[]{:S(2)}) collective-permute-start(bf16[144,256]{1,0:T(8,128)(2,1)S(1)} %get-tuple-element.24), channel_id=1, source_target_pairs={{0,8},{1,9},{2,10},{3,11},{4,12},{5,13},{6,14},{7,15},{8,0},{9,1},... | collective-permute-start | bytes 221192 | tf_op jit(solution)/shard_map/ppermute | solution.py:27
  134.9 3.6 %collective-permute-start.31 = (bf16[144,256]{1,0:T(8,128)(2,1)S(1)}, bf16[144,256]{1,0:T(8,128)(2,1)S(1)}, u32[]{:S(2)}, u32[]{:S(2)}) collective-permute-start(bf16[144,256]{1,0:T(8,128)(2,1)S(1)} %get-tuple-element.24), channel_id=1, source_target_pairs={{0,12},{1,13},{2,14},{3,15},{4,0},{5,1},{6,2},{7,3},{8,4},{9,5},{1... | collective-permute-start | bytes 221192 | tf_op jit(solution)/shard_map/ppermute | solution.py:27
  141.0 3.0 %collective-permute-start.40 = (bf16[144,256]{1,0:T(8,128)(2,1)S(1)}, bf16[144,256]{1,0:T(8,128)(2,1)S(1)}, u32[]{:S(2)}, u32[]{:S(2)}) collective-permute-start(bf16[144,256]{1,0:T(8,128)(2,1)S(1)} %get-tuple-element.26), channel_id=1, source_target_pairs={{0,12},{1,13},{2,14},{3,15},{4,0},{5,1},{6,2},{7,3},{8,4},{9,5},{1... | collective-permute-start | bytes 221192 | tf_op jit(solution)/shard_map/ppermute | solution.py:27
  148.1 5.9 %collective-permute-done.23 = bf16[576,256]{1,0:T(8,128)(2,1)S(1)} collective-permute-done((bf16[576,256]{1,0:T(8,128)(2,1)S(1)}, bf16[576,256]{1,0:T(8,128)(2,1)S(1)}, u32[]{:S(2)}, u32[]{:S(2)}) %collective-permute-start.23) | collective-permute-done | bytes 294944 | tf_op jit(solution)/shard_map/ppermute | solution.py:23
  154.4 5.0 %collective-permute-done.32 = bf16[576,256]{1,0:T(8,128)(2,1)S(1)} collective-permute-done((bf16[576,256]{1,0:T(8,128)(2,1)S(1)}, bf16[576,256]{1,0:T(8,128)(2,1)S(1)}, u32[]{:S(2)}, u32[]{:S(2)}) %collective-permute-start.32) | collective-permute-done | bytes 294944 | tf_op jit(solution)/shard_map/ppermute | solution.py:23
  159.8 2.8 %collective-permute-done.41 = bf16[576,256]{1,0:T(8,128)(2,1)S(1)} collective-permute-done((bf16[576,256]{1,0:T(8,128)(2,1)S(1)}, bf16[576,256]{1,0:T(8,128)(2,1)S(1)}, u32[]{:S(2)}, u32[]{:S(2)}) %collective-permute-start.41) | collective-permute-done | bytes 294944 | tf_op jit(solution)/shard_map/ppermute | solution.py:23
  162.9 13.5 %backward.1 = bf16[2,8,64,256]{3,2,1,0:T(8,128)(2,1)} custom-call(bf16[2,8,64,256]{3,2,1,0:T(8,128)(2,1)} %get-tuple-element.18.grad, bf16[4,64,256]{2,1,0:T(8,128)(2,1)} %fusion.5.halos, f32[1024,128]{1,0:T(8,128)} %broadcast_in_dim.97.mask, bf16[27,256,256]{2,1,0:T(8,128)(2,1)} %weight.5), custom_call_target="tpu_custom_call" | custom-call | flops 3623878656 | bytes 6291456 | tf_op jit(solution)/shard_map/backward/pallas_call | solution.py:383
  (202 shorter events, 52.2 us)
Async XLA Ops:
  0.6 24.8 %collective-permute-start.2 = (s32[2,2]{1,0:T(2,128)}, s32[2,2]{1,0:T(2,128)S(1)}, u32[]{:S(2)}, u32[]{:S(2)}) collective-permute-start(s32[2,2]{1,0:T(2,128)} %param.11), channel_id=1, source_target_pairs={{0,4},{1,5},{2,6},{3,7},{4,8},{5,9},{6,10},{7,11},{8,12},{9,13},{1... | collective-permute-start | bytes 56 | tf_op jit(solution)/shard_map/ppermute | solution.py:27
  3.7 21.9 %collective-permute-start.4 = (s32[2,2]{1,0:T(2,128)}, s32[2,2]{1,0:T(2,128)S(1)}, u32[]{:S(2)}, u32[]{:S(2)}) collective-permute-start(s32[2,2]{1,0:T(2,128)} %param.11), channel_id=1, source_target_pairs={{0,8},{1,9},{2,10},{3,11},{4,12},{5,13},{6,14},{7,15},{8,0},{9,1},... | collective-permute-start | bytes 56 | tf_op jit(solution)/shard_map/ppermute | solution.py:27
  6.3 20.3 %collective-permute-start.6 = (s32[2,2]{1,0:T(2,128)}, s32[2,2]{1,0:T(2,128)S(1)}, u32[]{:S(2)}, u32[]{:S(2)}) collective-permute-start(s32[2,2]{1,0:T(2,128)} %param.11), channel_id=1, source_target_pairs={{0,12},{1,13},{2,14},{3,15},{4,0},{5,1},{6,2},{7,3},{8,4},{9,5},{1... | collective-permute-start | bytes 56 | tf_op jit(solution)/shard_map/ppermute | solution.py:27
  9.4 17.8 %collective-permute-start = (bf16[2,2,64,256]{3,2,1,0:T(8,128)(2,1)S(1)}, bf16[2,2,64,256]{3,2,1,0:T(8,128)(2,1)S(1)}, u32[]{:S(2)}, u32[]{:S(2)}) collective-permute-start(bf16[2,2,64,256]{3,2,1,0:T(8,128)(2,1)S(1)} %maximum_select_fusion.6), channel_id=1, source_target_pairs={{0,2},{1,3},{2,0},{3,1},{4,6},{5,7},{6,4},{7,5},{8,10},{9,11},{10,... | collective-permute-start | bytes 393224 | tf_op jit(solution)/shard_map/ppermute | solution.py:23
  14.4 33.0 %collective-permute-start.13 = (bf16[2,8,64,128]{3,2,1,0:T(8,128)(2,1)S(1)}, bf16[2,8,64,128]{3,2,1,0:T(8,128)(2,1)S(1)}, u32[]{:S(2)}, u32[]{:S(2)}) collective-permute-start(bf16[2,8,64,128]{3,2,1,0:T(8,128)(2,1)S(1)} %get-tuple-element.40), channel_id=1, source_target_pairs={{0,1},{1,0},{2,3},{3,2},{4,5},{5,4},{6,7},{7,6},{8,9},{9,8},{10,11... | collective-permute-start | bytes 786440 | tf_op jit(solution)/shard_map/ppermute | solution.py:23
  54.2 23.1 %collective-permute-start.9 = (bf16[4,2,64,256]{3,2,1,0:T(8,128)(2,1)S(1)}, bf16[4,2,64,256]{3,2,1,0:T(8,128)(2,1)S(1)}, u32[]{:S(2)}, u32[]{:S(2)}) collective-permute-start(bf16[4,2,64,256]{3,2,1,0:T(8,128)(2,1)S(1)} %pad_maximum_fusion.4), channel_id=1, source_target_pairs={{0,1},{1,0},{2,3},{3,2},{4,5},{5,4},{6,7},{7,6},{8,9},{9,8},{10,11... | collective-permute-start | bytes 786440 | tf_op jit(solution)/shard_map/ppermute | solution.py:23
  55.1 28.8 %collective-permute-start.14 = (bf16[4,64,128]{2,1,0:T(8,128)(2,1)S(1)}, bf16[4,64,128]{2,1,0:T(8,128)(2,1)S(1)}, u32[]{:S(2)}, u32[]{:S(2)}) collective-permute-start(bf16[4,64,128]{2,1,0:T(8,128)(2,1)S(1)} %get-tuple-element.55), channel_id=1, source_target_pairs={{0,1},{1,0},{2,3},{3,2},{4,5},{5,4},{6,7},{7,6},{8,9},{9,8},{10,11... | collective-permute-start | bytes 196616 | tf_op jit(solution)/shard_map/ppermute | solution.py:23
  55.6 28.3 %collective-permute-start.15 = (bf16[2,8,64,256]{3,2,1,0:T(8,128)(2,1)S(1)}, bf16[2,8,64,256]{3,2,1,0:T(8,128)(2,1)S(1)}, u32[]{:S(2)}, u32[]{:S(2)}) collective-permute-start(bf16[2,8,64,256]{3,2,1,0:T(8,128)(2,1)S(1)} %copy-done.1), channel_id=1, source_target_pairs={{0,1},{1,0},{2,3},{3,2},{4,5},{5,4},{6,7},{7,6},{8,9},{9,8},{10,11... | collective-permute-start | bytes 1572872 | tf_op jit(solution)/shard_map/ppermute | solution.py:23
  79.7 16.9 %collective-permute-start.12 = (bf16[4,64,256]{2,1,0:T(8,128)(2,1)S(1)}, bf16[4,64,256]{2,1,0:T(8,128)(2,1)S(1)}, u32[]{:S(2)}, u32[]{:S(2)}) collective-permute-start(bf16[4,64,256]{2,1,0:T(8,128)(2,1)S(1)} %broadcast_select_fusion.1), channel_id=1, source_target_pairs={{0,4},{1,5},{2,6},{3,7},{4,8},{5,9},{6,10},{7,11},{8,12},{9,13},{1... | collective-permute-start | bytes 393224 | tf_op jit(solution)/shard_map/ppermute | solution.py:27
  79.9 16.8 %collective-permute-start.11 = (bf16[4,64,256]{2,1,0:T(8,128)(2,1)S(1)}, bf16[4,64,256]{2,1,0:T(8,128)(2,1)S(1)}, u32[]{:S(2)}, u32[]{:S(2)}) collective-permute-start(bf16[4,64,256]{2,1,0:T(8,128)(2,1)S(1)} %broadcast_select_fusion.3), channel_id=1, source_target_pairs={{0,8},{1,9},{2,10},{3,11},{4,12},{5,13},{6,14},{7,15},{8,0},{9,1},... | collective-permute-start | bytes 393224 | tf_op jit(solution)/shard_map/ppermute | solution.py:27
  80.1 16.7 %collective-permute-start.10 = (bf16[4,64,256]{2,1,0:T(8,128)(2,1)S(1)}, bf16[4,64,256]{2,1,0:T(8,128)(2,1)S(1)}, u32[]{:S(2)}, u32[]{:S(2)}) collective-permute-start(bf16[4,64,256]{2,1,0:T(8,128)(2,1)S(1)} %broadcast_select_fusion.5), channel_id=1, source_target_pairs={{0,12},{1,13},{2,14},{3,15},{4,0},{5,1},{6,2},{7,3},{8,4},{9,5},{1... | collective-permute-start | bytes 393224 | tf_op jit(solution)/shard_map/ppermute | solution.py:27
  94.5 16.2 %collective-permute-start.25 = (bf16[576,256]{1,0:T(8,128)(2,1)S(1)}, bf16[576,256]{1,0:T(8,128)(2,1)S(1)}, u32[]{:S(2)}, u32[]{:S(2)}) collective-permute-start(bf16[576,256]{1,0:T(8,128)(2,1)S(1)} %dynamic-slice_bitcast_fusion.1), channel_id=1, source_target_pairs={{0,2},{1,3},{2,0},{3,1},{4,6},{5,7},{6,4},{7,5},{8,10},{9,11},{10,... | collective-permute-start | bytes 884744 | tf_op jit(solution)/shard_map/ppermute | solution.py:23
  96.6 19.2 %collective-permute-start.34 = (bf16[576,256]{1,0:T(8,128)(2,1)S(1)}, bf16[576,256]{1,0:T(8,128)(2,1)S(1)}, u32[]{:S(2)}, u32[]{:S(2)}) collective-permute-start(bf16[576,256]{1,0:T(8,128)(2,1)S(1)} %dynamic-slice_bitcast_fusion), channel_id=1, source_target_pairs={{0,2},{1,3},{2,0},{3,1},{4,6},{5,7},{6,4},{7,5},{8,10},{9,11},{10,... | collective-permute-start | bytes 884744 | tf_op jit(solution)/shard_map/ppermute | solution.py:23
  104.5 13.1 %collective-permute-start.17 = (bf16[144,256]{1,0:T(8,128)(2,1)S(1)}, bf16[144,256]{1,0:T(8,128)(2,1)S(1)}, u32[]{:S(2)}, u32[]{:S(2)}) collective-permute-start(bf16[144,256]{1,0:T(8,128)(2,1)S(1)} %get-tuple-element.46), channel_id=1, source_target_pairs={{0,4},{1,5},{2,6},{3,7},{4,8},{5,9},{6,10},{7,11},{8,12},{9,13},{1... | collective-permute-start | bytes 221192 | tf_op jit(solution)/shard_map/ppermute | solution.py:27
  105.1 13.8 %collective-permute-start.18 = (bf16[144,256]{1,0:T(8,128)(2,1)S(1)}, bf16[144,256]{1,0:T(8,128)(2,1)S(1)}, u32[]{:S(2)}, u32[]{:S(2)}) collective-permute-start(bf16[144,256]{1,0:T(8,128)(2,1)S(1)} %get-tuple-element.48), channel_id=1, source_target_pairs={{0,8},{1,9},{2,10},{3,11},{4,12},{5,13},{6,14},{7,15},{8,0},{9,1},... | collective-permute-start | bytes 221192 | tf_op jit(solution)/shard_map/ppermute | solution.py:27
  106.7 13.1 %collective-permute-start.19 = (bf16[144,256]{1,0:T(8,128)(2,1)S(1)}, bf16[144,256]{1,0:T(8,128)(2,1)S(1)}, u32[]{:S(2)}, u32[]{:S(2)}) collective-permute-start(bf16[144,256]{1,0:T(8,128)(2,1)S(1)} %get-tuple-element.47), channel_id=1, source_target_pairs={{0,12},{1,13},{2,14},{3,15},{4,0},{5,1},{6,2},{7,3},{8,4},{9,5},{1... | collective-permute-start | bytes 221192 | tf_op jit(solution)/shard_map/ppermute | solution.py:27
  119.7 12.4 %collective-permute-start.36 = (bf16[144,256]{1,0:T(8,128)(2,1)S(1)}, bf16[144,256]{1,0:T(8,128)(2,1)S(1)}, u32[]{:S(2)}, u32[]{:S(2)}) collective-permute-start(bf16[144,256]{1,0:T(8,128)(2,1)S(1)} %get-tuple-element.54), channel_id=1, source_target_pairs={{0,8},{1,9},{2,10},{3,11},{4,12},{5,13},{6,14},{7,15},{8,0},{9,1},... | collective-permute-start | bytes 221192 | tf_op jit(solution)/shard_map/ppermute | solution.py:27
  126.1 12.9 %collective-permute-start.21 = (bf16[144,256]{1,0:T(8,128)(2,1)S(1)}, bf16[144,256]{1,0:T(8,128)(2,1)S(1)}, u32[]{:S(2)}, u32[]{:S(2)}) collective-permute-start(bf16[144,256]{1,0:T(8,128)(2,1)S(1)} %get-tuple-element.22), channel_id=1, source_target_pairs={{0,8},{1,9},{2,10},{3,11},{4,12},{5,13},{6,14},{7,15},{8,0},{9,1},... | collective-permute-start | bytes 221192 | tf_op jit(solution)/shard_map/ppermute | solution.py:27
  128.5 12.5 %collective-permute-start.22 = (bf16[144,256]{1,0:T(8,128)(2,1)S(1)}, bf16[144,256]{1,0:T(8,128)(2,1)S(1)}, u32[]{:S(2)}, u32[]{:S(2)}) collective-permute-start(bf16[144,256]{1,0:T(8,128)(2,1)S(1)} %get-tuple-element.22), channel_id=1, source_target_pairs={{0,12},{1,13},{2,14},{3,15},{4,0},{5,1},{6,2},{7,3},{8,4},{9,5},{1... | collective-permute-start | bytes 221192 | tf_op jit(solution)/shard_map/ppermute | solution.py:27
  144.7 14.8 %collective-permute-start.32 = (bf16[576,256]{1,0:T(8,128)(2,1)S(1)}, bf16[576,256]{1,0:T(8,128)(2,1)S(1)}, u32[]{:S(2)}, u32[]{:S(2)}) collective-permute-start(bf16[576,256]{1,0:T(8,128)(2,1)S(1)} %constant_dynamic-update-slice_fusion.4), channel_id=1, source_target_pairs={{0,2},{1,3},{2,0},{3,1},{4,6},{5,7},{6,4},{7,5},{8,10},{9,11},{10,... | collective-permute-start | bytes 884744 | tf_op jit(solution)/shard_map/ppermute | solution.py:23
  147.5 15.1 %collective-permute-start.41 = (bf16[576,256]{1,0:T(8,128)(2,1)S(1)}, bf16[576,256]{1,0:T(8,128)(2,1)S(1)}, u32[]{:S(2)}, u32[]{:S(2)}) collective-permute-start(bf16[576,256]{1,0:T(8,128)(2,1)S(1)} %constant_dynamic-update-slice_fusion), channel_id=1, source_target_pairs={{0,2},{1,3},{2,0},{3,1},{4,6},{5,7},{6,4},{7,5},{8,10},{9,11},{10,... | collective-permute-start | bytes 884744 | tf_op jit(solution)/shard_map/ppermute | solution.py:23
  154.3 22.1 %collective-permute-start.24 = (bf16[1152,256]{1,0:T(8,128)(2,1)S(1)}, bf16[1152,256]{1,0:T(8,128)(2,1)S(1)}, u32[]{:S(2)}, u32[]{:S(2)}) collective-permute-start(bf16[1152,256]{1,0:T(8,128)(2,1)S(1)} %maximum_select_fusion.3), channel_id=1, source_target_pairs={{0,1},{1,0},{2,3},{3,2},{4,5},{5,4},{6,7},{7,6},{8,9},{9,8},{10,11... | collective-permute-start | bytes 1769480 | tf_op jit(solution)/shard_map/ppermute | solution.py:23
  159.7 16.8 %collective-permute-start.33 = (bf16[1152,256]{1,0:T(8,128)(2,1)S(1)}, bf16[1152,256]{1,0:T(8,128)(2,1)S(1)}, u32[]{:S(2)}, u32[]{:S(2)}) collective-permute-start(bf16[1152,256]{1,0:T(8,128)(2,1)S(1)} %maximum_select_fusion.4), channel_id=1, source_target_pairs={{0,1},{1,0},{2,3},{3,2},{4,5},{5,4},{6,7},{7,6},{8,9},{9,8},{10,11... | collective-permute-start | bytes 1769480 | tf_op jit(solution)/shard_map/ppermute | solution.py:23
  162.9 13.8 %collective-permute-start.42 = (bf16[1152,256]{1,0:T(8,128)(2,1)S(1)}, bf16[1152,256]{1,0:T(8,128)(2,1)S(1)}, u32[]{:S(2)}, u32[]{:S(2)}) collective-permute-start(bf16[1152,256]{1,0:T(8,128)(2,1)S(1)} %maximum_select_fusion.5), channel_id=1, source_target_pairs={{0,1},{1,0},{2,3},{3,2},{4,5},{5,4},{6,7},{7,6},{8,9},{9,8},{10,11... | collective-permute-start | bytes 1769480 | tf_op jit(solution)/shard_map/ppermute | solution.py:23
  (28 other events, 197.8 us)

commit v3 on v2

v3 whole, which is shorter than its diff:
```python
import functools

import jax
import jax.numpy as jnp
from jax import lax
from jax.experimental import pallas as pl
from jax.experimental.pallas import tpu as pltpu
from jax.sharding import PartitionSpec as P

VMEM_LIMIT = 56 * 1024 * 1024
SIDES = (1, 1, 0, 0)


def params():
    return pltpu.CompilerParams(vmem_limit_bytes=VMEM_LIMIT)


def cost(flops, bytes_accessed):
    return pl.CostEstimate(flops=flops, bytes_accessed=bytes_accessed, transcendentals=0)


def swap(x, size, bit):
    return lax.ppermute(x, "zslab", [(i, i ^ bit) for i in range(size)])


def rotate(x, size, steps):
    return lax.ppermute(x, "zslab", [(i, (i + 4 * steps) % size) for i in range(size)])


def wanted(links):
    return links.T.reshape(4)


def exact_terms(x):
    high = lax.reduce_precision(x, 8, 7)
    middle = lax.reduce_precision(x - high, 8, 7)
    low = x - high - middle
    return [term.astype(jnp.bfloat16) for term in (high, middle, low)]


def sum_terms(rows):
    return jnp.sum(rows.astype(jnp.float32), axis=tuple(range(rows.ndim - 1)))


def extra_rows(rows):
    rows = jnp.stack(rows)
    return jnp.concatenate([rows, jnp.zeros((16 - rows.shape[0], rows.shape[1]), rows.dtype)])


def gather_group(x, size, first):
    second = 3 - first
    pair = jnp.stack([x, swap(x, size, first)])
    other = swap(pair, size, second)
    if first == 1:
        return jnp.concatenate([pair, other])
    return jnp.stack([pair[0], other[0], pair[1], other[1]])


def group_links(codes, size):
    return codes[:, :4].astype(jnp.int32).reshape(16)


def pick_kernel(outer, where, links, planes, picks, table):
    for place in range(outer * 4):
        table[place] = 0
    for plane in range(16):
        dev, brick, side = plane // 4, plane // 2 % 2, plane % 2
        dest = links[dev * 4 + brick * 2 + side]

        @pl.when((dest >= 0) & ((dest // 2) % 4 == where[1]))
        def _():
            steps = lax.rem(dest // 8 - where[0] + outer, outer)
            slot = dest % 2 + (0 if side == 1 else 2)
            table[steps * 4 + slot] = plane

    def copy(place, carry):
        source = table[place]
        picks[place // 4, pl.ds(pl.multiple_of((place % 4) * 64, 64), 64), :] = planes[
            source // 4, pl.ds(pl.multiple_of((source % 4) * 64, 64), 64), :
        ]
        return carry

    lax.fori_loop(0, outer * 4, copy, 0)


def pick(links, planes, size):
    me = lax.axis_index("zslab")
    outer = size // 4
    where = jnp.stack([me // 4, me % 4]).astype(jnp.int32)
    smem = pl.BlockSpec(memory_space=pltpu.SMEM)
    return pl.pallas_call(
        functools.partial(pick_kernel, outer),
        in_specs=[smem, smem, pl.BlockSpec(memory_space=pltpu.VMEM)],
        out_shape=jax.ShapeDtypeStruct((outer, 256, planes.shape[2]), planes.dtype),
        scratch_shapes=[pltpu.SMEM((outer * 4,), jnp.int32)],
        compiler_params=params(),
        cost_estimate=cost(0, 2 * 1024 * 1024),
        name="pick_planes",
    )(where, links, planes)


def spread_picks(picks, links, size):
    me = lax.axis_index("zslab")
    outer = size // 4
    want = wanted(links)
    step = (me // 4 - jnp.maximum(want, 0) // 8) % outer
    halos = jnp.zeros((4, 64, picks[0].shape[1]), picks[0].dtype)
    extra = []
    for steps in range(outer):
        got = rotate(picks[steps], size, steps) if steps else picks[0]
        here = (step == steps) & (want >= 0)
        halos = jnp.where(here[:, None, None], got[:256].reshape(halos.shape), halos)
        extra.append(got[256:])
    return halos, extra


def take_rows(x, place, rows):
    return lax.dynamic_slice_in_dim(x, place * rows, rows, axis=0)


def bits(size):
    return [1 << k for k in range(1, size.bit_length() - 1)]


def halve(keep, got, size, bit):
    mine = (lax.axis_index("zslab") // bit) % 2
    half = keep.shape[0] // 2
    give = take_rows(keep, 1 - mine, half) + take_rows(got, 1 - mine, half).astype(jnp.float32)
    stay = take_rows(keep, mine, half) + take_rows(got, mine, half).astype(jnp.float32)
    return give.astype(jnp.bfloat16), stay


def sum_and_gather(give, stay, size):
    order = bits(size)
    got = swap(give, size, order[0])
    for bit in order[1:]:
        give, stay = halve(stay, got, size, bit)
        got = swap(give, size, bit)
    whole = (stay + got.astype(jnp.float32)).astype(jnp.bfloat16)
    for bit in reversed(order):
        mine = (lax.axis_index("zslab") // bit) % 2
        got = swap(whole, size, bit)
        whole = jnp.where(mine == 0, jnp.concatenate([whole, got]), jnp.concatenate([got, whole]))
    return whole


def shifted(x, rows, cols):
    count = x.shape[0]
    index = lax.broadcasted_iota(jnp.int32, x.shape, 0)
    row = (index // 8) % 8 + rows
    col = index % 8 + cols
    move = 8 * rows + cols
    if move:
        x = pltpu.roll(x, (-move) % count, 0)
    inside = (row >= 0) & (row < 8) & (col >= 0) & (col < 8)
    return jnp.where(inside, x, 0.0)


def shifted_lanes(x, rows, cols):
    index = lax.broadcasted_iota(jnp.int32, x.shape, 1)
    row = (index // 8) % 8 + rows
    col = index % 8 + cols
    move = 8 * rows + cols
    if move:
        x = pltpu.roll(x, (-move) % x.shape[1], 1)
    inside = (row >= 0) & (row < 8) & (col >= 0) & (col < 8)
    return jnp.where(inside, x, 0.0)


def both(ref, z):
    return jnp.concatenate([ref[0, z], ref[1, z]], axis=0)


def wide(mask):
    return jnp.concatenate([mask, mask], axis=1) > 0


def activate(pre, cotangent, keep):
    sigma = 1.0 / (1.0 + jnp.exp(-pre))
    out = jnp.where(keep, pre * sigma, 0.0)
    grad = jnp.where(keep, cotangent * sigma * (1.0 + pre * (1.0 - sigma)), 0.0)
    return out, grad


def forward_kernel(feats, mask, weight, bias, cotangent, out, grad, edge, bias_sum, cols, pre):
    width = feats.shape[3]

    def fill(z, carry):
        keep = wide(mask[pl.ds(pl.multiple_of(z * 128, 128), 128), :])
        plane = jnp.where(keep, both(feats, z).astype(jnp.float32), 0.0)
        for p in range(3):
            for q in range(3):
                at = (3 * p + q) * width
                cols[pl.ds(pl.multiple_of(z * 128, 128), 128), at : at + width] = shifted(
                    plane, p - 1, q - 1
                ).astype(jnp.bfloat16)
        return carry

    lax.fori_loop(0, 8, fill, 0)
    taps = [weight[9 * a : 9 * a + 9].reshape(9 * width, width) for a in range(3)]
    pre[...] = jnp.dot(cols[...], taps[1], preferred_element_type=jnp.float32) + bias[...]
    pre[128:, :] += jnp.dot(cols[:896, :], taps[0], preferred_element_type=jnp.float32)
    pre[:896, :] += jnp.dot(cols[128:, :], taps[2], preferred_element_type=jnp.float32)
    edge[0] = pre[:128, :]
    edge[1] = pre[896:, :]
    bias_sum[...] = jnp.zeros_like(bias_sum)

    def finish(z, carry):
        rows = pl.ds(pl.multiple_of(z * 128, 128), 128)
        keep = wide(mask[rows, :])
        act, slope = activate(pre[rows, :], both(cotangent, z).astype(jnp.float32), keep)
        act = act.astype(jnp.bfloat16)
        slope = slope.astype(jnp.bfloat16)
        for b in range(2):
            out[b, z] = act[64 * b : 64 * b + 64]
        grad[pl.ds(pl.multiple_of((z - 1) * 128, 128), 128), :] = slope
        bias_sum[...] += jnp.sum(slope.astype(jnp.float32), axis=0, keepdims=True)
        return carry

    lax.fori_loop(1, 7, finish, 0)


def forward_inside(feats, mask, weight, bias, cotangent):
    width = feats.shape[3]
    return pl.pallas_call(
        forward_kernel,
        out_shape=(
            jax.ShapeDtypeStruct(feats.shape, jnp.bfloat16),
            jax.ShapeDtypeStruct((768, width), jnp.bfloat16),
            jax.ShapeDtypeStruct((2, 128, width), jnp.float32),
            jax.ShapeDtypeStruct((1, width), jnp.float32),
        ),
        scratch_shapes=[
            pltpu.VMEM((1024, 9 * width), jnp.bfloat16),
            pltpu.VMEM((1024, width), jnp.float32),
        ],
        compiler_params=params(),
        cost_estimate=cost(2 * 1024 * 27 * width * width, 6 * 1024 * 1024),
        name="forward_inside",
    )(feats, mask, weight, bias, cotangent)


def edge_kernel(halos, mask, weight, edge, cotangent, inside, out_in, out, rims, bias_sum):
    width = halos.shape[2]
    side = pl.program_id(0)
    halo = halos[0].astype(jnp.float32)
    cols = jnp.concatenate(
        [shifted(halo, p - 1, q - 1).astype(jnp.bfloat16) for p in range(3) for q in range(3)], axis=1
    )
    taps = weight[...].reshape(9 * width, width)
    pre = edge[0] + jnp.dot(cols, taps, preferred_element_type=jnp.float32)
    act, slope = activate(pre, both(cotangent, 0).astype(jnp.float32), wide(mask[...]))
    act = act.astype(jnp.bfloat16)
    slope = slope.astype(jnp.bfloat16)
    for b in range(2):
        out[b, 0] = act[64 * b : 64 * b + 64]
        rims[b, 0] = slope[64 * b : 64 * b + 64]

    @pl.when(side == 0)
    def _():
        bias_sum[...] = inside[...]

    bias_sum[...] += jnp.sum(slope.astype(jnp.float32), axis=0, keepdims=True)


def forward_edges(halos, mask, weight, edge, cotangent, inside, out):
    width = halos.shape[2]
    plane = pl.BlockSpec((2, 1, 64, width), lambda i: (0, 7 * i, 0, 0))
    once = pl.BlockSpec((1, width), lambda i: (0, 0))
    return pl.pallas_call(
        edge_kernel,
        grid=(2,),
        in_specs=[
            pl.BlockSpec((1, 128, width), lambda i: (i, 0, 0)),
            pl.BlockSpec((128, 128), lambda i: (7 * i, 0)),
            pl.BlockSpec((9, width, width), lambda i: (2 * i, 0, 0)),
            pl.BlockSpec((1, 128, width), lambda i: (i, 0, 0)),
            plane,
            once,
            pl.BlockSpec(memory_space=pl.ANY),
        ],
        out_specs=(plane, pl.BlockSpec((2, 1, 64, width), lambda i: (0, i, 0, 0)), once),
        out_shape=(
            jax.ShapeDtypeStruct(out.shape, out.dtype),
            jax.ShapeDtypeStruct((2, 2, 64, width), jnp.bfloat16),
            jax.ShapeDtypeStruct((1, width), jnp.float32),
        ),
        input_output_aliases={6: 0},
        compiler_params=params(),
        cost_estimate=cost(2 * 256 * 9 * width * width, 3 * 1024 * 1024),
        name="forward_edges",
    )(halos.reshape(2, 128, width), mask, weight, edge, cotangent, inside, out)


def turned_kernel(ref, turned):
    half = ref.shape[3]

    def fill(z, carry):
        plane = both(ref, z).astype(jnp.float32).T
        for p in range(3):
            for q in range(3):
                at = (3 * p + q) * half
                turned[at : at + half, pl.ds(pl.multiple_of(z * 128, 128), 128)] = shifted_lanes(
                    plane, p - 1, q - 1
                ).astype(jnp.bfloat16)
        return carry

    lax.fori_loop(0, 8, fill, 0)


def turn_features(feats):
    half = feats.shape[3]
    return pl.pallas_call(
        turned_kernel,
        out_shape=jax.ShapeDtypeStruct((9 * half, 1024), jnp.bfloat16),
        compiler_params=params(),
        cost_estimate=cost(0, 6 * 1024 * 1024),
        name="turn_features",
    )(feats)


def inner_terms_kernel(mine, theirs, grad, their_grad, terms):
    for a in range(3):
        lanes = slice(128 * a, 128 * a + 768)
        terms[a] = jnp.dot(mine[:, lanes], grad[...], preferred_element_type=jnp.float32)
        terms[a] += jnp.dot(theirs[:, lanes], their_grad[...], preferred_element_type=jnp.float32)


def inner_terms(mine, theirs, grad, their_grad):
    rows, width = mine.shape[0], grad.shape[1]
    return pl.pallas_call(
        inner_terms_kernel,
        out_shape=jax.ShapeDtypeStruct((3, rows, width), jnp.float32),
        compiler_params=params(),
        cost_estimate=cost(2 * 1536 * 3 * rows * width, 8 * 1024 * 1024),
        name="inner_terms",
    )(mine, theirs, grad, their_grad)


def outer_terms_kernel(a, upper, mine_low, theirs_low, mine_high, theirs_high, rims, inner, give, stay, cols, total):
    half = cols.shape[0] // 9
    for place, ref in enumerate((mine_low, theirs_low, mine_high, theirs_high)):
        lanes = slice(128 * place, 128 * place + 128)
        if ref.shape[0] == 128:
            plane = ref[...].astype(jnp.float32).T
            for p in range(3):
                for q in range(3):
                    at = (3 * p + q) * half
                    cols[at : at + half, lanes] = shifted_lanes(plane, p - 1, q - 1).astype(jnp.bfloat16)
        else:
            cols[:, lanes] = ref[...]
    total[...] = inner[0] + jnp.dot(cols[...], rims[...], preferred_element_type=jnp.float32)
    rows = give.shape[0]
    mine = upper[0]
    give[...] = total[pl.ds(pl.multiple_of((1 - mine) * rows, 16), rows), :].astype(jnp.bfloat16)
    stay[...] = total[pl.ds(pl.multiple_of(mine * rows, 16), rows), :]


def outer_terms(a, mine, theirs, halos, their_halos, rims, inner, size):
    rows, width = inner.shape[1], inner.shape[2]
    half = rows // 9
    first = bits(size)[0]
    upper = ((lax.axis_index("zslab") // first) % 2).astype(jnp.int32).reshape(1)

    def lanes(place):
        return pl.BlockSpec((rows, 128), lambda i: (0, place))

    def halo(side):
        return pl.BlockSpec((128, half), lambda i: (side, 0))

    low = (halos, their_halos, halo(0)) if a == 0 else (mine, theirs, lanes(a - 1))
    high = (halos, their_halos, halo(1)) if a == 2 else (mine, theirs, lanes(6 + a))
    return pl.pallas_call(
        functools.partial(outer_terms_kernel, a),
        grid=(1,),
        in_specs=[
            pl.BlockSpec(memory_space=pltpu.SMEM),
            low[2],
            low[2],
            high[2],
            high[2],
            pl.BlockSpec((512, width), lambda i: (0, 0)),
            pl.BlockSpec((1, rows, width), lambda i: (a, 0, 0)),
        ],
        out_specs=(
            pl.BlockSpec((rows // 2, width), lambda i: (0, 0)),
            pl.BlockSpec((rows // 2, width), lambda i: (0, 0)),
        ),
        out_shape=(
            jax.ShapeDtypeStruct((rows // 2, width), jnp.bfloat16),
            jax.ShapeDtypeStruct((rows // 2, width), jnp.float32),
        ),
        scratch_shapes=[pltpu.VMEM((rows, 512), jnp.bfloat16), pltpu.VMEM((rows, width), jnp.float32)],
        compiler_params=params(),
        cost_estimate=cost(2 * 512 * rows * width, 4 * 1024 * 1024),
        name="outer_terms",
    )(upper, low[0], low[1], high[0], high[1], rims, inner)


def backward_kernel(first, last, grad, rims, halos, mask, weight, *rest):
    grad_feats, cols = rest[-2:]
    width = grad.shape[1]
    place = 0
    for plane in range(first - 1, last + 2):
        if plane < 0 or plane > 7:
            rows = halos[(0 if plane < 0 else 128) : (128 if plane < 0 else 256)]
        elif plane in (0, 7):
            side = plane // 7
            rows = jnp.concatenate([rims[0, side], rims[1, side]], axis=0)
        else:
            rows = grad[128 * (plane - 1) : 128 * plane]
        rows = rows.astype(jnp.float32)
        for p in range(3):
            for q in range(3):
                at = (3 * p + q) * width
                cols[place : place + 128, at : at + width] = shifted(rows, 1 - p, 1 - q).astype(jnp.bfloat16)
        place += 128
    count = 128 * (last - first + 1)
    total = jnp.zeros((count, width), jnp.float32)
    for a in range(3):
        for pq in range(9):
            piece = cols[(2 - a) * 128 : (2 - a) * 128 + count, pq * width : (pq + 1) * width]
            total += lax.dot_general(
                piece, weight[9 * a + pq], (((1,), (1,)), ((), ())), preferred_element_type=jnp.float32
            )
    for z in range(last - first + 1):
        rows = slice(128 * z, 128 * z + 128)
        done = jnp.where(wide(mask[rows, :]), total[rows, :], 0.0).astype(jnp.bfloat16)
        for b in range(2):
            grad_feats[b, z] = done[64 * b : 64 * b + 64]


def backward(first, last, grad, rims, halos, mask, weight, done):
    width = grad.shape[1]
    count = last - first + 1
    block = first // count

    def whole(x):
        return pl.BlockSpec(x.shape, lambda i: (0,) * x.ndim)

    given = [grad, rims, halos, mask, weight] + ([] if done is None else [done])
    return pl.pallas_call(
        functools.partial(backward_kernel, first, last),
        grid=(1,),
        in_specs=[
            whole(grad),
            whole(rims),
            whole(halos),
            pl.BlockSpec((128 * count, 128), lambda i: (block, 0)),
            whole(weight),
        ]
        + ([] if done is None else [pl.BlockSpec(memory_space=pl.ANY)]),
        out_specs=pl.BlockSpec((2, count, 64, width), lambda i: (0, block, 0, 0)),
        out_shape=jax.ShapeDtypeStruct((2, 8, 64, width), jnp.bfloat16),
        scratch_shapes=[pltpu.VMEM((128 * (count + 2), 9 * width), jnp.bfloat16)],
        input_output_aliases={} if done is None else {5: 0},
        compiler_params=params(),
        cost_estimate=cost(2 * 128 * count * 27 * width * width, 5 * 1024 * 1024),
        name="backward",
    )(*given)


def per_device(size, feats, voxmask, links, weight, bias, cotangent):
    width = feats.shape[3]
    half = width // 2
    core = lax.axis_index("zslab") % 2

    def halves(x):
        parts = x.reshape(x.shape[:-1] + (2, half))
        first, second = parts[..., 0, :], parts[..., 1, :]
        return jnp.where(core == 0, first, second), jnp.where(core == 0, second, first)

    keep = (voxmask == 1).reshape(2, 8, 64, 1)
    rims = jnp.stack([feats[:, 0], feats[:, 7]], axis=1)
    rims = jnp.where(jnp.stack([keep[:, 0], keep[:, 7]], axis=1), rims, jnp.zeros_like(rims))
    codes = jnp.pad(links.reshape(4).astype(jnp.bfloat16), (0, width - 4))
    parcel = jnp.concatenate([rims.reshape(256, width), extra_rows([codes])])
    group = gather_group(parcel, size, 2)
    near = group_links(group[:, 256], size)
    picks = pick(near, group, size)

    mask = jnp.broadcast_to(keep.transpose(1, 0, 2, 3).astype(jnp.float32).reshape(1024, 1), (1024, 128))
    own, give = halves(jnp.where(keep, feats, jnp.zeros_like(feats)))
    theirs = swap(give, size, 1)
    turned = turn_features(own)
    their_turned = turn_features(theirs)

    picks, feats, cotangent = lax.optimization_barrier((picks, feats, cotangent))
    halos, _ = spread_picks([picks[k] for k in range(size // 4)], links, size)

    out, grad, edge, inside = forward_inside(feats, mask, weight, bias.reshape(1, width), cotangent)
    their_grad = swap(grad, size, 1)
    inner = inner_terms(turned, their_turned, grad, their_grad)

    out, grad_rims, bias_local = forward_edges(halos, mask, weight, edge, cotangent, inside, out)
    own_halos, give = halves(halos.reshape(256, width))
    their_halos = swap(give, size, 1)

    parcel = jnp.concatenate([grad_rims.reshape(256, width), extra_rows(exact_terms(bias_local[0]))])
    group = gather_group(parcel, size, 1)
    bias_group = sum_terms(group[:, 256:])
    picks = pick(near, group, size)
    extra = extra_rows(exact_terms(bias_group))
    grad_halos, extra = spread_picks(
        [jnp.concatenate([picks[k], extra]) for k in range(size // 4)], links, size
    )
    grad_bias = sum_terms(jnp.stack(extra))

    sides = [group[who, :256].reshape(2, 2, 64, width)[:, side].reshape(128, width) for side in (0, 1) for who in (0, 1)]
    rims_rows = jnp.concatenate(sides)
    parts = []
    for a in range(3):
        give, stay = outer_terms(a, turned, their_turned, own_halos, their_halos, rims_rows, inner, size)
        part = sum_and_gather(give, stay, size)
        other = swap(part, size, 1)
        part = part.reshape(9, 1, half, width)
        other = other.reshape(9, 1, half, width)
        parts.append(
            jnp.where(
                core == 0, jnp.concatenate([part, other], axis=1), jnp.concatenate([other, part], axis=1)
            ).reshape(9, width, width)
        )
    grad_weight = jnp.concatenate(parts, axis=0)

    flat_halos = grad_halos.reshape(256, width)
    grad_feats = None
    for first, last in ((2, 3), (4, 5), (0, 1), (6, 7)):
        given = flat_halos if first in (0, 6) else halos.reshape(256, width)
        grad_feats = backward(first, last, grad, grad_rims, given, mask, weight, grad_feats)
    return out, grad_feats, grad_weight, grad_bias


def solution(mesh):
    return jax.shard_map(
        functools.partial(per_device, mesh.shape["zslab"]),
        mesh=mesh,
        in_specs=(
            P(("groups", "zslab"), None, None, None),
            P(("groups", "zslab"), None),
            P(("groups", "zslab"), None),
            P(),
            P(),
            P(("groups", "zslab"), None, None, None),
        ),
        out_specs=(
            P(("groups", "zslab"), None, None, None),
            P(("groups", "zslab"), None, None, None),
            P("groups", None, None),
            P("groups"),
        ),
        check_vma=False,
    )
```

time: 179 us -> 162 us (0.905)
  starting transfers between devices: 53.1 us -> 27.4 us
  blocking collectives: 21.1 us -> 0 us
  Pallas kernels: 39.4 us -> 58.6 us
  waiting for transfers between devices: 39.8 us -> 46.1 us
  other arithmetic: 9.93 us -> 13.4 us
    ppermute x27 -> x6, starting transfers between devices: 44.6 us -> 9.8 us  [rotate(): lax.ppermute(x, 'zslab', [(i, (i + 4 * steps) % size) for i in range(size)])]
    all_gather x1 -> x0, blocking collectives: 21.1 us -> none  [per_device(): lax.all_gather(bias_local, 'zslab', axis=0, tiled=True)]
    pallas_call x5 -> x14, Pallas kernels: 39.4 us -> 58.6 us  [the longest x4 16.5 us: backward(): pl.pallas_call(functools.partial(backward_kernel, first, last), grid=(1,)...]
    ppermute x16 -> x28, waiting for transfers between devices: 27.4 us -> 40.1 us  [swap(): return lax.ppermute(x, 'zslab', [(i, i ^ bit) for i in range(size)])]
    ppermute x16 -> x28, starting transfers between devices: 8.49 us -> 17.6 us  [swap(): return lax.ppermute(x, 'zslab', [(i, i ^ bit) for i in range(size)])]
    ppermute x27 -> x6, waiting for transfers between devices: 12.5 us -> 5.95 us  [rotate(): lax.ppermute(x, 'zslab', [(i, (i + 4 * steps) % size) for i in range(size)])]
    gather x8 -> x0, local copies, waits for them, and re-layouts: 4.44 us -> none  [fetch_halos(): got = jnp.take(planes, places[steps], axis=0)]
    select_n x14 -> x15, other arithmetic: 5.48 us -> 5.81 us  [the longest x3 2.93 us: spread_picks(): jnp.where(here[:, None, None], got[:256].reshape(halos.shape), halos)]
  transfers between devices with their start and end apart: 43 -> 34, of which waited for: 13 -> 18; matrix products, arithmetic and copies ran while one was open for 11% -> 11% of each run, Pallas kernels for 22% -> 35%
where the time goes in v3:
time: 162 us; the launch traced here: 161 us
  Pallas kernels  58.6 us (36%)
  waiting for transfers between devices  46.1 us (28%)
  starting transfers between devices  27.4 us (17%)
  local copies, waits for them, and re-layouts  14.7 us (9%)
  other arithmetic  13.4 us (8%)
    ppermute x28, waiting for transfers between devices, swap(): return lax.ppermute(x, 'zslab', [(i, i ^ bit) for i in range(size)])  40.1 us
    ppermute x28, starting transfers between devices, swap(): return lax.ppermute(x, 'zslab', [(i, i ^ bit) for i in range(size)])  17.6 us
    pallas_call x4, Pallas kernels, backward(): pl.pallas_call(functools.partial(backward_kernel, first, last), grid=(1,)...  16.5 us
    ppermute x6, starting transfers between devices, rotate(): lax.ppermute(x, 'zslab', [(i, (i + 4 * steps) % size) for i in range(size)])  9.8 us
    pallas_call x3, Pallas kernels, outer_terms(): pl.pallas_call(functools.partial(outer_terms_kernel, a), grid=(1,), in_sp...  9.67 us
    pallas_call x1, Pallas kernels, forward_inside(): pl.pallas_call(forward_kernel, out_shape=(jax.ShapeDtypeStruct(feats.shap...  8.69 us
    pallas_call x2, Pallas kernels, turn_features(): pl.pallas_call(turned_kernel, out_shape=jax.ShapeDtypeStruct((9 * half, 1...  8.65 us
    pallas_call x1, Pallas kernels, inner_terms(): pl.pallas_call(inner_terms_kernel, out_shape=jax.ShapeDtypeStruct((3, row...  7.24 us
  transfers between devices with their start and end apart: 34, of which 18 were waited for; matrix products, arithmetic and copies ran while one was open for 11% of the time, Pallas kernels for 35%

profile of v3, /device:TPU:0, one launch (start us, length us, event | category | flops | bytes accessed | tf_op | source)
XLA Modules:
  0.0 161.3 jit_solution(264609547678568558)
XLA Ops:
  3.7 3.0 %collective-permute-start = (bf16[272,256]{1,0:T(8,128)(2,1)S(1)}, bf16[272,256]{1,0:T(8,128)(2,1)S(1)}, u32[]{:S(2)}, u32[]{:S(2)}) collective-permute-start(bf16[272,256]{1,0:T(8,128)(2,1)S(1)} %get-tuple-element.62), channel_id=1, source_target_pairs={{0,2},{1,3},{2,0},{3,1},{4,6},{5,7},{6,4},{7,5},{8,10},{9,11},{10,... | collective-permute-start | bytes 417800 | tf_op jit(solution)/shard_map/ppermute | solution.py:23
  12.3 4.3 %turn_features.2.mine.mine_high.mine_low = bf16[1152,1024]{1,0:T(8,128)(2,1)} custom-call(bf16[2,8,64,128]{3,2,1,0:T(8,128)(2,1)} %get-tuple-element.41.ref), custom_call_target="tpu_custom_call" | custom-call | bytes 6291456 | tf_op jit(solution)/shard_map/turn_features/pallas_call | solution.py:313
  17.9 4.3 %turn_features.3.theirs.theirs_high.theirs_low = bf16[1152,1024]{1,0:T(8,128)(2,1)} custom-call(bf16[2,8,64,128]{3,2,1,0:T(8,128)(2,1)} %copy-done.7), custom_call_target="tpu_custom_call" | custom-call | bytes 6291456 | tf_op jit(solution)/shard_map/turn_features/pallas_call | solution.py:313
  23.2 2.4 %pick_planes.2 = bf16[4,256,256]{2,1,0:T(8,128)(2,1)} custom-call(s32[2]{0:T(128)} %pad_add_fusion.1.where, s32[16]{0:T(128)} %reshape.309.links, bf16[4,272,256]{2,1,0:T(8,128)(2,1)} %copy-done.1), custom_call_target="tpu_custom_call" | custom-call | bytes 2097152 | tf_op jit(solution)/shard_map/pick_planes/pallas_call | solution.py:91
  28.3 2.6 %collective-permute-start.3 = (bf16[256,256]{1,0:T(8,128)(2,1)S(1)}, bf16[256,256]{1,0:T(8,128)(2,1)S(1)}, u32[]{:S(2)}, u32[]{:S(2)}) collective-permute-start(bf16[256,256]{1,0:T(8,128)(2,1)S(1)} %get-tuple-element.55), channel_id=1, source_target_pairs={{0,8},{1,9},{2,10},{3,11},{4,12},{5,13},{6,14},{7,15},{8,0},{9,1},... | collective-permute-start | bytes 393224 | tf_op jit(solution)/shard_map/ppermute | solution.py:27
  33.3 8.7 %forward_inside.1 = (bf16[2,8,64,256]{3,2,1,0:T(8,128)(2,1)}, bf16[768,256]{1,0:T(8,128)(2,1)}, f32[2,128,256]{2,1,0:T(8,128)}, f32[1,256]{1,0:T(1,128)}) custom-call(bf16[2,8,64,256]{3,2,1,0:T(8,128)(2,1)} %feats, f32[1024,128]{1,0:T(8,128)} %broadcast_in_dim.148.mask, bf16[27,256,256]{2,1,0:T(8,128)(2,1)} %weight.11, f32[1,256]{1,0:T(1,128)} %bitcast.149, ...), custom_call_target="tpu_custom_call" | custom-call | flops 3623878656 | bytes 6291456 | tf_op jit(solution)/shard_map/forward_inside/pallas_call | solution.py:225
  45.2 3.0 %forward_edges.1 = (bf16[2,8,64,256]{3,2,1,0:T(8,128)(2,1)}, bf16[2,2,64,256]{3,2,1,0:T(8,128)(2,1)}, f32[1,256]{1,0:T(1,128)}) custom-call(bf16[2,128,256]{2,1,0:T(8,128)(2,1)} %select_select_fusion.1.halos, f32[1024,128]{1,0:T(8,128)} %broadcast_in_dim.148.mask, bf16[27,256,256]{2,1,0:T(8,128)(2,1)} %weight.11, ...), custom_call_target="tpu_custom_call", output_to_operand_aliasing={{0}: (6, {})} | custom-call | flops 301989888 | bytes 3145728 | tf_op jit(solution)/shard_map/forward_edges/pallas_call | solution.py:270
  53.4 7.2 %inner_terms.1.inner = f32[3,1152,256]{2,1,0:T(8,128)} custom-call(bf16[1152,1024]{1,0:T(8,128)(2,1)} %turn_features.2.mine.mine_high.mine_low, bf16[1152,1024]{1,0:T(8,128)(2,1)} %turn_features.3.theirs.theirs_high.theirs_low, bf16[768,256]{1,0:T(8,128)(2,1)} %get-tuple-element.27.grad, bf16[768,256]{1,0:T(8,128)(2,1)} %copy-done.9), custom_call_target="tpu_custom_call" | custom-call | flops 2717908992 | bytes 8388608 | tf_op jit(solution)/shard_map/inner_terms/pallas_call | solution.py:331
  61.3 3.2 %outer_terms.5 = (bf16[576,256]{1,0:T(8,128)(2,1)}, f32[576,256]{1,0:T(8,128)}) custom-call(s32[1]{0:T(128)} %bitcast.27.upper, bf16[1152,1024]{1,0:T(8,128)(2,1)} %turn_features.2.mine.mine_high.mine_low, bf16[1152,1024]{1,0:T(8,128)(2,1)} %turn_features.3.theirs.theirs_high.theirs_low, bf16[256,128]{1,0:T(8,128)(2,1)} %get-tuple-element.68.mine_low.mine_high, ...), custom_call_target="tpu_custom_call" | custom-call | flops 301989888 | bytes 4194304 | tf_op jit(solution)/shard_map/outer_terms/pallas_call | solution.py:373
  66.1 3.2 %outer_terms.3 = (bf16[576,256]{1,0:T(8,128)(2,1)}, f32[576,256]{1,0:T(8,128)}) custom-call(s32[1]{0:T(128)} %bitcast.27.upper, bf16[256,128]{1,0:T(8,128)(2,1)} %get-tuple-element.68.mine_low.mine_high, bf16[256,128]{1,0:T(8,128)(2,1)} %copy-done.6, bf16[1152,1024]{1,0:T(8,128)(2,1)} %turn_features.2.mine.mine_high.mine_low, ...), custom_call_target="tpu_custom_call" | custom-call | flops 301989888 | bytes 4194304 | tf_op jit(solution)/shard_map/outer_terms/pallas_call | solution.py:373
  69.8 3.2 %outer_terms.4 = (bf16[576,256]{1,0:T(8,128)(2,1)}, f32[576,256]{1,0:T(8,128)}) custom-call(s32[1]{0:T(128)} %bitcast.27.upper, bf16[1152,1024]{1,0:T(8,128)(2,1)} %turn_features.2.mine.mine_high.mine_low, bf16[1152,1024]{1,0:T(8,128)(2,1)} %turn_features.3.theirs.theirs_high.theirs_low, bf16[1152,1024]{1,0:T(8,128)(2,1)} %turn_features.2.mine.mine_high.mine_low, ...), custom_call_target="tpu_custom_call" | custom-call | flops 301989888 | bytes 4194304 | tf_op jit(solution)/shard_map/outer_terms/pallas_call | solution.py:373
  75.4 2.5 %pick_planes.3 = bf16[4,256,256]{2,1,0:T(8,128)(2,1)} custom-call(s32[2]{0:T(128)} %pad_add_fusion.1.where, s32[16]{0:T(128)} %reshape.309.links, bf16[4,272,256]{2,1,0:T(8,128)(2,1)} %copy-done), custom_call_target="tpu_custom_call" | custom-call | bytes 2097152 | tf_op jit(solution)/shard_map/pick_planes/pallas_call | solution.py:91
  87.0 4.3 %collective-permute-done.8 = bf16[272,256]{1,0:T(8,128)(2,1)S(1)} collective-permute-done((bf16[272,256]{1,0:T(8,128)(2,1)S(1)}, bf16[272,256]{1,0:T(8,128)(2,1)S(1)}, u32[]{:S(2)}, u32[]{:S(2)}) %collective-permute-start.8) | collective-permute-done | bytes 139296 | tf_op jit(solution)/shard_map/ppermute | solution.py:27
  97.0 3.3 %collective-permute-done.14 = bf16[288,256]{1,0:T(8,128)(2,1)S(1)} collective-permute-done((bf16[288,256]{1,0:T(8,128)(2,1)S(1)}, bf16[288,256]{1,0:T(8,128)(2,1)S(1)}, u32[]{:S(2)}, u32[]{:S(2)}) %collective-permute-start.14) | collective-permute-done | bytes 147488 | tf_op jit(solution)/shard_map/ppermute | solution.py:23
  100.3 2.4 %collective-permute-done.21 = bf16[288,256]{1,0:T(8,128)(2,1)S(1)} collective-permute-done((bf16[288,256]{1,0:T(8,128)(2,1)S(1)}, bf16[288,256]{1,0:T(8,128)(2,1)S(1)}, u32[]{:S(2)}, u32[]{:S(2)}) %collective-permute-start.21) | collective-permute-done | bytes 147488 | tf_op jit(solution)/shard_map/ppermute | solution.py:23
  103.3 4.6 %collective-permute-done.29 = bf16[144,256]{1,0:T(8,128)(2,1)S(1)} collective-permute-done((bf16[144,256]{1,0:T(8,128)(2,1)S(1)}, bf16[144,256]{1,0:T(8,128)(2,1)S(1)}, u32[]{:S(2)}, u32[]{:S(2)}) %collective-permute-start.29) | collective-permute-done | bytes 73760 | tf_op jit(solution)/shard_map/ppermute | solution.py:23
  119.2 2.8 %collective-permute-done.31 = bf16[288,256]{1,0:T(8,128)(2,1)S(1)} collective-permute-done((bf16[288,256]{1,0:T(8,128)(2,1)S(1)}, bf16[288,256]{1,0:T(8,128)(2,1)S(1)}, u32[]{:S(2)}, u32[]{:S(2)}) %collective-permute-start.31) | collective-permute-done | bytes 147488 | tf_op jit(solution)/shard_map/ppermute | solution.py:23
  123.4 3.1 %collective-permute-done.24 = bf16[288,256]{1,0:T(8,128)(2,1)S(1)} collective-permute-done((bf16[288,256]{1,0:T(8,128)(2,1)S(1)}, bf16[288,256]{1,0:T(8,128)(2,1)S(1)}, u32[]{:S(2)}, u32[]{:S(2)}) %collective-permute-start.24) | collective-permute-done | bytes 147488 | tf_op jit(solution)/shard_map/ppermute | solution.py:23
  130.8 6.0 %collective-permute-done.25 = bf16[576,256]{1,0:T(8,128)(2,1)S(1)} collective-permute-done((bf16[576,256]{1,0:T(8,128)(2,1)S(1)}, bf16[576,256]{1,0:T(8,128)(2,1)S(1)}, u32[]{:S(2)}, u32[]{:S(2)}) %collective-permute-start.25) | collective-permute-done | bytes 294944 | tf_op jit(solution)/shard_map/ppermute | solution.py:23
  137.1 4.5 %collective-permute-done.18 = bf16[576,256]{1,0:T(8,128)(2,1)S(1)} collective-permute-done((bf16[576,256]{1,0:T(8,128)(2,1)S(1)}, bf16[576,256]{1,0:T(8,128)(2,1)S(1)}, u32[]{:S(2)}, u32[]{:S(2)}) %collective-permute-start.18) | collective-permute-done | bytes 294944 | tf_op jit(solution)/shard_map/ppermute | solution.py:23
  141.9 4.1 %backward.4.rest_0_ = bf16[2,8,64,256]{3,2,1,0:T(8,128)(2,1)} custom-call(bf16[768,256]{1,0:T(8,128)(2,1)} %get-tuple-element.27.grad, bf16[2,2,64,256]{3,2,1,0:T(8,128)(2,1)} %get-tuple-element.28.rims, bf16[256,256]{1,0:T(8,128)(2,1)} %get-tuple-element.69.halos, f32[1024,128]{1,0:T(8,128)} %broadcast_in_dim.148.mask, bf16[27,256,256]{2,1,0:T(8,128)(2,1)} %weight.11), custom_call_target="tpu_custom_call" | custom-call | flops 905969664 | bytes 5242880 | tf_op jit(solution)/shard_map/backward/pallas_call | solution.py:442
  146.1 4.1 %backward.5.rest_0_ = bf16[2,8,64,256]{3,2,1,0:T(8,128)(2,1)} custom-call(bf16[768,256]{1,0:T(8,128)(2,1)} %get-tuple-element.27.grad, bf16[2,2,64,256]{3,2,1,0:T(8,128)(2,1)} %get-tuple-element.28.rims, bf16[256,256]{1,0:T(8,128)(2,1)} %get-tuple-element.69.halos, f32[1024,128]{1,0:T(8,128)} %broadcast_in_dim.148.mask, ...), custom_call_target="tpu_custom_call", output_to_operand_aliasing={{}: (5, {})} | custom-call | flops 905969664 | bytes 5242880 | tf_op jit(solution)/shard_map/backward/pallas_call | solution.py:442
  150.2 4.1 %backward.6.rest_0_ = bf16[2,8,64,256]{3,2,1,0:T(8,128)(2,1)} custom-call(bf16[768,256]{1,0:T(8,128)(2,1)} %get-tuple-element.27.grad, bf16[2,2,64,256]{3,2,1,0:T(8,128)(2,1)} %get-tuple-element.28.rims, bf16[256,256]{1,0:T(8,128)(2,1)} %get-tuple-element.70.halos, f32[1024,128]{1,0:T(8,128)} %broadcast_in_dim.148.mask, ...), custom_call_target="tpu_custom_call", output_to_operand_aliasing={{}: (5, {})} | custom-call | flops 905969664 | bytes 5242880 | tf_op jit(solution)/shard_map/backward/pallas_call | solution.py:442
  154.3 4.1 %backward.7 = bf16[2,8,64,256]{3,2,1,0:T(8,128)(2,1)} custom-call(bf16[768,256]{1,0:T(8,128)(2,1)} %get-tuple-element.27.grad, bf16[2,2,64,256]{3,2,1,0:T(8,128)(2,1)} %get-tuple-element.28.rims, bf16[256,256]{1,0:T(8,128)(2,1)} %get-tuple-element.70.halos, f32[1024,128]{1,0:T(8,128)} %broadcast_in_dim.148.mask, ...), custom_call_target="tpu_custom_call", output_to_operand_aliasing={{}: (5, {})} | custom-call | flops 905969664 | bytes 5242880 | tf_op jit(solution)/shard_map/backward/pallas_call | solution.py:442
  (202 shorter events, 65.0 us)
Async XLA Ops:
  11.6 10.6 %collective-permute-start.1 = (bf16[2,272,256]{2,1,0:T(8,128)(2,1)S(1)}, bf16[2,272,256]{2,1,0:T(8,128)(2,1)S(1)}, u32[]{:S(2)}, u32[]{:S(2)}) collective-permute-start(bf16[2,272,256]{2,1,0:T(8,128)(2,1)S(1)} %pad_maximum_fusion.3), channel_id=1, source_target_pairs={{0,1},{1,0},{2,3},{3,2},{4,5},{5,4},{6,7},{7,6},{8,9},{9,8},{10,11... | collective-permute-start | bytes 835592 | tf_op jit(solution)/shard_map/ppermute | solution.py:23
  26.7 15.6 %collective-permute-start.4 = (bf16[256,256]{1,0:T(8,128)(2,1)S(1)}, bf16[256,256]{1,0:T(8,128)(2,1)S(1)}, u32[]{:S(2)}, u32[]{:S(2)}) collective-permute-start(bf16[256,256]{1,0:T(8,128)(2,1)S(1)} %get-tuple-element.54), channel_id=1, source_target_pairs={{0,4},{1,5},{2,6},{3,7},{4,8},{5,9},{6,10},{7,11},{8,12},{9,13},{1... | collective-permute-start | bytes 393224 | tf_op jit(solution)/shard_map/ppermute | solution.py:27
  28.3 14.2 %collective-permute-start.3 = (bf16[256,256]{1,0:T(8,128)(2,1)S(1)}, bf16[256,256]{1,0:T(8,128)(2,1)S(1)}, u32[]{:S(2)}, u32[]{:S(2)}) collective-permute-start(bf16[256,256]{1,0:T(8,128)(2,1)S(1)} %get-tuple-element.55), channel_id=1, source_target_pairs={{0,8},{1,9},{2,10},{3,11},{4,12},{5,13},{6,14},{7,15},{8,0},{9,1},... | collective-permute-start | bytes 393224 | tf_op jit(solution)/shard_map/ppermute | solution.py:27
  30.9 11.8 %collective-permute-start.2 = (bf16[256,256]{1,0:T(8,128)(2,1)S(1)}, bf16[256,256]{1,0:T(8,128)(2,1)S(1)}, u32[]{:S(2)}, u32[]{:S(2)}) collective-permute-start(bf16[256,256]{1,0:T(8,128)(2,1)S(1)} %get-tuple-element.56), channel_id=1, source_target_pairs={{0,12},{1,13},{2,14},{3,15},{4,0},{5,1},{6,2},{7,3},{8,4},{9,5},{1... | collective-permute-start | bytes 393224 | tf_op jit(solution)/shard_map/ppermute | solution.py:27
  42.2 10.5 %collective-permute-start.12 = (bf16[768,256]{1,0:T(8,128)(2,1)}, bf16[768,256]{1,0:T(8,128)(2,1)S(1)}, u32[]{:S(2)}, u32[]{:S(2)}) collective-permute-start(bf16[768,256]{1,0:T(8,128)(2,1)} %get-tuple-element.27.grad), channel_id=1, source_target_pairs={{0,1},{1,0},{2,3},{3,2},{4,5},{5,4},{6,7},{7,6},{8,9},{9,8},{10,11... | collective-permute-start | bytes 1179656 | tf_op jit(solution)/shard_map/ppermute | solution.py:23
  43.8 16.8 %collective-permute-start.10 = (bf16[256,128]{1,0:T(8,128)(2,1)S(1)}, bf16[256,128]{1,0:T(8,128)(2,1)S(1)}, u32[]{:S(2)}, u32[]{:S(2)}) collective-permute-start(bf16[256,128]{1,0:T(8,128)(2,1)S(1)} %get-tuple-element.67), channel_id=1, source_target_pairs={{0,1},{1,0},{2,3},{3,2},{4,5},{5,4},{6,7},{7,6},{8,9},{9,8},{10,11... | collective-permute-start | bytes 196616 | tf_op jit(solution)/shard_map/ppermute | solution.py:23
  51.4 23.2 %collective-permute-start.6 = (bf16[2,272,256]{2,1,0:T(8,128)(2,1)S(1)}, bf16[2,272,256]{2,1,0:T(8,128)(2,1)S(1)}, u32[]{:S(2)}, u32[]{:S(2)}) collective-permute-start(bf16[2,272,256]{2,1,0:T(8,128)(2,1)S(1)} %pad_maximum_fusion.4), channel_id=1, source_target_pairs={{0,2},{1,3},{2,0},{3,1},{4,6},{5,7},{6,4},{7,5},{8,10},{9,11},{10,... | collective-permute-start | bytes 835592 | tf_op jit(solution)/shard_map/ppermute | solution.py:23
  64.6 16.8 %collective-permute-start.27 = (bf16[576,256]{1,0:T(8,128)(2,1)}, bf16[576,256]{1,0:T(8,128)(2,1)S(1)}, u32[]{:S(2)}, u32[]{:S(2)}) collective-permute-start(bf16[576,256]{1,0:T(8,128)(2,1)} %get-tuple-element.35), channel_id=1, source_target_pairs={{0,2},{1,3},{2,0},{3,1},{4,6},{5,7},{6,4},{7,5},{8,10},{9,11},{10,... | collective-permute-start | bytes 884744 | tf_op jit(solution)/shard_map/ppermute | solution.py:23
  69.3 14.5 %collective-permute-start.13 = (bf16[576,256]{1,0:T(8,128)(2,1)}, bf16[576,256]{1,0:T(8,128)(2,1)S(1)}, u32[]{:S(2)}, u32[]{:S(2)}) collective-permute-start(bf16[576,256]{1,0:T(8,128)(2,1)} %get-tuple-element.31), channel_id=1, source_target_pairs={{0,2},{1,3},{2,0},{3,1},{4,6},{5,7},{6,4},{7,5},{8,10},{9,11},{10,... | collective-permute-start | bytes 884744 | tf_op jit(solution)/shard_map/ppermute | solution.py:23
  73.0 13.2 %collective-permute-start.20 = (bf16[576,256]{1,0:T(8,128)(2,1)}, bf16[576,256]{1,0:T(8,128)(2,1)S(1)}, u32[]{:S(2)}, u32[]{:S(2)}) collective-permute-start(bf16[576,256]{1,0:T(8,128)(2,1)} %get-tuple-element.33), channel_id=1, source_target_pairs={{0,2},{1,3},{2,0},{3,1},{4,6},{5,7},{6,4},{7,5},{8,10},{9,11},{10,... | collective-permute-start | bytes 884744 | tf_op jit(solution)/shard_map/ppermute | solution.py:23
  79.5 11.8 %collective-permute-start.8 = (bf16[272,256]{1,0:T(8,128)(2,1)S(1)}, bf16[272,256]{1,0:T(8,128)(2,1)S(1)}, u32[]{:S(2)}, u32[]{:S(2)}) collective-permute-start(bf16[272,256]{1,0:T(8,128)(2,1)S(1)} %concatenate.107), channel_id=1, source_target_pairs={{0,8},{1,9},{2,10},{3,11},{4,12},{5,13},{6,14},{7,15},{8,0},{9,1},... | collective-permute-start | bytes 417800 | tf_op jit(solution)/shard_map/ppermute | solution.py:27
  79.9 11.4 %collective-permute-start.9 = (bf16[272,256]{1,0:T(8,128)(2,1)S(1)}, bf16[272,256]{1,0:T(8,128)(2,1)S(1)}, u32[]{:S(2)}, u32[]{:S(2)}) collective-permute-start(bf16[272,256]{1,0:T(8,128)(2,1)S(1)} %concatenate.108), channel_id=1, source_target_pairs={{0,4},{1,5},{2,6},{3,7},{4,8},{5,9},{6,10},{7,11},{8,12},{9,13},{1... | collective-permute-start | bytes 417800 | tf_op jit(solution)/shard_map/ppermute | solution.py:27
  81.4 11.6 %collective-permute-start.7 = (bf16[272,256]{1,0:T(8,128)(2,1)S(1)}, bf16[272,256]{1,0:T(8,128)(2,1)S(1)}, u32[]{:S(2)}, u32[]{:S(2)}) collective-permute-start(bf16[272,256]{1,0:T(8,128)(2,1)S(1)} %concatenate.106), channel_id=1, source_target_pairs={{0,12},{1,13},{2,14},{3,15},{4,0},{5,1},{6,2},{7,3},{8,4},{9,5},{1... | collective-permute-start | bytes 417800 | tf_op jit(solution)/shard_map/ppermute | solution.py:27
  83.8 12.3 %collective-permute-start.28 = (bf16[288,256]{1,0:T(8,128)(2,1)S(1)}, bf16[288,256]{1,0:T(8,128)(2,1)S(1)}, u32[]{:S(2)}, u32[]{:S(2)}) collective-permute-start(bf16[288,256]{1,0:T(8,128)(2,1)S(1)} %get-tuple-element.46), channel_id=1, source_target_pairs={{0,4},{1,5},{2,6},{3,7},{4,0},{5,1},{6,2},{7,3},{8,12},{9,13},{10,... | collective-permute-start | bytes 442376 | tf_op jit(solution)/shard_map/ppermute | solution.py:23
  86.2 14.0 %collective-permute-start.14 = (bf16[288,256]{1,0:T(8,128)(2,1)S(1)}, bf16[288,256]{1,0:T(8,128)(2,1)S(1)}, u32[]{:S(2)}, u32[]{:S(2)}) collective-permute-start(bf16[288,256]{1,0:T(8,128)(2,1)S(1)} %get-tuple-element.42), channel_id=1, source_target_pairs={{0,4},{1,5},{2,6},{3,7},{4,0},{5,1},{6,2},{7,3},{8,12},{9,13},{10,... | collective-permute-start | bytes 442376 | tf_op jit(solution)/shard_map/ppermute | solution.py:23
  91.2 11.5 %collective-permute-start.21 = (bf16[288,256]{1,0:T(8,128)(2,1)S(1)}, bf16[288,256]{1,0:T(8,128)(2,1)S(1)}, u32[]{:S(2)}, u32[]{:S(2)}) collective-permute-start(bf16[288,256]{1,0:T(8,128)(2,1)S(1)} %get-tuple-element.44), channel_id=1, source_target_pairs={{0,4},{1,5},{2,6},{3,7},{4,0},{5,1},{6,2},{7,3},{8,12},{9,13},{10,... | collective-permute-start | bytes 442376 | tf_op jit(solution)/shard_map/ppermute | solution.py:23
  96.1 11.8 %collective-permute-start.29 = (bf16[144,256]{1,0:T(8,128)(2,1)S(1)}, bf16[144,256]{1,0:T(8,128)(2,1)S(1)}, u32[]{:S(2)}, u32[]{:S(2)}) collective-permute-start(bf16[144,256]{1,0:T(8,128)(2,1)S(1)} %add_convert_fusion.4), channel_id=1, source_target_pairs={{0,8},{1,9},{2,10},{3,11},{4,12},{5,13},{6,14},{7,15},{8,0},{9,1},... | collective-permute-start | bytes 221192 | tf_op jit(solution)/shard_map/ppermute | solution.py:23
  100.3 10.0 %collective-permute-start.15 = (bf16[144,256]{1,0:T(8,128)(2,1)S(1)}, bf16[144,256]{1,0:T(8,128)(2,1)S(1)}, u32[]{:S(2)}, u32[]{:S(2)}) collective-permute-start(bf16[144,256]{1,0:T(8,128)(2,1)S(1)} %add_convert_fusion.8), channel_id=1, source_target_pairs={{0,8},{1,9},{2,10},{3,11},{4,12},{5,13},{6,14},{7,15},{8,0},{9,1},... | collective-permute-start | bytes 221192 | tf_op jit(solution)/shard_map/ppermute | solution.py:23
  117.0 10.1 %collective-permute-start.17 = (bf16[288,256]{1,0:T(8,128)(2,1)S(1)}, bf16[288,256]{1,0:T(8,128)(2,1)S(1)}, u32[]{:S(2)}, u32[]{:S(2)}) collective-permute-start(bf16[288,256]{1,0:T(8,128)(2,1)S(1)} %maximum_select_fusion.9), channel_id=1, source_target_pairs={{0,4},{1,5},{2,6},{3,7},{4,0},{5,1},{6,2},{7,3},{8,12},{9,13},{10,... | collective-permute-start | bytes 442376 | tf_op jit(solution)/shard_map/ppermute | solution.py:23
  126.6 10.1 %collective-permute-start.25 = (bf16[576,256]{1,0:T(8,128)(2,1)S(1)}, bf16[576,256]{1,0:T(8,128)(2,1)S(1)}, u32[]{:S(2)}, u32[]{:S(2)}) collective-permute-start(bf16[576,256]{1,0:T(8,128)(2,1)S(1)} %maximum_select_fusion.7), channel_id=1, source_target_pairs={{0,2},{1,3},{2,0},{3,1},{4,6},{5,7},{6,4},{7,5},{8,10},{9,11},{10,... | collective-permute-start | bytes 884744 | tf_op jit(solution)/shard_map/ppermute | solution.py:23
  127.3 14.3 %collective-permute-start.18 = (bf16[576,256]{1,0:T(8,128)(2,1)S(1)}, bf16[576,256]{1,0:T(8,128)(2,1)S(1)}, u32[]{:S(2)}, u32[]{:S(2)}) collective-permute-start(bf16[576,256]{1,0:T(8,128)(2,1)S(1)} %maximum_select_fusion.6), channel_id=1, source_target_pairs={{0,2},{1,3},{2,0},{3,1},{4,6},{5,7},{6,4},{7,5},{8,10},{9,11},{10,... | collective-permute-start | bytes 884744 | tf_op jit(solution)/shard_map/ppermute | solution.py:23
  130.7 27.8 %collective-permute-start.33 = (bf16[1152,256]{1,0:T(8,128)(2,1)S(1)}, bf16[1152,256]{1,0:T(8,128)(2,1)S(1)}, u32[]{:S(2)}, u32[]{:S(2)}) collective-permute-start(bf16[1152,256]{1,0:T(8,128)(2,1)S(1)} %maximum_select_fusion.5), channel_id=1, source_target_pairs={{0,1},{1,0},{2,3},{3,2},{4,5},{5,4},{6,7},{7,6},{8,9},{9,8},{10,11... | collective-permute-start | bytes 1769480 | tf_op jit(solution)/shard_map/ppermute | solution.py:23
  137.0 21.7 %collective-permute-start.26 = (bf16[1152,256]{1,0:T(8,128)(2,1)S(1)}, bf16[1152,256]{1,0:T(8,128)(2,1)S(1)}, u32[]{:S(2)}, u32[]{:S(2)}) collective-permute-start(bf16[1152,256]{1,0:T(8,128)(2,1)S(1)} %maximum_select_fusion.4), channel_id=1, source_target_pairs={{0,1},{1,0},{2,3},{3,2},{4,5},{5,4},{6,7},{7,6},{8,9},{9,8},{10,11... | collective-permute-start | bytes 1769480 | tf_op jit(solution)/shard_map/ppermute | solution.py:23
  141.9 17.2 %collective-permute-start.19 = (bf16[1152,256]{1,0:T(8,128)(2,1)S(1)}, bf16[1152,256]{1,0:T(8,128)(2,1)S(1)}, u32[]{:S(2)}, u32[]{:S(2)}) collective-permute-start(bf16[1152,256]{1,0:T(8,128)(2,1)S(1)} %maximum_select_fusion.3), channel_id=1, source_target_pairs={{0,1},{1,0},{2,3},{3,2},{4,5},{5,4},{6,7},{7,6},{8,9},{9,8},{10,11... | collective-permute-start | bytes 1769480 | tf_op jit(solution)/shard_map/ppermute | solution.py:23
  (20 other events, 97.2 us)

commit v4 on v0

v4 whole, which is shorter than its diff:
```python
import functools

import jax
import jax.numpy as jnp
from jax import lax
from jax.experimental import pallas as pl
from jax.experimental.pallas import tpu as pltpu
from jax.sharding import PartitionSpec as P

VMEM_LIMIT = 40 * 1024 * 1024
EXTRA = 16


def params():
    return pltpu.CompilerParams(vmem_limit_bytes=VMEM_LIMIT)


def cost(flops, bytes_accessed):
    return pl.CostEstimate(flops=flops, bytes_accessed=bytes_accessed, transcendentals=0)


def near(x):
    return pltpu.with_memory_space_constraint(x, pltpu.VMEM)


SCALARS = pl.BlockSpec(memory_space=pltpu.SMEM)
WHOLE = pl.BlockSpec(memory_space=pltpu.VMEM)
FAR = pl.BlockSpec(memory_space=pl.ANY)


def swap(x, size, bit):
    return lax.ppermute(x, "zslab", [(i, i ^ bit) for i in range(size)])


def rotate(x, size, steps):
    return lax.ppermute(x, "zslab", [(i, (i + 4 * steps) % size) for i in range(size)])


def orders(size):
    bits = [1 << k for k in range(1, size.bit_length() - 1)]
    return bits, [bits[1], bits[0]] + bits[2:]


def swap_stage(x, size, stage):
    both = orders(size)
    return lax.ppermute(x, "zslab", [(i, i ^ both[i % 2][stage]) for i in range(size)])


def stage_half(size, stage, other=False):
    me = lax.axis_index("zslab")
    low, high = (order[stage] for order in orders(size))
    core = me % 2 == (1 if other else 0)
    return jnp.where(core, (me // low) % 2, (me // high) % 2)


def take_rows(x, place, rows):
    return lax.dynamic_slice_in_dim(x, place * rows, rows, axis=0)


def halve(stay, got, mine):
    half = stay.shape[0] // 2
    give = take_rows(stay, 1 - mine, half) + take_rows(got, 1 - mine, half).astype(jnp.float32)
    keep = take_rows(stay, mine, half) + take_rows(got, mine, half).astype(jnp.float32)
    return give.astype(jnp.bfloat16), keep


def join(part, got, mine):
    return jnp.where(mine == 0, jnp.concatenate([part, got]), jnp.concatenate([got, part]))


def mask_rows(voxmask, z):
    lanes = slice(64 * z, 64 * z + 64)
    line = jnp.concatenate([voxmask[0:1, lanes], voxmask[1:2, lanes]], axis=1)
    return jnp.broadcast_to((line == 1).astype(jnp.float32), (128, 128)).T


def wide(mask):
    return jnp.concatenate([mask, mask], axis=1) > 0


def both(ref, z):
    return jnp.concatenate([ref[0, z], ref[1, z]], axis=0)


def inside(shape, dim, rows, cols):
    index = lax.broadcasted_iota(jnp.int32, shape, dim)
    row = (index // 8) % 8 + rows
    col = index % 8 + cols
    return (row >= 0) & (row < 8) & (col >= 0) & (col < 8)


def windows(shape, dim):
    return [inside(shape, dim, p, q) for p in (-1, 0, 1) for q in (-1, 0, 1)]


def shifts(x, dim, valid, sign=1):
    count = x.shape[dim]
    moved = []
    for place in range(9):
        at = place if sign == 1 else 8 - place
        move = 8 * (at // 3 - 1) + at % 3 - 1
        turned = pltpu.roll(x, (-move) % count, dim) if move else x
        moved.append(jnp.where(valid[at], turned, 0.0).astype(jnp.bfloat16))
    return moved


def activate(pre, cotangent, keep):
    sigma = 1.0 / (1.0 + jnp.exp(-pre))
    out = jnp.where(keep, pre * sigma, 0.0)
    grad = jnp.where(keep, cotangent * sigma * (1.0 + pre * (1.0 - sigma)), 0.0)
    return out.astype(jnp.bfloat16), grad.astype(jnp.bfloat16)


def write_exact(rows, ref):
    high = rows.astype(jnp.bfloat16)
    left = rows - high.astype(jnp.float32)
    middle = left.astype(jnp.bfloat16)
    low = (left - middle.astype(jnp.float32)).astype(jnp.bfloat16)
    zeros = jnp.zeros((EXTRA - 3, rows.shape[1]), jnp.float32)
    terms = [term.astype(jnp.float32) for term in (high, middle, low)]
    ref[256:272, :] = jnp.concatenate(terms + [zeros], axis=0).astype(jnp.bfloat16)


def read_extra(ref):
    return jnp.sum(ref[256:272, :].astype(jnp.float32), axis=0, keepdims=True)


def rims_kernel(links, low, high, voxmask, parcel):
    width = low.shape[3]
    for side, ref in ((0, low), (1, high)):
        keep = wide(mask_rows(voxmask, 7 * side))
        plane = jnp.where(keep, both(ref, 0).astype(jnp.float32), 0.0)
        parcel[128 * side : 128 * side + 128, :] = plane.astype(jnp.bfloat16)
    lane = lax.broadcasted_iota(jnp.int32, (EXTRA, width), 1)
    codes = jnp.zeros((EXTRA, width), jnp.float32)
    for place in range(4):
        codes = jnp.where(lane == place, links[place // 2, place % 2].astype(jnp.float32), codes)
    parcel[256:272, :] = codes.astype(jnp.bfloat16)


def rims(links, feats, voxmask):
    width = feats.shape[3]

    def plane(z):
        return pl.BlockSpec((2, 1, 64, width), lambda i: (0, z, 0, 0))

    return pl.pallas_call(
        rims_kernel,
        grid=(1,),
        in_specs=[SCALARS, plane(0), plane(7), WHOLE],
        out_specs=WHOLE,
        out_shape=pltpu.VMEM((256 + EXTRA, width), jnp.bfloat16),
        compiler_params=params(),
        cost_estimate=cost(0, 512 * 1024),
        name="rims",
    )(links, feats, feats, voxmask)


def prepare_kernel(core, feats, voxmask, mask, give, turned):
    half = feats.shape[3] // 2
    valid = windows((half, 128), 1)
    for z in range(8):
        rows = slice(128 * z, 128 * z + 128)
        keep = mask_rows(voxmask, z)
        mask[rows, :] = keep
        plane = jnp.where(wide(keep), both(feats, z).astype(jnp.float32), 0.0)
        first = core[0] == 0
        own = jnp.where(first, plane[:, :half], plane[:, half:])
        give[rows, :] = jnp.where(first, plane[:, half:], plane[:, :half]).astype(jnp.bfloat16)
        for place, moved in enumerate(shifts(own.T, 1, valid)):
            turned[place * half : (place + 1) * half, rows] = moved


def prepare(core, feats, voxmask):
    half = feats.shape[3] // 2
    return pl.pallas_call(
        prepare_kernel,
        in_specs=[SCALARS, WHOLE, WHOLE],
        out_specs=(WHOLE, WHOLE, WHOLE),
        out_shape=(
            pltpu.VMEM((1024, 128), jnp.float32),
            pltpu.VMEM((1024, half), jnp.bfloat16),
            pltpu.VMEM((9 * half, 1024), jnp.bfloat16),
        ),
        compiler_params=params(),
        cost_estimate=cost(0, 8 * 1024 * 1024),
        name="prepare",
    )(core, near(feats), voxmask)


def turn_kernel(rows, turned):
    half = rows.shape[1]
    valid = windows((half, 128), 1)
    for z in range(8):
        span = slice(128 * z, 128 * z + 128)
        for place, moved in enumerate(shifts(rows[span, :].astype(jnp.float32).T, 1, valid)):
            turned[place * half : (place + 1) * half, span] = moved


def turn(rows):
    half = rows.shape[1]
    return pl.pallas_call(
        turn_kernel,
        in_specs=[WHOLE],
        out_specs=WHOLE,
        out_shape=pltpu.VMEM((9 * half, 1024), jnp.bfloat16),
        compiler_params=params(),
        cost_estimate=cost(0, 6 * 1024 * 1024),
        name="turn",
    )(near(rows))


def copy_picks(outer, table, parcels, picks):
    for steps in range(outer):
        for slot in range(4):
            plane = table[steps * 4 + slot]
            start = pl.ds(pl.multiple_of((plane % 4) * 64, 64), 64)
            for dev in range(4):

                @pl.when(plane // 4 == dev)
                def _():
                    picks[steps][64 * slot : 64 * slot + 64, :] = parcels[dev][start, :]


def route_kernel(outer, where, *refs):
    parcels, (table, *picks), (codes, links, done) = refs[:4], refs[4:-3], refs[-3:]
    for dev in range(4):
        row = parcels[dev][256:272, :128].astype(jnp.float32)
        codes[8 * dev : 8 * dev + 8, :] = row[:8, :].astype(jnp.int32)
    copy = pltpu.make_async_copy(codes, links, done)
    copy.start()
    copy.wait()
    for place in range(outer * 4):
        table[place] = 0
    for plane in range(16):
        dev, side, brick = plane // 4, plane // 2 % 2, plane % 2
        dest = links[dev * 8, brick * 2 + side]

        @pl.when((dest >= 0) & ((dest // 2) % 4 == where[1]))
        def _():
            steps = lax.rem(dest // 8 - where[0] + outer, outer)
            table[steps * 4 + dest % 2 + (0 if side == 1 else 2)] = plane

    copy_picks(outer, table, parcels, picks)


def route(where, parcels, outer):
    width = parcels[0].shape[1]
    results = pl.pallas_call(
        functools.partial(route_kernel, outer),
        in_specs=[SCALARS] + [WHOLE] * 4,
        out_specs=[SCALARS] + [WHOLE] * outer,
        out_shape=[jax.ShapeDtypeStruct((outer * 4,), jnp.int32)]
        + [pltpu.VMEM((256, width), jnp.bfloat16)] * outer,
        scratch_shapes=[
            pltpu.VMEM((32, 128), jnp.int32),
            pltpu.SMEM((32, 128), jnp.int32),
            pltpu.SemaphoreType.DMA(()),
        ],
        compiler_params=params(),
        cost_estimate=cost(0, 1024 * 1024),
        name="route",
    )(where, *[near(x) for x in parcels])
    return results[0], results[1:]


def repeat_kernel(outer, table, *refs):
    parcels, picks = refs[:4], refs[4:]
    copy_picks(outer, table, parcels, picks)
    total = sum(read_extra(ref) for ref in parcels)
    for ref in picks:
        write_exact(total, ref)


def repeat_route(table, parcels, outer):
    width = parcels[0].shape[1]
    return pl.pallas_call(
        functools.partial(repeat_kernel, outer),
        in_specs=[SCALARS] + [WHOLE] * 4,
        out_specs=[WHOLE] * outer,
        out_shape=[pltpu.VMEM((256 + EXTRA, width), jnp.bfloat16)] * outer,
        compiler_params=params(),
        cost_estimate=cost(0, 1024 * 1024),
        name="repeat_route",
    )(table, *[near(x) for x in parcels])


def chosen(step, slot, arrived):
    rows = slice(64 * slot, 64 * slot + 64)
    plane = jnp.zeros((64, arrived[0].shape[1]), jnp.float32)
    for steps, ref in enumerate(arrived):
        plane = jnp.where(step[slot] == steps, ref[rows, :].astype(jnp.float32), plane)
    return plane


def forward_kernel(feats, mask, weight, bias, cotangent, out, grad, edge, bias_sum, cols, pre):
    width = feats.shape[3]
    valid = windows((128, width), 0)
    for z in range(8):
        rows = slice(128 * z, 128 * z + 128)
        plane = jnp.where(wide(mask[rows, :]), both(feats, z).astype(jnp.float32), 0.0)
        for place, moved in enumerate(shifts(plane, 0, valid)):
            cols[rows, place * width : (place + 1) * width] = moved
    taps = [weight[9 * a : 9 * a + 9].reshape(9 * width, width) for a in range(3)]
    pre[...] = jnp.dot(cols[...], taps[1], preferred_element_type=jnp.float32) + bias[...]
    pre[128:, :] += jnp.dot(cols[:896, :], taps[0], preferred_element_type=jnp.float32)
    pre[:896, :] += jnp.dot(cols[128:, :], taps[2], preferred_element_type=jnp.float32)
    edge[0] = pre[:128, :]
    edge[1] = pre[896:, :]
    total = jnp.zeros((1, width), jnp.float32)
    for z in range(1, 7):
        rows = slice(128 * z, 128 * z + 128)
        act, slope = activate(pre[rows, :], both(cotangent, z).astype(jnp.float32), wide(mask[rows, :]))
        for b in range(2):
            out[b, z] = act[64 * b : 64 * b + 64]
        grad[128 * (z - 1) : 128 * z, :] = slope
        total += jnp.sum(slope.astype(jnp.float32), axis=0, keepdims=True)
    bias_sum[...] = total


def forward_inside(feats, mask, weight, bias, cotangent):
    width = feats.shape[3]
    return pl.pallas_call(
        forward_kernel,
        in_specs=[WHOLE] * 5,
        out_specs=(WHOLE,) * 4,
        out_shape=(
            pltpu.VMEM(feats.shape, jnp.bfloat16),
            pltpu.VMEM((768, width), jnp.bfloat16),
            pltpu.VMEM((2, 128, width), jnp.float32),
            pltpu.VMEM((1, width), jnp.float32),
        ),
        scratch_shapes=[
            pltpu.VMEM((1024, 9 * width), jnp.bfloat16),
            pltpu.VMEM((1024, width), jnp.float32),
        ],
        compiler_params=params(),
        cost_estimate=cost(2 * 1024 * 27 * width * width, 6 * 1024 * 1024),
        name="forward_inside",
    )(near(feats), near(mask), near(weight), bias, near(cotangent))


def inner_terms_kernel(mine, theirs, grad, their_grad, terms):
    rows = mine.shape[0]
    for a in range(3):
        lanes = slice(128 * a, 128 * a + 768)
        terms[a * rows : (a + 1) * rows, :] = jnp.dot(
            mine[:, lanes], grad[...], preferred_element_type=jnp.float32
        ) + jnp.dot(theirs[:, lanes], their_grad[...], preferred_element_type=jnp.float32)


def inner_terms(mine, theirs, grad, their_grad):
    rows, width = mine.shape[0], grad.shape[1]
    return pl.pallas_call(
        inner_terms_kernel,
        in_specs=[WHOLE] * 4,
        out_specs=WHOLE,
        out_shape=pltpu.VMEM((3 * rows, width), jnp.float32),
        compiler_params=params(),
        cost_estimate=cost(2 * 1536 * 3 * rows * width, 8 * 1024 * 1024),
        name="inner_terms",
    )(near(mine), near(theirs), near(grad), near(their_grad))


def edge_kernel(core, step, mask, weight, edge, cotangent, inner, out_in, *refs):
    arrived, (out, parcel, own, give) = refs[:-4], refs[-4:]
    width = edge.shape[2]
    half = width // 2
    valid = windows((128, width), 0)
    total = inner[...]
    for side in range(2):
        rows = slice(128 * side, 128 * side + 128)
        halo = jnp.concatenate([chosen(step, 2 * side + b, arrived) for b in range(2)], axis=0)
        first = core[0] == 0
        own[rows, :] = jnp.where(first, halo[:, :half], halo[:, half:]).astype(jnp.bfloat16)
        give[rows, :] = jnp.where(first, halo[:, half:], halo[:, :half]).astype(jnp.bfloat16)
        cols = jnp.concatenate(shifts(halo, 0, valid), axis=1)
        taps = weight[18 * side : 18 * side + 9].reshape(9 * width, width)
        pre = edge[side] + jnp.dot(cols, taps, preferred_element_type=jnp.float32)
        z = 7 * side
        keep = wide(mask[128 * z : 128 * z + 128, :])
        act, slope = activate(pre, both(cotangent, z).astype(jnp.float32), keep)
        for b in range(2):
            out[b, z] = act[64 * b : 64 * b + 64]
        parcel[rows, :] = slope
        total += jnp.sum(slope.astype(jnp.float32), axis=0, keepdims=True)
    write_exact(total, parcel)


def forward_edges(core, step, mask, weight, edge, cotangent, inner, out, arrived):
    width = edge.shape[2]
    return pl.pallas_call(
        edge_kernel,
        in_specs=[SCALARS, SCALARS] + [WHOLE] * (6 + len(arrived)),
        out_specs=(WHOLE,) * 4,
        out_shape=(
            pltpu.VMEM(out.shape, out.dtype),
            pltpu.VMEM((256 + EXTRA, width), jnp.bfloat16),
            pltpu.VMEM((256, width // 2), jnp.bfloat16),
            pltpu.VMEM((256, width // 2), jnp.bfloat16),
        ),
        input_output_aliases={7: 0},
        compiler_params=params(),
        cost_estimate=cost(2 * 256 * 9 * width * width, 3 * 1024 * 1024),
        name="forward_edges",
    )(
        core,
        step,
        near(mask),
        near(weight),
        near(edge),
        near(cotangent),
        near(inner),
        near(out),
        *[near(x) for x in arrived],
    )


def outer_terms_kernel(upper, mine, theirs, halos, their_halos, parcel, their_parcel, inner, give, stay, ends, cols, total):
    rows = mine.shape[0]
    half = rows // 9
    valid = windows((half, 128), 1)
    for who, ref in enumerate((halos, their_halos)):
        for side in range(2):
            plane = ref[128 * side : 128 * side + 128, :].astype(jnp.float32).T
            lanes = slice(256 * side + 128 * who, 256 * side + 128 * who + 128)
            for place, moved in enumerate(shifts(plane, 1, valid)):
                ends[place * half : (place + 1) * half, lanes] = moved
    facing = jnp.concatenate([parcel[:128], their_parcel[:128], parcel[128:256], their_parcel[128:256]], axis=0)
    for a in range(3):
        if a == 0:
            cols[:, :256] = ends[:, :256]
        else:
            cols[:, :128] = mine[:, 128 * (a - 1) : 128 * a]
            cols[:, 128:256] = theirs[:, 128 * (a - 1) : 128 * a]
        if a == 2:
            cols[:, 256:] = ends[:, 256:]
        else:
            cols[:, 256:384] = mine[:, 128 * (6 + a) : 128 * (7 + a)]
            cols[:, 384:] = theirs[:, 128 * (6 + a) : 128 * (7 + a)]
        span = slice(a * rows, (a + 1) * rows)
        total[span, :] = inner[span, :] + jnp.dot(cols[...], facing, preferred_element_type=jnp.float32)
    count = give.shape[0]
    give[...] = total[pl.ds(pl.multiple_of((1 - upper[0]) * count, 16), count), :].astype(jnp.bfloat16)
    stay[...] = total[pl.ds(pl.multiple_of(upper[0] * count, 16), count), :]


def outer_terms(upper, mine, theirs, halos, their_halos, parcel, their_parcel, inner):
    rows, width = inner.shape
    return pl.pallas_call(
        outer_terms_kernel,
        in_specs=[SCALARS] + [WHOLE] * 7,
        out_specs=(WHOLE, WHOLE),
        out_shape=(pltpu.VMEM((rows // 2, width), jnp.bfloat16), pltpu.VMEM((rows // 2, width), jnp.float32)),
        scratch_shapes=[
            pltpu.VMEM((rows // 3, 512), jnp.bfloat16),
            pltpu.VMEM((rows // 3, 512), jnp.bfloat16),
            pltpu.VMEM((rows, width), jnp.float32),
        ],
        compiler_params=params(),
        cost_estimate=cost(2 * 512 * rows * width, 8 * 1024 * 1024),
        name="outer_terms",
    )(upper, *[near(x) for x in (mine, theirs, halos, their_halos, parcel, their_parcel, inner)])


def backward_rows(planes, mask, weight, cols, place):
    width = weight.shape[1]
    valid = windows((128, width), 0)
    for index, plane in enumerate(planes):
        rows = slice(128 * (place + index), 128 * (place + index) + 128)
        for at, moved in enumerate(shifts(plane.astype(jnp.float32), 0, valid, -1)):
            cols[rows, at * width : (at + 1) * width] = moved
    count = 128 * (len(planes) - 2)
    total = jnp.zeros((count, width), jnp.float32)
    for a in range(3):
        for at in range(9):
            start = 128 * (place + 2 - a)
            total += lax.dot_general(
                cols[start : start + count, at * width : (at + 1) * width],
                weight[9 * a + at],
                (((1,), (1,)), ((), ())),
                preferred_element_type=jnp.float32,
            )
    return jnp.where(wide(mask), total, 0.0).astype(jnp.bfloat16)


def backward_inner_kernel(grad, parcel, mask, weight, grad_feats, cols):
    done = backward_rows(
        [grad[128 * (z - 1) : 128 * z, :] for z in range(1, 7)], mask[256:768, :], weight, cols, 0
    )
    for z in range(2, 6):
        for b in range(2):
            start = 128 * (z - 2) + 64 * b
            grad_feats[b, z] = done[start : start + 64]


def backward_inner(grad, parcel, mask, weight):
    width = grad.shape[1]
    return pl.pallas_call(
        backward_inner_kernel,
        in_specs=[WHOLE] * 4,
        out_specs=WHOLE,
        out_shape=pltpu.VMEM((2, 8, 64, width), jnp.bfloat16),
        scratch_shapes=[pltpu.VMEM((768, 9 * width), jnp.bfloat16)],
        compiler_params=params(),
        cost_estimate=cost(2 * 512 * 27 * width * width, 5 * 1024 * 1024),
        name="backward_inner",
    )(near(grad), near(parcel), near(mask), near(weight))


def backward_outer_kernel(step, grad, parcel, mask, weight, done, *refs):
    arrived, (grad_feats, bias_sum, cols) = refs[:-3], refs[-3:]
    for side in range(2):
        halo = jnp.concatenate([chosen(step, 2 * side + b, arrived) for b in range(2)], axis=0)
        rim = parcel[128 * side : 128 * side + 128, :]
        if side == 0:
            planes = [halo, rim, grad[:128, :], grad[128:256, :]]
        else:
            planes = [grad[512:640, :], grad[640:768, :], rim, halo]
        first = 6 * side
        rows = backward_rows(planes, mask[128 * first : 128 * first + 256, :], weight, cols, 4 * side)
        for z in range(2):
            for b in range(2):
                start = 128 * z + 64 * b
                grad_feats[b, first + z] = rows[start : start + 64]
    bias_sum[...] = sum(read_extra(ref) for ref in arrived)


def backward_outer(step, grad, parcel, mask, weight, done, arrived):
    width = grad.shape[1]
    return pl.pallas_call(
        backward_outer_kernel,
        in_specs=[SCALARS] + [WHOLE] * (5 + len(arrived)),
        out_specs=(WHOLE, WHOLE),
        out_shape=(pltpu.VMEM((2, 8, 64, width), jnp.bfloat16), pltpu.VMEM((1, width), jnp.float32)),
        scratch_shapes=[pltpu.VMEM((1024, 9 * width), jnp.bfloat16)],
        input_output_aliases={5: 0},
        compiler_params=params(),
        cost_estimate=cost(2 * 512 * 27 * width * width, 5 * 1024 * 1024),
        name="backward_outer",
    )(step, near(grad), near(parcel), near(mask), near(weight), near(done), *[near(x) for x in arrived])


def assemble_kernel(place, *refs):
    parts, out, done = refs[:4], refs[4], refs[5]
    half = out.shape[1] // 2
    taps = out.shape[0] // 2
    rest = parts[0].shape[0] - taps * half
    for index, ref in enumerate(parts):
        core, second = place[2 * index], place[2 * index + 1]
        for who in range(2):
            for upper in range(2):

                @pl.when((core == who) & (second == upper))
                def _():
                    full, cut = (taps + 1, 0) if upper else (0, taps * half)
                    body = rest if upper else 0
                    copies = [
                        pltpu.make_async_copy(
                            ref.at[pl.ds(body + half * tap, half)],
                            out.at[full + tap, pl.ds(half * who, half)],
                            done.at[index, tap],
                        )
                        for tap in range(taps)
                    ]
                    copies.append(
                        pltpu.make_async_copy(
                            ref.at[pl.ds(cut, rest)],
                            out.at[taps, pl.ds(half * who + rest * upper, rest)],
                            done.at[index, taps],
                        )
                    )
                    for copy in copies:
                        copy.start()

    for index, ref in enumerate(parts):
        for tap in range(taps):
            pltpu.make_async_copy(
                ref.at[pl.ds(half * tap, half)], out.at[tap, pl.ds(0, half)], done.at[index, tap]
            ).wait()
        pltpu.make_async_copy(ref.at[pl.ds(0, rest)], out.at[taps, pl.ds(0, rest)], done.at[index, taps]).wait()


def assemble(place, parts):
    rows, width = parts[0].shape
    taps = rows * 4 // width
    return pl.pallas_call(
        assemble_kernel,
        in_specs=[SCALARS] + [WHOLE] * 4,
        out_specs=FAR,
        out_shape=jax.ShapeDtypeStruct((taps, width, width), jnp.bfloat16),
        scratch_shapes=[pltpu.SemaphoreType.DMA((4, taps // 2 + 1))],
        compiler_params=params(),
        cost_estimate=cost(0, 8 * rows * width * 2),
        name="assemble",
    )(place, *[near(x) for x in parts])


def gather_group(parcel, size):
    inner = swap(parcel, size, 2)
    return [parcel, inner, swap(parcel, size, 1), swap(inner, size, 1)]


def per_device(size, feats, voxmask, links, weight, bias, cotangent):
    width = feats.shape[3]
    outer = size // 4
    me = lax.axis_index("zslab")
    core = (me % 2).astype(jnp.int32).reshape(1)
    where = jnp.stack([me // 4, me % 4]).astype(jnp.int32)
    want = links.T.reshape(4)
    step = jnp.where(want >= 0, (me // 4 - want // 8) % outer, -1)

    parcels = gather_group(rims(links, feats, voxmask), size)
    table, picks = route(where, parcels, outer)
    mask, give, turned = prepare(core, feats, voxmask)

    *picks, give, feats, cotangent = lax.optimization_barrier((*picks, give, feats, cotangent))
    arrived = [rotate(pick, size, steps) if steps else pick for steps, pick in enumerate(picks)]
    their_turned = turn(swap(give, size, 1))
    out, grad, edge, bias_local = forward_inside(feats, mask, weight, bias.reshape(1, width), cotangent)
    inner = inner_terms(turned, their_turned, grad, swap(grad, size, 1))

    *arrived, inner = lax.optimization_barrier((*arrived, inner))
    out, parcel, halos, give = forward_edges(core, step, mask, weight, edge, cotangent, bias_local, out, arrived)
    their_halos = swap(give, size, 1)
    parcels = gather_group(parcel, size)

    stages = len(orders(size)[0])
    halves = [stage_half(size, stage) for stage in range(stages)]
    give, stay = outer_terms(
        halves[0].astype(jnp.int32).reshape(1), turned, their_turned, halos, their_halos, parcel, parcels[2], inner
    )
    picks = repeat_route(table, parcels, outer)
    arrived = [rotate(pick, size, steps) if steps else pick for steps, pick in enumerate(picks)]
    got = swap_stage(give, size, 0)
    grad_feats = backward_inner(grad, parcel, mask, weight)
    stay, grad_feats = lax.optimization_barrier((stay, grad_feats))
    for stage in range(1, stages):
        give, stay = halve(stay, got, halves[stage])
        got = swap_stage(give, size, stage)
    part = (stay + got.astype(jnp.float32)).astype(jnp.bfloat16)
    for stage in reversed(range(1, stages)):
        part = join(part, swap_stage(part, size, stage), halves[stage])
    grad_feats, grad_bias = backward_outer(step, grad, parcel, mask, weight, grad_feats, arrived)
    last = swap_stage(part, size, 0)
    other = swap(part, size, 1)
    last, grad_feats, grad_bias = lax.optimization_barrier((last, grad_feats, grad_bias))
    other_last = swap(last, size, 1)
    theirs = stage_half(size, 0, other=True)
    place = jnp.stack([core[0], halves[0], core[0], 1 - halves[0], 1 - core[0], theirs, 1 - core[0], 1 - theirs])
    grad_weight = assemble(place.astype(jnp.int32), [part, last, other, other_last])
    return out, grad_feats, grad_weight, grad_bias.reshape(width)


def solution(mesh):
    return jax.shard_map(
        functools.partial(per_device, mesh.shape["zslab"]),
        mesh=mesh,
        in_specs=(
            P(("groups", "zslab"), None, None, None),
            P(("groups", "zslab"), None),
            P(("groups", "zslab"), None),
            P(),
            P(),
            P(("groups", "zslab"), None, None, None),
        ),
        out_specs=(
            P(("groups", "zslab"), None, None, None),
            P(("groups", "zslab"), None, None, None),
            P("groups", None, None),
            P("groups"),
        ),
        check_vma=False,
    )
```

time: 300 us -> 157 us (0.52)
  blocking collectives: 160 us -> 0 us
  matrix products: 50.5 us -> 0 us
  waiting for transfers between devices: 41 us -> 73.1 us
  Pallas kernels: 0 us -> 30.5 us
  starting transfers between devices: 0.08 us -> 20.6 us
  between operations: 14.7 us -> 1.08 us
  local copies, waits for them, and re-layouts: 17.4 us -> 28.8 us
  other arithmetic: 12.8 us -> 1.66 us
    psum x1 -> x0, blocking collectives: 160 us -> none  [per_device(): weight_sum, bias_sum = lax.psum((weight_local, bias_local), 'zslab')]
    ppermute x0 -> x23, waiting for transfers between devices: none -> 73.1 us  [the longest x6 43.8 us: swap_stage(): lax.ppermute(x, 'zslab', [(i, i ^ both[i % 2][stage]) for i in range(size)])]
    dot_general x81 -> x0, matrix products: 50.5 us -> none  [the longest x27 30.9 us: weight_terms(): lax.dot_general(piece, grad_rows, (((0,), (0,)), ((), ())), preferred_ele...]
    all_gather x2 -> x0, waiting for transfers between devices: 41 us -> none  [the longest x1 41 us: per_device(): all_rims = lax.all_gather(rims, 'zslab', axis=0, tiled=True)]
    pallas_call x0 -> x12, Pallas kernels: none -> 30.5 us  [the longest x1 4.67 us: forward_inside(): pl.pallas_call(forward_kernel, in_specs=[WHOLE] * 5, out_specs=(WHOLE,) *...]
    unnamed x26 -> x71, local copies, waits for them, and re-layouts: 0.3 us -> 28.5 us
    ppermute x0 -> x23, starting transfers between devices: none -> 20.6 us  [the longest x6 9.92 us: rotate(): lax.ppermute(x, 'zslab', [(i, (i + 4 * steps) % size) for i in range(size)])]
    concatenate x9 -> x0, other arithmetic: 7.52 us -> none  [extend_with(): stacked = jnp.concatenate([below[:, None], planes, above[:, None]], axis=1)]
  transfers between devices with their start and end apart: 2 -> 23, of which waited for: 1 -> 12; matrix products, arithmetic and copies ran while one was open for 3% -> 2% of each run, Pallas kernels for 0% -> 9%
where the time goes in v4:
time: 157 us; the launch traced here: 156 us
  waiting for transfers between devices  73.1 us (47%)
  Pallas kernels  30.5 us (19%)
  local copies, waits for them, and re-layouts  28.8 us (18%)
  starting transfers between devices  20.6 us (13%)
  other arithmetic  1.66 us (1%)
    ppermute x6, waiting for transfers between devices, swap_stage(): lax.ppermute(x, 'zslab', [(i, i ^ both[i % 2][stage]) for i in range(size)])  43.8 us
    unnamed x71, local copies, waits for them, and re-layouts  28.5 us
    ppermute x11, waiting for transfers between devices, swap(): return lax.ppermute(x, 'zslab', [(i, i ^ bit) for i in range(size)])  19.7 us
    ppermute x6, starting transfers between devices, rotate(): lax.ppermute(x, 'zslab', [(i, (i + 4 * steps) % size) for i in range(size)])  9.92 us
    ppermute x6, waiting for transfers between devices, rotate(): lax.ppermute(x, 'zslab', [(i, (i + 4 * steps) % size) for i in range(size)])  9.55 us
    ppermute x6, starting transfers between devices, swap_stage(): lax.ppermute(x, 'zslab', [(i, i ^ both[i % 2][stage]) for i in range(size)])  5.56 us
    ppermute x11, starting transfers between devices, swap(): return lax.ppermute(x, 'zslab', [(i, i ^ bit) for i in range(size)])  5.13 us
    pallas_call x1, Pallas kernels, forward_inside(): pl.pallas_call(forward_kernel, in_specs=[WHOLE] * 5, out_specs=(WHOLE,) *...  4.67 us
  transfers between devices with their start and end apart: 23, of which 12 were waited for; matrix products, arithmetic and copies ran while one was open for 2% of the time, Pallas kernels for 9%

profile of v4, /device:TPU:0, one launch (start us, length us, event | category | flops | bytes accessed | tf_op | source)
XLA Modules:
  0.0 155.7 jit_solution(15349674391004987538)
XLA Ops:
  3.8 3.0 %collective-permute-start = (bf16[272,256]{1,0:T(8,128)(2,1)S(1)}, bf16[272,256]{1,0:T(8,128)(2,1)S(1)}, u32[]{:S(2)}, u32[]{:S(2)}) collective-permute-start(bf16[272,256]{1,0:T(8,128)(2,1)S(1)} %rims.1.refs_0_), channel_id=1, source_target_pairs={{0,2},{1,3},{2,0},{3,1},{4,6},{5,7},{6,4},{7,5},{8,10},{9,11},{10,... | collective-permute-start | bytes 417800 | tf_op jit(solution)/shard_map/ppermute | solution.py:32
  6.8 3.7 %collective-permute-done.refs_1_ = bf16[272,256]{1,0:T(8,128)(2,1)S(1)} collective-permute-done((bf16[272,256]{1,0:T(8,128)(2,1)S(1)}, bf16[272,256]{1,0:T(8,128)(2,1)S(1)}, u32[]{:S(2)}, u32[]{:S(2)}) %collective-permute-start) | collective-permute-done | bytes 139296 | tf_op jit(solution)/shard_map/ppermute | solution.py:32
  12.2 2.2 %prepare.1 = (f32[1024,128]{1,0:T(8,128)S(1)}, bf16[1024,128]{1,0:T(8,128)(2,1)S(1)}, bf16[1152,1024]{1,0:T(8,128)(2,1)S(1)}) custom-call(s32[1]{0:T(128)} %bitcast.core, bf16[2,8,64,256]{3,2,1,0:T(8,128)(2,1)S(1)} %copy-done.1, s32[2,512]{1,0:T(2,128)S(1)} %copy-done.28), custom_call_target="tpu_custom_call" | custom-call | bytes 8388608 | tf_op jit(solution)/shard_map/prepare/pallas_call | solution.py:176
  16.0 2.8 %route.1 = (s32[16]{0:T(128)S(1)}, bf16[256,256]{1,0:T(8,128)(2,1)S(1)}, bf16[256,256]{1,0:T(8,128)(2,1)}, bf16[256,256]{1,0:T(8,128)(2,1)}, bf16[256,256]{1,0:T(8,128)(2,1)S(1)}) custom-call(s32[2]{0:T(128)S(1)} %pad_add_fusion.where, bf16[272,256]{1,0:T(8,128)(2,1)S(1)} %rims.1.refs_0_, bf16[272,256]{1,0:T(8,128)(2,1)S(1)} %collective-permute-done.refs_1_, ...), custom_call_target="tpu_custom_call" | custom-call | bytes 1048576 | tf_op jit(solution)/shard_map/route/pallas_call | solution.py:249
  18.8 2.0 %copy-done.5 = bf16[27,256,256]{2,1,0:T(8,128)(2,1)S(1)} copy-done((bf16[27,256,256]{2,1,0:T(8,128)(2,1)S(1)}, bf16[27,256,256]{2,1,0:T(8,128)(2,1)}, u32[]{:S(2)}) %copy-start.5) | copy-done | bytes 3538968
  20.8 4.7 %forward_inside.1 = (bf16[2,8,64,256]{3,2,1,0:T(8,128)(2,1)S(1)}, bf16[768,256]{1,0:T(8,128)(2,1)}, f32[2,128,256]{2,1,0:T(8,128)S(1)}, f32[1,256]{1,0:T(1,128)S(1)}) custom-call(bf16[2,8,64,256]{3,2,1,0:T(8,128)(2,1)S(1)} %copy-done.2, f32[1024,128]{1,0:T(8,128)S(1)} %get-tuple-element.45.mask, bf16[27,256,256]{2,1,0:T(8,128)(2,1)S(1)} %copy-done.5, ...), custom_call_target="tpu_custom_call" | custom-call | flops 3623878656 | bytes 6291456 | tf_op jit(solution)/shard_map/forward_inside/pallas_call | solution.py:323
  28.7 2.6 %collective-permute-start.4 = (bf16[256,256]{1,0:T(8,128)(2,1)}, bf16[256,256]{1,0:T(8,128)(2,1)S(1)}, u32[]{:S(2)}, u32[]{:S(2)}) collective-permute-start(bf16[256,256]{1,0:T(8,128)(2,1)} %get-tuple-element.58), channel_id=1, source_target_pairs={{0,8},{1,9},{2,10},{3,11},{4,12},{5,13},{6,14},{7,15},{8,0},{9,1},... | collective-permute-start | bytes 393224 | tf_op jit(solution)/shard_map/ppermute | solution.py:36
  36.8 4.2 %inner_terms.1.inner = f32[3456,256]{1,0:T(8,128)S(1)} custom-call(bf16[1152,1024]{1,0:T(8,128)(2,1)S(1)} %copy-done.10, bf16[1152,1024]{1,0:T(8,128)(2,1)S(1)} %turn.1.theirs, bf16[768,256]{1,0:T(8,128)(2,1)} %get-tuple-element.62.grad, bf16[768,256]{1,0:T(8,128)(2,1)} %collective-permute-done.7.their_grad), custom_call_target="tpu_custom_call" | custom-call | flops 2717908992 | bytes 8388608 | tf_op jit(solution)/shard_map/inner_terms/pallas_call | solution.py:354
  47.0 2.0 %copy-done.4 = f32[3456,256]{1,0:T(8,128)S(1)} copy-done((f32[3456,256]{1,0:T(8,128)S(1)}, f32[3456,256]{1,0:T(8,128)}, u32[]{:S(2)}) %copy-start.4) | copy-done | bytes 3538968
  51.5 2.7 %outer_terms.1 = (bf16[1728,256]{1,0:T(8,128)(2,1)}, f32[1728,256]{1,0:T(8,128)S(1)}) custom-call(s32[1]{0:T(128)} %bitcast.5.upper, bf16[1152,1024]{1,0:T(8,128)(2,1)S(1)} %copy-done.11, bf16[1152,1024]{1,0:T(8,128)(2,1)S(1)} %turn.1.theirs, bf16[256,128]{1,0:T(8,128)(2,1)S(1)} %copy-done.26, bf16[256,128]{1,0:T(8,128)(2,1)S(1)} %collective-permute-done.8.their_halos, ...), custom_call_target="tpu_custom_call" | custom-call | flops 905969664 | bytes 8388608 | tf_op jit(solution)/shard_map/outer_terms/pallas_call | solution.py:450
  57.0 2.0 %copy-done.7 = bf16[27,256,256]{2,1,0:T(8,128)(2,1)S(1)} copy-done((bf16[27,256,256]{2,1,0:T(8,128)(2,1)S(1)}, bf16[27,256,256]{2,1,0:T(8,128)(2,1)}, u32[]{:S(2)}) %copy-start.7) | copy-done | bytes 3538968
  60.0 3.2 %backward_inner.1.done = bf16[2,8,64,256]{3,2,1,0:T(8,128)(2,1)S(1)} custom-call(bf16[768,256]{1,0:T(8,128)(2,1)} %get-tuple-element.62.grad, bf16[272,256]{1,0:T(8,128)(2,1)S(1)} %get-tuple-element.70.parcel.refs_0_, f32[1024,128]{1,0:T(8,128)S(1)} %copy-done.17, bf16[27,256,256]{2,1,0:T(8,128)(2,1)S(1)} %copy-done.7), custom_call_target="tpu_custom_call" | custom-call | flops 1811939328 | bytes 5242880 | tf_op jit(solution)/shard_map/backward_inner/pallas_call | solution.py:499
  63.3 5.5 %collective-permute-done.10 = bf16[1728,256]{1,0:T(8,128)(2,1)S(1)} collective-permute-done((bf16[1728,256]{1,0:T(8,128)(2,1)}, bf16[1728,256]{1,0:T(8,128)(2,1)S(1)}, u32[]{:S(2)}, u32[]{:S(2)}) %collective-permute-start.10) | collective-permute-done | bytes 884768 | tf_op jit(solution)/shard_map/ppermute | solution.py:46
  71.1 7.2 %collective-permute-done.11 = bf16[864,256]{1,0:T(8,128)(2,1)S(1)} collective-permute-done((bf16[864,256]{1,0:T(8,128)(2,1)}, bf16[864,256]{1,0:T(8,128)(2,1)S(1)}, u32[]{:S(2)}, u32[]{:S(2)}) %collective-permute-start.11) | collective-permute-done | bytes 442400 | tf_op jit(solution)/shard_map/ppermute | solution.py:46
  79.3 10.7 %collective-permute-done.12 = bf16[432,256]{1,0:T(8,128)(2,1)S(1)} collective-permute-done((bf16[432,256]{1,0:T(8,128)(2,1)S(1)}, bf16[432,256]{1,0:T(8,128)(2,1)S(1)}, u32[]{:S(2)}, u32[]{:S(2)}) %collective-permute-start.12) | collective-permute-done | bytes 221216 | tf_op jit(solution)/shard_map/ppermute | solution.py:46
  90.2 12.2 %collective-permute-done.13 = bf16[432,256]{1,0:T(8,128)(2,1)S(1)} collective-permute-done((bf16[432,256]{1,0:T(8,128)(2,1)S(1)}, bf16[432,256]{1,0:T(8,128)(2,1)S(1)}, u32[]{:S(2)}, u32[]{:S(2)}) %collective-permute-start.13) | collective-permute-done | bytes 221216 | tf_op jit(solution)/shard_map/ppermute | solution.py:46
  102.6 8.3 %collective-permute-done.14 = bf16[864,256]{1,0:T(8,128)(2,1)S(1)} collective-permute-done((bf16[864,256]{1,0:T(8,128)(2,1)S(1)}, bf16[864,256]{1,0:T(8,128)(2,1)S(1)}, u32[]{:S(2)}, u32[]{:S(2)}) %collective-permute-start.14) | collective-permute-done | bytes 442400 | tf_op jit(solution)/shard_map/ppermute | solution.py:46
  113.2 12.5 %collective-permute-done.16.refs_1_ = bf16[272,256]{1,0:T(8,128)(2,1)S(1)} collective-permute-done((bf16[272,256]{1,0:T(8,128)(2,1)S(1)}, bf16[272,256]{1,0:T(8,128)(2,1)S(1)}, u32[]{:S(2)}, u32[]{:S(2)}) %collective-permute-start.16) | collective-permute-done | bytes 139296 | tf_op jit(solution)/shard_map/ppermute | solution.py:32
  129.9 2.3 %collective-permute-start.20 = (bf16[272,256]{1,0:T(8,128)(2,1)S(1)}, bf16[272,256]{1,0:T(8,128)(2,1)S(1)}, u32[]{:S(2)}, u32[]{:S(2)}) collective-permute-start(bf16[272,256]{1,0:T(8,128)(2,1)S(1)} %get-tuple-element.80), channel_id=1, source_target_pairs={{0,12},{1,13},{2,14},{3,15},{4,0},{5,1},{6,2},{7,3},{8,4},{9,5},{1... | collective-permute-start | bytes 417800 | tf_op jit(solution)/shard_map/ppermute | solution.py:36
  132.3 4.4 %collective-permute-done.18.refs_1_ = bf16[272,256]{1,0:T(8,128)(2,1)S(1)} collective-permute-done((bf16[272,256]{1,0:T(8,128)(2,1)S(1)}, bf16[272,256]{1,0:T(8,128)(2,1)S(1)}, u32[]{:S(2)}, u32[]{:S(2)}) %collective-permute-start.18) | collective-permute-done | bytes 139296 | tf_op jit(solution)/shard_map/ppermute | solution.py:36
  136.7 5.2 %collective-permute-done.19.refs_2_ = bf16[272,256]{1,0:T(8,128)(2,1)S(1)} collective-permute-done((bf16[272,256]{1,0:T(8,128)(2,1)S(1)}, bf16[272,256]{1,0:T(8,128)(2,1)S(1)}, u32[]{:S(2)}, u32[]{:S(2)}) %collective-permute-start.19) | collective-permute-done | bytes 139296 | tf_op jit(solution)/shard_map/ppermute | solution.py:36
  141.8 2.0 %copy-done.8 = bf16[27,256,256]{2,1,0:T(8,128)(2,1)S(1)} copy-done((bf16[27,256,256]{2,1,0:T(8,128)(2,1)S(1)}, bf16[27,256,256]{2,1,0:T(8,128)(2,1)}, u32[]{:S(2)}) %copy-start.8) | copy-done | bytes 3538968
  144.9 3.1 %backward_outer.1 = (bf16[2,8,64,256]{3,2,1,0:T(8,128)(2,1)S(1)}, f32[1,256]{1,0:T(1,128)S(1)}) custom-call(s32[4]{0:T(128)S(1)} %copy-done.32, bf16[768,256]{1,0:T(8,128)(2,1)} %get-tuple-element.62.grad, bf16[272,256]{1,0:T(8,128)(2,1)S(1)} %get-tuple-element.70.parcel.refs_0_, f32[1024,128]{1,0:T(8,128)S(1)} %copy-done.18, ...), custom_call_target="tpu_custom_call", output_to_operand_aliasing={{0}: (5, {})} | custom-call | flops 1811939328 | bytes 5242880 | tf_op jit(solution)/shard_map/backward_outer/pallas_call | solution.py:531
  151.9 3.7 %assemble.1 = bf16[27,256,256]{2,1,0:T(8,128)(2,1)} custom-call(s32[8]{0:T(128)S(1)} %stack.33.place, bf16[1728,256]{1,0:T(8,128)(2,1)S(1)} %maximum_select_fusion.refs_0_, bf16[1728,256]{1,0:T(8,128)(2,1)S(1)} %collective-permute-done.15.refs_1_, bf16[1728,256]{1,0:T(8,128)(2,1)} %collective-permute-done.21.refs_2_, ...), custom_call_target="tpu_custom_call" | custom-call | bytes 7077888 | tf_op jit(solution)/shard_map/assemble/pallas_call | solution.py:587
  (115 shorter events, 42.6 us)
Async XLA Ops:
  3.8 6.7 %collective-permute-start = (bf16[272,256]{1,0:T(8,128)(2,1)S(1)}, bf16[272,256]{1,0:T(8,128)(2,1)S(1)}, u32[]{:S(2)}, u32[]{:S(2)}) collective-permute-start(bf16[272,256]{1,0:T(8,128)(2,1)S(1)} %rims.1.refs_0_), channel_id=1, source_target_pairs={{0,2},{1,3},{2,0},{3,1},{4,6},{5,7},{6,4},{7,5},{8,10},{9,11},{10,... | collective-permute-start | bytes 417800 | tf_op jit(solution)/shard_map/ppermute | solution.py:32
  6.8 9.1 %collective-permute-start.1 = (bf16[272,256]{1,0:T(8,128)(2,1)S(1)}, bf16[272,256]{1,0:T(8,128)(2,1)S(1)}, u32[]{:S(2)}, u32[]{:S(2)}) collective-permute-start(bf16[272,256]{1,0:T(8,128)(2,1)S(1)} %rims.1.refs_0_), channel_id=1, source_target_pairs={{0,1},{1,0},{2,3},{3,2},{4,5},{5,4},{6,7},{7,6},{8,9},{9,8},{10,11... | collective-permute-start | bytes 417800 | tf_op jit(solution)/shard_map/ppermute | solution.py:32
  10.5 5.5 %collective-permute-start.2 = (bf16[272,256]{1,0:T(8,128)(2,1)S(1)}, bf16[272,256]{1,0:T(8,128)(2,1)S(1)}, u32[]{:S(2)}, u32[]{:S(2)}) collective-permute-start(bf16[272,256]{1,0:T(8,128)(2,1)S(1)} %collective-permute-done.refs_1_), channel_id=1, source_target_pairs={{0,1},{1,0},{2,3},{3,2},{4,5},{5,4},{6,7},{7,6},{8,9},{9,8},{10,11... | collective-permute-start | bytes 417800 | tf_op jit(solution)/shard_map/ppermute | solution.py:32
  26.2 9.0 %collective-permute-start.7 = (bf16[768,256]{1,0:T(8,128)(2,1)}, bf16[768,256]{1,0:T(8,128)(2,1)}, u32[]{:S(2)}, u32[]{:S(2)}) collective-permute-start(bf16[768,256]{1,0:T(8,128)(2,1)} %get-tuple-element.62.grad), channel_id=1, source_target_pairs={{0,1},{1,0},{2,3},{3,2},{4,5},{5,4},{6,7},{7,6},{8,9},{9,8},{10,11... | collective-permute-start | bytes 1179656 | tf_op jit(solution)/shard_map/ppermute | solution.py:32
  26.7 6.0 %collective-permute-start.6 = (bf16[1024,128]{1,0:T(8,128)(2,1)S(1)}, bf16[1024,128]{1,0:T(8,128)(2,1)S(1)}, u32[]{:S(2)}, u32[]{:S(2)}) collective-permute-start(bf16[1024,128]{1,0:T(8,128)(2,1)S(1)} %get-tuple-element.61), channel_id=1, source_target_pairs={{0,1},{1,0},{2,3},{3,2},{4,5},{5,4},{6,7},{7,6},{8,9},{9,8},{10,11... | collective-permute-start | bytes 786440 | tf_op jit(solution)/shard_map/ppermute | solution.py:32
  26.9 15.9 %collective-permute-start.3 = (bf16[256,256]{1,0:T(8,128)(2,1)}, bf16[256,256]{1,0:T(8,128)(2,1)S(1)}, u32[]{:S(2)}, u32[]{:S(2)}) collective-permute-start(bf16[256,256]{1,0:T(8,128)(2,1)} %get-tuple-element.57), channel_id=1, source_target_pairs={{0,4},{1,5},{2,6},{3,7},{4,8},{5,9},{6,10},{7,11},{8,12},{9,13},{1... | collective-permute-start | bytes 393224 | tf_op jit(solution)/shard_map/ppermute | solution.py:36
  28.7 14.1 %collective-permute-start.4 = (bf16[256,256]{1,0:T(8,128)(2,1)}, bf16[256,256]{1,0:T(8,128)(2,1)S(1)}, u32[]{:S(2)}, u32[]{:S(2)}) collective-permute-start(bf16[256,256]{1,0:T(8,128)(2,1)} %get-tuple-element.58), channel_id=1, source_target_pairs={{0,8},{1,9},{2,10},{3,11},{4,12},{5,13},{6,14},{7,15},{8,0},{9,1},... | collective-permute-start | bytes 393224 | tf_op jit(solution)/shard_map/ppermute | solution.py:36
  31.3 11.5 %collective-permute-start.5 = (bf16[256,256]{1,0:T(8,128)(2,1)S(1)}, bf16[256,256]{1,0:T(8,128)(2,1)S(1)}, u32[]{:S(2)}, u32[]{:S(2)}) collective-permute-start(bf16[256,256]{1,0:T(8,128)(2,1)S(1)} %get-tuple-element.59), channel_id=1, source_target_pairs={{0,12},{1,13},{2,14},{3,15},{4,0},{5,1},{6,2},{7,3},{8,4},{9,5},{1... | collective-permute-start | bytes 393224 | tf_op jit(solution)/shard_map/ppermute | solution.py:36
  45.4 1.6 %collective-permute-start.9 = (bf16[272,256]{1,0:T(8,128)(2,1)S(1)}, bf16[272,256]{1,0:T(8,128)(2,1)S(1)}, u32[]{:S(2)}, u32[]{:S(2)}) collective-permute-start(bf16[272,256]{1,0:T(8,128)(2,1)S(1)} %get-tuple-element.70.parcel.refs_0_), channel_id=1, source_target_pairs={{0,1},{1,0},{2,3},{3,2},{4,5},{5,4},{6,7},{7,6},{8,9},{9,8},{10,11... | collective-permute-start | bytes 417800 | tf_op jit(solution)/shard_map/ppermute | solution.py:32
  45.4 1.6 %collective-permute-start.8 = (bf16[256,128]{1,0:T(8,128)(2,1)}, bf16[256,128]{1,0:T(8,128)(2,1)S(1)}, u32[]{:S(2)}, u32[]{:S(2)}) collective-permute-start(bf16[256,128]{1,0:T(8,128)(2,1)} %get-tuple-element.69), channel_id=1, source_target_pairs={{0,1},{1,0},{2,3},{3,2},{4,5},{5,4},{6,7},{7,6},{8,9},{9,8},{10,11... | collective-permute-start | bytes 196616 | tf_op jit(solution)/shard_map/ppermute | solution.py:32
  55.5 13.3 %collective-permute-start.10 = (bf16[1728,256]{1,0:T(8,128)(2,1)}, bf16[1728,256]{1,0:T(8,128)(2,1)S(1)}, u32[]{:S(2)}, u32[]{:S(2)}) collective-permute-start(bf16[1728,256]{1,0:T(8,128)(2,1)} %get-tuple-element.74), channel_id=1, source_target_pairs={{0,2},{1,5},{2,0},{3,7},{4,6},{5,1},{6,4},{7,3},{8,10},{9,13},{10,... | collective-permute-start | bytes 2654216 | tf_op jit(solution)/shard_map/ppermute | solution.py:46
  69.8 8.5 %collective-permute-start.11 = (bf16[864,256]{1,0:T(8,128)(2,1)}, bf16[864,256]{1,0:T(8,128)(2,1)S(1)}, u32[]{:S(2)}, u32[]{:S(2)}) collective-permute-start(bf16[864,256]{1,0:T(8,128)(2,1)} %get-tuple-element.86), channel_id=1, source_target_pairs={{0,4},{1,3},{2,6},{3,1},{4,0},{5,7},{6,2},{7,5},{8,12},{9,11},{10,... | collective-permute-start | bytes 1327112 | tf_op jit(solution)/shard_map/ppermute | solution.py:46
  78.3 11.7 %collective-permute-start.12 = (bf16[432,256]{1,0:T(8,128)(2,1)S(1)}, bf16[432,256]{1,0:T(8,128)(2,1)S(1)}, u32[]{:S(2)}, u32[]{:S(2)}) collective-permute-start(bf16[432,256]{1,0:T(8,128)(2,1)S(1)} %add_convert_fusion.2), channel_id=1, source_target_pairs={{0,8},{1,9},{2,10},{3,11},{4,12},{5,13},{6,14},{7,15},{8,0},{9,1},... | collective-permute-start | bytes 663560 | tf_op jit(solution)/shard_map/ppermute | solution.py:46
  90.1 51.7 %copy-start.32 = (s32[4]{0:T(128)S(1)}, s32[4]{0:T(128)}, u32[]{:S(2)}) copy-start(s32[4]{0:T(128)} %copy-done.31) | copy-start | bytes 52
  90.1 12.2 %collective-permute-start.13 = (bf16[432,256]{1,0:T(8,128)(2,1)S(1)}, bf16[432,256]{1,0:T(8,128)(2,1)S(1)}, u32[]{:S(2)}, u32[]{:S(2)}) collective-permute-start(bf16[432,256]{1,0:T(8,128)(2,1)S(1)} %add_convert_fusion.1), channel_id=1, source_target_pairs={{0,8},{1,9},{2,10},{3,11},{4,12},{5,13},{6,14},{7,15},{8,0},{9,1},... | collective-permute-start | bytes 663560 | tf_op jit(solution)/shard_map/ppermute | solution.py:46
  102.5 8.4 %collective-permute-start.14 = (bf16[864,256]{1,0:T(8,128)(2,1)S(1)}, bf16[864,256]{1,0:T(8,128)(2,1)S(1)}, u32[]{:S(2)}, u32[]{:S(2)}) collective-permute-start(bf16[864,256]{1,0:T(8,128)(2,1)S(1)} %maximum_select_fusion.1), channel_id=1, source_target_pairs={{0,4},{1,3},{2,6},{3,1},{4,0},{5,7},{6,2},{7,5},{8,12},{9,11},{10,... | collective-permute-start | bytes 1327112 | tf_op jit(solution)/shard_map/ppermute | solution.py:46
  111.1 36.9 %collective-permute-start.15 = (bf16[1728,256]{1,0:T(8,128)(2,1)S(1)}, bf16[1728,256]{1,0:T(8,128)(2,1)S(1)}, u32[]{:S(2)}, u32[]{:S(2)}) collective-permute-start(bf16[1728,256]{1,0:T(8,128)(2,1)S(1)} %maximum_select_fusion.refs_0_), channel_id=1, source_target_pairs={{0,2},{1,5},{2,0},{3,7},{4,6},{5,1},{6,4},{7,3},{8,10},{9,13},{10,... | collective-permute-start | bytes 2654216 | tf_op jit(solution)/shard_map/ppermute | solution.py:46
  112.7 13.0 %collective-permute-start.16 = (bf16[272,256]{1,0:T(8,128)(2,1)S(1)}, bf16[272,256]{1,0:T(8,128)(2,1)S(1)}, u32[]{:S(2)}, u32[]{:S(2)}) collective-permute-start(bf16[272,256]{1,0:T(8,128)(2,1)S(1)} %get-tuple-element.70.parcel.refs_0_), channel_id=1, source_target_pairs={{0,2},{1,3},{2,0},{3,1},{4,6},{5,7},{6,4},{7,5},{8,10},{9,11},{10,... | collective-permute-start | bytes 417800 | tf_op jit(solution)/shard_map/ppermute | solution.py:32
  125.7 1.4 collective-permute-start.17
  128.1 8.5 %collective-permute-start.18 = (bf16[272,256]{1,0:T(8,128)(2,1)S(1)}, bf16[272,256]{1,0:T(8,128)(2,1)S(1)}, u32[]{:S(2)}, u32[]{:S(2)}) collective-permute-start(bf16[272,256]{1,0:T(8,128)(2,1)S(1)} %get-tuple-element.78), channel_id=1, source_target_pairs={{0,4},{1,5},{2,6},{3,7},{4,8},{5,9},{6,10},{7,11},{8,12},{9,13},{1... | collective-permute-start | bytes 417800 | tf_op jit(solution)/shard_map/ppermute | solution.py:36
  129.6 12.2 %collective-permute-start.19 = (bf16[272,256]{1,0:T(8,128)(2,1)S(1)}, bf16[272,256]{1,0:T(8,128)(2,1)S(1)}, u32[]{:S(2)}, u32[]{:S(2)}) collective-permute-start(bf16[272,256]{1,0:T(8,128)(2,1)S(1)} %get-tuple-element.79), channel_id=1, source_target_pairs={{0,8},{1,9},{2,10},{3,11},{4,12},{5,13},{6,14},{7,15},{8,0},{9,1},... | collective-permute-start | bytes 417800 | tf_op jit(solution)/shard_map/ppermute | solution.py:36
  129.9 11.9 %collective-permute-start.20 = (bf16[272,256]{1,0:T(8,128)(2,1)S(1)}, bf16[272,256]{1,0:T(8,128)(2,1)S(1)}, u32[]{:S(2)}, u32[]{:S(2)}) collective-permute-start(bf16[272,256]{1,0:T(8,128)(2,1)S(1)} %get-tuple-element.80), channel_id=1, source_target_pairs={{0,12},{1,13},{2,14},{3,15},{4,0},{5,1},{6,2},{7,3},{8,4},{9,5},{1... | collective-permute-start | bytes 417800 | tf_op jit(solution)/shard_map/ppermute | solution.py:36
  148.0 2.8 %collective-permute-start.21 = (bf16[1728,256]{1,0:T(8,128)(2,1)S(1)}, bf16[1728,256]{1,0:T(8,128)(2,1)}, u32[]{:S(2)}, u32[]{:S(2)}) collective-permute-start(bf16[1728,256]{1,0:T(8,128)(2,1)S(1)} %maximum_select_fusion.refs_0_), channel_id=1, source_target_pairs={{0,1},{1,0},{2,3},{3,2},{4,5},{5,4},{6,7},{7,6},{8,9},{9,8},{10,11... | collective-permute-start | bytes 2654216 | tf_op jit(solution)/shard_map/ppermute | solution.py:32
  148.1 3.8 %collective-permute-start.22 = (bf16[1728,256]{1,0:T(8,128)(2,1)S(1)}, bf16[1728,256]{1,0:T(8,128)(2,1)}, u32[]{:S(2)}, u32[]{:S(2)}) collective-permute-start(bf16[1728,256]{1,0:T(8,128)(2,1)S(1)} %collective-permute-done.15.refs_1_), channel_id=1, source_target_pairs={{0,1},{1,0},{2,3},{3,2},{4,5},{5,4},{6,7},{7,6},{8,9},{9,8},{10,11... | collective-permute-start | bytes 2654216 | tf_op jit(solution)/shard_map/ppermute | solution.py:32
  (33 other events, 128.6 us)

commit v5 on v4

v5 whole, which is shorter than its diff:
```python
import functools

import jax
import jax.numpy as jnp
from jax import lax
from jax.experimental import pallas as pl
from jax.experimental.pallas import tpu as pltpu
from jax.sharding import PartitionSpec as P

VMEM_LIMIT = 16 * 1024 * 1024
EXTRA = 16


def params():
    return pltpu.CompilerParams(vmem_limit_bytes=VMEM_LIMIT)


def cost(flops, bytes_accessed):
    return pl.CostEstimate(flops=flops, bytes_accessed=bytes_accessed, transcendentals=0)


def near(x):
    return pltpu.with_memory_space_constraint(x, pltpu.VMEM)


def far(x):
    return pltpu.with_memory_space_constraint(x, pltpu.HBM)


SCALARS = pl.BlockSpec(memory_space=pltpu.SMEM)
WHOLE = pl.BlockSpec(memory_space=pltpu.VMEM)
FAR = pl.BlockSpec(memory_space=pl.ANY)


def swap(x, size, bit):
    return lax.ppermute(x, "zslab", [(i, i ^ bit) for i in range(size)])


def rotate(x, size, steps):
    return lax.ppermute(x, "zslab", [(i, (i + 4 * steps) % size) for i in range(size)])


def orders(size):
    bits = [1 << k for k in range(1, size.bit_length() - 1)]
    return bits, [bits[1], bits[0]] + bits[2:]


def swap_stage(x, size, stage):
    both = orders(size)
    return lax.ppermute(x, "zslab", [(i, i ^ both[i % 2][stage]) for i in range(size)])


def stage_half(size, stage, other=False):
    me = lax.axis_index("zslab")
    low, high = (order[stage] for order in orders(size))
    core = me % 2 == (1 if other else 0)
    return jnp.where(core, (me // low) % 2, (me // high) % 2)


def take_rows(x, place, rows):
    return lax.dynamic_slice_in_dim(x, place * rows, rows, axis=0)


def halve(stay, got, mine):
    half = stay.shape[0] // 2
    give = take_rows(stay, 1 - mine, half) + take_rows(got, 1 - mine, half).astype(jnp.float32)
    keep = take_rows(stay, mine, half) + take_rows(got, mine, half).astype(jnp.float32)
    return give.astype(jnp.bfloat16), keep


def join(part, got, mine):
    return jnp.where(mine == 0, jnp.concatenate([part, got]), jnp.concatenate([got, part]))


def mask_rows(voxmask, z):
    lanes = slice(64 * z, 64 * z + 64)
    line = jnp.concatenate([voxmask[0:1, lanes], voxmask[1:2, lanes]], axis=1)
    return jnp.broadcast_to((line == 1).astype(jnp.float32), (128, 128)).T


def wide(mask):
    return jnp.concatenate([mask, mask], axis=1) > 0


def both(ref, z):
    return jnp.concatenate([ref[0, z], ref[1, z]], axis=0)


def inside(shape, dim, rows, cols):
    index = lax.broadcasted_iota(jnp.int32, shape, dim)
    row = (index // 8) % 8 + rows
    col = index % 8 + cols
    return (row >= 0) & (row < 8) & (col >= 0) & (col < 8)


def windows(shape, dim):
    return [inside(shape, dim, p, q) for p in (-1, 0, 1) for q in (-1, 0, 1)]


def shifts(x, dim, valid, sign=1):
    count = x.shape[dim]
    moved = []
    for place in range(9):
        at = place if sign == 1 else 8 - place
        move = 8 * (at // 3 - 1) + at % 3 - 1
        turned = pltpu.roll(x, (-move) % count, dim) if move else x
        moved.append(jnp.where(valid[at], turned, 0.0).astype(jnp.bfloat16))
    return moved


def activate(pre, cotangent, keep):
    sigma = 1.0 / (1.0 + jnp.exp(-pre))
    out = jnp.where(keep, pre * sigma, 0.0)
    grad = jnp.where(keep, cotangent * sigma * (1.0 + pre * (1.0 - sigma)), 0.0)
    return out.astype(jnp.bfloat16), grad.astype(jnp.bfloat16)


def write_exact(rows, ref):
    high = rows.astype(jnp.bfloat16)
    left = rows - high.astype(jnp.float32)
    middle = left.astype(jnp.bfloat16)
    low = (left - middle.astype(jnp.float32)).astype(jnp.bfloat16)
    zeros = jnp.zeros((EXTRA - 3, rows.shape[1]), jnp.float32)
    terms = [term.astype(jnp.float32) for term in (high, middle, low)]
    ref[256:272, :] = jnp.concatenate(terms + [zeros], axis=0).astype(jnp.bfloat16)


def read_extra(ref):
    return jnp.sum(ref[256:272, :].astype(jnp.float32), axis=0, keepdims=True)


def rims_kernel(links, feats, voxmask, parcel, planes, masks, codes, done):
    width = feats.shape[3]
    copies = [
        pltpu.make_async_copy(feats.at[:, pl.ds(0, 1)], planes.at[0], done.at[0]),
        pltpu.make_async_copy(feats.at[:, pl.ds(7, 1)], planes.at[1], done.at[1]),
        pltpu.make_async_copy(voxmask, masks, done.at[2]),
        pltpu.make_async_copy(links, codes, done.at[3]),
    ]
    for copy in copies:
        copy.start()
    for copy in copies:
        copy.wait()
    for side in range(2):
        keep = wide(mask_rows(masks, 7 * side))
        plane = jnp.concatenate([planes[side, 0, 0], planes[side, 1, 0]], axis=0).astype(jnp.float32)
        parcel[128 * side : 128 * side + 128, :] = jnp.where(keep, plane, 0.0).astype(jnp.bfloat16)
    lane = lax.broadcasted_iota(jnp.int32, (EXTRA, width), 1)
    row = jnp.zeros((EXTRA, width), jnp.float32)
    for place in range(4):
        row = jnp.where(lane == place, codes[place // 2, place % 2].astype(jnp.float32), row)
    parcel[256:272, :] = row.astype(jnp.bfloat16)


def rims(links, feats, voxmask):
    width = feats.shape[3]
    return pl.pallas_call(
        rims_kernel,
        in_specs=[FAR] * 3,
        out_specs=WHOLE,
        out_shape=pltpu.VMEM((256 + EXTRA, width), jnp.bfloat16),
        scratch_shapes=[
            pltpu.VMEM((2, 2, 1, 64, width), jnp.bfloat16),
            pltpu.VMEM(voxmask.shape, jnp.int32),
            pltpu.SMEM(links.shape, jnp.int32),
            pltpu.SemaphoreType.DMA((4,)),
        ],
        compiler_params=params(),
        cost_estimate=cost(1024, 1024),
        name="rims",
    )(far(links), far(feats), far(voxmask))


def prepare_kernel(feats, voxmask, mask, rows, give, turned, planes, masks, done):
    half = feats.shape[3] // 2
    copies = [
        pltpu.make_async_copy(feats, planes, done.at[0]),
        pltpu.make_async_copy(voxmask, masks, done.at[1]),
    ]
    for copy in copies:
        copy.start()
    valid = windows((half, 128), 1)
    for copy in copies:
        copy.wait()
    first = lax.axis_index("zslab") % 2 == 0
    for z in range(8):
        span = slice(128 * z, 128 * z + 128)
        keep = mask_rows(masks, z)
        mask[span, :] = keep
        plane = jnp.where(wide(keep), both(planes, z).astype(jnp.float32), 0.0)
        rows[span, :] = plane.astype(jnp.bfloat16)
        own = jnp.where(first, plane[:, :half], plane[:, half:])
        give[span, :] = jnp.where(first, plane[:, half:], plane[:, :half]).astype(jnp.bfloat16)
        for place, moved in enumerate(shifts(own.T, 1, valid)):
            turned[place * half : (place + 1) * half, span] = moved


def prepare(feats, voxmask):
    width = feats.shape[3]
    half = width // 2
    return pl.pallas_call(
        prepare_kernel,
        in_specs=[FAR, FAR],
        out_specs=(WHOLE,) * 4,
        out_shape=(
            pltpu.VMEM((1024, 128), jnp.float32),
            pltpu.VMEM((1024, width), jnp.bfloat16),
            pltpu.VMEM((1024, half), jnp.bfloat16),
            pltpu.VMEM((9 * half, 1024), jnp.bfloat16),
        ),
        scratch_shapes=[
            pltpu.VMEM(feats.shape, jnp.bfloat16),
            pltpu.VMEM(voxmask.shape, jnp.int32),
            pltpu.SemaphoreType.DMA((2,)),
        ],
        compiler_params=params(),
        cost_estimate=cost(1024, 1024),
        name="prepare",
    )(far(feats), far(voxmask))


def turn_kernel(rows, turned):
    half = rows.shape[1]
    valid = windows((half, 128), 1)
    for z in range(8):
        span = slice(128 * z, 128 * z + 128)
        for place, moved in enumerate(shifts(rows[span, :].astype(jnp.float32).T, 1, valid)):
            turned[place * half : (place + 1) * half, span] = moved


def turn(rows):
    half = rows.shape[1]
    return pl.pallas_call(
        turn_kernel,
        in_specs=[WHOLE],
        out_specs=WHOLE,
        out_shape=pltpu.VMEM((9 * half, 1024), jnp.bfloat16),
        compiler_params=params(),
        cost_estimate=cost(1024, 1024),
        name="turn",
    )(near(rows))


def copy_picks(outer, table, parcels, picks):
    for steps in range(outer):
        for slot in range(4):
            plane = table[steps * 4 + slot]
            start = pl.ds(pl.multiple_of((plane % 4) * 64, 64), 64)
            for dev in range(4):

                @pl.when(plane // 4 == dev)
                def _():
                    picks[steps][64 * slot : 64 * slot + 64, :] = parcels[dev][start, :]


def route_kernel(outer, *refs):
    me = lax.axis_index("zslab")
    parcels, (table, *picks), (codes, links, done) = refs[:4], refs[4:-3], refs[-3:]
    for dev in range(4):
        row = parcels[dev][256:272, :128].astype(jnp.float32)
        codes[8 * dev : 8 * dev + 8, :] = row[:8, :].astype(jnp.int32)
    copy = pltpu.make_async_copy(codes, links, done)
    copy.start()
    copy.wait()
    for place in range(outer * 4):
        table[place] = 0
    for plane in range(16):
        dev, side, brick = plane // 4, plane // 2 % 2, plane % 2
        dest = links[dev * 8, brick * 2 + side]

        @pl.when((dest >= 0) & ((dest // 2) % 4 == me % 4))
        def _():
            steps = lax.rem(dest // 8 - me // 4 + outer, outer)
            table[steps * 4 + dest % 2 + (0 if side == 1 else 2)] = plane

    for brick in range(2):
        for side in range(2):
            dest = links[0, brick * 2 + side]
            steps = lax.rem(me // 4 - dest // 8 + outer, outer)
            table[outer * 4 + 2 * side + brick] = jnp.where(dest >= 0, steps, -1)

    copy_picks(outer, table, parcels, picks)


def route(parcels, outer):
    width = parcels[0].shape[1]
    results = pl.pallas_call(
        functools.partial(route_kernel, outer),
        in_specs=[WHOLE] * 4,
        out_specs=[SCALARS] + [WHOLE] * outer,
        out_shape=[jax.ShapeDtypeStruct((outer * 4 + 4,), jnp.int32)]
        + [pltpu.VMEM((256, width), jnp.bfloat16)] * outer,
        scratch_shapes=[
            pltpu.VMEM((32, 128), jnp.int32),
            pltpu.SMEM((32, 128), jnp.int32),
            pltpu.SemaphoreType.DMA(()),
        ],
        compiler_params=params(),
        cost_estimate=cost(1024, 1024),
        name="route",
    )(*[near(x) for x in parcels])
    return results[0], results[1:]


def repeat_kernel(outer, table, *refs):
    parcels, picks = refs[:4], refs[4:]
    copy_picks(outer, table, parcels, picks)
    total = sum(read_extra(ref) for ref in parcels)
    for ref in picks:
        write_exact(total, ref)


def repeat_route(table, parcels, outer):
    width = parcels[0].shape[1]
    return pl.pallas_call(
        functools.partial(repeat_kernel, outer),
        in_specs=[SCALARS] + [WHOLE] * 4,
        out_specs=[WHOLE] * outer,
        out_shape=[pltpu.VMEM((256 + EXTRA, width), jnp.bfloat16)] * outer,
        compiler_params=params(),
        cost_estimate=cost(1024, 1024),
        name="repeat_route",
    )(table, *[near(x) for x in parcels])


def chosen(table, slot, arrived):
    rows = slice(64 * slot, 64 * slot + 64)
    plane = jnp.zeros((64, arrived[0].shape[1]), jnp.float32)
    for steps, ref in enumerate(arrived):
        plane = jnp.where(table[4 * len(arrived) + slot] == steps, ref[rows, :].astype(jnp.float32), plane)
    return plane


def forward_kernel(rows, mask, weight, bias, cotangent, out, grad, edge, bias_sum, near_weight, ends, cols, pre, slopes, shift, done):
    width = rows.shape[1]
    copies = [pltpu.make_async_copy(bias, shift, done.at[4])]
    for a in (1, 0, 2):
        taps = pl.ds(9 * a, 9)
        copies.append(pltpu.make_async_copy(weight.at[taps], near_weight.at[taps], done.at[a]))
    copies.append(pltpu.make_async_copy(cotangent, slopes, done.at[3]))
    for copy in copies:
        copy.start()
    valid = windows((128, width), 0)
    for z in range(8):
        span = slice(128 * z, 128 * z + 128)
        for place, moved in enumerate(shifts(rows[span, :].astype(jnp.float32), 0, valid)):
            cols[span, place * width : (place + 1) * width] = moved

    def taps(a):
        return near_weight[9 * a : 9 * a + 9].reshape(9 * width, width)

    copies[0].wait()
    copies[1].wait()
    pre[...] = jnp.dot(cols[...], taps(1), preferred_element_type=jnp.float32) + shift[...]
    copies[2].wait()
    pre[128:, :] += jnp.dot(cols[:896, :], taps(0), preferred_element_type=jnp.float32)
    copies[3].wait()
    pre[:896, :] += jnp.dot(cols[128:, :], taps(2), preferred_element_type=jnp.float32)
    copies[4].wait()
    for side in range(2):
        edge[side] = pre[896 * side : 896 * side + 128, :]
        ends[side] = both(slopes, 7 * side)
    total = jnp.zeros((1, width), jnp.float32)
    for z in range(1, 7):
        span = slice(128 * z, 128 * z + 128)
        act, slope = activate(pre[span, :], both(slopes, z).astype(jnp.float32), wide(mask[span, :]))
        for b in range(2):
            out[b, z] = act[64 * b : 64 * b + 64]
        grad[128 * (z - 1) : 128 * z, :] = slope
        total += jnp.sum(slope.astype(jnp.float32), axis=0, keepdims=True)
    bias_sum[...] = total


def forward_inside(rows, mask, weight, bias, cotangent):
    width = rows.shape[1]
    return pl.pallas_call(
        forward_kernel,
        in_specs=[WHOLE, WHOLE, FAR, FAR, FAR],
        out_specs=(WHOLE,) * 6,
        out_shape=(
            jax.ShapeDtypeStruct(cotangent.shape, jnp.bfloat16),
            pltpu.VMEM((768, width), jnp.bfloat16),
            pltpu.VMEM((2, 128, width), jnp.float32),
            pltpu.VMEM((1, width), jnp.float32),
            pltpu.VMEM(weight.shape, jnp.bfloat16),
            pltpu.VMEM((2, 128, width), jnp.bfloat16),
        ),
        scratch_shapes=[
            pltpu.VMEM((1024, 9 * width), jnp.bfloat16),
            pltpu.VMEM((1024, width), jnp.float32),
            pltpu.VMEM(cotangent.shape, jnp.bfloat16),
            pltpu.VMEM((1, width), jnp.float32),
            pltpu.SemaphoreType.DMA((5,)),
        ],
        compiler_params=params(),
        cost_estimate=cost(1024, 1024),
        name="forward_inside",
    )(near(rows), near(mask), far(weight), far(bias), far(cotangent))


def inner_terms_kernel(mine, theirs, grad, their_grad, terms):
    rows = mine.shape[0]
    for a in range(3):
        lanes = slice(128 * a, 128 * a + 768)
        terms[a * rows : (a + 1) * rows, :] = jnp.dot(
            mine[:, lanes], grad[...], preferred_element_type=jnp.float32
        ) + jnp.dot(theirs[:, lanes], their_grad[...], preferred_element_type=jnp.float32)


def inner_terms(mine, theirs, grad, their_grad):
    rows, width = mine.shape[0], grad.shape[1]
    return pl.pallas_call(
        inner_terms_kernel,
        in_specs=[WHOLE] * 4,
        out_specs=WHOLE,
        out_shape=pltpu.VMEM((3 * rows, width), jnp.float32),
        compiler_params=params(),
        cost_estimate=cost(1024, 1024),
        name="inner_terms",
    )(near(mine), near(theirs), near(grad), near(their_grad))


def edge_kernel(table, mask, weight, edge, ends, inner, out_in, *refs):
    arrived, (out, parcel, own, give, planes, done) = refs[:-6], refs[-6:]
    width = edge.shape[2]
    half = width // 2
    valid = windows((128, width), 0)
    total = inner[...]
    for side in range(2):
        rows = slice(128 * side, 128 * side + 128)
        halo = jnp.concatenate([chosen(table, 2 * side + b, arrived) for b in range(2)], axis=0)
        first = lax.axis_index("zslab") % 2 == 0
        own[rows, :] = jnp.where(first, halo[:, :half], halo[:, half:]).astype(jnp.bfloat16)
        give[rows, :] = jnp.where(first, halo[:, half:], halo[:, :half]).astype(jnp.bfloat16)
        cols = jnp.concatenate(shifts(halo, 0, valid), axis=1)
        taps = weight[18 * side : 18 * side + 9].reshape(9 * width, width)
        pre = edge[side] + jnp.dot(cols, taps, preferred_element_type=jnp.float32)
        z = 7 * side
        keep = wide(mask[128 * z : 128 * z + 128, :])
        act, slope = activate(pre, ends[side].astype(jnp.float32), keep)
        for b in range(2):
            planes[side, b, 0] = act[64 * b : 64 * b + 64]
        pltpu.make_async_copy(planes.at[side], out.at[:, pl.ds(z, 1)], done.at[side]).start()
        parcel[rows, :] = slope
        total += jnp.sum(slope.astype(jnp.float32), axis=0, keepdims=True)
    write_exact(total, parcel)
    for side in range(2):
        pltpu.make_async_copy(planes.at[side], out.at[:, pl.ds(7 * side, 1)], done.at[side]).wait()


def forward_edges(table, mask, weight, edge, ends, inner, out, arrived):
    width = edge.shape[2]
    return pl.pallas_call(
        edge_kernel,
        in_specs=[SCALARS] + [WHOLE] * 5 + [FAR] + [WHOLE] * len(arrived),
        out_specs=(FAR, WHOLE, WHOLE, WHOLE),
        out_shape=(
            jax.ShapeDtypeStruct(out.shape, out.dtype),
            pltpu.VMEM((256 + EXTRA, width), jnp.bfloat16),
            pltpu.VMEM((256, width // 2), jnp.bfloat16),
            pltpu.VMEM((256, width // 2), jnp.bfloat16),
        ),
        scratch_shapes=[pltpu.VMEM((2, 2, 1, 64, width), jnp.bfloat16), pltpu.SemaphoreType.DMA((2,))],
        input_output_aliases={6: 0},
        compiler_params=params(),
        cost_estimate=cost(1024, 1024),
        name="forward_edges",
    )(
        table,
        near(mask),
        near(weight),
        near(edge),
        near(ends),
        near(inner),
        out,
        *[near(x) for x in arrived],
    )


def outer_terms_kernel(taps, size, mine, theirs, halos, their_halos, parcel, their_parcel, inner, give, stay, cols, total):
    half = mine.shape[0] // 9
    piece = half // 2
    valid = windows((half, 128), 1)
    facing = jnp.concatenate([parcel[:128], their_parcel[:128], parcel[128:256], their_parcel[128:256]], axis=0)
    for a in range(3):
        first, last = max(taps[0], 9 * a), min(taps[1], 9 * a + 9)
        if first >= last:
            continue
        low, high = (first - 9 * a) * half, (last - 9 * a) * half
        for place, (ref, ends) in enumerate(((mine, halos), (theirs, their_halos), (mine, halos), (theirs, their_halos))):
            side = place // 2
            plane = a - 1 + 7 * side
            lanes = slice(128 * place, 128 * place + 128)
            if 0 <= plane < 8:
                cols[low:high, lanes] = ref[low:high, 128 * plane : 128 * plane + 128]
            else:
                moved = shifts(ends[128 * side : 128 * side + 128, :].astype(jnp.float32).T, 1, valid)
                for at in range(first - 9 * a, last - 9 * a):
                    cols[at * half : (at + 1) * half, lanes] = moved[at]
        start = (first - taps[0]) * half
        total[start : start + high - low, :] = inner[first * half : last * half, :] + jnp.dot(
            cols[low:high, :], facing, preferred_element_type=jnp.float32
        )
    upper = stage_half(size, 0)
    for tap in range(taps[1] - taps[0]):
        rows = slice(piece * tap, piece * tap + piece)
        other = pl.ds(pl.multiple_of(half * tap + (1 - upper) * piece, 16), piece)
        own = pl.ds(pl.multiple_of(half * tap + upper * piece, 16), piece)
        give[rows, :] = total[other, :].astype(jnp.bfloat16)
        stay[rows, :] = total[own, :]


def outer_terms(taps, size, mine, theirs, halos, their_halos, parcel, their_parcel, inner):
    width = inner.shape[1]
    half = mine.shape[0] // 9
    count = taps[1] - taps[0]
    rows = count * half // 2
    return pl.pallas_call(
        functools.partial(outer_terms_kernel, taps, size),
        in_specs=[WHOLE] * 7,
        out_specs=(WHOLE, WHOLE),
        out_shape=(pltpu.VMEM((rows, width), jnp.bfloat16), pltpu.VMEM((rows, width), jnp.float32)),
        scratch_shapes=[
            pltpu.VMEM((9 * half, 512), jnp.bfloat16),
            pltpu.VMEM((count * half, width), jnp.float32),
        ],
        compiler_params=params(),
        cost_estimate=cost(1024, 1024),
        name="outer_terms",
    )(*[near(x) for x in (mine, theirs, halos, their_halos, parcel, their_parcel, inner)])


def backward_rows(planes, mask, weight, cols, place):
    width = weight.shape[1]
    valid = windows((128, width), 0)
    for index, plane in enumerate(planes):
        rows = slice(128 * (place + index), 128 * (place + index) + 128)
        for at, moved in enumerate(shifts(plane.astype(jnp.float32), 0, valid, -1)):
            cols[rows, at * width : (at + 1) * width] = moved
    count = 128 * (len(planes) - 2)
    total = jnp.zeros((count, width), jnp.float32)
    for a in range(3):
        for at in range(9):
            start = 128 * (place + 2 - a)
            total += lax.dot_general(
                cols[start : start + count, at * width : (at + 1) * width],
                weight[9 * a + at],
                (((1,), (1,)), ((), ())),
                preferred_element_type=jnp.float32,
            )
    return jnp.where(wide(mask), total, 0.0).astype(jnp.bfloat16)


def backward_inner_kernel(grad, mask, weight, grad_feats, cols):
    planes = [grad[128 * (z - 1) : 128 * z, :] for z in range(1, 7)]
    done = backward_rows(planes, mask[256:768, :], weight, cols, 0)
    for z in range(2, 6):
        for b in range(2):
            start = 128 * (z - 2) + 64 * b
            grad_feats[b, z] = done[start : start + 64]


def backward_inner(grad, mask, weight):
    width = grad.shape[1]
    return pl.pallas_call(
        backward_inner_kernel,
        in_specs=[WHOLE] * 3,
        out_specs=WHOLE,
        out_shape=jax.ShapeDtypeStruct((2, 8, 64, width), jnp.bfloat16),
        scratch_shapes=[pltpu.VMEM((768, 9 * width), jnp.bfloat16)],
        compiler_params=params(),
        cost_estimate=cost(1024, 1024),
        name="backward_inner",
    )(near(grad), near(mask), near(weight))


def backward_outer_kernel(table, grad, parcel, mask, weight, done, *refs):
    arrived, (grad_feats, bias_sum, cols, planes, sent) = refs[:-5], refs[-5:]
    for side in range(2):
        halo = jnp.concatenate([chosen(table, 2 * side + b, arrived) for b in range(2)], axis=0)
        rim = parcel[128 * side : 128 * side + 128, :]
        if side == 0:
            around = [halo, rim, grad[:128, :], grad[128:256, :]]
        else:
            around = [grad[512:640, :], grad[640:768, :], rim, halo]
        first = 6 * side
        rows = backward_rows(around, mask[128 * first : 128 * first + 256, :], weight, cols, 4 * side)
        for z in range(2):
            for b in range(2):
                start = 128 * z + 64 * b
                planes[side, b, z] = rows[start : start + 64]
        pltpu.make_async_copy(planes.at[side], grad_feats.at[:, pl.ds(first, 2)], sent.at[side]).start()
    bias_sum[...] = sum(read_extra(ref) for ref in arrived)
    for side in range(2):
        pltpu.make_async_copy(planes.at[side], grad_feats.at[:, pl.ds(6 * side, 2)], sent.at[side]).wait()


def backward_outer(table, grad, parcel, mask, weight, done, arrived):
    width = grad.shape[1]
    return pl.pallas_call(
        backward_outer_kernel,
        in_specs=[SCALARS] + [WHOLE] * 4 + [FAR] + [WHOLE] * len(arrived),
        out_specs=(FAR, WHOLE),
        out_shape=(jax.ShapeDtypeStruct(done.shape, done.dtype), jax.ShapeDtypeStruct((1, width), jnp.float32)),
        scratch_shapes=[
            pltpu.VMEM((1024, 9 * width), jnp.bfloat16),
            pltpu.VMEM((2, 2, 2, 64, width), jnp.bfloat16),
            pltpu.SemaphoreType.DMA((2,)),
        ],
        input_output_aliases={5: 0},
        compiler_params=params(),
        cost_estimate=cost(1024, 1024),
        name="backward_outer",
    )(table, near(grad), near(parcel), near(mask), near(weight), done, *[near(x) for x in arrived])


def assemble_kernel(first, size, *refs):
    parts, (out, done) = refs[:4], refs[-2:]
    count = parts[0].shape[0]
    core = lax.axis_index("zslab") % 2
    mine, theirs = stage_half(size, 0), stage_half(size, 0, other=True)
    places = (2 * core + mine, 2 * core + 1 - mine, 2 - 2 * core + theirs, 3 - 2 * core - theirs)
    copies = [
        pltpu.make_async_copy(ref, out.at[pl.ds(first, count), place], done.at[index])
        for index, (ref, place) in enumerate(zip(parts, places))
    ]
    for copy in copies:
        copy.start()
    for copy in copies:
        copy.wait()


def assemble(first, size, parts, shape, done):
    given = [] if done is None else [done]
    return pl.pallas_call(
        functools.partial(assemble_kernel, first, size),
        in_specs=[WHOLE] * 4 + [FAR] * len(given),
        out_specs=FAR,
        out_shape=jax.ShapeDtypeStruct(shape, jnp.bfloat16),
        scratch_shapes=[pltpu.SemaphoreType.DMA((4,))],
        input_output_aliases={4: 0} if given else {},
        compiler_params=params(),
        cost_estimate=cost(1024, 1024),
        name="assemble",
    )(*[near(x) for x in parts], *given)


def gather_group(parcel, size):
    inner = swap(parcel, size, 2)
    return [parcel, inner, swap(parcel, size, 1), swap(inner, size, 1)]


def per_device(size, feats, voxmask, links, weight, bias, cotangent):
    width = feats.shape[3]
    outer = size // 4

    parcels = gather_group(rims(links, feats, voxmask), size)
    mask, rows, give, turned = prepare(feats, voxmask)
    rows, parcels[1] = lax.optimization_barrier((rows, parcels[1]))
    out, grad, edge, bias_local, weight, ends = forward_inside(rows, mask, weight, bias.reshape(1, width), cotangent)
    *parcels, grad = lax.optimization_barrier((*parcels, grad))
    table, picks = route(parcels, outer)

    *picks, give = lax.optimization_barrier((*picks, give))
    arrived = [rotate(pick, size, steps) if steps else pick for steps, pick in enumerate(picks)]
    their_turned = turn(swap(give, size, 1))
    inner = inner_terms(turned, their_turned, grad, swap(grad, size, 1))

    *arrived, inner = lax.optimization_barrier((*arrived, inner))
    out, parcel, halos, give = forward_edges(table, mask, weight, edge, ends, bias_local, out, arrived)
    their_halos = swap(give, size, 1)
    parcels = gather_group(parcel, size)

    stages = len(orders(size)[0])
    halves = [stage_half(size, stage) for stage in range(stages)]
    count = weight.shape[0]
    cuts = [(0, count // 2), (count // 2, count)]
    sums = []
    for taps in cuts:
        give, stay = outer_terms(taps, size, turned, their_turned, halos, their_halos, parcel, parcels[2], inner)
        sums.append((stay, swap_stage(give, size, 0)))

    grad_feats = backward_inner(grad, mask, weight)
    picks = repeat_route(table, parcels, outer)
    (stay, got), other = sums
    stay, grad_feats, *picks = lax.optimization_barrier((stay, grad_feats, *picks))
    sums = [(stay, got), other]
    arrived = [rotate(pick, size, steps) if steps else pick for steps, pick in enumerate(picks)]
    for stage in range(1, stages):
        for index, (stay, got) in enumerate(sums):
            give, stay = halve(stay, got, halves[stage])
            sums[index] = (stay, swap_stage(give, size, stage))
    parts = [(stay + got.astype(jnp.float32)).astype(jnp.bfloat16) for stay, got in sums]
    parts[0], *arrived = lax.optimization_barrier((parts[0], *arrived))
    for stage in reversed(range(1, stages)):
        parts = [join(part, swap_stage(part, size, stage), halves[stage]) for part in parts]
    grad_feats, grad_bias = backward_outer(table, grad, parcel, mask, weight, grad_feats, arrived)

    grad_weight = None
    for taps, part in zip(cuts, parts):
        last = swap_stage(part, size, 0)
        other = swap(part, size, 1)
        if grad_weight is None:
            last, grad_feats, grad_bias = lax.optimization_barrier((last, grad_feats, grad_bias))
        pieces = [x.reshape(taps[1] - taps[0], width // 4, width) for x in (part, last, other, swap(last, size, 1))]
        grad_weight = assemble(taps[0], size, pieces, (count, 4, width // 4, width), grad_weight)
    return out, grad_feats, grad_weight.reshape(count, width, width), grad_bias.reshape(width)


def solution(mesh):
    return jax.shard_map(
        functools.partial(per_device, mesh.shape["zslab"]),
        mesh=mesh,
        in_specs=(
            P(("groups", "zslab"), None, None, None),
            P(("groups", "zslab"), None),
            P(("groups", "zslab"), None),
            P(),
            P(),
            P(("groups", "zslab"), None, None, None),
        ),
        out_specs=(
            P(("groups", "zslab"), None, None, None),
            P(("groups", "zslab"), None, None, None),
            P("groups", None, None),
            P("groups"),
        ),
        check_vma=False,
    )
```

time: 157 us -> 140 us (0.89)
  waiting for transfers between devices: 73.1 us -> 49.1 us
  local copies, waits for them, and re-layouts: 28.8 us -> 12.4 us
  other arithmetic: 1.66 us -> 12.8 us
  starting transfers between devices: 20.6 us -> 28.1 us
  Pallas kernels: 30.5 us -> 35.5 us
    unnamed x71 -> x50, local copies, waits for them, and re-layouts: 28.5 us -> 12.4 us
    ppermute x6 -> x12, waiting for transfers between devices: 43.8 us -> 28.6 us  [swap_stage(): lax.ppermute(x, 'zslab', [(i, i ^ both[i % 2][stage]) for i in range(size)])]
    pallas_call x9 -> x11, Pallas kernels: 24.5 us -> 30.3 us  [the longest x1 8.68 us: forward_inside(): pl.pallas_call(forward_kernel, in_specs=[WHOLE, WHOLE, FAR, FAR, FAR], ou...]
    ppermute x6 -> x12, starting transfers between devices: 5.56 us -> 11.3 us  [swap_stage(): lax.ppermute(x, 'zslab', [(i, i ^ both[i % 2][stage]) for i in range(size)])]
    ppermute x6, waiting for transfers between devices: 9.55 us -> 4.11 us  [rotate(): lax.ppermute(x, 'zslab', [(i, (i + 4 * steps) % size) for i in range(size)])]
    convert_element_type x2 -> x4, other arithmetic: 1.08 us -> 6.41 us  [halve(): return (give.astype(jnp.bfloat16), keep)]
    select_n x2 -> x4, other arithmetic: 0.42 us -> 4.3 us  [join(): jnp.where(mine == 0, jnp.concatenate([part, got]), jnp.concatenate([got,...]
    ppermute x11 -> x13, waiting for transfers between devices: 19.7 us -> 16.5 us  [swap(): return lax.ppermute(x, 'zslab', [(i, i ^ bit) for i in range(size)])]
  transfers between devices with their start and end apart: 23 -> 31, of which waited for: 12 -> 14; matrix products, arithmetic and copies ran while one was open for 2% -> 9% of each run, Pallas kernels for 9% -> 21%
where the time goes in v5:
time: 140 us; the launch traced here: 139 us
  waiting for transfers between devices  49.1 us (35%)
  Pallas kernels  35.5 us (25%)
  starting transfers between devices  28.1 us (20%)
  other arithmetic  12.8 us (9%)
  local copies, waits for them, and re-layouts  12.4 us (9%)
    ppermute x12, waiting for transfers between devices, swap_stage(): lax.ppermute(x, 'zslab', [(i, i ^ both[i % 2][stage]) for i in range(size)])  28.6 us
    ppermute x13, waiting for transfers between devices, swap(): return lax.ppermute(x, 'zslab', [(i, i ^ bit) for i in range(size)])  16.5 us
    unnamed x50, local copies, waits for them, and re-layouts  12.4 us
    ppermute x12, starting transfers between devices, swap_stage(): lax.ppermute(x, 'zslab', [(i, i ^ both[i % 2][stage]) for i in range(size)])  11.3 us
    ppermute x6, starting transfers between devices, rotate(): lax.ppermute(x, 'zslab', [(i, (i + 4 * steps) % size) for i in range(size)])  10.4 us
    pallas_call x1, Pallas kernels, forward_inside(): pl.pallas_call(forward_kernel, in_specs=[WHOLE, WHOLE, FAR, FAR, FAR], ou...  8.68 us
    ppermute x13, starting transfers between devices, swap(): return lax.ppermute(x, 'zslab', [(i, i ^ bit) for i in range(size)])  6.45 us
    convert_element_type x4, other arithmetic, halve(): return (give.astype(jnp.bfloat16), keep)  6.41 us
  transfers between devices with their start and end apart: 31, of which 14 were waited for; matrix products, arithmetic and copies ran while one was open for 9% of the time, Pallas kernels for 21%

profile of v5, /device:TPU:0, one launch (start us, length us, event | category | flops | bytes accessed | tf_op | source)
XLA Modules:
  0.0 139.2 jit_solution(13433846218590765815)
XLA Ops:
  1.7 3.0 %collective-permute-start = (bf16[272,256]{1,0:T(8,128)(2,1)S(1)}, bf16[272,256]{1,0:T(8,128)(2,1)S(1)}, u32[]{:S(2)}, u32[]{:S(2)}) collective-permute-start(bf16[272,256]{1,0:T(8,128)(2,1)S(1)} %rims.1.refs_0_), channel_id=1, source_target_pairs={{0,2},{1,3},{2,0},{3,1},{4,6},{5,7},{6,4},{7,5},{8,10},{9,11},{10,... | collective-permute-start | bytes 417800 | tf_op jit(solution)/shard_map/ppermute | solution.py:36
  4.8 3.7 %collective-permute-done.refs_1_ = bf16[272,256]{1,0:T(8,128)(2,1)S(1)} collective-permute-done((bf16[272,256]{1,0:T(8,128)(2,1)S(1)}, bf16[272,256]{1,0:T(8,128)(2,1)S(1)}, u32[]{:S(2)}, u32[]{:S(2)}) %collective-permute-start) | collective-permute-done | bytes 139296 | tf_op jit(solution)/shard_map/ppermute | solution.py:36
  8.4 3.3 %prepare.1 = (f32[1024,128]{1,0:T(8,128)S(1)}, bf16[1024,256]{1,0:T(8,128)(2,1)S(1)}, bf16[1024,128]{1,0:T(8,128)(2,1)S(1)}, bf16[1152,1024]{1,0:T(8,128)(2,1)S(1)}) custom-call(bf16[2,8,64,256]{3,2,1,0:T(8,128)(2,1)} %feats.3, s32[2,512]{1,0:T(2,128)} %voxmask.3), custom_call_target="tpu_custom_call" | custom-call | flops 1024 | bytes 1024 | tf_op jit(solution)/shard_map/prepare/pallas_call | solution.py:201
  11.8 8.7 %forward_inside.1 = (bf16[2,8,64,256]{3,2,1,0:T(8,128)(2,1)}, bf16[768,256]{1,0:T(8,128)(2,1)S(1)}, f32[2,128,256]{2,1,0:T(8,128)S(1)}, f32[1,256]{1,0:T(1,128)S...) custom-call(bf16[1024,256]{1,0:T(8,128)(2,1)S(1)} %get-tuple-element.66.rows, ...), custom_call_target="tpu_custom_call" | custom-call | flops 1024 | bytes 1024 | tf_op jit(solution)/shard_map/forward_inside/pallas_call | solution.py:376
  21.0 2.2 %route.1 = (s32[20]{0:T(128)S(1)}, bf16[256,256]{1,0:T(8,128)(2,1)S(1)}, bf16[256,256]{1,0:T(8,128)(2,1)S(1)}, bf16[256,256]{1,0:T(8,128)(2,1)S(1)}, bf16[256,256]{1,0:T(8,128)(2,1)S(1)}) custom-call(bf16[272,256]{1,0:T(8,128)(2,1)S(1)} %rims.1.refs_0_, bf16[272,256]{1,0:T(8,128)(2,1)S(1)} %collective-permute-done.refs_1_, ...), custom_call_target="tpu_custom_call" | custom-call | flops 1024 | bytes 1024 | tf_op jit(solution)/shard_map/route/pallas_call | solution.py:287
  23.3 1.8 %collective-permute-start.3 = (bf16[256,256]{1,0:T(8,128)(2,1)S(1)}, bf16[256,256]{1,0:T(8,128)(2,1)S(1)}, u32[]{:S(2)}, u32[]{:S(2)}) collective-permute-start(bf16[256,256]{1,0:T(8,128)(2,1)S(1)} %get-tuple-element.85), channel_id=1, source_target_pairs={{0,4},{1,5},{2,6},{3,7},{4,8},{5,9},{6,10},{7,11},{8,12},{9,13},{1... | collective-permute-start | bytes 393224 | tf_op jit(solution)/shard_map/ppermute | solution.py:40
  25.1 2.6 %collective-permute-start.4 = (bf16[256,256]{1,0:T(8,128)(2,1)S(1)}, bf16[256,256]{1,0:T(8,128)(2,1)S(1)}, u32[]{:S(2)}, u32[]{:S(2)}) collective-permute-start(bf16[256,256]{1,0:T(8,128)(2,1)S(1)} %get-tuple-element.86), channel_id=1, source_target_pairs={{0,8},{1,9},{2,10},{3,11},{4,12},{5,13},{6,14},{7,15},{8,0},{9,1},... | collective-permute-start | bytes 393224 | tf_op jit(solution)/shard_map/ppermute | solution.py:40
  29.9 2.9 %inner_terms.1.inner = f32[3456,256]{1,0:T(8,128)S(1)} custom-call(bf16[1152,1024]{1,0:T(8,128)(2,1)S(1)} %get-tuple-element.88.mine, bf16[1152,1024]{1,0:T(8,128)(2,1)S(1)} %turn.1.theirs, bf16[768,256]{1,0:T(8,128)(2,1)S(1)} %get-tuple-element.90.grad, bf16[768,256]{1,0:T(8,128)(2,1)S(1)} %collective-permute-done.7.their_grad), custom_call_target="tpu_custom_call" | custom-call | flops 1024 | bytes 1024 | tf_op jit(solution)/shard_map/inner_terms/pallas_call | solution.py:412
  32.8 4.1 %collective-permute-done.4.refs_2_ = bf16[256,256]{1,0:T(8,128)(2,1)S(1)} collective-permute-done((bf16[256,256]{1,0:T(8,128)(2,1)S(1)}, bf16[256,256]{1,0:T(8,128)(2,1)S(1)}, u32[]{:S(2)}, u32[]{:S(2)}) %collective-permute-start.4) | collective-permute-done | bytes 131104 | tf_op jit(solution)/shard_map/ppermute | solution.py:40
  37.0 1.9 %forward_edges.1 = (bf16[2,8,64,256]{3,2,1,0:T(8,128)(2,1)}, bf16[272,256]{1,0:T(8,128)(2,1)S(1)}, bf16[256,128]{1,0:T(8,128)(2,1)S(1)}, bf16[256,128]{1,0:T(8,128)(2,1)S(1)}) custom-call(s32[20]{0:T(128)S(1)} %get-tuple-element.73.table, f32[1024,128]{1,0:T(8,128)S(1)} %get-tuple-element.67.mask, ...), custom_call_target="tpu_custom_call", output_to_operand_aliasing={{0}: (6, {})} | custom-call | flops 1024 | bytes 1024 | tf_op jit(solution)/shard_map/forward_edges/pallas_call | solution.py:453
  40.4 1.9 %outer_terms.3 = (bf16[896,256]{1,0:T(8,128)(2,1)}, f32[896,256]{1,0:T(8,128)S(1)}) custom-call(bf16[1152,1024]{1,0:T(8,128)(2,1)S(1)} %get-tuple-element.88.mine, bf16[1152,1024]{1,0:T(8,128)(2,1)S(1)} %turn.1.theirs, bf16[256,128]{1,0:T(8,128)(2,1)S(1)} %get-tuple-element.96.halos, bf16[256,128]{1,0:T(8,128)(2,1)S(1)} %collective-permute-done.8.their_halos, ...), custom_call_target="tpu_custom_call" | custom-call | flops 1024 | bytes 1024 | tf_op jit(solution)/shard_map/outer_terms/pallas_call | solution.py:518
  44.8 1.9 %outer_terms.2 = (bf16[832,256]{1,0:T(8,128)(2,1)}, f32[832,256]{1,0:T(8,128)S(1)}) custom-call(bf16[1152,1024]{1,0:T(8,128)(2,1)S(1)} %get-tuple-element.88.mine, bf16[1152,1024]{1,0:T(8,128)(2,1)S(1)} %turn.1.theirs, bf16[256,128]{1,0:T(8,128)(2,1)S(1)} %get-tuple-element.96.halos, bf16[256,128]{1,0:T(8,128)(2,1)S(1)} %collective-permute-done.8.their_halos, ...), custom_call_target="tpu_custom_call" | custom-call | flops 1024 | bytes 1024 | tf_op jit(solution)/shard_map/outer_terms/pallas_call | solution.py:518
  49.7 9.9 %collective-permute-done.10.refs_1_ = bf16[272,256]{1,0:T(8,128)(2,1)} collective-permute-done((bf16[272,256]{1,0:T(8,128)(2,1)S(1)}, bf16[272,256]{1,0:T(8,128)(2,1)}, u32[]{:S(2)}, u32[]{:S(2)}) %collective-permute-start.10) | collective-permute-done | bytes 139296 | tf_op jit(solution)/shard_map/ppermute | solution.py:36
  59.6 2.2 %add_convert_fusion = (bf16[448,256]{1,0:T(8,128)(2,1)}, f32[448,256]{1,0:T(8,128)}) fusion(f32[896,256]{1,0:T(8,128)} %copy-done.11, s32[]{:T(128)S(6)} %select_n.130, bf16[896,256]{1,0:T(8,128)(2,1)} %collective-permute-done.21, s32[]{:T(128)S(6)} %select_n.128), kind=kLoop, calls=%fused_computation.1 | loop fusion | flops 573440 | bytes 2064392 | tf_op jit(solution)/shard_map/convert_element_type | solution.py:68
  61.9 3.3 %collective-permute-start.22 = (bf16[448,256]{1,0:T(8,128)(2,1)}, bf16[448,256]{1,0:T(8,128)(2,1)}, u32[]{:S(2)}, u32[]{:S(2)}) collective-permute-start(bf16[448,256]{1,0:T(8,128)(2,1)} %get-tuple-element.124), channel_id=1, source_target_pairs={{0,4},{1,3},{2,6},{3,1},{4,0},{5,7},{6,2},{7,5},{8,12},{9,11},{10,... | collective-permute-start | bytes 688136 | tf_op jit(solution)/shard_map/ppermute | solution.py:50
  67.2 2.9 %backward_inner.1.done = bf16[2,8,64,256]{3,2,1,0:T(8,128)(2,1)} custom-call(bf16[768,256]{1,0:T(8,128)(2,1)S(1)} %copy-done.4, f32[1024,128]{1,0:T(8,128)S(1)} %copy-done.1, bf16[27,256,256]{2,1,0:T(8,128)(2,1)S(1)} %get-tuple-element.74.weight), custom_call_target="tpu_custom_call" | custom-call | flops 1024 | bytes 1024 | tf_op jit(solution)/shard_map/backward_inner/pallas_call | solution.py:565
  71.7 2.1 %add_convert_fusion.1 = (bf16[416,256]{1,0:T(8,128)(2,1)}, f32[416,256]{1,0:T(8,128)}) fusion(f32[832,256]{1,0:T(8,128)S(1)} %copy-done.13, s32[]{:T(128)S(6)} %select_n.122, bf16[832,256]{1,0:T(8,128)(2,1)} %collective-permute-done.12, s32[]{:T(128)S(6)} %select_n.120), kind=kLoop, calls=%fused_computation.4 | loop fusion | flops 532480 | bytes 1916936 | tf_op jit(solution)/shard_map/convert_element_type | solution.py:68
  73.9 2.0 %collective-permute-start.15 = (bf16[272,256]{1,0:T(8,128)(2,1)}, bf16[272,256]{1,0:T(8,128)(2,1)S(1)}, u32[]{:S(2)}, u32[]{:S(2)}) collective-permute-start(bf16[272,256]{1,0:T(8,128)(2,1)} %copy-done.24), channel_id=1, source_target_pairs={{0,4},{1,5},{2,6},{3,7},{4,8},{5,9},{6,10},{7,11},{8,12},{9,13},{1... | collective-permute-start | bytes 417800 | tf_op jit(solution)/shard_map/ppermute | solution.py:40
  81.0 6.5 %collective-permute-done.13 = bf16[416,256]{1,0:T(8,128)(2,1)} collective-permute-done((bf16[416,256]{1,0:T(8,128)(2,1)}, bf16[416,256]{1,0:T(8,128)(2,1)}, u32[]{:S(2)}, u32[]{:S(2)}) %collective-permute-start.13) | collective-permute-done | bytes 213024 | tf_op jit(solution)/shard_map/ppermute | solution.py:50
  88.6 9.5 %collective-permute-done.23 = bf16[224,256]{1,0:T(8,128)(2,1)S(1)} collective-permute-done((bf16[224,256]{1,0:T(8,128)(2,1)S(1)}, bf16[224,256]{1,0:T(8,128)(2,1)S(1)}, u32[]{:S(2)}, u32[]{:S(2)}) %collective-permute-start.23) | collective-permute-done | bytes 114720 | tf_op jit(solution)/shard_map/ppermute | solution.py:50
  107.2 3.1 %collective-permute-done.18 = bf16[208,256]{1,0:T(8,128)(2,1)S(1)} collective-permute-done((bf16[208,256]{1,0:T(8,128)(2,1)S(1)}, bf16[208,256]{1,0:T(8,128)(2,1)S(1)}, u32[]{:S(2)}, u32[]{:S(2)}) %collective-permute-start.18) | collective-permute-done | bytes 106528 | tf_op jit(solution)/shard_map/ppermute | solution.py:50
  111.1 2.4 %collective-permute-done.25 = bf16[448,256]{1,0:T(8,128)(2,1)} collective-permute-done((bf16[448,256]{1,0:T(8,128)(2,1)}, bf16[448,256]{1,0:T(8,128)(2,1)}, u32[]{:S(2)}, u32[]{:S(2)}) %collective-permute-start.25) | collective-permute-done | bytes 229408 | tf_op jit(solution)/shard_map/ppermute | solution.py:50
  116.5 3.0 %collective-permute-done.19 = bf16[416,256]{1,0:T(8,128)(2,1)} collective-permute-done((bf16[416,256]{1,0:T(8,128)(2,1)}, bf16[416,256]{1,0:T(8,128)(2,1)}, u32[]{:S(2)}, u32[]{:S(2)}) %collective-permute-start.19) | collective-permute-done | bytes 213024 | tf_op jit(solution)/shard_map/ppermute | solution.py:50
  130.0 3.9 %backward_outer.1 = (bf16[2,8,64,256]{3,2,1,0:T(8,128)(2,1)}, f32[1,256]{1,0:T(1,128)}) custom-call(s32[20]{0:T(128)S(1)} %get-tuple-element.73.table, bf16[768,256]{1,0:T(8,128)(2,1)S(1)} %copy-done.5, bf16[272,256]{1,0:T(8,128)(2,1)S(1)} %copy-done.8, f32[1024,128]{1,0:T(8,128)S(1)} %copy-done.2, ...), custom_call_target="tpu_custom_call", output_to_operand_aliasing={{0}: (5, {})} | custom-call | flops 1024 | bytes 1024 | tf_op jit(solution)/shard_map/backward_outer/pallas_call | solution.py:600
  (112 shorter events, 49.0 us)
Async XLA Ops:
  1.7 6.7 %collective-permute-start = (bf16[272,256]{1,0:T(8,128)(2,1)S(1)}, bf16[272,256]{1,0:T(8,128)(2,1)S(1)}, u32[]{:S(2)}, u32[]{:S(2)}) collective-permute-start(bf16[272,256]{1,0:T(8,128)(2,1)S(1)} %rims.1.refs_0_), channel_id=1, source_target_pairs={{0,2},{1,3},{2,0},{3,1},{4,6},{5,7},{6,4},{7,5},{8,10},{9,11},{10,... | collective-permute-start | bytes 417800 | tf_op jit(solution)/shard_map/ppermute | solution.py:36
  4.8 15.7 %collective-permute-start.1 = (bf16[272,256]{1,0:T(8,128)(2,1)S(1)}, bf16[272,256]{1,0:T(8,128)(2,1)S(1)}, u32[]{:S(2)}, u32[]{:S(2)}) collective-permute-start(bf16[272,256]{1,0:T(8,128)(2,1)S(1)} %rims.1.refs_0_), channel_id=1, source_target_pairs={{0,1},{1,0},{2,3},{3,2},{4,5},{5,4},{6,7},{7,6},{8,9},{9,8},{10,11... | collective-permute-start | bytes 417800 | tf_op jit(solution)/shard_map/ppermute | solution.py:36
  8.4 12.0 %collective-permute-start.2 = (bf16[272,256]{1,0:T(8,128)(2,1)S(1)}, bf16[272,256]{1,0:T(8,128)(2,1)S(1)}, u32[]{:S(2)}, u32[]{:S(2)}) collective-permute-start(bf16[272,256]{1,0:T(8,128)(2,1)S(1)} %collective-permute-done.refs_1_), channel_id=1, source_target_pairs={{0,1},{1,0},{2,3},{3,2},{4,5},{5,4},{6,7},{7,6},{8,9},{9,8},{10,11... | collective-permute-start | bytes 417800 | tf_op jit(solution)/shard_map/ppermute | solution.py:36
  20.5 9.4 %collective-permute-start.7 = (bf16[768,256]{1,0:T(8,128)(2,1)S(1)}, bf16[768,256]{1,0:T(8,128)(2,1)S(1)}, u32[]{:S(2)}, u32[]{:S(2)}) collective-permute-start(bf16[768,256]{1,0:T(8,128)(2,1)S(1)} %get-tuple-element.90.grad), channel_id=1, source_target_pairs={{0,1},{1,0},{2,3},{3,2},{4,5},{5,4},{6,7},{7,6},{8,9},{9,8},{10,11... | collective-permute-start | bytes 1179656 | tf_op jit(solution)/shard_map/ppermute | solution.py:36
  23.3 9.6 %collective-permute-start.3 = (bf16[256,256]{1,0:T(8,128)(2,1)S(1)}, bf16[256,256]{1,0:T(8,128)(2,1)S(1)}, u32[]{:S(2)}, u32[]{:S(2)}) collective-permute-start(bf16[256,256]{1,0:T(8,128)(2,1)S(1)} %get-tuple-element.85), channel_id=1, source_target_pairs={{0,4},{1,5},{2,6},{3,7},{4,8},{5,9},{6,10},{7,11},{8,12},{9,13},{1... | collective-permute-start | bytes 393224 | tf_op jit(solution)/shard_map/ppermute | solution.py:40
  25.1 11.8 %collective-permute-start.4 = (bf16[256,256]{1,0:T(8,128)(2,1)S(1)}, bf16[256,256]{1,0:T(8,128)(2,1)S(1)}, u32[]{:S(2)}, u32[]{:S(2)}) collective-permute-start(bf16[256,256]{1,0:T(8,128)(2,1)S(1)} %get-tuple-element.86), channel_id=1, source_target_pairs={{0,8},{1,9},{2,10},{3,11},{4,12},{5,13},{6,14},{7,15},{8,0},{9,1},... | collective-permute-start | bytes 393224 | tf_op jit(solution)/shard_map/ppermute | solution.py:40
  27.7 9.2 %collective-permute-start.5 = (bf16[256,256]{1,0:T(8,128)(2,1)S(1)}, bf16[256,256]{1,0:T(8,128)(2,1)S(1)}, u32[]{:S(2)}, u32[]{:S(2)}) collective-permute-start(bf16[256,256]{1,0:T(8,128)(2,1)S(1)} %get-tuple-element.87), channel_id=1, source_target_pairs={{0,12},{1,13},{2,14},{3,15},{4,0},{5,1},{6,2},{7,3},{8,4},{9,5},{1... | collective-permute-start | bytes 393224 | tf_op jit(solution)/shard_map/ppermute | solution.py:40
  43.3 16.4 %collective-permute-start.21 = (bf16[896,256]{1,0:T(8,128)(2,1)}, bf16[896,256]{1,0:T(8,128)(2,1)}, u32[]{:S(2)}, u32[]{:S(2)}) collective-permute-start(bf16[896,256]{1,0:T(8,128)(2,1)} %get-tuple-element.121), channel_id=1, source_target_pairs={{0,2},{1,5},{2,0},{3,7},{4,6},{5,1},{6,4},{7,3},{8,10},{9,13},{10,... | collective-permute-start | bytes 1376264 | tf_op jit(solution)/shard_map/ppermute | solution.py:50
  47.7 24.0 %collective-permute-start.12 = (bf16[832,256]{1,0:T(8,128)(2,1)}, bf16[832,256]{1,0:T(8,128)(2,1)}, u32[]{:S(2)}, u32[]{:S(2)}) collective-permute-start(bf16[832,256]{1,0:T(8,128)(2,1)} %get-tuple-element.106), channel_id=1, source_target_pairs={{0,2},{1,5},{2,0},{3,7},{4,6},{5,1},{6,4},{7,3},{8,10},{9,13},{10,... | collective-permute-start | bytes 1277960 | tf_op jit(solution)/shard_map/ppermute | solution.py:50
  48.2 11.5 %collective-permute-start.10 = (bf16[272,256]{1,0:T(8,128)(2,1)S(1)}, bf16[272,256]{1,0:T(8,128)(2,1)}, u32[]{:S(2)}, u32[]{:S(2)}) collective-permute-start(bf16[272,256]{1,0:T(8,128)(2,1)S(1)} %get-tuple-element.98.parcel.refs_0_), channel_id=1, source_target_pairs={{0,2},{1,3},{2,0},{3,1},{4,6},{5,7},{6,4},{7,5},{8,10},{9,11},{10,... | collective-permute-start | bytes 417800 | tf_op jit(solution)/shard_map/ppermute | solution.py:36
  59.6 10.5 %collective-permute-start.11 = (bf16[272,256]{1,0:T(8,128)(2,1)}, bf16[272,256]{1,0:T(8,128)(2,1)}, u32[]{:S(2)}, u32[]{:S(2)}) collective-permute-start(bf16[272,256]{1,0:T(8,128)(2,1)} %collective-permute-done.10.refs_1_), channel_id=1, source_target_pairs={{0,1},{1,0},{2,3},{3,2},{4,5},{5,4},{6,7},{7,6},{8,9},{9,8},{10,11... | collective-permute-start | bytes 417800 | tf_op jit(solution)/shard_map/ppermute | solution.py:36
  61.9 16.7 %collective-permute-start.22 = (bf16[448,256]{1,0:T(8,128)(2,1)}, bf16[448,256]{1,0:T(8,128)(2,1)}, u32[]{:S(2)}, u32[]{:S(2)}) collective-permute-start(bf16[448,256]{1,0:T(8,128)(2,1)} %get-tuple-element.124), channel_id=1, source_target_pairs={{0,4},{1,3},{2,6},{3,1},{4,0},{5,7},{6,2},{7,5},{8,12},{9,11},{10,... | collective-permute-start | bytes 688136 | tf_op jit(solution)/shard_map/ppermute | solution.py:50
  73.8 13.6 %collective-permute-start.13 = (bf16[416,256]{1,0:T(8,128)(2,1)}, bf16[416,256]{1,0:T(8,128)(2,1)}, u32[]{:S(2)}, u32[]{:S(2)}) collective-permute-start(bf16[416,256]{1,0:T(8,128)(2,1)} %get-tuple-element.126), channel_id=1, source_target_pairs={{0,4},{1,3},{2,6},{3,1},{4,0},{5,7},{6,2},{7,5},{8,12},{9,11},{10,... | collective-permute-start | bytes 638984 | tf_op jit(solution)/shard_map/ppermute | solution.py:50
  73.9 28.0 %collective-permute-start.15 = (bf16[272,256]{1,0:T(8,128)(2,1)}, bf16[272,256]{1,0:T(8,128)(2,1)S(1)}, u32[]{:S(2)}, u32[]{:S(2)}) collective-permute-start(bf16[272,256]{1,0:T(8,128)(2,1)} %copy-done.24), channel_id=1, source_target_pairs={{0,4},{1,5},{2,6},{3,7},{4,8},{5,9},{6,10},{7,11},{8,12},{9,13},{1... | collective-permute-start | bytes 417800 | tf_op jit(solution)/shard_map/ppermute | solution.py:40
  75.9 26.7 %collective-permute-start.16 = (bf16[272,256]{1,0:T(8,128)(2,1)}, bf16[272,256]{1,0:T(8,128)(2,1)S(1)}, u32[]{:S(2)}, u32[]{:S(2)}) collective-permute-start(bf16[272,256]{1,0:T(8,128)(2,1)} %copy-done.23), channel_id=1, source_target_pairs={{0,8},{1,9},{2,10},{3,11},{4,12},{5,13},{6,14},{7,15},{8,0},{9,1},... | collective-permute-start | bytes 417800 | tf_op jit(solution)/shard_map/ppermute | solution.py:40
  77.5 25.7 %collective-permute-start.17 = (bf16[272,256]{1,0:T(8,128)(2,1)}, bf16[272,256]{1,0:T(8,128)(2,1)S(1)}, u32[]{:S(2)}, u32[]{:S(2)}) collective-permute-start(bf16[272,256]{1,0:T(8,128)(2,1)} %copy-done.22), channel_id=1, source_target_pairs={{0,12},{1,13},{2,14},{3,15},{4,0},{5,1},{6,2},{7,3},{8,4},{9,5},{1... | collective-permute-start | bytes 417800 | tf_op jit(solution)/shard_map/ppermute | solution.py:40
  79.6 18.5 %collective-permute-start.23 = (bf16[224,256]{1,0:T(8,128)(2,1)S(1)}, bf16[224,256]{1,0:T(8,128)(2,1)S(1)}, u32[]{:S(2)}, u32[]{:S(2)}) collective-permute-start(bf16[224,256]{1,0:T(8,128)(2,1)S(1)} %add_convert_fusion.3), channel_id=1, source_target_pairs={{0,8},{1,9},{2,10},{3,11},{4,12},{5,13},{6,14},{7,15},{8,0},{9,1},... | collective-permute-start | bytes 344072 | tf_op jit(solution)/shard_map/ppermute | solution.py:50
  88.5 12.4 %collective-permute-start.14 = (bf16[208,256]{1,0:T(8,128)(2,1)S(1)}, bf16[208,256]{1,0:T(8,128)(2,1)S(1)}, u32[]{:S(2)}, u32[]{:S(2)}) collective-permute-start(bf16[208,256]{1,0:T(8,128)(2,1)S(1)} %add_convert_fusion.5), channel_id=1, source_target_pairs={{0,8},{1,9},{2,10},{3,11},{4,12},{5,13},{6,14},{7,15},{8,0},{9,1},... | collective-permute-start | bytes 319496 | tf_op jit(solution)/shard_map/ppermute | solution.py:50
  99.1 7.3 %collective-permute-start.24 = (bf16[224,256]{1,0:T(8,128)(2,1)S(1)}, bf16[224,256]{1,0:T(8,128)(2,1)S(1)}, u32[]{:S(2)}, u32[]{:S(2)}) collective-permute-start(bf16[224,256]{1,0:T(8,128)(2,1)S(1)} %add_convert_fusion.2), channel_id=1, source_target_pairs={{0,8},{1,9},{2,10},{3,11},{4,12},{5,13},{6,14},{7,15},{8,0},{9,1},... | collective-permute-start | bytes 344072 | tf_op jit(solution)/shard_map/ppermute | solution.py:50
  111.1 8.4 %collective-permute-start.19 = (bf16[416,256]{1,0:T(8,128)(2,1)}, bf16[416,256]{1,0:T(8,128)(2,1)}, u32[]{:S(2)}, u32[]{:S(2)}) collective-permute-start(bf16[416,256]{1,0:T(8,128)(2,1)} %maximum_select_fusion.3), channel_id=1, source_target_pairs={{0,4},{1,3},{2,6},{3,1},{4,0},{5,7},{6,2},{7,5},{8,12},{9,11},{10,... | collective-permute-start | bytes 638984 | tf_op jit(solution)/shard_map/ppermute | solution.py:50
  114.9 8.5 %collective-permute-start.26 = (bf16[896,256]{1,0:T(8,128)(2,1)S(1)}, bf16[896,256]{1,0:T(8,128)(2,1)S(1)}, u32[]{:S(2)}, u32[]{:S(2)}) collective-permute-start(bf16[896,256]{1,0:T(8,128)(2,1)S(1)} %maximum_select_fusion), channel_id=1, source_target_pairs={{0,2},{1,5},{2,0},{3,7},{4,6},{5,1},{6,4},{7,3},{8,10},{9,13},{10,... | collective-permute-start | bytes 1376264 | tf_op jit(solution)/shard_map/ppermute | solution.py:50
  120.8 13.7 %collective-permute-start.20 = (bf16[832,256]{1,0:T(8,128)(2,1)S(1)}, bf16[832,256]{1,0:T(8,128)(2,1)S(1)}, u32[]{:S(2)}, u32[]{:S(2)}) collective-permute-start(bf16[832,256]{1,0:T(8,128)(2,1)S(1)} %maximum_select_fusion.1), channel_id=1, source_target_pairs={{0,2},{1,5},{2,0},{3,7},{4,6},{5,1},{6,4},{7,3},{8,10},{9,13},{10,... | collective-permute-start | bytes 1277960 | tf_op jit(solution)/shard_map/ppermute | solution.py:50
  122.4 15.3 %collective-permute-start.27 = (bf16[896,256]{1,0:T(8,128)(2,1)S(1)}, bf16[896,256]{1,0:T(8,128)(2,1)S(1)}, u32[]{:S(2)}, u32[]{:S(2)}) collective-permute-start(bf16[896,256]{1,0:T(8,128)(2,1)S(1)} %maximum_select_fusion), channel_id=1, source_target_pairs={{0,1},{1,0},{2,3},{3,2},{4,5},{5,4},{6,7},{7,6},{8,9},{9,8},{10,11... | collective-permute-start | bytes 1376264 | tf_op jit(solution)/shard_map/ppermute | solution.py:36
  123.5 14.3 %collective-permute-start.28 = (bf16[896,256]{1,0:T(8,128)(2,1)S(1)}, bf16[896,256]{1,0:T(8,128)(2,1)S(1)}, u32[]{:S(2)}, u32[]{:S(2)}) collective-permute-start(bf16[896,256]{1,0:T(8,128)(2,1)S(1)} %collective-permute-done.26), channel_id=1, source_target_pairs={{0,1},{1,0},{2,3},{3,2},{4,5},{5,4},{6,7},{7,6},{8,9},{9,8},{10,11... | collective-permute-start | bytes 1376264 | tf_op jit(solution)/shard_map/ppermute | solution.py:36
  (32 other events, 108.1 us)

commit v6 on v5

--- a/solution.py
+++ b/solution.py
@@ -7,7 +7,7 @@
 from jax.experimental.pallas import tpu as pltpu
 from jax.sharding import PartitionSpec as P
 
-VMEM_LIMIT = 16 * 1024 * 1024
+VMEM_LIMIT = 11 * 1024 * 1024
 EXTRA = 16
 
 
@@ -173,17 +173,14 @@
 
 def prepare_kernel(feats, voxmask, mask, rows, give, turned, planes, masks, done):
     half = feats.shape[3] // 2
-    copies = [
-        pltpu.make_async_copy(feats, planes, done.at[0]),
-        pltpu.make_async_copy(voxmask, masks, done.at[1]),
-    ]
-    for copy in copies:
-        copy.start()
+    pltpu.make_async_copy(voxmask, masks, done.at[8]).start()
+    for z in range(8):
+        pltpu.make_async_copy(feats.at[:, pl.ds(z, 1)], planes.at[:, pl.ds(z, 1)], done.at[z]).start()
     valid = windows((half, 128), 1)
-    for copy in copies:
-        copy.wait()
     first = lax.axis_index("zslab") % 2 == 0
+    pltpu.make_async_copy(voxmask, masks, done.at[8]).wait()
     for z in range(8):
+        pltpu.make_async_copy(feats.at[:, pl.ds(z, 1)], planes.at[:, pl.ds(z, 1)], done.at[z]).wait()
         span = slice(128 * z, 128 * z + 128)
         keep = mask_rows(masks, z)
         mask[span, :] = keep
@@ -211,7 +208,7 @@
         scratch_shapes=[
             pltpu.VMEM(feats.shape, jnp.bfloat16),
             pltpu.VMEM(voxmask.shape, jnp.int32),
-            pltpu.SemaphoreType.DMA((2,)),
+            pltpu.SemaphoreType.DMA((9,)),
         ],
         compiler_params=params(),
         cost_estimate=cost(1024, 1024),
@@ -241,21 +238,18 @@
     )(near(rows))
 
 
-def copy_picks(outer, table, parcels, picks):
+def copy_picks(outer, table, parcels, picks, planes):
+    for dev in range(4):
+        planes[256 * dev : 256 * dev + 256, :] = parcels[dev][:256, :]
     for steps in range(outer):
         for slot in range(4):
-            plane = table[steps * 4 + slot]
-            start = pl.ds(pl.multiple_of((plane % 4) * 64, 64), 64)
-            for dev in range(4):
-
-                @pl.when(plane // 4 == dev)
-                def _():
-                    picks[steps][64 * slot : 64 * slot + 64, :] = parcels[dev][start, :]
+            start = pl.multiple_of(table[steps * 4 + slot] * 64, 64)
+            picks[steps][64 * slot : 64 * slot + 64, :] = planes[pl.ds(start, 64), :]
 
 
 def route_kernel(outer, *refs):
     me = lax.axis_index("zslab")
-    parcels, (table, *picks), (codes, links, done) = refs[:4], refs[4:-3], refs[-3:]
+    parcels, (table, *picks), (codes, links, planes, done) = refs[:4], refs[4:-4], refs[-4:]
     for dev in range(4):
         row = parcels[dev][256:272, :128].astype(jnp.float32)
         codes[8 * dev : 8 * dev + 8, :] = row[:8, :].astype(jnp.int32)
@@ -279,7 +273,7 @@
             steps = lax.rem(me // 4 - dest // 8 + outer, outer)
             table[outer * 4 + 2 * side + brick] = jnp.where(dest >= 0, steps, -1)
 
-    copy_picks(outer, table, parcels, picks)
+    copy_picks(outer, table, parcels, picks, planes)
 
 
 def route(parcels, outer):
@@ -293,6 +287,7 @@
         scratch_shapes=[
             pltpu.VMEM((32, 128), jnp.int32),
             pltpu.SMEM((32, 128), jnp.int32),
+            pltpu.VMEM((1024, width), jnp.bfloat16),
             pltpu.SemaphoreType.DMA(()),
         ],
         compiler_params=params(),
@@ -303,8 +298,8 @@
 
 
 def repeat_kernel(outer, table, *refs):
-    parcels, picks = refs[:4], refs[4:]
-    copy_picks(outer, table, parcels, picks)
+    parcels, picks, planes = refs[:4], refs[4:-1], refs[-1]
+    copy_picks(outer, table, parcels, picks, planes)
     total = sum(read_extra(ref) for ref in parcels)
     for ref in picks:
         write_exact(total, ref)
@@ -317,6 +312,7 @@
         in_specs=[SCALARS] + [WHOLE] * 4,
         out_specs=[WHOLE] * outer,
         out_shape=[pltpu.VMEM((256 + EXTRA, width), jnp.bfloat16)] * outer,
+        scratch_shapes=[pltpu.VMEM((1024, width), jnp.bfloat16)],
         compiler_params=params(),
         cost_estimate=cost(1024, 1024),
         name="repeat_route",
@@ -331,13 +327,24 @@
     return plane
 
 
+def fetch_taps(weight, near_weight, done):
+    for tap in range(weight.shape[0]):
+        pltpu.make_async_copy(weight.at[tap], near_weight.at[tap], done.at[tap]).start()
+
+
+def await_taps(first, last, weight, near_weight, done):
+    for tap in range(first, last):
+        pltpu.make_async_copy(weight.at[tap], near_weight.at[tap], done.at[tap]).wait()
+
+
 def forward_kernel(rows, mask, weight, bias, cotangent, out, grad, edge, bias_sum, near_weight, ends, cols, pre, slopes, shift, done):
     width = rows.shape[1]
-    copies = [pltpu.make_async_copy(bias, shift, done.at[4])]
-    for a in (1, 0, 2):
-        taps = pl.ds(9 * a, 9)
-        copies.append(pltpu.make_async_copy(weight.at[taps], near_weight.at[taps], done.at[a]))
-    copies.append(pltpu.make_async_copy(cotangent, slopes, done.at[3]))
+    count = weight.shape[0]
+    copies = [pltpu.make_async_copy(bias, shift, done.at[count])]
+    for z in range(8):
+        part = pl.ds(z, 1)
+        copies.append(pltpu.make_async_copy(cotangent.at[:, part], slopes.at[:, part], done.at[count + 1 + z]))
+    fetch_taps(weight, near_weight, done)
     for copy in copies:
         copy.start()
     valid = windows((128, width), 0)
@@ -350,13 +357,14 @@
         return near_weight[9 * a : 9 * a + 9].reshape(9 * width, width)
 
     copies[0].wait()
-    copies[1].wait()
+    await_taps(9, 18, weight, near_weight, done)
     pre[...] = jnp.dot(cols[...], taps(1), preferred_element_type=jnp.float32) + shift[...]
-    copies[2].wait()
+    await_taps(0, 9, weight, near_weight, done)
     pre[128:, :] += jnp.dot(cols[:896, :], taps(0), preferred_element_type=jnp.float32)
-    copies[3].wait()
+    await_taps(18, 27, weight, near_weight, done)
     pre[:896, :] += jnp.dot(cols[128:, :], taps(2), preferred_element_type=jnp.float32)
-    copies[4].wait()
+    for copy in copies[1:]:
+        copy.wait()
     for side in range(2):
         edge[side] = pre[896 * side : 896 * side + 128, :]
         ends[side] = both(slopes, 7 * side)
@@ -390,7 +398,7 @@
             pltpu.VMEM((1024, width), jnp.float32),
             pltpu.VMEM(cotangent.shape, jnp.bfloat16),
             pltpu.VMEM((1, width), jnp.float32),
-            pltpu.SemaphoreType.DMA((5,)),
+            pltpu.SemaphoreType.DMA((weight.shape[0] + 9,)),
         ],
         compiler_params=params(),
         cost_estimate=cost(1024, 1024),
@@ -530,13 +538,15 @@
     )(*[near(x) for x in (mine, theirs, halos, their_halos, parcel, their_parcel, inner)])
 
 
-def backward_rows(planes, mask, weight, cols, place):
+def backward_rows(planes, mask, weight, cols, place, await_weight=None):
     width = weight.shape[1]
     valid = windows((128, width), 0)
     for index, plane in enumerate(planes):
         rows = slice(128 * (place + index), 128 * (place + index) + 128)
         for at, moved in enumerate(shifts(plane.astype(jnp.float32), 0, valid, -1)):
             cols[rows, at * width : (at + 1) * width] = moved
+    if await_weight:
+        await_weight()
     count = 128 * (len(planes) - 2)
     total = jnp.zeros((count, width), jnp.float32)
     for a in range(3):
@@ -575,7 +585,8 @@
 
 
 def backward_outer_kernel(table, grad, parcel, mask, weight, done, *refs):
-    arrived, (grad_feats, bias_sum, cols, planes, sent) = refs[:-5], refs[-5:]
+    arrived, (grad_feats, bias_sum, cols, planes, near_weight, fetched, sent) = refs[:-7], refs[-7:]
+    fetch_taps(weight, near_weight, fetched)
     for side in range(2):
         halo = jnp.concatenate([chosen(table, 2 * side + b, arrived) for b in range(2)], axis=0)
         rim = parcel[128 * side : 128 * side + 128, :]
@@ -584,7 +595,9 @@
         else:
             around = [grad[512:640, :], grad[640:768, :], rim, halo]
         first = 6 * side
-        rows = backward_rows(around, mask[128 * first : 128 * first + 256, :], weight, cols, 4 * side)
+        await_now = (lambda: await_taps(0, weight.shape[0], weight, near_weight, fetched)) if side == 0 else None
+        keep = mask[128 * first : 128 * first + 256, :]
+        rows = backward_rows(around, keep, near_weight, cols, 4 * side, await_now)
         for z in range(2):
             for b in range(2):
                 start = 128 * z + 64 * b
@@ -599,19 +612,21 @@
     width = grad.shape[1]
     return pl.pallas_call(
         backward_outer_kernel,
-        in_specs=[SCALARS] + [WHOLE] * 4 + [FAR] + [WHOLE] * len(arrived),
+        in_specs=[SCALARS] + [WHOLE] * 3 + [FAR, FAR] + [WHOLE] * len(arrived),
         out_specs=(FAR, WHOLE),
         out_shape=(jax.ShapeDtypeStruct(done.shape, done.dtype), jax.ShapeDtypeStruct((1, width), jnp.float32)),
         scratch_shapes=[
             pltpu.VMEM((1024, 9 * width), jnp.bfloat16),
             pltpu.VMEM((2, 2, 2, 64, width), jnp.bfloat16),
+            pltpu.VMEM(weight.shape, jnp.bfloat16),
+            pltpu.SemaphoreType.DMA((weight.shape[0],)),
             pltpu.SemaphoreType.DMA((2,)),
         ],
         input_output_aliases={5: 0},
         compiler_params=params(),
         cost_estimate=cost(1024, 1024),
         name="backward_outer",
-    )(table, near(grad), near(parcel), near(mask), near(weight), done, *[near(x) for x in arrived])
+    )(table, near(grad), near(parcel), near(mask), far(weight), done, *[near(x) for x in arrived])
 
 
 def assemble_kernel(first, size, *refs):
@@ -645,19 +660,18 @@
     )(*[near(x) for x in parts], *given)
 
 
-def gather_group(parcel, size):
-    inner = swap(parcel, size, 2)
-    return [parcel, inner, swap(parcel, size, 1), swap(inner, size, 1)]
+def gather_group(parcel, size, before=()):
+    inner, *before = lax.optimization_barrier((swap(parcel, size, 2), *before))
+    return [parcel, inner, swap(parcel, size, 1), swap(inner, size, 1)], *before
 
 
 def per_device(size, feats, voxmask, links, weight, bias, cotangent):
     width = feats.shape[3]
     outer = size // 4
 
-    parcels = gather_group(rims(links, feats, voxmask), size)
     mask, rows, give, turned = prepare(feats, voxmask)
-    rows, parcels[1] = lax.optimization_barrier((rows, parcels[1]))
-    out, grad, edge, bias_local, weight, ends = forward_inside(rows, mask, weight, bias.reshape(1, width), cotangent)
+    parcels, rows = gather_group(rims(links, feats, voxmask), size, (rows,))
+    out, grad, edge, bias_local, taps, ends = forward_inside(rows, mask, weight, bias.reshape(1, width), cotangent)
     *parcels, grad = lax.optimization_barrier((*parcels, grad))
     table, picks = route(parcels, outer)
 
@@ -666,24 +680,24 @@
     their_turned = turn(swap(give, size, 1))
     inner = inner_terms(turned, their_turned, grad, swap(grad, size, 1))
 
-    *arrived, inner = lax.optimization_barrier((*arrived, inner))
-    out, parcel, halos, give = forward_edges(table, mask, weight, edge, ends, bias_local, out, arrived)
+    grad_feats = backward_inner(grad, mask, taps)
+    *arrived, inner, grad_feats = lax.optimization_barrier((*arrived, inner, grad_feats))
+    out, parcel, halos, give = forward_edges(table, mask, taps, edge, ends, bias_local, out, arrived)
     their_halos = swap(give, size, 1)
-    parcels = gather_group(parcel, size)
+    parcels, halos = gather_group(parcel, size, (halos,))
 
     stages = len(orders(size)[0])
     halves = [stage_half(size, stage) for stage in range(stages)]
     count = weight.shape[0]
     cuts = [(0, count // 2), (count // 2, count)]
     sums = []
-    for taps in cuts:
-        give, stay = outer_terms(taps, size, turned, their_turned, halos, their_halos, parcel, parcels[2], inner)
+    for cut in cuts:
+        give, stay = outer_terms(cut, size, turned, their_turned, halos, their_halos, parcel, parcels[2], inner)
         sums.append((stay, swap_stage(give, size, 0)))
 
-    grad_feats = backward_inner(grad, mask, weight)
     picks = repeat_route(table, parcels, outer)
     (stay, got), other = sums
-    stay, grad_feats, *picks = lax.optimization_barrier((stay, grad_feats, *picks))
+    stay, *picks = lax.optimization_barrier((stay, *picks))
     sums = [(stay, got), other]
     arrived = [rotate(pick, size, steps) if steps else pick for steps, pick in enumerate(picks)]
     for stage in range(1, stages):
@@ -697,13 +711,13 @@
     grad_feats, grad_bias = backward_outer(table, grad, parcel, mask, weight, grad_feats, arrived)
 
     grad_weight = None
-    for taps, part in zip(cuts, parts):
+    for cut, part in zip(cuts, parts):
         last = swap_stage(part, size, 0)
         other = swap(part, size, 1)
         if grad_weight is None:
             last, grad_feats, grad_bias = lax.optimization_barrier((last, grad_feats, grad_bias))
-        pieces = [x.reshape(taps[1] - taps[0], width // 4, width) for x in (part, last, other, swap(last, size, 1))]
-        grad_weight = assemble(taps[0], size, pieces, (count, 4, width // 4, width), grad_weight)
+        pieces = [x.reshape(cut[1] - cut[0], width // 4, width) for x in (part, last, other, swap(last, size, 1))]
+        grad_weight = assemble(cut[0], size, pieces, (count, 4, width // 4, width), grad_weight)
     return out, grad_feats, grad_weight.reshape(count, width, width), grad_bias.reshape(width)
 
 

time: 140 us -> 123 us (0.88)
  local copies, waits for them, and re-layouts: 12.4 us -> 0.01 us
  waiting for transfers between devices: 49.1 us -> 44.3 us
  other arithmetic: 12.8 us -> 8.43 us
  starting transfers between devices: 28.1 us -> 31.2 us
  Pallas kernels: 35.5 us -> 37.7 us
    unnamed x50 -> x2, local copies, waits for them, and re-layouts: 12.4 us -> 0.01 us
    ppermute x13, waiting for transfers between devices: 16.5 us -> 5.56 us  [swap(): return lax.ppermute(x, 'zslab', [(i, i ^ bit) for i in range(size)])]
    ppermute x12, waiting for transfers between devices: 28.6 us -> 37.9 us  [swap_stage(): lax.ppermute(x, 'zslab', [(i, i ^ both[i % 2][stage]) for i in range(size)])]
    select_n x4, other arithmetic: 4.3 us -> 0.53 us  [join(): jnp.where(mine == 0, jnp.concatenate([part, got]), jnp.concatenate([got,...]
    ppermute x6, waiting for transfers between devices: 4.11 us -> 0.87 us  [rotate(): lax.ppermute(x, 'zslab', [(i, (i + 4 * steps) % size) for i in range(size)])]
    ppermute x12, starting transfers between devices: 11.3 us -> 14 us  [swap_stage(): lax.ppermute(x, 'zslab', [(i, i ^ both[i % 2][stage]) for i in range(size)])]
    pallas_call x1, Pallas kernels: 3.92 us -> 6.13 us  [backward_outer(): pl.pallas_call(backward_outer_kernel, in_specs=[SCALARS] + [WHOLE] * 3 +...]
  transfers between devices with their start and end apart: 31 -> 31, of which waited for: 14 -> 13; matrix products, arithmetic and copies ran while one was open for 9% -> 7% of each run, Pallas kernels for 21% -> 26%
where the time goes in v6:
time: 123 us
  waiting for transfers between devices  44.3 us (36%)
  Pallas kernels  37.7 us (31%)
  starting transfers between devices  31.2 us (25%)
  other arithmetic  8.43 us (7%)
    ppermute x12, waiting for transfers between devices, swap_stage(): lax.ppermute(x, 'zslab', [(i, i ^ both[i % 2][stage]) for i in range(size)])  37.9 us
    ppermute x12, starting transfers between devices, swap_stage(): lax.ppermute(x, 'zslab', [(i, i ^ both[i % 2][stage]) for i in range(size)])  14 us
    ppermute x6, starting transfers between devices, rotate(): lax.ppermute(x, 'zslab', [(i, (i + 4 * steps) % size) for i in range(size)])  10.1 us
    pallas_call x1, Pallas kernels, forward_inside(): pl.pallas_call(forward_kernel, in_specs=[WHOLE, WHOLE, FAR, FAR, FAR], ou...  9.36 us
    ppermute x13, starting transfers between devices, swap(): return lax.ppermute(x, 'zslab', [(i, i ^ bit) for i in range(size)])  7.17 us
    pallas_call x1, Pallas kernels, backward_outer(): pl.pallas_call(backward_outer_kernel, in_specs=[SCALARS] + [WHOLE] * 3 +...  6.13 us
    convert_element_type x4, other arithmetic, halve(): return (give.astype(jnp.bfloat16), keep)  5.98 us
    ppermute x13, waiting for transfers between devices, swap(): return lax.ppermute(x, 'zslab', [(i, i ^ bit) for i in range(size)])  5.56 us
  transfers between devices with their start and end apart: 31, of which 13 were waited for; matrix products, arithmetic and copies ran while one was open for 7% of the time, Pallas kernels for 26%

profile of v6, /device:TPU:0, one launch (start us, length us, event | category | flops | bytes accessed | tf_op | source)
XLA Modules:
  0.0 122.8 jit_solution(2663267123605686042)
XLA Ops:
  1.7 3.0 %collective-permute-start = (bf16[272,256]{1,0:T(8,128)(2,1)S(1)}, bf16[272,256]{1,0:T(8,128)(2,1)S(1)}, u32[]{:S(2)}, u32[]{:S(2)}) collective-permute-start(bf16[272,256]{1,0:T(8,128)(2,1)S(1)} %rims.1.refs_0_), channel_id=1, source_target_pairs={{0,2},{1,3},{2,0},{3,1},{4,6},{5,7},{6,4},{7,5},{8,10},{9,11},{10,... | collective-permute-start | bytes 417800 | tf_op jit(solution)/shard_map/ppermute | solution.py:36
  4.8 3.9 %prepare.1 = (f32[1024,128]{1,0:T(8,128)S(1)}, bf16[1024,256]{1,0:T(8,128)(2,1)S(1)}, bf16[1024,128]{1,0:T(8,128)(2,1)S(1)}, bf16[1152,1024]{1,0:T(8,128)(2,1)S(1)}) custom-call(bf16[2,8,64,256]{3,2,1,0:T(8,128)(2,1)} %feats.3, s32[2,512]{1,0:T(2,128)} %voxmask.3), custom_call_target="tpu_custom_call" | custom-call | flops 1024 | bytes 1024 | tf_op jit(solution)/shard_map/prepare/pallas_call | solution.py:198
  9.2 9.4 %forward_inside.1 = (bf16[2,8,64,256]{3,2,1,0:T(8,128)(2,1)}, bf16[768,256]{1,0:T(8,128)(2,1)S(1)}, f32[2,128,256]{2,1,0:T(8,128)S(1)}, f32[1,256]{1,0:T(1,128)S...) custom-call(bf16[1024,256]{1,0:T(8,128)(2,1)S(1)} %get-tuple-element.68.rows, ...), custom_call_target="tpu_custom_call" | custom-call | flops 1024 | bytes 1024 | tf_op jit(solution)/shard_map/forward_inside/pallas_call | solution.py:384
  22.5 2.6 %collective-permute-start.4 = (bf16[256,256]{1,0:T(8,128)(2,1)S(1)}, bf16[256,256]{1,0:T(8,128)(2,1)S(1)}, u32[]{:S(2)}, u32[]{:S(2)}) collective-permute-start(bf16[256,256]{1,0:T(8,128)(2,1)S(1)} %get-tuple-element.88), channel_id=1, source_target_pairs={{0,8},{1,9},{2,10},{3,11},{4,12},{5,13},{6,14},{7,15},{8,0},{9,1},... | collective-permute-start | bytes 393224 | tf_op jit(solution)/shard_map/ppermute | solution.py:40
  26.5 2.9 %backward_inner.1.done = bf16[2,8,64,256]{3,2,1,0:T(8,128)(2,1)} custom-call(bf16[768,256]{1,0:T(8,128)(2,1)S(1)} %get-tuple-element.92.grad, f32[1024,128]{1,0:T(8,128)S(1)} %get-tuple-element.69.mask, bf16[27,256,256]{2,1,0:T(8,128)(2,1)S(1)} %get-tuple-element.76.weight), custom_call_target="tpu_custom_call" | custom-call | flops 1024 | bytes 1024 | tf_op jit(solution)/shard_map/backward_inner/pallas_call | solution.py:575
  30.2 2.9 %inner_terms.1.inner = f32[3456,256]{1,0:T(8,128)S(1)} custom-call(bf16[1152,1024]{1,0:T(8,128)(2,1)S(1)} %get-tuple-element.90.mine, bf16[1152,1024]{1,0:T(8,128)(2,1)S(1)} %turn.1.theirs, bf16[768,256]{1,0:T(8,128)(2,1)S(1)} %get-tuple-element.92.grad, bf16[768,256]{1,0:T(8,128)(2,1)S(1)} %collective-permute-done.7.their_grad), custom_call_target="tpu_custom_call" | custom-call | flops 1024 | bytes 1024 | tf_op jit(solution)/shard_map/inner_terms/pallas_call | solution.py:420
  34.0 2.0 %forward_edges.1 = (bf16[2,8,64,256]{3,2,1,0:T(8,128)(2,1)}, bf16[272,256]{1,0:T(8,128)(2,1)S(1)}, bf16[256,128]{1,0:T(8,128)(2,1)S(1)}, bf16[256,128]{1,0:T(8,128)(2,1)S(1)}) custom-call(s32[20]{0:T(128)S(1)} %get-tuple-element.75.table, f32[1024,128]{1,0:T(8,128)S(1)} %get-tuple-element.69.mask, ...), custom_call_target="tpu_custom_call", output_to_operand_aliasing={{0}: (6, {})} | custom-call | flops 1024 | bytes 1024 | tf_op jit(solution)/shard_map/forward_edges/pallas_call | solution.py:461
  37.9 3.6 %collective-permute-done.8.refs_1_ = bf16[272,256]{1,0:T(8,128)(2,1)S(1)} collective-permute-done((bf16[272,256]{1,0:T(8,128)(2,1)S(1)}, bf16[272,256]{1,0:T(8,128)(2,1)S(1)}, u32[]{:S(2)}, u32[]{:S(2)}) %collective-permute-start.8) | collective-permute-done | bytes 139296 | tf_op jit(solution)/shard_map/ppermute | solution.py:36
  41.5 1.9 %outer_terms.3 = (bf16[896,256]{1,0:T(8,128)(2,1)}, f32[896,256]{1,0:T(8,128)S(1)}) custom-call(bf16[1152,1024]{1,0:T(8,128)(2,1)S(1)} %get-tuple-element.90.mine, bf16[1152,1024]{1,0:T(8,128)(2,1)S(1)} %turn.1.theirs, bf16[256,128]{1,0:T(8,128)(2,1)S(1)} %get-tuple-element.100.halos, bf16[256,128]{1,0:T(8,128)(2,1)S(1)} %collective-permute-done.9.their_halos, ...), custom_call_target="tpu_custom_call" | custom-call | flops 1024 | bytes 1024 | tf_op jit(solution)/shard_map/outer_terms/pallas_call | solution.py:526
  44.9 1.9 %outer_terms.2 = (bf16[832,256]{1,0:T(8,128)(2,1)}, f32[832,256]{1,0:T(8,128)S(1)}) custom-call(bf16[1152,1024]{1,0:T(8,128)(2,1)S(1)} %get-tuple-element.90.mine, bf16[1152,1024]{1,0:T(8,128)(2,1)S(1)} %turn.1.theirs, bf16[256,128]{1,0:T(8,128)(2,1)S(1)} %get-tuple-element.100.halos, bf16[256,128]{1,0:T(8,128)(2,1)S(1)} %collective-permute-done.9.their_halos, ...), custom_call_target="tpu_custom_call" | custom-call | flops 1024 | bytes 1024 | tf_op jit(solution)/shard_map/outer_terms/pallas_call | solution.py:526
  47.7 4.6 %collective-permute-done.21 = bf16[896,256]{1,0:T(8,128)(2,1)} collective-permute-done((bf16[896,256]{1,0:T(8,128)(2,1)}, bf16[896,256]{1,0:T(8,128)(2,1)}, u32[]{:S(2)}, u32[]{:S(2)}) %collective-permute-start.21) | collective-permute-done | bytes 458784 | tf_op jit(solution)/shard_map/ppermute | solution.py:50
  52.3 2.0 %add_convert_fusion = (bf16[448,256]{1,0:T(8,128)(2,1)}, f32[448,256]{1,0:T(8,128)}) fusion(f32[896,256]{1,0:T(8,128)S(1)} %get-tuple-element.124, s32[]{:T(128)S(6)} %select_n.130, bf16[896,256]{1,0:T(8,128)(2,1)} %collective-permute-done.21, s32[]{:T(128)S(6)} %select_n.128), kind=kLoop, calls=%fused_computation.1 | loop fusion | flops 573440 | bytes 2064392 | tf_op jit(solution)/shard_map/convert_element_type | solution.py:68
  54.3 3.4 %collective-permute-start.22 = (bf16[448,256]{1,0:T(8,128)(2,1)}, bf16[448,256]{1,0:T(8,128)(2,1)}, u32[]{:S(2)}, u32[]{:S(2)}) collective-permute-start(bf16[448,256]{1,0:T(8,128)(2,1)} %get-tuple-element.128), channel_id=1, source_target_pairs={{0,4},{1,3},{2,6},{3,1},{4,0},{5,7},{6,2},{7,5},{8,12},{9,11},{10,... | collective-permute-start | bytes 688136 | tf_op jit(solution)/shard_map/ppermute | solution.py:50
  58.3 2.0 %add_convert_fusion.1 = (bf16[416,256]{1,0:T(8,128)(2,1)}, f32[416,256]{1,0:T(8,128)}) fusion(f32[832,256]{1,0:T(8,128)S(1)} %get-tuple-element.109, s32[]{:T(128)S(6)} %select_n.122, bf16[832,256]{1,0:T(8,128)(2,1)} %collective-permute-done.12, s32[]{:T(128)S(6)} %select_n.120), kind=kLoop, calls=%fused_computation.4 | loop fusion | flops 532480 | bytes 1916936 | tf_op jit(solution)/shard_map/convert_element_type | solution.py:68
  60.3 3.2 %collective-permute-start.13 = (bf16[416,256]{1,0:T(8,128)(2,1)}, bf16[416,256]{1,0:T(8,128)(2,1)S(1)}, u32[]{:S(2)}, u32[]{:S(2)}) collective-permute-start(bf16[416,256]{1,0:T(8,128)(2,1)} %get-tuple-element.130), channel_id=1, source_target_pairs={{0,4},{1,3},{2,6},{3,1},{4,0},{5,7},{6,2},{7,5},{8,12},{9,11},{10,... | collective-permute-start | bytes 638984 | tf_op jit(solution)/shard_map/ppermute | solution.py:50
  65.1 2.9 %collective-permute-start.17 = (bf16[272,256]{1,0:T(8,128)(2,1)S(1)}, bf16[272,256]{1,0:T(8,128)(2,1)S(1)}, u32[]{:S(2)}, u32[]{:S(2)}) collective-permute-start(bf16[272,256]{1,0:T(8,128)(2,1)S(1)} %get-tuple-element.114), channel_id=1, source_target_pairs={{0,12},{1,13},{2,14},{3,15},{4,0},{5,1},{6,2},{7,3},{8,4},{9,5},{1... | collective-permute-start | bytes 417800 | tf_op jit(solution)/shard_map/ppermute | solution.py:40
  70.4 3.6 %collective-permute-done.13 = bf16[416,256]{1,0:T(8,128)(2,1)S(1)} collective-permute-done((bf16[416,256]{1,0:T(8,128)(2,1)}, bf16[416,256]{1,0:T(8,128)(2,1)S(1)}, u32[]{:S(2)}, u32[]{:S(2)}) %collective-permute-start.13) | collective-permute-done | bytes 213024 | tf_op jit(solution)/shard_map/ppermute | solution.py:50
  75.1 10.5 %collective-permute-done.23 = bf16[224,256]{1,0:T(8,128)(2,1)S(1)} collective-permute-done((bf16[224,256]{1,0:T(8,128)(2,1)S(1)}, bf16[224,256]{1,0:T(8,128)(2,1)S(1)}, u32[]{:S(2)}, u32[]{:S(2)}) %collective-permute-start.23) | collective-permute-done | bytes 114720 | tf_op jit(solution)/shard_map/ppermute | solution.py:50
  88.0 2.6 %collective-permute-start.18 = (bf16[208,256]{1,0:T(8,128)(2,1)S(1)}, bf16[208,256]{1,0:T(8,128)(2,1)S(1)}, u32[]{:S(2)}, u32[]{:S(2)}) collective-permute-start(bf16[208,256]{1,0:T(8,128)(2,1)S(1)} %add_convert_fusion.4), channel_id=1, source_target_pairs={{0,8},{1,9},{2,10},{3,11},{4,12},{5,13},{6,14},{7,15},{8,0},{9,1},... | collective-permute-start | bytes 319496 | tf_op jit(solution)/shard_map/ppermute | solution.py:50
  90.6 3.8 %collective-permute-done.24 = bf16[224,256]{1,0:T(8,128)(2,1)S(1)} collective-permute-done((bf16[224,256]{1,0:T(8,128)(2,1)S(1)}, bf16[224,256]{1,0:T(8,128)(2,1)S(1)}, u32[]{:S(2)}, u32[]{:S(2)}) %collective-permute-start.24) | collective-permute-done | bytes 114720 | tf_op jit(solution)/shard_map/ppermute | solution.py:50
  96.7 5.9 %collective-permute-done.25 = bf16[448,256]{1,0:T(8,128)(2,1)S(1)} collective-permute-done((bf16[448,256]{1,0:T(8,128)(2,1)S(1)}, bf16[448,256]{1,0:T(8,128)(2,1)S(1)}, u32[]{:S(2)}, u32[]{:S(2)}) %collective-permute-start.25) | collective-permute-done | bytes 229408 | tf_op jit(solution)/shard_map/ppermute | solution.py:50
  102.9 4.3 %collective-permute-done.19 = bf16[416,256]{1,0:T(8,128)(2,1)S(1)} collective-permute-done((bf16[416,256]{1,0:T(8,128)(2,1)S(1)}, bf16[416,256]{1,0:T(8,128)(2,1)S(1)}, u32[]{:S(2)}, u32[]{:S(2)}) %collective-permute-start.19) | collective-permute-done | bytes 213024 | tf_op jit(solution)/shard_map/ppermute | solution.py:50
  107.5 3.8 %collective-permute-done.26 = bf16[896,256]{1,0:T(8,128)(2,1)S(1)} collective-permute-done((bf16[896,256]{1,0:T(8,128)(2,1)S(1)}, bf16[896,256]{1,0:T(8,128)(2,1)S(1)}, u32[]{:S(2)}, u32[]{:S(2)}) %collective-permute-start.26) | collective-permute-done | bytes 458784 | tf_op jit(solution)/shard_map/ppermute | solution.py:50
  111.3 6.1 %backward_outer.1 = (bf16[2,8,64,256]{3,2,1,0:T(8,128)(2,1)}, f32[1,256]{1,0:T(1,128)}) custom-call(s32[20]{0:T(128)S(1)} %get-tuple-element.75.table, bf16[768,256]{1,0:T(8,128)(2,1)S(1)} %get-tuple-element.92.grad, bf16[272,256]{1,0:T(8,128)(2,1)S(1)} %get-tuple-element.98.parcel.refs_0_, ...), custom_call_target="tpu_custom_call", output_to_operand_aliasing={{0}: (5, {})} | custom-call | flops 1024 | bytes 1024 | tf_op jit(solution)/shard_map/backward_outer/pallas_call | solution.py:613
  (64 shorter events, 28.9 us)
Async XLA Ops:
  4.8 13.8 %collective-permute-start.1 = (bf16[272,256]{1,0:T(8,128)(2,1)S(1)}, bf16[272,256]{1,0:T(8,128)(2,1)S(1)}, u32[]{:S(2)}, u32[]{:S(2)}) collective-permute-start(bf16[272,256]{1,0:T(8,128)(2,1)S(1)} %rims.1.refs_0_), channel_id=1, source_target_pairs={{0,1},{1,0},{2,3},{3,2},{4,5},{5,4},{6,7},{7,6},{8,9},{9,8},{10,11... | collective-permute-start | bytes 417800 | tf_op jit(solution)/shard_map/ppermute | solution.py:36
  8.7 10.0 %collective-permute-start.2 = (bf16[272,256]{1,0:T(8,128)(2,1)S(1)}, bf16[272,256]{1,0:T(8,128)(2,1)S(1)}, u32[]{:S(2)}, u32[]{:S(2)}) collective-permute-start(bf16[272,256]{1,0:T(8,128)(2,1)S(1)} %collective-permute-done.refs_1_), channel_id=1, source_target_pairs={{0,1},{1,0},{2,3},{3,2},{4,5},{5,4},{6,7},{7,6},{8,9},{9,8},{10,11... | collective-permute-start | bytes 417800 | tf_op jit(solution)/shard_map/ppermute | solution.py:36
  18.6 11.6 %collective-permute-start.7 = (bf16[768,256]{1,0:T(8,128)(2,1)S(1)}, bf16[768,256]{1,0:T(8,128)(2,1)S(1)}, u32[]{:S(2)}, u32[]{:S(2)}) collective-permute-start(bf16[768,256]{1,0:T(8,128)(2,1)S(1)} %get-tuple-element.92.grad), channel_id=1, source_target_pairs={{0,1},{1,0},{2,3},{3,2},{4,5},{5,4},{6,7},{7,6},{8,9},{9,8},{10,11... | collective-permute-start | bytes 1179656 | tf_op jit(solution)/shard_map/ppermute | solution.py:36
  20.4 9.0 %collective-permute-start.6 = (bf16[1024,128]{1,0:T(8,128)(2,1)S(1)}, bf16[1024,128]{1,0:T(8,128)(2,1)S(1)}, u32[]{:S(2)}, u32[]{:S(2)}) collective-permute-start(bf16[1024,128]{1,0:T(8,128)(2,1)S(1)} %get-tuple-element.91), channel_id=1, source_target_pairs={{0,1},{1,0},{2,3},{3,2},{4,5},{5,4},{6,7},{7,6},{8,9},{9,8},{10,11... | collective-permute-start | bytes 786440 | tf_op jit(solution)/shard_map/ppermute | solution.py:36
  21.0 12.2 %collective-permute-start.3 = (bf16[256,256]{1,0:T(8,128)(2,1)S(1)}, bf16[256,256]{1,0:T(8,128)(2,1)S(1)}, u32[]{:S(2)}, u32[]{:S(2)}) collective-permute-start(bf16[256,256]{1,0:T(8,128)(2,1)S(1)} %get-tuple-element.87), channel_id=1, source_target_pairs={{0,4},{1,5},{2,6},{3,7},{4,8},{5,9},{6,10},{7,11},{8,12},{9,13},{1... | collective-permute-start | bytes 393224 | tf_op jit(solution)/shard_map/ppermute | solution.py:40
  22.5 11.5 %collective-permute-start.4 = (bf16[256,256]{1,0:T(8,128)(2,1)S(1)}, bf16[256,256]{1,0:T(8,128)(2,1)S(1)}, u32[]{:S(2)}, u32[]{:S(2)}) collective-permute-start(bf16[256,256]{1,0:T(8,128)(2,1)S(1)} %get-tuple-element.88), channel_id=1, source_target_pairs={{0,8},{1,9},{2,10},{3,11},{4,12},{5,13},{6,14},{7,15},{8,0},{9,1},... | collective-permute-start | bytes 393224 | tf_op jit(solution)/shard_map/ppermute | solution.py:40
  25.1 8.9 %collective-permute-start.5 = (bf16[256,256]{1,0:T(8,128)(2,1)S(1)}, bf16[256,256]{1,0:T(8,128)(2,1)S(1)}, u32[]{:S(2)}, u32[]{:S(2)}) collective-permute-start(bf16[256,256]{1,0:T(8,128)(2,1)S(1)} %get-tuple-element.89), channel_id=1, source_target_pairs={{0,12},{1,13},{2,14},{3,15},{4,0},{5,1},{6,2},{7,3},{8,4},{9,5},{1... | collective-permute-start | bytes 393224 | tf_op jit(solution)/shard_map/ppermute | solution.py:40
  43.5 8.8 %collective-permute-start.21 = (bf16[896,256]{1,0:T(8,128)(2,1)}, bf16[896,256]{1,0:T(8,128)(2,1)}, u32[]{:S(2)}, u32[]{:S(2)}) collective-permute-start(bf16[896,256]{1,0:T(8,128)(2,1)} %get-tuple-element.125), channel_id=1, source_target_pairs={{0,2},{1,5},{2,0},{3,7},{4,6},{5,1},{6,4},{7,3},{8,10},{9,13},{10,... | collective-permute-start | bytes 1376264 | tf_op jit(solution)/shard_map/ppermute | solution.py:50
  46.8 11.5 %collective-permute-start.12 = (bf16[832,256]{1,0:T(8,128)(2,1)}, bf16[832,256]{1,0:T(8,128)(2,1)}, u32[]{:S(2)}, u32[]{:S(2)}) collective-permute-start(bf16[832,256]{1,0:T(8,128)(2,1)} %get-tuple-element.110), channel_id=1, source_target_pairs={{0,2},{1,5},{2,0},{3,7},{4,6},{5,1},{6,4},{7,3},{8,10},{9,13},{10,... | collective-permute-start | bytes 1277960 | tf_op jit(solution)/shard_map/ppermute | solution.py:50
  47.4 10.2 %collective-permute-start.11 = (bf16[272,256]{1,0:T(8,128)(2,1)S(1)}, bf16[272,256]{1,0:T(8,128)(2,1)S(1)}, u32[]{:S(2)}, u32[]{:S(2)}) collective-permute-start(bf16[272,256]{1,0:T(8,128)(2,1)S(1)} %collective-permute-done.8.refs_1_), channel_id=1, source_target_pairs={{0,1},{1,0},{2,3},{3,2},{4,5},{5,4},{6,7},{7,6},{8,9},{9,8},{10,11... | collective-permute-start | bytes 417800 | tf_op jit(solution)/shard_map/ppermute | solution.py:36
  54.3 13.8 %collective-permute-start.22 = (bf16[448,256]{1,0:T(8,128)(2,1)}, bf16[448,256]{1,0:T(8,128)(2,1)}, u32[]{:S(2)}, u32[]{:S(2)}) collective-permute-start(bf16[448,256]{1,0:T(8,128)(2,1)} %get-tuple-element.128), channel_id=1, source_target_pairs={{0,4},{1,3},{2,6},{3,1},{4,0},{5,7},{6,2},{7,5},{8,12},{9,11},{10,... | collective-permute-start | bytes 688136 | tf_op jit(solution)/shard_map/ppermute | solution.py:50
  60.3 13.8 %collective-permute-start.13 = (bf16[416,256]{1,0:T(8,128)(2,1)}, bf16[416,256]{1,0:T(8,128)(2,1)S(1)}, u32[]{:S(2)}, u32[]{:S(2)}) collective-permute-start(bf16[416,256]{1,0:T(8,128)(2,1)} %get-tuple-element.130), channel_id=1, source_target_pairs={{0,4},{1,3},{2,6},{3,1},{4,0},{5,7},{6,2},{7,5},{8,12},{9,11},{10,... | collective-permute-start | bytes 638984 | tf_op jit(solution)/shard_map/ppermute | solution.py:50
  63.5 24.5 %collective-permute-start.15 = (bf16[272,256]{1,0:T(8,128)(2,1)S(1)}, bf16[272,256]{1,0:T(8,128)(2,1)S(1)}, u32[]{:S(2)}, u32[]{:S(2)}) collective-permute-start(bf16[272,256]{1,0:T(8,128)(2,1)S(1)} %get-tuple-element.112), channel_id=1, source_target_pairs={{0,4},{1,5},{2,6},{3,7},{4,8},{5,9},{6,10},{7,11},{8,12},{9,13},{1... | collective-permute-start | bytes 417800 | tf_op jit(solution)/shard_map/ppermute | solution.py:40
  63.5 24.5 %collective-permute-start.16 = (bf16[272,256]{1,0:T(8,128)(2,1)S(1)}, bf16[272,256]{1,0:T(8,128)(2,1)S(1)}, u32[]{:S(2)}, u32[]{:S(2)}) collective-permute-start(bf16[272,256]{1,0:T(8,128)(2,1)S(1)} %get-tuple-element.113), channel_id=1, source_target_pairs={{0,8},{1,9},{2,10},{3,11},{4,12},{5,13},{6,14},{7,15},{8,0},{9,1},... | collective-permute-start | bytes 417800 | tf_op jit(solution)/shard_map/ppermute | solution.py:40
  65.1 22.8 %collective-permute-start.17 = (bf16[272,256]{1,0:T(8,128)(2,1)S(1)}, bf16[272,256]{1,0:T(8,128)(2,1)S(1)}, u32[]{:S(2)}, u32[]{:S(2)}) collective-permute-start(bf16[272,256]{1,0:T(8,128)(2,1)S(1)} %get-tuple-element.114), channel_id=1, source_target_pairs={{0,12},{1,13},{2,14},{3,15},{4,0},{5,1},{6,2},{7,3},{8,4},{9,5},{1... | collective-permute-start | bytes 417800 | tf_op jit(solution)/shard_map/ppermute | solution.py:40
  69.1 16.5 %collective-permute-start.23 = (bf16[224,256]{1,0:T(8,128)(2,1)S(1)}, bf16[224,256]{1,0:T(8,128)(2,1)S(1)}, u32[]{:S(2)}, u32[]{:S(2)}) collective-permute-start(bf16[224,256]{1,0:T(8,128)(2,1)S(1)} %add_convert_fusion.3), channel_id=1, source_target_pairs={{0,8},{1,9},{2,10},{3,11},{4,12},{5,13},{6,14},{7,15},{8,0},{9,1},... | collective-permute-start | bytes 344072 | tf_op jit(solution)/shard_map/ppermute | solution.py:50
  75.0 12.0 %collective-permute-start.14 = (bf16[208,256]{1,0:T(8,128)(2,1)S(1)}, bf16[208,256]{1,0:T(8,128)(2,1)S(1)}, u32[]{:S(2)}, u32[]{:S(2)}) collective-permute-start(bf16[208,256]{1,0:T(8,128)(2,1)S(1)} %add_convert_fusion.5), channel_id=1, source_target_pairs={{0,8},{1,9},{2,10},{3,11},{4,12},{5,13},{6,14},{7,15},{8,0},{9,1},... | collective-permute-start | bytes 319496 | tf_op jit(solution)/shard_map/ppermute | solution.py:50
  86.5 7.8 %collective-permute-start.24 = (bf16[224,256]{1,0:T(8,128)(2,1)S(1)}, bf16[224,256]{1,0:T(8,128)(2,1)S(1)}, u32[]{:S(2)}, u32[]{:S(2)}) collective-permute-start(bf16[224,256]{1,0:T(8,128)(2,1)S(1)} %add_convert_fusion.2), channel_id=1, source_target_pairs={{0,8},{1,9},{2,10},{3,11},{4,12},{5,13},{6,14},{7,15},{8,0},{9,1},... | collective-permute-start | bytes 344072 | tf_op jit(solution)/shard_map/ppermute | solution.py:50
  94.5 8.1 %collective-permute-start.25 = (bf16[448,256]{1,0:T(8,128)(2,1)S(1)}, bf16[448,256]{1,0:T(8,128)(2,1)S(1)}, u32[]{:S(2)}, u32[]{:S(2)}) collective-permute-start(bf16[448,256]{1,0:T(8,128)(2,1)S(1)} %maximum_select_fusion.2), channel_id=1, source_target_pairs={{0,4},{1,3},{2,6},{3,1},{4,0},{5,7},{6,2},{7,5},{8,12},{9,11},{10,... | collective-permute-start | bytes 688136 | tf_op jit(solution)/shard_map/ppermute | solution.py:50
  95.6 11.6 %collective-permute-start.19 = (bf16[416,256]{1,0:T(8,128)(2,1)S(1)}, bf16[416,256]{1,0:T(8,128)(2,1)S(1)}, u32[]{:S(2)}, u32[]{:S(2)}) collective-permute-start(bf16[416,256]{1,0:T(8,128)(2,1)S(1)} %maximum_select_fusion.3), channel_id=1, source_target_pairs={{0,4},{1,3},{2,6},{3,1},{4,0},{5,7},{6,2},{7,5},{8,12},{9,11},{10,... | collective-permute-start | bytes 638984 | tf_op jit(solution)/shard_map/ppermute | solution.py:50
  102.8 8.5 %collective-permute-start.26 = (bf16[896,256]{1,0:T(8,128)(2,1)S(1)}, bf16[896,256]{1,0:T(8,128)(2,1)S(1)}, u32[]{:S(2)}, u32[]{:S(2)}) collective-permute-start(bf16[896,256]{1,0:T(8,128)(2,1)S(1)} %maximum_select_fusion), channel_id=1, source_target_pairs={{0,2},{1,5},{2,0},{3,7},{4,6},{5,1},{6,4},{7,3},{8,10},{9,13},{10,... | collective-permute-start | bytes 1376264 | tf_op jit(solution)/shard_map/ppermute | solution.py:50
  107.3 10.7 %collective-permute-start.20 = (bf16[832,256]{1,0:T(8,128)(2,1)S(1)}, bf16[832,256]{1,0:T(8,128)(2,1)S(1)}, u32[]{:S(2)}, u32[]{:S(2)}) collective-permute-start(bf16[832,256]{1,0:T(8,128)(2,1)S(1)} %maximum_select_fusion.1), channel_id=1, source_target_pairs={{0,2},{1,5},{2,0},{3,7},{4,6},{5,1},{6,4},{7,3},{8,10},{9,13},{10,... | collective-permute-start | bytes 1277960 | tf_op jit(solution)/shard_map/ppermute | solution.py:50
  107.4 13.9 %collective-permute-start.27 = (bf16[896,256]{1,0:T(8,128)(2,1)S(1)}, bf16[896,256]{1,0:T(8,128)(2,1)S(1)}, u32[]{:S(2)}, u32[]{:S(2)}) collective-permute-start(bf16[896,256]{1,0:T(8,128)(2,1)S(1)} %maximum_select_fusion), channel_id=1, source_target_pairs={{0,1},{1,0},{2,3},{3,2},{4,5},{5,4},{6,7},{7,6},{8,9},{9,8},{10,11... | collective-permute-start | bytes 1376264 | tf_op jit(solution)/shard_map/ppermute | solution.py:36
  111.3 10.0 %collective-permute-start.28 = (bf16[896,256]{1,0:T(8,128)(2,1)S(1)}, bf16[896,256]{1,0:T(8,128)(2,1)S(1)}, u32[]{:S(2)}, u32[]{:S(2)}) collective-permute-start(bf16[896,256]{1,0:T(8,128)(2,1)S(1)} %collective-permute-done.26), channel_id=1, source_target_pairs={{0,1},{1,0},{2,3},{3,2},{4,5},{5,4},{6,7},{7,6},{8,9},{9,8},{10,11... | collective-permute-start | bytes 1376264 | tf_op jit(solution)/shard_map/ppermute | solution.py:36
  (8 other events, 63.5 us)

commit v7 on v6

--- a/solution.py
+++ b/solution.py
@@ -7,12 +7,11 @@
 from jax.experimental.pallas import tpu as pltpu
 from jax.sharding import PartitionSpec as P
 
-VMEM_LIMIT = 11 * 1024 * 1024
 EXTRA = 16
 
 
-def params():
-    return pltpu.CompilerParams(vmem_limit_bytes=VMEM_LIMIT)
+def params(mebibytes=6):
+    return pltpu.CompilerParams(vmem_limit_bytes=mebibytes * 1024 * 1024)
 
 
 def cost(flops, bytes_accessed):
@@ -40,21 +39,16 @@
     return lax.ppermute(x, "zslab", [(i, (i + 4 * steps) % size) for i in range(size)])
 
 
-def orders(size):
-    bits = [1 << k for k in range(1, size.bit_length() - 1)]
-    return bits, [bits[1], bits[0]] + bits[2:]
+def stage_count(size):
+    return size.bit_length() - 2
 
 
 def swap_stage(x, size, stage):
-    both = orders(size)
-    return lax.ppermute(x, "zslab", [(i, i ^ both[i % 2][stage]) for i in range(size)])
-
-
-def stage_half(size, stage, other=False):
-    me = lax.axis_index("zslab")
-    low, high = (order[stage] for order in orders(size))
-    core = me % 2 == (1 if other else 0)
-    return jnp.where(core, (me // low) % 2, (me // high) % 2)
+    return swap(x, size, 2 << stage)
+
+
+def stage_half(size, stage):
+    return (lax.axis_index("zslab") // (2 << stage)) % 2
 
 
 def take_rows(x, place, rows):
@@ -171,11 +165,25 @@
     )(far(links), far(feats), far(voxmask))
 
 
-def prepare_kernel(feats, voxmask, mask, rows, give, turned, planes, masks, done):
+def fetch_taps(weight, near_weight, done):
+    for tap in range(weight.shape[0]):
+        pltpu.make_async_copy(weight.at[tap], near_weight.at[tap], done.at[tap]).start()
+
+
+def await_taps(first, last, weight, near_weight, done):
+    for tap in range(first, last):
+        pltpu.make_async_copy(weight.at[tap], near_weight.at[tap], done.at[tap]).wait()
+
+
+def prepare_kernel(feats, voxmask, weight, cotangent, mask, rows, give, turned, taps, slopes, planes, masks, done, fetched):
     half = feats.shape[3] // 2
+    count = weight.shape[0]
     pltpu.make_async_copy(voxmask, masks, done.at[8]).start()
     for z in range(8):
         pltpu.make_async_copy(feats.at[:, pl.ds(z, 1)], planes.at[:, pl.ds(z, 1)], done.at[z]).start()
+    fetch_taps(weight, taps, fetched)
+    for z in range(8):
+        pltpu.make_async_copy(cotangent.at[:, pl.ds(z, 1)], slopes.at[:, pl.ds(z, 1)], fetched.at[count + z]).start()
     valid = windows((half, 128), 1)
     first = lax.axis_index("zslab") % 2 == 0
     pltpu.make_async_copy(voxmask, masks, done.at[8]).wait()
@@ -190,30 +198,36 @@
         give[span, :] = jnp.where(first, plane[:, half:], plane[:, :half]).astype(jnp.bfloat16)
         for place, moved in enumerate(shifts(own.T, 1, valid)):
             turned[place * half : (place + 1) * half, span] = moved
-
-
-def prepare(feats, voxmask):
+    await_taps(0, count, weight, taps, fetched)
+    for z in range(8):
+        pltpu.make_async_copy(cotangent.at[:, pl.ds(z, 1)], slopes.at[:, pl.ds(z, 1)], fetched.at[count + z]).wait()
+
+
+def prepare(feats, voxmask, weight, cotangent):
     width = feats.shape[3]
     half = width // 2
     return pl.pallas_call(
         prepare_kernel,
-        in_specs=[FAR, FAR],
-        out_specs=(WHOLE,) * 4,
+        in_specs=[FAR] * 4,
+        out_specs=(WHOLE,) * 6,
         out_shape=(
             pltpu.VMEM((1024, 128), jnp.float32),
             pltpu.VMEM((1024, width), jnp.bfloat16),
             pltpu.VMEM((1024, half), jnp.bfloat16),
             pltpu.VMEM((9 * half, 1024), jnp.bfloat16),
+            pltpu.VMEM(weight.shape, jnp.bfloat16),
+            pltpu.VMEM(cotangent.shape, jnp.bfloat16),
         ),
         scratch_shapes=[
             pltpu.VMEM(feats.shape, jnp.bfloat16),
             pltpu.VMEM(voxmask.shape, jnp.int32),
             pltpu.SemaphoreType.DMA((9,)),
+            pltpu.SemaphoreType.DMA((weight.shape[0] + 8,)),
         ],
-        compiler_params=params(),
+        compiler_params=params(10),
         cost_estimate=cost(1024, 1024),
         name="prepare",
-    )(far(feats), far(voxmask))
+    )(far(feats), far(voxmask), far(weight), far(cotangent))
 
 
 def turn_kernel(rows, turned):
@@ -327,26 +341,8 @@
     return plane
 
 
-def fetch_taps(weight, near_weight, done):
-    for tap in range(weight.shape[0]):
-        pltpu.make_async_copy(weight.at[tap], near_weight.at[tap], done.at[tap]).start()
-
-
-def await_taps(first, last, weight, near_weight, done):
-    for tap in range(first, last):
-        pltpu.make_async_copy(weight.at[tap], near_weight.at[tap], done.at[tap]).wait()
-
-
-def forward_kernel(rows, mask, weight, bias, cotangent, out, grad, edge, bias_sum, near_weight, ends, cols, pre, slopes, shift, done):
+def forward_kernel(rows, mask, weight, bias, slopes, out, grad, edge, bias_sum, cols, pre):
     width = rows.shape[1]
-    count = weight.shape[0]
-    copies = [pltpu.make_async_copy(bias, shift, done.at[count])]
-    for z in range(8):
-        part = pl.ds(z, 1)
-        copies.append(pltpu.make_async_copy(cotangent.at[:, part], slopes.at[:, part], done.at[count + 1 + z]))
-    fetch_taps(weight, near_weight, done)
-    for copy in copies:
-        copy.start()
     valid = windows((128, width), 0)
     for z in range(8):
         span = slice(128 * z, 128 * z + 128)
@@ -354,20 +350,13 @@
             cols[span, place * width : (place + 1) * width] = moved
 
     def taps(a):
-        return near_weight[9 * a : 9 * a + 9].reshape(9 * width, width)
-
-    copies[0].wait()
-    await_taps(9, 18, weight, near_weight, done)
-    pre[...] = jnp.dot(cols[...], taps(1), preferred_element_type=jnp.float32) + shift[...]
-    await_taps(0, 9, weight, near_weight, done)
+        return weight[9 * a : 9 * a + 9].reshape(9 * width, width)
+
+    pre[...] = jnp.dot(cols[...], taps(1), preferred_element_type=jnp.float32) + bias[...]
     pre[128:, :] += jnp.dot(cols[:896, :], taps(0), preferred_element_type=jnp.float32)
-    await_taps(18, 27, weight, near_weight, done)
     pre[:896, :] += jnp.dot(cols[128:, :], taps(2), preferred_element_type=jnp.float32)
-    for copy in copies[1:]:
-        copy.wait()
     for side in range(2):
         edge[side] = pre[896 * side : 896 * side + 128, :]
-        ends[side] = both(slopes, 7 * side)
     total = jnp.zeros((1, width), jnp.float32)
     for z in range(1, 7):
         span = slice(128 * z, 128 * z + 128)
@@ -383,27 +372,22 @@
     width = rows.shape[1]
     return pl.pallas_call(
         forward_kernel,
-        in_specs=[WHOLE, WHOLE, FAR, FAR, FAR],
-        out_specs=(WHOLE,) * 6,
+        in_specs=[WHOLE] * 5,
+        out_specs=(WHOLE,) * 4,
         out_shape=(
             jax.ShapeDtypeStruct(cotangent.shape, jnp.bfloat16),
             pltpu.VMEM((768, width), jnp.bfloat16),
             pltpu.VMEM((2, 128, width), jnp.float32),
             pltpu.VMEM((1, width), jnp.float32),
-            pltpu.VMEM(weight.shape, jnp.bfloat16),
-            pltpu.VMEM((2, 128, width), jnp.bfloat16),
         ),
         scratch_shapes=[
             pltpu.VMEM((1024, 9 * width), jnp.bfloat16),
             pltpu.VMEM((1024, width), jnp.float32),
-            pltpu.VMEM(cotangent.shape, jnp.bfloat16),
-            pltpu.VMEM((1, width), jnp.float32),
-            pltpu.SemaphoreType.DMA((weight.shape[0] + 9,)),
         ],
-        compiler_params=params(),
+        compiler_params=params(12),
         cost_estimate=cost(1024, 1024),
         name="forward_inside",
-    )(near(rows), near(mask), far(weight), far(bias), far(cotangent))
+    )(near(rows), near(mask), near(weight), bias, near(cotangent))
 
 
 def inner_terms_kernel(mine, theirs, grad, their_grad, terms):
@@ -422,7 +406,7 @@
         in_specs=[WHOLE] * 4,
         out_specs=WHOLE,
         out_shape=pltpu.VMEM((3 * rows, width), jnp.float32),
-        compiler_params=params(),
+        compiler_params=params(10),
         cost_estimate=cost(1024, 1024),
         name="inner_terms",
     )(near(mine), near(theirs), near(grad), near(their_grad))
@@ -445,7 +429,7 @@
         pre = edge[side] + jnp.dot(cols, taps, preferred_element_type=jnp.float32)
         z = 7 * side
         keep = wide(mask[128 * z : 128 * z + 128, :])
-        act, slope = activate(pre, ends[side].astype(jnp.float32), keep)
+        act, slope = activate(pre, both(ends, z).astype(jnp.float32), keep)
         for b in range(2):
             planes[side, b, 0] = act[64 * b : 64 * b + 64]
         pltpu.make_async_copy(planes.at[side], out.at[:, pl.ds(z, 1)], done.at[side]).start()
@@ -532,7 +516,7 @@
             pltpu.VMEM((9 * half, 512), jnp.bfloat16),
             pltpu.VMEM((count * half, width), jnp.float32),
         ],
-        compiler_params=params(),
+        compiler_params=params(8),
         cost_estimate=cost(1024, 1024),
         name="outer_terms",
     )(*[near(x) for x in (mine, theirs, halos, their_halos, parcel, their_parcel, inner)])
@@ -578,7 +562,7 @@
         out_specs=WHOLE,
         out_shape=jax.ShapeDtypeStruct((2, 8, 64, width), jnp.bfloat16),
         scratch_shapes=[pltpu.VMEM((768, 9 * width), jnp.bfloat16)],
-        compiler_params=params(),
+        compiler_params=params(10),
         cost_estimate=cost(1024, 1024),
         name="backward_inner",
     )(near(grad), near(mask), near(weight))
@@ -623,7 +607,7 @@
             pltpu.SemaphoreType.DMA((2,)),
         ],
         input_output_aliases={5: 0},
-        compiler_params=params(),
+        compiler_params=params(12),
         cost_estimate=cost(1024, 1024),
         name="backward_outer",
     )(table, near(grad), near(parcel), near(mask), far(weight), done, *[near(x) for x in arrived])
@@ -633,8 +617,8 @@
     parts, (out, done) = refs[:4], refs[-2:]
     count = parts[0].shape[0]
     core = lax.axis_index("zslab") % 2
-    mine, theirs = stage_half(size, 0), stage_half(size, 0, other=True)
-    places = (2 * core + mine, 2 * core + 1 - mine, 2 - 2 * core + theirs, 3 - 2 * core - theirs)
+    mine = stage_half(size, 0)
+    places = (2 * core + mine, 2 * core + 1 - mine, 2 - 2 * core + mine, 3 - 2 * core - mine)
     copies = [
         pltpu.make_async_copy(ref, out.at[pl.ds(first, count), place], done.at[index])
         for index, (ref, place) in enumerate(zip(parts, places))
@@ -669,9 +653,9 @@
     width = feats.shape[3]
     outer = size // 4
 
-    mask, rows, give, turned = prepare(feats, voxmask)
+    mask, rows, give, turned, taps, ends = prepare(feats, voxmask, weight, cotangent)
     parcels, rows = gather_group(rims(links, feats, voxmask), size, (rows,))
-    out, grad, edge, bias_local, taps, ends = forward_inside(rows, mask, weight, bias.reshape(1, width), cotangent)
+    out, grad, edge, bias_local = forward_inside(rows, mask, taps, bias.reshape(1, width), ends)
     *parcels, grad = lax.optimization_barrier((*parcels, grad))
     table, picks = route(parcels, outer)
 
@@ -686,19 +670,22 @@
     their_halos = swap(give, size, 1)
     parcels, halos = gather_group(parcel, size, (halos,))
 
-    stages = len(orders(size)[0])
+    stages = stage_count(size)
     halves = [stage_half(size, stage) for stage in range(stages)]
     count = weight.shape[0]
-    cuts = [(0, count // 2), (count // 2, count)]
+    cuts = [(count * k // 3, count * (k + 1) // 3) for k in range(3)]
     sums = []
     for cut in cuts:
         give, stay = outer_terms(cut, size, turned, their_turned, halos, their_halos, parcel, parcels[2], inner)
+        if len(sums) == 2:
+            arrived_first, give = lax.optimization_barrier((sums[0][1], give))
+            sums[0] = (sums[0][0], arrived_first)
         sums.append((stay, swap_stage(give, size, 0)))
 
     picks = repeat_route(table, parcels, outer)
-    (stay, got), other = sums
+    (stay, got), *others = sums
     stay, *picks = lax.optimization_barrier((stay, *picks))
-    sums = [(stay, got), other]
+    sums = [(stay, got), *others]
     arrived = [rotate(pick, size, steps) if steps else pick for steps, pick in enumerate(picks)]
     for stage in range(1, stages):
         for index, (stay, got) in enumerate(sums):
@@ -706,16 +693,17 @@
             sums[index] = (stay, swap_stage(give, size, stage))
     parts = [(stay + got.astype(jnp.float32)).astype(jnp.bfloat16) for stay, got in sums]
     parts[0], *arrived = lax.optimization_barrier((parts[0], *arrived))
+    grad_feats, grad_bias = backward_outer(table, grad, parcel, mask, weight, grad_feats, arrived)
     for stage in reversed(range(1, stages)):
-        parts = [join(part, swap_stage(part, size, stage), halves[stage]) for part in parts]
-    grad_feats, grad_bias = backward_outer(table, grad, parcel, mask, weight, grad_feats, arrived)
+        gathered = [swap_stage(part, size, stage) for part in parts]
+        if stage == 1:
+            gathered[0], grad_feats, grad_bias = lax.optimization_barrier((gathered[0], grad_feats, grad_bias))
+        parts = [join(part, got, halves[stage]) for part, got in zip(parts, gathered)]
 
     grad_weight = None
     for cut, part in zip(cuts, parts):
         last = swap_stage(part, size, 0)
         other = swap(part, size, 1)
-        if grad_weight is None:
-            last, grad_feats, grad_bias = lax.optimization_barrier((last, grad_feats, grad_bias))
         pieces = [x.reshape(cut[1] - cut[0], width // 4, width) for x in (part, last, other, swap(last, size, 1))]
         grad_weight = assemble(cut[0], size, pieces, (count, 4, width // 4, width), grad_weight)
     return out, grad_feats, grad_weight.reshape(count, width, width), grad_bias.reshape(width)

time: 123 us -> 132 us (1.073)
  starting transfers between devices: 31.2 us -> 39.4 us
  local copies, waits for them, and re-layouts: 0.01 us -> 7.88 us
  waiting for transfers between devices: 44.3 us -> 40.8 us
  other arithmetic: 8.43 us -> 6.3 us
  Pallas kernels: 37.7 us -> 36.1 us
    ppermute x12 -> x0, waiting for transfers between devices: 37.9 us -> none  [swap_stage(): lax.ppermute(x, 'zslab', [(i, i ^ both[i % 2][stage]) for i in range(size)])]
    ppermute x13 -> x33, waiting for transfers between devices: 5.56 us -> 39.9 us  [swap(): return lax.ppermute(x, 'zslab', [(i, i ^ bit) for i in range(size)])]
    ppermute x13 -> x33, starting transfers between devices: 7.17 us -> 30 us  [swap(): return lax.ppermute(x, 'zslab', [(i, i ^ bit) for i in range(size)])]
    ppermute x12 -> x0, starting transfers between devices: 14 us -> none  [swap_stage(): lax.ppermute(x, 'zslab', [(i, i ^ both[i % 2][stage]) for i in range(size)])]
    unnamed x2 -> x38, local copies, waits for them, and re-layouts: 0.01 us -> 7.88 us
    pallas_call x2, Pallas kernels: 13.2 us -> 10.1 us  [the longest x1 5.37 us: prepare(): pl.pallas_call(prepare_kernel, in_specs=[FAR] * 4, out_specs=(WHOLE,) * 6...]
    convert_element_type x4 -> x6, other arithmetic: 5.98 us -> 3.99 us  [halve(): return (give.astype(jnp.bfloat16), keep)]
    pallas_call x2 -> x3, Pallas kernels: 2.49 us -> 3.17 us  [assemble(): pl.pallas_call(functools.partial(assemble_kernel, first, size), in_specs=...]
  transfers between devices with their start and end apart: 31 -> 39, of which waited for: 13 -> 12; matrix products, arithmetic and copies ran while one was open for 7% -> 5% of each run, Pallas kernels for 26% -> 23%
where the time goes in v7:
time: 132 us
  waiting for transfers between devices  40.8 us (31%)
  starting transfers between devices  39.4 us (30%)
  Pallas kernels  36.1 us (27%)
  local copies, waits for them, and re-layouts  7.88 us (6%)
  other arithmetic  6.3 us (5%)
    ppermute x33, waiting for transfers between devices, swap(): return lax.ppermute(x, 'zslab', [(i, i ^ bit) for i in range(size)])  39.9 us
    ppermute x33, starting transfers between devices, swap(): return lax.ppermute(x, 'zslab', [(i, i ^ bit) for i in range(size)])  30 us
    ppermute x6, starting transfers between devices, rotate(): lax.ppermute(x, 'zslab', [(i, (i + 4 * steps) % size) for i in range(size)])  9.34 us
    unnamed x38, local copies, waits for them, and re-layouts  7.88 us
    pallas_call x1, Pallas kernels, backward_outer(): pl.pallas_call(backward_outer_kernel, in_specs=[SCALARS] + [WHOLE] * 3 +...  6.13 us
    pallas_call x1, Pallas kernels, prepare(): pl.pallas_call(prepare_kernel, in_specs=[FAR] * 4, out_specs=(WHOLE,) * 6...  5.37 us
    pallas_call x1, Pallas kernels, forward_inside(): pl.pallas_call(forward_kernel, in_specs=[WHOLE] * 5, out_specs=(WHOLE,) *...  4.7 us
    pallas_call x3, Pallas kernels, outer_terms(): pl.pallas_call(functools.partial(outer_terms_kernel, taps, size), in_spec...  4.09 us
  transfers between devices with their start and end apart: 39, of which 12 were waited for; matrix products, arithmetic and copies ran while one was open for 5% of the time, Pallas kernels for 23%

profile of v7, /device:TPU:0, one launch (start us, length us, event | category | flops | bytes accessed | tf_op | source)
XLA Modules:
  0.0 131.6 jit_solution(2956593744826761000)
XLA Ops:
  1.7 3.0 %collective-permute-start = (bf16[272,256]{1,0:T(8,128)(2,1)S(1)}, bf16[272,256]{1,0:T(8,128)(2,1)S(1)}, u32[]{:S(2)}, u32[]{:S(2)}) collective-permute-start(bf16[272,256]{1,0:T(8,128)(2,1)S(1)} %rims.1.refs_0_), channel_id=1, source_target_pairs={{0,2},{1,3},{2,0},{3,1},{4,6},{5,7},{6,4},{7,5},{8,10},{9,11},{10,... | collective-permute-start | bytes 417800 | tf_op jit(solution)/shard_map/ppermute | solution.py:35
  4.8 5.4 %prepare.1 = (f32[1024,128]{1,0:T(8,128)S(1)}, bf16[1024,256]{1,0:T(8,128)(2,1)S(1)}, bf16[1024,128]{1,0:T(8,128)(2,1)S(1)}, bf16[1152,1024]{1,0:T(8,128)(2,1)S(...) custom-call(bf16[2,8,64,256]{3,2,1,0:T(8,128)(2,1)} %feats.3, s32[2,512]{1,0:T(2,128)} %voxmask.3, ...), custom_call_target="tpu_custom_call" | custom-call | flops 1024 | bytes 1024 | tf_op jit(solution)/shard_map/prepare/pallas_call | solution.py:209
  10.8 4.7 %forward_inside.1 = (bf16[2,8,64,256]{3,2,1,0:T(8,128)(2,1)}, bf16[768,256]{1,0:T(8,128)(2,1)S(1)}, f32[2,128,256]{2,1,0:T(8,128)S(1)}, f32[1,256]{1,0:T(1,128)S(1)}) custom-call(bf16[1024,256]{1,0:T(8,128)(2,1)S(1)} %get-tuple-element.72.rows, f32[1024,128]{1,0:T(8,128)S(1)} %get-tuple-element.73.mask, bf16[27,256,256]{2,1,0:T(8,128)(2,1)S(1)} %get-tuple-element.74.weight, ...), custom_call_target="tpu_custom_call" | custom-call | flops 1024 | bytes 1024 | tf_op jit(solution)/shard_map/forward_inside/pallas_call | solution.py:373
  15.5 1.7 %route.1 = (s32[20]{0:T(128)S(1)}, bf16[256,256]{1,0:T(8,128)(2,1)S(1)}, bf16[256,256]{1,0:T(8,128)(2,1)S(1)}, bf16[256,256]{1,0:T(8,128)(2,1)S(1)}, bf16[256,256]{1,0:T(8,128)(2,1)S(1)}) custom-call(bf16[272,256]{1,0:T(8,128)(2,1)S(1)} %rims.1.refs_0_, bf16[272,256]{1,0:T(8,128)(2,1)S(1)} %collective-permute-done.refs_1_, ...), custom_call_target="tpu_custom_call" | custom-call | flops 1024 | bytes 1024 | tf_op jit(solution)/shard_map/route/pallas_call | solution.py:295
  19.3 2.6 %collective-permute-start.4 = (bf16[256,256]{1,0:T(8,128)(2,1)S(1)}, bf16[256,256]{1,0:T(8,128)(2,1)S(1)}, u32[]{:S(2)}, u32[]{:S(2)}) collective-permute-start(bf16[256,256]{1,0:T(8,128)(2,1)S(1)} %get-tuple-element.92), channel_id=1, source_target_pairs={{0,8},{1,9},{2,10},{3,11},{4,12},{5,13},{6,14},{7,15},{8,0},{9,1},... | collective-permute-start | bytes 393224 | tf_op jit(solution)/shard_map/ppermute | solution.py:39
  23.3 2.9 %backward_inner.1.done = bf16[2,8,64,256]{3,2,1,0:T(8,128)(2,1)} custom-call(bf16[768,256]{1,0:T(8,128)(2,1)S(1)} %get-tuple-element.96.grad, f32[1024,128]{1,0:T(8,128)S(1)} %get-tuple-element.73.mask, bf16[27,256,256]{2,1,0:T(8,128)(2,1)S(1)} %get-tuple-element.74.weight), custom_call_target="tpu_custom_call" | custom-call | flops 1024 | bytes 1024 | tf_op jit(solution)/shard_map/backward_inner/pallas_call | solution.py:559
  27.0 3.0 %inner_terms.1.inner = f32[3456,256]{1,0:T(8,128)S(1)} custom-call(bf16[1152,1024]{1,0:T(8,128)(2,1)S(1)} %get-tuple-element.94.mine, bf16[1152,1024]{1,0:T(8,128)(2,1)S(1)} %turn.1.theirs, bf16[768,256]{1,0:T(8,128)(2,1)S(1)} %get-tuple-element.96.grad, bf16[768,256]{1,0:T(8,128)(2,1)S(1)} %collective-permute-done.7.their_grad), custom_call_target="tpu_custom_call" | custom-call | flops 1024 | bytes 1024 | tf_op jit(solution)/shard_map/inner_terms/pallas_call | solution.py:404
  30.8 2.0 %forward_edges.1 = (bf16[2,8,64,256]{3,2,1,0:T(8,128)(2,1)}, bf16[272,256]{1,0:T(8,128)(2,1)S(1)}, bf16[256,128]{1,0:T(8,128)(2,1)S(1)}, bf16[256,128]{1,0:T(8,128)(2,1)S(1)}) custom-call(s32[20]{0:T(128)S(1)} %get-tuple-element.81.table, f32[1024,128]{1,0:T(8,128)S(1)} %get-tuple-element.73.mask, ...), custom_call_target="tpu_custom_call", output_to_operand_aliasing={{0}: (6, {})} | custom-call | flops 1024 | bytes 1024 | tf_op jit(solution)/shard_map/forward_edges/pallas_call | solution.py:445
  33.9 4.6 %collective-permute-done.8.refs_1_ = bf16[272,256]{1,0:T(8,128)(2,1)} collective-permute-done((bf16[272,256]{1,0:T(8,128)(2,1)S(1)}, bf16[272,256]{1,0:T(8,128)(2,1)}, u32[]{:S(2)}, u32[]{:S(2)}) %collective-permute-start.8) | collective-permute-done | bytes 139296 | tf_op jit(solution)/shard_map/ppermute | solution.py:35
  45.4 2.0 %copy-done.1 = f32[3456,256]{1,0:T(8,128)S(1)} copy-done((f32[3456,256]{1,0:T(8,128)S(1)}, f32[3456,256]{1,0:T(8,128)}, u32[]{:S(2)}) %copy-start.1) | copy-done | bytes 3538968
  54.8 3.4 %collective-permute-start.13 = (bf16[288,256]{1,0:T(8,128)(2,1)S(1)}, bf16[288,256]{1,0:T(8,128)(2,1)}, u32[]{:S(2)}, u32[]{:S(2)}) collective-permute-start(bf16[288,256]{1,0:T(8,128)(2,1)S(1)} %get-tuple-element.140), channel_id=1, source_target_pairs={{0,4},{1,5},{2,6},{3,7},{4,0},{5,1},{6,2},{7,3},{8,12},{9,13},{10,... | collective-permute-start | bytes 442376 | tf_op jit(solution)/shard_map/ppermute | solution.py:35
  65.4 5.5 %collective-permute-done.29 = bf16[288,256]{1,0:T(8,128)(2,1)} collective-permute-done((bf16[288,256]{1,0:T(8,128)(2,1)S(1)}, bf16[288,256]{1,0:T(8,128)(2,1)}, u32[]{:S(2)}, u32[]{:S(2)}) %collective-permute-start.29) | collective-permute-done | bytes 147488 | tf_op jit(solution)/shard_map/ppermute | solution.py:35
  71.9 7.8 %collective-permute-done.14 = bf16[144,256]{1,0:T(8,128)(2,1)S(1)} collective-permute-done((bf16[144,256]{1,0:T(8,128)(2,1)S(1)}, bf16[144,256]{1,0:T(8,128)(2,1)S(1)}, u32[]{:S(2)}, u32[]{:S(2)}) %collective-permute-start.14) | collective-permute-done | bytes 73760 | tf_op jit(solution)/shard_map/ppermute | solution.py:35
  80.6 3.0 %collective-permute-start.18 = (bf16[144,256]{1,0:T(8,128)(2,1)S(1)}, bf16[144,256]{1,0:T(8,128)(2,1)S(1)}, u32[]{:S(2)}, u32[]{:S(2)}) collective-permute-start(bf16[144,256]{1,0:T(8,128)(2,1)S(1)} %add_convert_fusion.7), channel_id=1, source_target_pairs={{0,8},{1,9},{2,10},{3,11},{4,12},{5,13},{6,14},{7,15},{8,0},{9,1},... | collective-permute-start | bytes 221192 | tf_op jit(solution)/shard_map/ppermute | solution.py:35
  83.7 2.0 %collective-permute-done.30 = bf16[144,256]{1,0:T(8,128)(2,1)S(1)} collective-permute-done((bf16[144,256]{1,0:T(8,128)(2,1)S(1)}, bf16[144,256]{1,0:T(8,128)(2,1)S(1)}, u32[]{:S(2)}, u32[]{:S(2)}) %collective-permute-start.30) | collective-permute-done | bytes 73760 | tf_op jit(solution)/shard_map/ppermute | solution.py:35
  87.1 6.1 %backward_outer.1 = (bf16[2,8,64,256]{3,2,1,0:T(8,128)(2,1)}, f32[1,256]{1,0:T(1,128)}) custom-call(s32[20]{0:T(128)S(1)} %copy-done.16, bf16[768,256]{1,0:T(8,128)(2,1)S(1)} %get-tuple-element.96.grad, bf16[272,256]{1,0:T(8,128)(2,1)S(1)} %get-tuple-element.102.parcel.refs_0_, ...), custom_call_target="tpu_custom_call", output_to_operand_aliasing={{0}: (5, {})} | custom-call | flops 1024 | bytes 1024 | tf_op jit(solution)/shard_map/backward_outer/pallas_call | solution.py:597
  93.3 2.5 %collective-permute-start.22 = (bf16[144,256]{1,0:T(8,128)(2,1)S(1)}, bf16[144,256]{1,0:T(8,128)(2,1)S(1)}, u32[]{:S(2)}, u32[]{:S(2)}) collective-permute-start(bf16[144,256]{1,0:T(8,128)(2,1)S(1)} %add_convert_fusion.6), channel_id=1, source_target_pairs={{0,8},{1,9},{2,10},{3,11},{4,12},{5,13},{6,14},{7,15},{8,0},{9,1},... | collective-permute-start | bytes 221192 | tf_op jit(solution)/shard_map/ppermute | solution.py:35
  96.4 2.4 %collective-permute-done.22 = bf16[144,256]{1,0:T(8,128)(2,1)S(1)} collective-permute-done((bf16[144,256]{1,0:T(8,128)(2,1)S(1)}, bf16[144,256]{1,0:T(8,128)(2,1)S(1)}, u32[]{:S(2)}, u32[]{:S(2)}) %collective-permute-start.22) | collective-permute-done | bytes 73760 | tf_op jit(solution)/shard_map/ppermute | solution.py:35
  98.8 2.9 %collective-permute-start.23 = (bf16[144,256]{1,0:T(8,128)(2,1)S(1)}, bf16[144,256]{1,0:T(8,128)(2,1)S(1)}, u32[]{:S(2)}, u32[]{:S(2)}) collective-permute-start(bf16[144,256]{1,0:T(8,128)(2,1)S(1)} %add_convert_fusion.5), channel_id=1, source_target_pairs={{0,8},{1,9},{2,10},{3,11},{4,12},{5,13},{6,14},{7,15},{8,0},{9,1},... | collective-permute-start | bytes 221192 | tf_op jit(solution)/shard_map/ppermute | solution.py:35
  102.6 2.1 %collective-permute-done.23 = bf16[144,256]{1,0:T(8,128)(2,1)S(1)} collective-permute-done((bf16[144,256]{1,0:T(8,128)(2,1)S(1)}, bf16[144,256]{1,0:T(8,128)(2,1)S(1)}, u32[]{:S(2)}, u32[]{:S(2)}) %collective-permute-start.23) | collective-permute-done | bytes 73760 | tf_op jit(solution)/shard_map/ppermute | solution.py:35
  104.7 3.9 %collective-permute-start.24 = (bf16[288,256]{1,0:T(8,128)(2,1)S(1)}, bf16[288,256]{1,0:T(8,128)(2,1)S(1)}, u32[]{:S(2)}, u32[]{:S(2)}) collective-permute-start(bf16[288,256]{1,0:T(8,128)(2,1)S(1)} %maximum_select_fusion.4), channel_id=1, source_target_pairs={{0,4},{1,5},{2,6},{3,7},{4,0},{5,1},{6,2},{7,3},{8,12},{9,13},{10,... | collective-permute-start | bytes 442376 | tf_op jit(solution)/shard_map/ppermute | solution.py:35
  112.4 6.0 %collective-permute-done.36 = bf16[576,256]{1,0:T(8,128)(2,1)S(1)} collective-permute-done((bf16[576,256]{1,0:T(8,128)(2,1)S(1)}, bf16[576,256]{1,0:T(8,128)(2,1)S(1)}, u32[]{:S(2)}, u32[]{:S(2)}) %collective-permute-start.36) | collective-permute-done | bytes 294944 | tf_op jit(solution)/shard_map/ppermute | solution.py:35
  118.9 5.8 %collective-permute-done.33 = bf16[576,256]{1,0:T(8,128)(2,1)S(1)} collective-permute-done((bf16[576,256]{1,0:T(8,128)(2,1)S(1)}, bf16[576,256]{1,0:T(8,128)(2,1)S(1)}, u32[]{:S(2)}, u32[]{:S(2)}) %collective-permute-start.33) | collective-permute-done | bytes 294944 | tf_op jit(solution)/shard_map/ppermute | solution.py:35
  125.3 2.9 %collective-permute-done.25 = bf16[576,256]{1,0:T(8,128)(2,1)S(1)} collective-permute-done((bf16[576,256]{1,0:T(8,128)(2,1)S(1)}, bf16[576,256]{1,0:T(8,128)(2,1)S(1)}, u32[]{:S(2)}, u32[]{:S(2)}) %collective-permute-start.25) | collective-permute-done | bytes 294944 | tf_op jit(solution)/shard_map/ppermute | solution.py:35
  (123 shorter events, 42.2 us)
Async XLA Ops:
  4.8 10.7 %collective-permute-start.1 = (bf16[272,256]{1,0:T(8,128)(2,1)S(1)}, bf16[272,256]{1,0:T(8,128)(2,1)S(1)}, u32[]{:S(2)}, u32[]{:S(2)}) collective-permute-start(bf16[272,256]{1,0:T(8,128)(2,1)S(1)} %rims.1.refs_0_), channel_id=1, source_target_pairs={{0,1},{1,0},{2,3},{3,2},{4,5},{5,4},{6,7},{7,6},{8,9},{9,8},{10,11... | collective-permute-start | bytes 417800 | tf_op jit(solution)/shard_map/ppermute | solution.py:35
  15.5 11.5 %collective-permute-start.7 = (bf16[768,256]{1,0:T(8,128)(2,1)S(1)}, bf16[768,256]{1,0:T(8,128)(2,1)S(1)}, u32[]{:S(2)}, u32[]{:S(2)}) collective-permute-start(bf16[768,256]{1,0:T(8,128)(2,1)S(1)} %get-tuple-element.96.grad), channel_id=1, source_target_pairs={{0,1},{1,0},{2,3},{3,2},{4,5},{5,4},{6,7},{7,6},{8,9},{9,8},{10,11... | collective-permute-start | bytes 1179656 | tf_op jit(solution)/shard_map/ppermute | solution.py:35
  17.2 9.0 %collective-permute-start.6 = (bf16[1024,128]{1,0:T(8,128)(2,1)S(1)}, bf16[1024,128]{1,0:T(8,128)(2,1)S(1)}, u32[]{:S(2)}, u32[]{:S(2)}) collective-permute-start(bf16[1024,128]{1,0:T(8,128)(2,1)S(1)} %get-tuple-element.95), channel_id=1, source_target_pairs={{0,1},{1,0},{2,3},{3,2},{4,5},{5,4},{6,7},{7,6},{8,9},{9,8},{10,11... | collective-permute-start | bytes 786440 | tf_op jit(solution)/shard_map/ppermute | solution.py:35
  17.8 12.2 %collective-permute-start.3 = (bf16[256,256]{1,0:T(8,128)(2,1)S(1)}, bf16[256,256]{1,0:T(8,128)(2,1)S(1)}, u32[]{:S(2)}, u32[]{:S(2)}) collective-permute-start(bf16[256,256]{1,0:T(8,128)(2,1)S(1)} %get-tuple-element.91), channel_id=1, source_target_pairs={{0,4},{1,5},{2,6},{3,7},{4,8},{5,9},{6,10},{7,11},{8,12},{9,13},{1... | collective-permute-start | bytes 393224 | tf_op jit(solution)/shard_map/ppermute | solution.py:39
  19.3 11.5 %collective-permute-start.4 = (bf16[256,256]{1,0:T(8,128)(2,1)S(1)}, bf16[256,256]{1,0:T(8,128)(2,1)S(1)}, u32[]{:S(2)}, u32[]{:S(2)}) collective-permute-start(bf16[256,256]{1,0:T(8,128)(2,1)S(1)} %get-tuple-element.92), channel_id=1, source_target_pairs={{0,8},{1,9},{2,10},{3,11},{4,12},{5,13},{6,14},{7,15},{8,0},{9,1},... | collective-permute-start | bytes 393224 | tf_op jit(solution)/shard_map/ppermute | solution.py:39
  21.9 8.9 %collective-permute-start.5 = (bf16[256,256]{1,0:T(8,128)(2,1)S(1)}, bf16[256,256]{1,0:T(8,128)(2,1)S(1)}, u32[]{:S(2)}, u32[]{:S(2)}) collective-permute-start(bf16[256,256]{1,0:T(8,128)(2,1)S(1)} %get-tuple-element.93), channel_id=1, source_target_pairs={{0,12},{1,13},{2,14},{3,15},{4,0},{5,1},{6,2},{7,3},{8,4},{9,5},{1... | collective-permute-start | bytes 393224 | tf_op jit(solution)/shard_map/ppermute | solution.py:39
  41.0 12.7 %collective-permute-start.12 = (bf16[576,256]{1,0:T(8,128)(2,1)}, bf16[576,256]{1,0:T(8,128)(2,1)}, u32[]{:S(2)}, u32[]{:S(2)}) collective-permute-start(bf16[576,256]{1,0:T(8,128)(2,1)} %get-tuple-element.114), channel_id=1, source_target_pairs={{0,2},{1,3},{2,0},{3,1},{4,6},{5,7},{6,4},{7,5},{8,10},{9,11},{10,... | collective-permute-start | bytes 884744 | tf_op jit(solution)/shard_map/ppermute | solution.py:35
  43.9 14.3 %collective-permute-start.28 = (bf16[576,256]{1,0:T(8,128)(2,1)}, bf16[576,256]{1,0:T(8,128)(2,1)}, u32[]{:S(2)}, u32[]{:S(2)}) collective-permute-start(bf16[576,256]{1,0:T(8,128)(2,1)} %get-tuple-element.133), channel_id=1, source_target_pairs={{0,2},{1,3},{2,0},{3,1},{4,6},{5,7},{6,4},{7,5},{8,10},{9,11},{10,... | collective-permute-start | bytes 884744 | tf_op jit(solution)/shard_map/ppermute | solution.py:35
  54.8 9.3 %collective-permute-start.13 = (bf16[288,256]{1,0:T(8,128)(2,1)S(1)}, bf16[288,256]{1,0:T(8,128)(2,1)}, u32[]{:S(2)}, u32[]{:S(2)}) collective-permute-start(bf16[288,256]{1,0:T(8,128)(2,1)S(1)} %get-tuple-element.140), channel_id=1, source_target_pairs={{0,4},{1,5},{2,6},{3,7},{4,0},{5,1},{6,2},{7,3},{8,12},{9,13},{10,... | collective-permute-start | bytes 442376 | tf_op jit(solution)/shard_map/ppermute | solution.py:35
  59.3 11.7 %collective-permute-start.29 = (bf16[288,256]{1,0:T(8,128)(2,1)S(1)}, bf16[288,256]{1,0:T(8,128)(2,1)}, u32[]{:S(2)}, u32[]{:S(2)}) collective-permute-start(bf16[288,256]{1,0:T(8,128)(2,1)S(1)} %get-tuple-element.136), channel_id=1, source_target_pairs={{0,4},{1,5},{2,6},{3,7},{4,0},{5,1},{6,2},{7,3},{8,12},{9,13},{10,... | collective-permute-start | bytes 442376 | tf_op jit(solution)/shard_map/ppermute | solution.py:35
  60.2 20.4 %collective-permute-start.15 = (bf16[272,256]{1,0:T(8,128)(2,1)S(1)}, bf16[272,256]{1,0:T(8,128)(2,1)S(1)}, u32[]{:S(2)}, u32[]{:S(2)}) collective-permute-start(bf16[272,256]{1,0:T(8,128)(2,1)S(1)} %get-tuple-element.118), channel_id=1, source_target_pairs={{0,4},{1,5},{2,6},{3,7},{4,8},{5,9},{6,10},{7,11},{8,12},{9,13},{1... | collective-permute-start | bytes 417800 | tf_op jit(solution)/shard_map/ppermute | solution.py:39
  61.4 19.2 %collective-permute-start.16 = (bf16[272,256]{1,0:T(8,128)(2,1)S(1)}, bf16[272,256]{1,0:T(8,128)(2,1)S(1)}, u32[]{:S(2)}, u32[]{:S(2)}) collective-permute-start(bf16[272,256]{1,0:T(8,128)(2,1)S(1)} %get-tuple-element.119), channel_id=1, source_target_pairs={{0,8},{1,9},{2,10},{3,11},{4,12},{5,13},{6,14},{7,15},{8,0},{9,1},... | collective-permute-start | bytes 417800 | tf_op jit(solution)/shard_map/ppermute | solution.py:39
  62.4 18.2 %collective-permute-start.17 = (bf16[272,256]{1,0:T(8,128)(2,1)S(1)}, bf16[272,256]{1,0:T(8,128)(2,1)S(1)}, u32[]{:S(2)}, u32[]{:S(2)}) collective-permute-start(bf16[272,256]{1,0:T(8,128)(2,1)S(1)} %get-tuple-element.120), channel_id=1, source_target_pairs={{0,12},{1,13},{2,14},{3,15},{4,0},{5,1},{6,2},{7,3},{8,4},{9,5},{1... | collective-permute-start | bytes 417800 | tf_op jit(solution)/shard_map/ppermute | solution.py:39
  64.0 19.6 %collective-permute-start.20 = (bf16[576,256]{1,0:T(8,128)(2,1)}, bf16[576,256]{1,0:T(8,128)(2,1)S(1)}, u32[]{:S(2)}, u32[]{:S(2)}) collective-permute-start(bf16[576,256]{1,0:T(8,128)(2,1)} %copy-done.18), channel_id=1, source_target_pairs={{0,2},{1,3},{2,0},{3,1},{4,6},{5,7},{6,4},{7,5},{8,10},{9,11},{10,... | collective-permute-start | bytes 884744 | tf_op jit(solution)/shard_map/ppermute | solution.py:35
  71.0 8.7 %collective-permute-start.14 = (bf16[144,256]{1,0:T(8,128)(2,1)S(1)}, bf16[144,256]{1,0:T(8,128)(2,1)S(1)}, u32[]{:S(2)}, u32[]{:S(2)}) collective-permute-start(bf16[144,256]{1,0:T(8,128)(2,1)S(1)} %add_convert_fusion.8), channel_id=1, source_target_pairs={{0,8},{1,9},{2,10},{3,11},{4,12},{5,13},{6,14},{7,15},{8,0},{9,1},... | collective-permute-start | bytes 221192 | tf_op jit(solution)/shard_map/ppermute | solution.py:35
  80.6 15.3 %collective-permute-start.18 = (bf16[144,256]{1,0:T(8,128)(2,1)S(1)}, bf16[144,256]{1,0:T(8,128)(2,1)S(1)}, u32[]{:S(2)}, u32[]{:S(2)}) collective-permute-start(bf16[144,256]{1,0:T(8,128)(2,1)S(1)} %add_convert_fusion.7), channel_id=1, source_target_pairs={{0,8},{1,9},{2,10},{3,11},{4,12},{5,13},{6,14},{7,15},{8,0},{9,1},... | collective-permute-start | bytes 221192 | tf_op jit(solution)/shard_map/ppermute | solution.py:35
  83.7 9.6 %collective-permute-start.21 = (bf16[288,256]{1,0:T(8,128)(2,1)S(1)}, bf16[288,256]{1,0:T(8,128)(2,1)S(1)}, u32[]{:S(2)}, u32[]{:S(2)}) collective-permute-start(bf16[288,256]{1,0:T(8,128)(2,1)S(1)} %get-tuple-element.138), channel_id=1, source_target_pairs={{0,4},{1,5},{2,6},{3,7},{4,0},{5,1},{6,2},{7,3},{8,12},{9,13},{10,... | collective-permute-start | bytes 442376 | tf_op jit(solution)/shard_map/ppermute | solution.py:35
  86.6 15.1 %collective-permute-start.31 = (bf16[144,256]{1,0:T(8,128)(2,1)S(1)}, bf16[144,256]{1,0:T(8,128)(2,1)S(1)}, u32[]{:S(2)}, u32[]{:S(2)}) collective-permute-start(bf16[144,256]{1,0:T(8,128)(2,1)S(1)} %add_convert_fusion.3), channel_id=1, source_target_pairs={{0,8},{1,9},{2,10},{3,11},{4,12},{5,13},{6,14},{7,15},{8,0},{9,1},... | collective-permute-start | bytes 221192 | tf_op jit(solution)/shard_map/ppermute | solution.py:35
  108.7 9.7 %collective-permute-start.36 = (bf16[576,256]{1,0:T(8,128)(2,1)S(1)}, bf16[576,256]{1,0:T(8,128)(2,1)S(1)}, u32[]{:S(2)}, u32[]{:S(2)}) collective-permute-start(bf16[576,256]{1,0:T(8,128)(2,1)S(1)} %maximum_select_fusion.2), channel_id=1, source_target_pairs={{0,2},{1,3},{2,0},{3,1},{4,6},{5,7},{6,4},{7,5},{8,10},{9,11},{10,... | collective-permute-start | bytes 884744 | tf_op jit(solution)/shard_map/ppermute | solution.py:35
  109.3 15.5 %collective-permute-start.37 = (bf16[576,256]{1,0:T(8,128)(2,1)S(1)}, bf16[576,256]{1,0:T(8,128)(2,1)S(1)}, u32[]{:S(2)}, u32[]{:S(2)}) collective-permute-start(bf16[576,256]{1,0:T(8,128)(2,1)S(1)} %maximum_select_fusion.2), channel_id=1, source_target_pairs={{0,1},{1,0},{2,3},{3,2},{4,5},{5,4},{6,7},{7,6},{8,9},{9,8},{10,11... | collective-permute-start | bytes 884744 | tf_op jit(solution)/shard_map/ppermute | solution.py:35
  109.4 15.3 %collective-permute-start.33 = (bf16[576,256]{1,0:T(8,128)(2,1)S(1)}, bf16[576,256]{1,0:T(8,128)(2,1)S(1)}, u32[]{:S(2)}, u32[]{:S(2)}) collective-permute-start(bf16[576,256]{1,0:T(8,128)(2,1)S(1)} %maximum_select_fusion.1), channel_id=1, source_target_pairs={{0,2},{1,3},{2,0},{3,1},{4,6},{5,7},{6,4},{7,5},{8,10},{9,11},{10,... | collective-permute-start | bytes 884744 | tf_op jit(solution)/shard_map/ppermute | solution.py:35
  111.8 16.3 %collective-permute-start.25 = (bf16[576,256]{1,0:T(8,128)(2,1)S(1)}, bf16[576,256]{1,0:T(8,128)(2,1)S(1)}, u32[]{:S(2)}, u32[]{:S(2)}) collective-permute-start(bf16[576,256]{1,0:T(8,128)(2,1)S(1)} %maximum_select_fusion), channel_id=1, source_target_pairs={{0,2},{1,3},{2,0},{3,1},{4,6},{5,7},{6,4},{7,5},{8,10},{9,11},{10,... | collective-permute-start | bytes 884744 | tf_op jit(solution)/shard_map/ppermute | solution.py:35
  118.4 9.7 %collective-permute-start.38 = (bf16[576,256]{1,0:T(8,128)(2,1)S(1)}, bf16[576,256]{1,0:T(8,128)(2,1)S(1)}, u32[]{:S(2)}, u32[]{:S(2)}) collective-permute-start(bf16[576,256]{1,0:T(8,128)(2,1)S(1)} %collective-permute-done.36), channel_id=1, source_target_pairs={{0,1},{1,0},{2,3},{3,2},{4,5},{5,4},{6,7},{7,6},{8,9},{9,8},{10,11... | collective-permute-start | bytes 884744 | tf_op jit(solution)/shard_map/ppermute | solution.py:35
  118.4 10.8 %collective-permute-start.34 = (bf16[576,256]{1,0:T(8,128)(2,1)S(1)}, bf16[576,256]{1,0:T(8,128)(2,1)S(1)}, u32[]{:S(2)}, u32[]{:S(2)}) collective-permute-start(bf16[576,256]{1,0:T(8,128)(2,1)S(1)} %maximum_select_fusion.1), channel_id=1, source_target_pairs={{0,1},{1,0},{2,3},{3,2},{4,5},{5,4},{6,7},{7,6},{8,9},{9,8},{10,11... | collective-permute-start | bytes 884744 | tf_op jit(solution)/shard_map/ppermute | solution.py:35
  (34 other events, 258.4 us)

commit v8 on v7

v8 whole, which is shorter than its diff:
```python
import functools

import jax
import jax.numpy as jnp
from jax import lax
from jax.experimental import pallas as pl
from jax.experimental.pallas import tpu as pltpu
from jax.sharding import PartitionSpec as P

EXTRA = 16


def params(mebibytes=6):
    return pltpu.CompilerParams(vmem_limit_bytes=mebibytes * 1024 * 1024)


def cost(flops, bytes_accessed):
    return pl.CostEstimate(flops=flops, bytes_accessed=bytes_accessed, transcendentals=0)


def near(x):
    return pltpu.with_memory_space_constraint(x, pltpu.VMEM)


def far(x):
    return pltpu.with_memory_space_constraint(x, pltpu.HBM)


SCALARS = pl.BlockSpec(memory_space=pltpu.SMEM)
WHOLE = pl.BlockSpec(memory_space=pltpu.VMEM)
FAR = pl.BlockSpec(memory_space=pl.ANY)


def swap(x, size, bit):
    return lax.ppermute(x, "zslab", [(i, i ^ bit) for i in range(size)])


def rotate(x, size, steps):
    return lax.ppermute(x, "zslab", [(i, (i + 4 * steps) % size) for i in range(size)])


def me():
    return lax.axis_index("zslab")


def units(outer):
    return -(-108 // outer)


def mask_rows(voxmask, z):
    lanes = slice(64 * z, 64 * z + 64)
    line = jnp.concatenate([voxmask[0:1, lanes], voxmask[1:2, lanes]], axis=1)
    return jnp.broadcast_to((line == 1).astype(jnp.float32), (128, 128)).T


def wide(mask):
    return jnp.concatenate([mask, mask], axis=1) > 0


def both(ref, z):
    return jnp.concatenate([ref[0, z], ref[1, z]], axis=0)


def inside(shape, dim, rows, cols):
    index = lax.broadcasted_iota(jnp.int32, shape, dim)
    row = (index // 8) % 8 + rows
    col = index % 8 + cols
    return (row >= 0) & (row < 8) & (col >= 0) & (col < 8)


def windows(shape, dim):
    return [inside(shape, dim, p, q) for p in (-1, 0, 1) for q in (-1, 0, 1)]


def shifts(x, dim, valid, sign=1):
    count = x.shape[dim]
    moved = []
    for place in range(9):
        at = place if sign == 1 else 8 - place
        move = 8 * (at // 3 - 1) + at % 3 - 1
        turned = pltpu.roll(x, (-move) % count, dim) if move else x
        moved.append(jnp.where(valid[at], turned, 0.0).astype(jnp.bfloat16))
    return moved


def activate(pre, cotangent, keep):
    sigma = 1.0 / (1.0 + jnp.exp(-pre))
    out = jnp.where(keep, pre * sigma, 0.0)
    grad = jnp.where(keep, cotangent * sigma * (1.0 + pre * (1.0 - sigma)), 0.0)
    return out.astype(jnp.bfloat16), grad.astype(jnp.bfloat16)


def write_exact(rows, ref):
    high = rows.astype(jnp.bfloat16)
    left = rows - high.astype(jnp.float32)
    middle = left.astype(jnp.bfloat16)
    low = (left - middle.astype(jnp.float32)).astype(jnp.bfloat16)
    zeros = jnp.zeros((EXTRA - 3, rows.shape[1]), jnp.float32)
    terms = [term.astype(jnp.float32) for term in (high, middle, low)]
    ref[256:272, :] = jnp.concatenate(terms + [zeros], axis=0).astype(jnp.bfloat16)


def read_extra(ref):
    return jnp.sum(ref[256:272, :].astype(jnp.float32), axis=0, keepdims=True)


def rims_kernel(links, feats, voxmask, parcel, planes, masks, codes, done):
    width = feats.shape[3]
    copies = [
        pltpu.make_async_copy(feats.at[:, pl.ds(0, 1)], planes.at[0], done.at[0]),
        pltpu.make_async_copy(feats.at[:, pl.ds(7, 1)], planes.at[1], done.at[1]),
        pltpu.make_async_copy(voxmask, masks, done.at[2]),
        pltpu.make_async_copy(links, codes, done.at[3]),
    ]
    for copy in copies:
        copy.start()
    for copy in copies:
        copy.wait()
    for side in range(2):
        keep = wide(mask_rows(masks, 7 * side))
        plane = jnp.concatenate([planes[side, 0, 0], planes[side, 1, 0]], axis=0).astype(jnp.float32)
        parcel[128 * side : 128 * side + 128, :] = jnp.where(keep, plane, 0.0).astype(jnp.bfloat16)
    lane = lax.broadcasted_iota(jnp.int32, (EXTRA, width), 1)
    row = jnp.zeros((EXTRA, width), jnp.float32)
    for place in range(4):
        row = jnp.where(lane == place, codes[place // 2, place % 2].astype(jnp.float32), row)
    parcel[256:272, :] = row.astype(jnp.bfloat16)


def rims(links, feats, voxmask):
    width = feats.shape[3]
    return pl.pallas_call(
        rims_kernel,
        in_specs=[FAR] * 3,
        out_specs=WHOLE,
        out_shape=pltpu.VMEM((256 + EXTRA, width), jnp.bfloat16),
        scratch_shapes=[
            pltpu.VMEM((2, 2, 1, 64, width), jnp.bfloat16),
            pltpu.VMEM(voxmask.shape, jnp.int32),
            pltpu.SMEM(links.shape, jnp.int32),
            pltpu.SemaphoreType.DMA((4,)),
        ],
        compiler_params=params(),
        cost_estimate=cost(1024, 1024),
        name="rims",
    )(far(links), far(feats), far(voxmask))


def fetch_taps(weight, near_weight, done):
    for tap in range(weight.shape[0]):
        pltpu.make_async_copy(weight.at[tap], near_weight.at[tap], done.at[tap]).start()


def await_taps(first, last, weight, near_weight, done):
    for tap in range(first, last):
        pltpu.make_async_copy(weight.at[tap], near_weight.at[tap], done.at[tap]).wait()


def aligned(index, rows):
    return pl.ds(pl.multiple_of(index * rows, rows), rows)


def quarters(flip, own, give_inner, give_core):
    position = me() % 4
    rows = flip.shape[0] // 4
    if own is not None:
        own[...] = flip[aligned(position, rows), :].astype(own.dtype)
    give_inner[...] = flip[aligned(1 - position // 2, 2 * rows), :].astype(jnp.bfloat16)
    give_core[...] = flip[aligned(position // 2 * 2 + 1 - position % 2, rows), :].astype(jnp.bfloat16)


def turn_rows(flip, lanes, valid, turned, first):
    rows = flip.shape[0]
    for place, moved in enumerate(shifts(flip[:, lanes].astype(jnp.float32), 1, valid)):
        turned[first + place * rows : first + (place + 1) * rows, lanes] = moved


def prepare_kernel(
    feats, voxmask, weight, cotangent, mask, rows, give_inner, give_core, turned, taps, slopes, planes, masks, flip, own, done, fetched
):
    count = weight.shape[0]
    pltpu.make_async_copy(voxmask, masks, done.at[8]).start()
    for z in range(8):
        pltpu.make_async_copy(feats.at[:, pl.ds(z, 1)], planes.at[:, pl.ds(z, 1)], done.at[z]).start()
    fetch_taps(weight, taps, fetched)
    for z in range(8):
        pltpu.make_async_copy(cotangent.at[:, pl.ds(z, 1)], slopes.at[:, pl.ds(z, 1)], fetched.at[count + z]).start()
    valid = windows((own.shape[0], 128), 1)
    pltpu.make_async_copy(voxmask, masks, done.at[8]).wait()
    for z in range(8):
        pltpu.make_async_copy(feats.at[:, pl.ds(z, 1)], planes.at[:, pl.ds(z, 1)], done.at[z]).wait()
        span = slice(128 * z, 128 * z + 128)
        keep = mask_rows(masks, z)
        mask[span, :] = keep
        plane = jnp.where(wide(keep), both(planes, z).astype(jnp.float32), 0.0)
        rows[span, :] = plane.astype(jnp.bfloat16)
        flip[:, span] = plane.T
    quarters(flip, own, give_inner, give_core)
    for z in range(8):
        turn_rows(own, slice(128 * z, 128 * z + 128), valid, turned, 0)
    await_taps(0, count, weight, taps, fetched)
    for z in range(8):
        pltpu.make_async_copy(cotangent.at[:, pl.ds(z, 1)], slopes.at[:, pl.ds(z, 1)], fetched.at[count + z]).wait()


def prepare(feats, voxmask, weight, cotangent):
    width = feats.shape[3]
    quarter = width // 4
    return pl.pallas_call(
        prepare_kernel,
        in_specs=[FAR] * 4,
        out_specs=(WHOLE,) * 7,
        out_shape=(
            pltpu.VMEM((1024, 128), jnp.float32),
            pltpu.VMEM((1024, width), jnp.bfloat16),
            pltpu.VMEM((2 * quarter, 1024), jnp.bfloat16),
            pltpu.VMEM((quarter, 1024), jnp.bfloat16),
            pltpu.VMEM((9 * quarter, 1024), jnp.bfloat16),
            pltpu.VMEM(weight.shape, jnp.bfloat16),
            pltpu.VMEM(cotangent.shape, jnp.bfloat16),
        ),
        scratch_shapes=[
            pltpu.VMEM(feats.shape, jnp.bfloat16),
            pltpu.VMEM(voxmask.shape, jnp.int32),
            pltpu.VMEM((width, 1024), jnp.float32),
            pltpu.VMEM((quarter, 1024), jnp.float32),
            pltpu.SemaphoreType.DMA((9,)),
            pltpu.SemaphoreType.DMA((weight.shape[0] + 8,)),
        ],
        compiler_params=params(12),
        cost_estimate=cost(1024, 1024),
        name="prepare",
    )(far(feats), far(voxmask), far(weight), far(cotangent))


def turn_kernel(inner, core, both_changed, turned):
    quarter = core.shape[0]
    valid = windows((quarter, 128), 1)
    mine = aligned(me() % 2, quarter)
    for z in range(8):
        lanes = slice(128 * z, 128 * z + 128)
        for index, rows in enumerate((inner[mine, lanes], core[:, lanes], both_changed[mine, lanes])):
            first = 9 * quarter * index
            for place, moved in enumerate(shifts(rows.astype(jnp.float32), 1, valid)):
                turned[first + place * quarter : first + (place + 1) * quarter, lanes] = moved


def turn(inner, core, both_changed):
    quarter = core.shape[0]
    return pl.pallas_call(
        turn_kernel,
        in_specs=[WHOLE] * 3,
        out_specs=WHOLE,
        out_shape=pltpu.VMEM((27 * quarter, 1024), jnp.bfloat16),
        compiler_params=params(10),
        cost_estimate=cost(1024, 1024),
        name="turn",
    )(near(inner), near(core), near(both_changed))


def copy_picks(outer, table, parcels, picks, planes):
    for dev in range(4):
        planes[256 * dev : 256 * dev + 256, :] = parcels[dev][:256, :]
    for steps in range(outer):
        for slot in range(4):
            start = pl.multiple_of(table[steps * 4 + slot] * 64, 64)
            picks[steps][64 * slot : 64 * slot + 64, :] = planes[pl.ds(start, 64), :]


def route_kernel(outer, *refs):
    position = me()
    parcels, (table, *picks), (codes, links, planes, done) = refs[:4], refs[4:-4], refs[-4:]
    for dev in range(4):
        row = parcels[dev][256:272, :128].astype(jnp.float32)
        codes[8 * dev : 8 * dev + 8, :] = row[:8, :].astype(jnp.int32)
    copy = pltpu.make_async_copy(codes, links, done)
    copy.start()
    copy.wait()
    for place in range(outer * 4):
        table[place] = 0
    for plane in range(16):
        dev, side, brick = plane // 4, plane // 2 % 2, plane % 2
        dest = links[dev * 8, brick * 2 + side]

        @pl.when((dest >= 0) & ((dest // 2) % 4 == position % 4))
        def _():
            steps = lax.rem(dest // 8 - position // 4 + outer, outer)
            table[steps * 4 + dest % 2 + (0 if side == 1 else 2)] = plane

    for brick in range(2):
        for side in range(2):
            dest = links[0, brick * 2 + side]
            steps = lax.rem(position // 4 - dest // 8 + outer, outer)
            table[outer * 4 + 2 * side + brick] = jnp.where(dest >= 0, steps, -1)

    copy_picks(outer, table, parcels, picks, planes)


def route(parcels, outer):
    width = parcels[0].shape[1]
    results = pl.pallas_call(
        functools.partial(route_kernel, outer),
        in_specs=[WHOLE] * 4,
        out_specs=[SCALARS] + [WHOLE] * outer,
        out_shape=[jax.ShapeDtypeStruct((outer * 4 + 4,), jnp.int32)]
        + [pltpu.VMEM((256, width), jnp.bfloat16)] * outer,
        scratch_shapes=[
            pltpu.VMEM((32, 128), jnp.int32),
            pltpu.SMEM((32, 128), jnp.int32),
            pltpu.VMEM((1024, width), jnp.bfloat16),
            pltpu.SemaphoreType.DMA(()),
        ],
        compiler_params=params(),
        cost_estimate=cost(1024, 1024),
        name="route",
    )(*[near(x) for x in parcels])
    return results[0], results[1:]


def repeat_kernel(outer, table, *refs):
    parcels, picks, planes = refs[:4], refs[4:-1], refs[-1]
    copy_picks(outer, table, parcels, picks, planes)
    total = sum(read_extra(ref) for ref in parcels)
    for ref in picks:
        write_exact(total, ref)


def repeat_route(table, parcels, outer):
    width = parcels[0].shape[1]
    return pl.pallas_call(
        functools.partial(repeat_kernel, outer),
        in_specs=[SCALARS] + [WHOLE] * 4,
        out_specs=[WHOLE] * outer,
        out_shape=[pltpu.VMEM((256 + EXTRA, width), jnp.bfloat16)] * outer,
        scratch_shapes=[pltpu.VMEM((1024, width), jnp.bfloat16)],
        compiler_params=params(),
        cost_estimate=cost(1024, 1024),
        name="repeat_route",
    )(table, *[near(x) for x in parcels])


def chosen(table, slot, arrived):
    rows = slice(64 * slot, 64 * slot + 64)
    plane = jnp.zeros((64, arrived[0].shape[1]), jnp.float32)
    for steps, ref in enumerate(arrived):
        plane = jnp.where(table[4 * len(arrived) + slot] == steps, ref[rows, :].astype(jnp.float32), plane)
    return plane


def forward_kernel(rows, mask, weight, bias, slopes, out, grad, edge, bias_sum, cols, pre):
    width = rows.shape[1]
    valid = windows((128, width), 0)
    for z in range(8):
        span = slice(128 * z, 128 * z + 128)
        for place, moved in enumerate(shifts(rows[span, :].astype(jnp.float32), 0, valid)):
            cols[span, place * width : (place + 1) * width] = moved

    def taps(a):
        return weight[9 * a : 9 * a + 9].reshape(9 * width, width)

    pre[...] = jnp.dot(cols[...], taps(1), preferred_element_type=jnp.float32) + bias[...]
    pre[128:, :] += jnp.dot(cols[:896, :], taps(0), preferred_element_type=jnp.float32)
    pre[:896, :] += jnp.dot(cols[128:, :], taps(2), preferred_element_type=jnp.float32)
    for side in range(2):
        edge[side] = pre[896 * side : 896 * side + 128, :]
    total = jnp.zeros((1, width), jnp.float32)
    for z in range(1, 7):
        span = slice(128 * z, 128 * z + 128)
        act, slope = activate(pre[span, :], both(slopes, z).astype(jnp.float32), wide(mask[span, :]))
        for b in range(2):
            out[b, z] = act[64 * b : 64 * b + 64]
        grad[128 * (z - 1) : 128 * z, :] = slope
        total += jnp.sum(slope.astype(jnp.float32), axis=0, keepdims=True)
    bias_sum[...] = total


def forward_inside(rows, mask, weight, bias, cotangent):
    width = rows.shape[1]
    return pl.pallas_call(
        forward_kernel,
        in_specs=[WHOLE] * 5,
        out_specs=(WHOLE,) * 4,
        out_shape=(
            jax.ShapeDtypeStruct(cotangent.shape, jnp.bfloat16),
            pltpu.VMEM((768, width), jnp.bfloat16),
            pltpu.VMEM((2, 128, width), jnp.float32),
            pltpu.VMEM((1, width), jnp.float32),
        ),
        scratch_shapes=[
            pltpu.VMEM((1024, 9 * width), jnp.bfloat16),
            pltpu.VMEM((1024, width), jnp.float32),
        ],
        compiler_params=params(12),
        cost_estimate=cost(1024, 1024),
        name="forward_inside",
    )(near(rows), near(mask), near(weight), bias, near(cotangent))


def inner_terms_kernel(mine, others, *refs):
    grads, terms = refs[:4], refs[4]
    rows = mine.shape[0]
    for a in range(3):
        lanes = slice(128 * a, 128 * a + 768)
        total = jnp.dot(mine[:, lanes], grads[0][...], preferred_element_type=jnp.float32)
        for index in range(3):
            total += jnp.dot(
                others[index * rows : (index + 1) * rows, lanes], grads[index + 1][...], preferred_element_type=jnp.float32
            )
        terms[a * rows : (a + 1) * rows, :] = total


def inner_terms(mine, others, grads):
    rows, width = mine.shape[0], grads[0].shape[1]
    return pl.pallas_call(
        inner_terms_kernel,
        in_specs=[WHOLE] * 6,
        out_specs=WHOLE,
        out_shape=pltpu.VMEM((3 * rows, width), jnp.float32),
        compiler_params=params(10),
        cost_estimate=cost(1024, 1024),
        name="inner_terms",
    )(near(mine), near(others), *[near(x) for x in grads])


def edge_kernel(table, mask, weight, edge, ends, inner, out_in, *refs):
    arrived, (out, to_inner, to_core, own, planes, flip, done) = refs[:-7], refs[-7:]
    width = edge.shape[2]
    valid = windows((128, width), 0)
    total = inner[...]
    for side in range(2):
        rows = slice(128 * side, 128 * side + 128)
        halo = jnp.concatenate([chosen(table, 2 * side + b, arrived) for b in range(2)], axis=0)
        flip[:, rows] = halo.T
        cols = jnp.concatenate(shifts(halo, 0, valid), axis=1)
        taps = weight[18 * side : 18 * side + 9].reshape(9 * width, width)
        pre = edge[side] + jnp.dot(cols, taps, preferred_element_type=jnp.float32)
        z = 7 * side
        keep = wide(mask[128 * z : 128 * z + 128, :])
        act, slope = activate(pre, both(ends, z).astype(jnp.float32), keep)
        for b in range(2):
            planes[side, b, 0] = act[64 * b : 64 * b + 64]
        pltpu.make_async_copy(planes.at[side], out.at[:, pl.ds(z, 1)], done.at[side]).start()
        to_inner[rows, :] = slope
        to_core[rows, :] = slope
        total += jnp.sum(slope.astype(jnp.float32), axis=0, keepdims=True)
    write_exact(total, to_inner)
    write_exact(total, to_core)
    quarters(flip, own, to_inner.at[272:], to_core.at[272:])
    for side in range(2):
        pltpu.make_async_copy(planes.at[side], out.at[:, pl.ds(7 * side, 1)], done.at[side]).wait()


def forward_edges(table, mask, weight, edge, ends, inner, out, arrived):
    width = edge.shape[2]
    quarter = width // 4
    return pl.pallas_call(
        edge_kernel,
        in_specs=[SCALARS] + [WHOLE] * 5 + [FAR] + [WHOLE] * len(arrived),
        out_specs=(FAR, WHOLE, WHOLE, WHOLE),
        out_shape=(
            jax.ShapeDtypeStruct(out.shape, out.dtype),
            pltpu.VMEM((256 + EXTRA + 2 * quarter, width), jnp.bfloat16),
            pltpu.VMEM((256 + EXTRA + quarter, width), jnp.bfloat16),
            pltpu.VMEM((quarter, 256), jnp.bfloat16),
        ),
        scratch_shapes=[
            pltpu.VMEM((2, 2, 1, 64, width), jnp.bfloat16),
            pltpu.VMEM((width, 256), jnp.float32),
            pltpu.SemaphoreType.DMA((2,)),
        ],
        input_output_aliases={6: 0},
        compiler_params=params(10),
        cost_estimate=cost(1024, 1024),
        name="forward_edges",
    )(
        table,
        near(mask),
        near(weight),
        near(edge),
        near(ends),
        near(inner),
        out,
        *[near(x) for x in arrived],
    )


def outer_terms_kernel(outer, mine, others, halos, *refs):
    parcels, inner = refs[:4], refs[4]
    gives, stay, cols, total = refs[5 : 4 + outer], refs[4 + outer], refs[5 + outer], refs[6 + outer]
    quarter = halos.shape[0]
    rows = 9 * quarter
    valid = windows((quarter, 128), 1)
    half = aligned(me() % 2, quarter)
    ends = (
        halos,
        parcels[1].at[272 : 272 + 2 * quarter].at[half],
        parcels[2].at[272 : 272 + quarter],
        parcels[3].at[272 : 272 + 2 * quarter].at[half],
    )
    facing = jnp.concatenate(
        [parcel[128 * side : 128 * side + 128, :] for side in range(2) for parcel in parcels], axis=0
    )
    for a in range(3):
        for side in range(2):
            plane = a - 1 + 7 * side
            for who in range(4):
                lanes = slice(128 * (4 * side + who), 128 * (4 * side + who) + 128)
                if 0 <= plane < 8:
                    ref, first = (mine, 0) if who == 0 else (others, rows * (who - 1))
                    cols[:, lanes] = ref[first : first + rows, 128 * plane : 128 * plane + 128]
                else:
                    moved = shifts(ends[who][:, 128 * side : 128 * side + 128].astype(jnp.float32), 1, valid)
                    for place in range(9):
                        cols[place * quarter : (place + 1) * quarter, lanes] = moved[place]
        span = slice(a * rows, (a + 1) * rows)
        total[span, :] = inner[span, :] + jnp.dot(cols[...], facing, preferred_element_type=jnp.float32)
    if total.shape[0] > 3 * rows:
        total[3 * rows :, :] = jnp.zeros((total.shape[0] - 3 * rows, total.shape[1]), jnp.float32)
    z = me() // 4
    for steps in range(outer):
        block = lax.rem(z + steps, outer)
        for unit in range(units(outer)):
            piece = total[aligned(block + outer * unit, 16), :]
            if steps:
                gives[steps - 1][16 * unit : 16 * unit + 16, :] = piece.astype(jnp.bfloat16)
            else:
                stay[16 * unit : 16 * unit + 16, :] = piece


def outer_terms(outer, mine, others, halos, parcels, inner):
    width = inner.shape[1]
    rows = 16 * units(outer)
    results = pl.pallas_call(
        functools.partial(outer_terms_kernel, outer),
        in_specs=[WHOLE] * 8,
        out_specs=[WHOLE] * outer,
        out_shape=[pltpu.VMEM((rows, width), jnp.bfloat16)] * (outer - 1) + [pltpu.VMEM((rows, width), jnp.float32)],
        scratch_shapes=[
            pltpu.VMEM((inner.shape[0] // 3, 1024), jnp.bfloat16),
            pltpu.VMEM((outer * rows, width), jnp.float32),
        ],
        compiler_params=params(12),
        cost_estimate=cost(1024, 1024),
        name="outer_terms",
    )(*[near(x) for x in (mine, others, halos, *parcels, inner)])
    return results[:-1], results[-1]


def backward_kernel(grad, parcel, mask, weight, grad_feats, partial, cols, total, near_weight, fetched):
    width = grad.shape[1]
    fetch_taps(weight, near_weight, fetched)
    valid = windows((128, width), 0)
    planes = [parcel[:128, :]] + [grad[128 * z : 128 * z + 128, :] for z in range(6)] + [parcel[128:256, :]]
    for z, plane in enumerate(planes):
        for at, moved in enumerate(shifts(plane.astype(jnp.float32), 0, valid, -1)):
            cols[128 * z : 128 * z + 128, at * width : (at + 1) * width] = moved
    for a in (1, 0, 2):
        await_taps(9 * a, 9 * a + 9, weight, near_weight, fetched)
        first, start, count = ((128, 0, 896), (0, 0, 1024), (0, 128, 896))[a]
        for at in range(9):
            piece = lax.dot_general(
                cols[first : first + count, at * width : (at + 1) * width],
                near_weight[9 * a + at],
                (((1,), (1,)), ((), ())),
                preferred_element_type=jnp.float32,
            )
            if a == 1 and at == 0:
                total[...] = piece
            else:
                total[start : start + count, :] += piece
    for z in range(1, 7):
        rows = slice(128 * z, 128 * z + 128)
        done = jnp.where(wide(mask[rows, :]), total[rows, :], 0.0).astype(jnp.bfloat16)
        for b in range(2):
            grad_feats[b, z] = done[64 * b : 64 * b + 64]
    for side in range(2):
        partial[side] = total[896 * side : 896 * side + 128, :]


def backward(grad, parcel, mask, weight):
    width = grad.shape[1]
    return pl.pallas_call(
        backward_kernel,
        in_specs=[WHOLE] * 3 + [FAR],
        out_specs=(WHOLE, WHOLE),
        out_shape=(jax.ShapeDtypeStruct((2, 8, 64, width), jnp.bfloat16), pltpu.VMEM((2, 128, width), jnp.float32)),
        scratch_shapes=[
            pltpu.VMEM((1024, 9 * width), jnp.bfloat16),
            pltpu.VMEM((1024, width), jnp.float32),
            pltpu.VMEM(weight.shape, jnp.bfloat16),
            pltpu.SemaphoreType.DMA((weight.shape[0],)),
        ],
        compiler_params=params(16),
        cost_estimate=cost(1024, 1024),
        name="backward",
    )(near(grad), near(parcel), near(mask), far(weight))


def backward_halos_kernel(table, partial, mask, weight, done, *refs):
    arrived, (grad_feats, bias_sum, planes, near_weight, fetched, sent) = refs[:-6], refs[-6:]
    width = weight.shape[1]
    fetch_taps(weight, near_weight, fetched)
    valid = windows((128, width), 0)
    await_taps(0, weight.shape[0], weight, near_weight, fetched)
    for side in range(2):
        halo = jnp.concatenate([chosen(table, 2 * side + b, arrived) for b in range(2)], axis=0)
        total = partial[side]
        for at, moved in enumerate(shifts(halo, 0, valid, -1)):
            total += lax.dot_general(
                moved,
                near_weight[18 * (1 - side) + at],
                (((1,), (1,)), ((), ())),
                preferred_element_type=jnp.float32,
            )
        rows = slice(896 * side, 896 * side + 128)
        done_rows = jnp.where(wide(mask[rows, :]), total, 0.0).astype(jnp.bfloat16)
        for b in range(2):
            planes[side, b, 0] = done_rows[64 * b : 64 * b + 64]
        pltpu.make_async_copy(planes.at[side], grad_feats.at[:, pl.ds(7 * side, 1)], sent.at[side]).start()
    bias_sum[...] = sum(read_extra(ref) for ref in arrived)
    for side in range(2):
        pltpu.make_async_copy(planes.at[side], grad_feats.at[:, pl.ds(7 * side, 1)], sent.at[side]).wait()


def backward_halos(table, partial, mask, weight, done, arrived):
    width = weight.shape[1]
    return pl.pallas_call(
        backward_halos_kernel,
        in_specs=[SCALARS, WHOLE, WHOLE, FAR, FAR] + [WHOLE] * len(arrived),
        out_specs=(FAR, WHOLE),
        out_shape=(jax.ShapeDtypeStruct(done.shape, done.dtype), jax.ShapeDtypeStruct((1, width), jnp.float32)),
        scratch_shapes=[
            pltpu.VMEM((2, 2, 1, 64, width), jnp.bfloat16),
            pltpu.VMEM(weight.shape, jnp.bfloat16),
            pltpu.SemaphoreType.DMA((weight.shape[0],)),
            pltpu.SemaphoreType.DMA((2,)),
        ],
        input_output_aliases={4: 0},
        compiler_params=params(10),
        cost_estimate=cost(1024, 1024),
        name="backward_halos",
    )(table, near(partial), near(mask), far(weight), done, *[near(x) for x in arrived])


def assemble_kernel(outer, places, *refs):
    parts, (out, done) = refs[: len(places)], refs[-2:]
    position = me()
    copies = []
    for index, (ref, (steps, inner, core)) in enumerate(zip(parts, places)):
        block = lax.rem(position // 4 - steps + outer, outer)
        quarter = 4 * ((position % 4) ^ (2 * inner + core))
        if outer == 4:
            copies.append((None, pltpu.make_async_copy(ref, out.at[:, quarter + block], done.at[index, 0])))
            continue
        for unit in range(units(outer)):
            place = block + outer * unit
            here = jnp.minimum(place, 107)
            target = out.at[here // 4, quarter + here % 4]
            copies.append((place < 108, pltpu.make_async_copy(ref.at[unit], target, done.at[index, unit])))
    for wait in (False, True):
        for condition, copy in copies:
            act = copy.wait if wait else copy.start
            if condition is None:
                act()
            else:
                pl.when(condition)(act)


def assemble(outer, places, parts, shape, given):
    before = [] if given is None else [given]
    rows = units(outer)
    return pl.pallas_call(
        functools.partial(assemble_kernel, outer, places),
        in_specs=[WHOLE] * len(parts) + [FAR] * len(before),
        out_specs=FAR,
        out_shape=jax.ShapeDtypeStruct(shape, jnp.bfloat16),
        scratch_shapes=[pltpu.SemaphoreType.DMA((len(parts), rows))],
        input_output_aliases={len(parts): 0} if before else {},
        compiler_params=params(),
        cost_estimate=cost(1024, 1024),
        name="assemble",
    )(*[near(x.reshape(rows, 16, shape[-1])) for x in parts], *before)


def per_device(size, feats, voxmask, links, weight, bias, cotangent):
    width = feats.shape[3]
    outer = size // 4

    parcel = rims(links, feats, voxmask)
    mask, rows, give_inner, give_core, turned, taps, ends = prepare(feats, voxmask, weight, cotangent)
    inner, rows = lax.optimization_barrier((swap(parcel, size, 2), rows))
    parcels = [parcel, inner, swap(parcel, size, 1), swap(inner, size, 1)]
    out, grad, edge, bias_local = forward_inside(rows, mask, taps, bias.reshape(1, width), ends)
    *parcels, grad = lax.optimization_barrier((*parcels, grad))
    table, picks = route(parcels, outer)

    *picks, give_inner, give_core = lax.optimization_barrier((*picks, give_inner, give_core))
    arrived = [rotate(pick, size, steps) if steps else pick for steps, pick in enumerate(picks)]
    got_inner, grad_inner = swap(give_inner, size, 2), swap(grad, size, 2)
    *arrived, got_inner, grad_inner = lax.optimization_barrier((*arrived, got_inner, grad_inner))
    others = turn(got_inner, swap(give_core, size, 1), swap(got_inner, size, 1))
    grads = [grad, grad_inner, swap(grad, size, 1), swap(grad_inner, size, 1)]

    out, to_inner, to_core, halos = forward_edges(table, mask, taps, edge, ends, bias_local, out, arrived)
    inner = swap(to_inner, size, 2)
    terms = inner_terms(turned, others, grads)
    inner, terms = lax.optimization_barrier((inner, terms))
    parcels = [to_inner, inner, swap(to_core, size, 1), swap(inner, size, 1)]

    gives, stay = outer_terms(outer, turned, others, halos, parcels, terms)
    gots = [rotate(give, size, steps + 1) for steps, give in enumerate(gives)]
    grad_feats, partial = backward(grad, to_inner, mask, weight)
    picks = repeat_route(table, parcels, outer)
    stay, partial, *picks = lax.optimization_barrier((stay, partial, *picks))
    part = (stay + sum(got.astype(jnp.float32) for got in gots)).astype(jnp.bfloat16)

    blocks = {(0, 0): part, (0, 1): swap(part, size, 2)}
    later, blocks[0, 1] = lax.optimization_barrier((part, blocks[0, 1]))
    for steps in [k for k in range(1, outer) if k in (1, outer - 1)] + list(range(2, outer - 1)):
        blocks[steps, 0] = rotate(part if steps in (1, outer - 1) else later, size, steps)
        blocks[steps, 1] = swap(blocks[steps, 0], size, 2)
    blocks[1, 1], *picks = lax.optimization_barrier((blocks[1, 1], *picks))
    arrived = [rotate(pick, size, steps) if steps else pick for steps, pick in enumerate(picks)]
    grad_feats, grad_bias = backward_halos(table, partial, mask, weight, grad_feats, arrived)

    early = [(0, 0), (0, 1), (1, 0), (outer - 1, 0)]
    grad_weight = None
    for chosen_blocks in (early, [key for key in blocks if key not in early]):
        places = [(steps, bit, core) for core in range(2) for steps, bit in chosen_blocks]
        parts = [blocks[key] for key in chosen_blocks]
        parts += [swap(x, size, 1) for x in parts]
        grad_weight = assemble(outer, places, parts, (27, 16, width // 16, width), grad_weight)
    return out, grad_feats, grad_weight.reshape(weight.shape), grad_bias.reshape(width)


def solution(mesh):
    return jax.shard_map(
        functools.partial(per_device, mesh.shape["zslab"]),
        mesh=mesh,
        in_specs=(
            P(("groups", "zslab"), None, None, None),
            P(("groups", "zslab"), None),
            P(("groups", "zslab"), None),
            P(),
            P(),
            P(("groups", "zslab"), None, None, None),
        ),
        out_specs=(
            P(("groups", "zslab"), None, None, None),
            P(("groups", "zslab"), None, None, None),
            P("groups", None, None),
            P("groups"),
        ),
        check_vma=False,
    )
```

time: 132 us -> 116 us (0.88)
  local copies, waits for them, and re-layouts: 7.88 us -> 0.01 us
  other arithmetic: 6.3 us -> 0.11 us
  Pallas kernels: 36.1 us -> 40.6 us
  starting transfers between devices: 39.4 us -> 35.3 us
  waiting for transfers between devices: 40.8 us -> 39.1 us
    ppermute x33 -> x24, waiting for transfers between devices: 39.9 us -> 4.18 us  [swap(): return lax.ppermute(x, 'zslab', [(i, i ^ bit) for i in range(size)])]
    ppermute x6 -> x12, waiting for transfers between devices: 0.83 us -> 34.9 us  [rotate(): lax.ppermute(x, 'zslab', [(i, (i + 4 * steps) % size) for i in range(size)])]
    ppermute x33 -> x24, starting transfers between devices: 30 us -> 13.1 us  [swap(): return lax.ppermute(x, 'zslab', [(i, i ^ bit) for i in range(size)])]
    ppermute x6 -> x12, starting transfers between devices: 9.34 us -> 22.2 us  [rotate(): lax.ppermute(x, 'zslab', [(i, (i + 4 * steps) % size) for i in range(size)])]
    unnamed x38 -> x2, local copies, waits for them, and re-layouts: 7.88 us -> 0.01 us
    convert_element_type x9 -> x1, other arithmetic: 5.84 us -> 0.11 us  [per_device(): (stay + sum((got.astype(jnp.float32) for got in gots))).astype(jnp.bfloat16)]
    pallas_call x11 -> x8, Pallas kernels: 25.4 us -> 30.6 us  [the longest x1 8.95 us: backward(): pl.pallas_call(backward_kernel, in_specs=[WHOLE] * 3 + [FAR], out_specs=(...]
  transfers between devices with their start and end apart: 39 -> 36, of which waited for: 12 -> 13; matrix products, arithmetic and copies ran while one was open for 5% -> 0% of each run, Pallas kernels for 23% -> 30%
where the time goes in v8:
time: 116 us
  Pallas kernels  40.6 us (35%)
  waiting for transfers between devices  39.1 us (34%)
  starting transfers between devices  35.3 us (30%)
    ppermute x12, waiting for transfers between devices, rotate(): lax.ppermute(x, 'zslab', [(i, (i + 4 * steps) % size) for i in range(size)])  34.9 us
    ppermute x12, starting transfers between devices, rotate(): lax.ppermute(x, 'zslab', [(i, (i + 4 * steps) % size) for i in range(size)])  22.2 us
    ppermute x24, starting transfers between devices, swap(): return lax.ppermute(x, 'zslab', [(i, i ^ bit) for i in range(size)])  13.1 us
    pallas_call x1, Pallas kernels, backward(): pl.pallas_call(backward_kernel, in_specs=[WHOLE] * 3 + [FAR], out_specs=(...  8.95 us
    pallas_call x2, Pallas kernels, assemble(): pl.pallas_call(functools.partial(assemble_kernel, outer, places), in_spec...  6.27 us
    pallas_call x1, Pallas kernels, backward_halos(): pl.pallas_call(backward_halos_kernel, in_specs=[SCALARS, WHOLE, WHOLE, FA...  4.95 us
    pallas_call x1, Pallas kernels, prepare(): pl.pallas_call(prepare_kernel, in_specs=[FAR] * 4, out_specs=(WHOLE,) * 7...  4.77 us
    pallas_call x1, Pallas kernels, forward_inside(): pl.pallas_call(forward_kernel, in_specs=[WHOLE] * 5, out_specs=(WHOLE,) *...  4.66 us
  transfers between devices with their start and end apart: 36, of which 13 were waited for; matrix products, arithmetic and copies ran while one was open for 0% of the time, Pallas kernels for 30%

profile of v8, /device:TPU:0, one launch (start us, length us, event | category | flops | bytes accessed | tf_op | source)
XLA Modules:
  0.0 116.1 jit_solution(12780840193834441124)
XLA Ops:
  1.7 3.0 %collective-permute-start = (bf16[272,256]{1,0:T(8,128)(2,1)S(1)}, bf16[272,256]{1,0:T(8,128)(2,1)S(1)}, u32[]{:S(2)}, u32[]{:S(2)}) collective-permute-start(bf16[272,256]{1,0:T(8,128)(2,1)S(1)} %rims.1.refs_0_), channel_id=1, source_target_pairs={{0,2},{1,3},{2,0},{3,1},{4,6},{5,7},{6,4},{7,5},{8,10},{9,11},{10,... | collective-permute-start | bytes 417800 | tf_op jit(solution)/shard_map/ppermute | solution.py:35
  4.8 4.8 %prepare.1 = (f32[1024,128]{1,0:T(8,128)S(1)}, bf16[1024,256]{1,0:T(8,128)(2,1)S(1)}, bf16[128,1024]{1,0:T(8,128)(2,1)S(1)}, bf16[64,1024]{1,0:T(8,128)(2,1)S(1)...) custom-call(bf16[2,8,64,256]{3,2,1,0:T(8,128)(2,1)} %feats.3, ...), custom_call_target="tpu_custom_call" | custom-call | flops 1024 | bytes 1024 | tf_op jit(solution)/shard_map/prepare/pallas_call | solution.py:209
  10.1 4.7 %forward_inside.1 = (bf16[2,8,64,256]{3,2,1,0:T(8,128)(2,1)}, bf16[768,256]{1,0:T(8,128)(2,1)S(1)}, f32[2,128,256]{2,1,0:T(8,128)S(1)}, f32[1,256]{1,0:T(1,128)S(1)}) custom-call(bf16[1024,256]{1,0:T(8,128)(2,1)S(1)} %get-tuple-element.72.rows, f32[1024,128]{1,0:T(8,128)S(1)} %get-tuple-element.73.mask, bf16[27,256,256]{2,1,0:T(8,128)(2,1)S(1)} %get-tuple-element.74.weight, ...), custom_call_target="tpu_custom_call" | custom-call | flops 1024 | bytes 1024 | tf_op jit(solution)/shard_map/forward_inside/pallas_call | solution.py:379
  14.9 1.7 %route.1 = (s32[20]{0:T(128)S(1)}, bf16[256,256]{1,0:T(8,128)(2,1)S(1)}, bf16[256,256]{1,0:T(8,128)(2,1)S(1)}, bf16[256,256]{1,0:T(8,128)(2,1)S(1)}, bf16[256,256]{1,0:T(8,128)(2,1)S(1)}) custom-call(bf16[272,256]{1,0:T(8,128)(2,1)S(1)} %rims.1.refs_0_, bf16[272,256]{1,0:T(8,128)(2,1)S(1)} %collective-permute-done.refs_1_, ...), custom_call_target="tpu_custom_call" | custom-call | flops 1024 | bytes 1024 | tf_op jit(solution)/shard_map/route/pallas_call | solution.py:301
  16.6 2.0 %collective-permute-start.6 = (bf16[128,1024]{1,0:T(8,128)(2,1)S(1)}, bf16[128,1024]{1,0:T(8,128)(2,1)S(1)}, u32[]{:S(2)}, u32[]{:S(2)}) collective-permute-start(bf16[128,1024]{1,0:T(8,128)(2,1)S(1)} %get-tuple-element.95), channel_id=1, source_target_pairs={{0,2},{1,3},{2,0},{3,1},{4,6},{5,7},{6,4},{7,5},{8,10},{9,11},{10,... | collective-permute-start | bytes 786440 | tf_op jit(solution)/shard_map/ppermute | solution.py:35
  20.2 2.6 %collective-permute-start.4 = (bf16[256,256]{1,0:T(8,128)(2,1)S(1)}, bf16[256,256]{1,0:T(8,128)(2,1)S(1)}, u32[]{:S(2)}, u32[]{:S(2)}) collective-permute-start(bf16[256,256]{1,0:T(8,128)(2,1)S(1)} %get-tuple-element.93), channel_id=1, source_target_pairs={{0,8},{1,9},{2,10},{3,11},{4,12},{5,13},{6,14},{7,15},{8,0},{9,1},... | collective-permute-start | bytes 393224 | tf_op jit(solution)/shard_map/ppermute | solution.py:39
  24.1 2.9 %collective-permute-done.3.refs_1_ = bf16[256,256]{1,0:T(8,128)(2,1)S(1)} collective-permute-done((bf16[256,256]{1,0:T(8,128)(2,1)S(1)}, bf16[256,256]{1,0:T(8,128)(2,1)S(1)}, u32[]{:S(2)}, u32[]{:S(2)}) %collective-permute-start.3) | collective-permute-done | bytes 131104 | tf_op jit(solution)/shard_map/ppermute | solution.py:39
  27.0 4.1 %collective-permute-done.4.refs_2_ = bf16[256,256]{1,0:T(8,128)(2,1)S(1)} collective-permute-done((bf16[256,256]{1,0:T(8,128)(2,1)S(1)}, bf16[256,256]{1,0:T(8,128)(2,1)S(1)}, u32[]{:S(2)}, u32[]{:S(2)}) %collective-permute-start.4) | collective-permute-done | bytes 131104 | tf_op jit(solution)/shard_map/ppermute | solution.py:39
  32.0 1.9 %forward_edges.1 = (bf16[2,8,64,256]{3,2,1,0:T(8,128)(2,1)}, bf16[400,256]{1,0:T(8,128)(2,1)S(1)}, bf16[336,256]{1,0:T(8,128)(2,1)S(1)}, bf16[64,256]{1,0:T(8,128)(2,1)S(1)}) custom-call(s32[20]{0:T(128)S(1)} %get-tuple-element.81.table, f32[1024,128]{1,0:T(8,128)S(1)} %get-tuple-element.73.mask, ...), custom_call_target="tpu_custom_call", output_to_operand_aliasing={{0}: (6, {})} | custom-call | flops 1024 | bytes 1024 | tf_op jit(solution)/shard_map/forward_edges/pallas_call | solution.py:456
  36.8 2.9 %inner_terms.1.refs_4_ = f32[1728,256]{1,0:T(8,128)S(1)} custom-call(bf16[576,1024]{1,0:T(8,128)(2,1)S(1)} %get-tuple-element.102.mine, bf16[1728,1024]{1,0:T(8,128)(2,1)S(1)} %turn.1.others, bf16[768,256]{1,0:T(8,128)(2,1)S(1)} %get-tuple-element.96.refs_0_.grad, bf16[768,256]{1,0:T(8,128)(2,1)S(1)} %collective-permute-done.7.refs_1_, ...), custom_call_target="tpu_custom_call" | custom-call | flops 1024 | bytes 1024 | tf_op jit(solution)/shard_map/inner_terms/pallas_call | solution.py:414
  42.7 1.8 %outer_terms.1 = (bf16[432,256]{1,0:T(8,128)(2,1)S(1)}, bf16[432,256]{1,0:T(8,128)(2,1)S(1)}, bf16[432,256]{1,0:T(8,128)(2,1)S(1)}, f32[432,256]{1,0:T(8,128)S(1)}) custom-call(bf16[576,1024]{1,0:T(8,128)(2,1)S(1)} %get-tuple-element.102.mine, bf16[1728,1024]{1,0:T(8,128)(2,1)S(1)} %turn.1.others, bf16[64,256]{1,0:T(8,128)(2,1)S(1)} %get-tuple-element.105.halos, ...), custom_call_target="tpu_custom_call" | custom-call | flops 1024 | bytes 1024 | tf_op jit(solution)/shard_map/outer_terms/pallas_call | solution.py:533
  44.5 4.1 %collective-permute-start.17 = (bf16[432,256]{1,0:T(8,128)(2,1)S(1)}, bf16[432,256]{1,0:T(8,128)(2,1)S(1)}, u32[]{:S(2)}, u32[]{:S(2)}) collective-permute-start(bf16[432,256]{1,0:T(8,128)(2,1)S(1)} %get-tuple-element.122), channel_id=1, source_target_pairs={{0,12},{1,13},{2,14},{3,15},{4,0},{5,1},{6,2},{7,3},{8,4},{9,5},{1... | collective-permute-start | bytes 663560 | tf_op jit(solution)/shard_map/ppermute | solution.py:39
  49.3 9.0 %backward.1 = (bf16[2,8,64,256]{3,2,1,0:T(8,128)(2,1)}, f32[2,128,256]{2,1,0:T(8,128)S(1)}) custom-call(bf16[768,256]{1,0:T(8,128)(2,1)S(1)} %get-tuple-element.96.refs_0_.grad, bf16[400,256]{1,0:T(8,128)(2,1)S(1)} %get-tuple-element.106.refs_0_.parcel, f32[1024,128]{1,0:T(8,128)S(1)} %get-tuple-element.73.mask, bf16[27,256,256]{2,1,0:T(8,128)(2,1)} %weight.5), custom_call_target="tpu_custom_call" | custom-call | flops 1024 | bytes 1024 | tf_op jit(solution)/shard_map/backward/pallas_call | solution.py:582
  58.9 9.8 %collective-permute-done.16 = bf16[432,256]{1,0:T(8,128)(2,1)S(1)} collective-permute-done((bf16[432,256]{1,0:T(8,128)(2,1)S(1)}, bf16[432,256]{1,0:T(8,128)(2,1)S(1)}, u32[]{:S(2)}, u32[]{:S(2)}) %collective-permute-start.16) | collective-permute-done | bytes 221216 | tf_op jit(solution)/shard_map/ppermute | solution.py:39
  69.5 3.7 %collective-permute-start.23 = (bf16[432,256]{1,0:T(8,128)(2,1)S(1)}, bf16[432,256]{1,0:T(8,128)(2,1)S(1)}, u32[]{:S(2)}, u32[]{:S(2)}) collective-permute-start(bf16[432,256]{1,0:T(8,128)(2,1)S(1)} %add_convert_fusion), channel_id=1, source_target_pairs={{0,12},{1,13},{2,14},{3,15},{4,0},{5,1},{6,2},{7,3},{8,4},{9,5},{1... | collective-permute-start | bytes 663560 | tf_op jit(solution)/shard_map/ppermute | solution.py:39
  73.2 5.8 %collective-permute-done.18 = bf16[432,256]{1,0:T(8,128)(2,1)S(1)} collective-permute-done((bf16[432,256]{1,0:T(8,128)(2,1)S(1)}, bf16[432,256]{1,0:T(8,128)(2,1)S(1)}, u32[]{:S(2)}, u32[]{:S(2)}) %collective-permute-start.18) | collective-permute-done | bytes 221216 | tf_op jit(solution)/shard_map/ppermute | solution.py:39
  79.7 5.9 %collective-permute-start.26 = (bf16[432,256]{1,0:T(8,128)(2,1)S(1)}, bf16[432,256]{1,0:T(8,128)(2,1)S(1)}, u32[]{:S(2)}, u32[]{:S(2)}) collective-permute-start(bf16[432,256]{1,0:T(8,128)(2,1)S(1)} %add_convert_fusion), channel_id=1, source_target_pairs={{0,8},{1,9},{2,10},{3,11},{4,12},{5,13},{6,14},{7,15},{8,0},{9,1},... | collective-permute-start | bytes 663560 | tf_op jit(solution)/shard_map/ppermute | solution.py:39
  87.7 4.2 %collective-permute-done.26 = bf16[432,256]{1,0:T(8,128)(2,1)S(1)} collective-permute-done((bf16[432,256]{1,0:T(8,128)(2,1)S(1)}, bf16[432,256]{1,0:T(8,128)(2,1)S(1)}, u32[]{:S(2)}, u32[]{:S(2)}) %collective-permute-start.26) | collective-permute-done | bytes 221216 | tf_op jit(solution)/shard_map/ppermute | solution.py:39
  94.5 5.8 %collective-permute-done.20.refs_1_ = bf16[272,256]{1,0:T(8,128)(2,1)S(1)} collective-permute-done((bf16[272,256]{1,0:T(8,128)(2,1)S(1)}, bf16[272,256]{1,0:T(8,128)(2,1)S(1)}, u32[]{:S(2)}, u32[]{:S(2)}) %collective-permute-start.20) | collective-permute-done | bytes 139296 | tf_op jit(solution)/shard_map/ppermute | solution.py:39
  100.8 1.9 %collective-permute-done.21.refs_2_ = bf16[272,256]{1,0:T(8,128)(2,1)S(1)} collective-permute-done((bf16[272,256]{1,0:T(8,128)(2,1)S(1)}, bf16[272,256]{1,0:T(8,128)(2,1)S(1)}, u32[]{:S(2)}, u32[]{:S(2)}) %collective-permute-start.21) | collective-permute-done | bytes 139296 | tf_op jit(solution)/shard_map/ppermute | solution.py:39
  102.7 1.6 %collective-permute-start.22 = (bf16[272,256]{1,0:T(8,128)(2,1)S(1)}, bf16[272,256]{1,0:T(8,128)(2,1)S(1)}, u32[]{:S(2)}, u32[]{:S(2)}) collective-permute-start(bf16[272,256]{1,0:T(8,128)(2,1)S(1)} %get-tuple-element.130), channel_id=1, source_target_pairs={{0,12},{1,13},{2,14},{3,15},{4,0},{5,1},{6,2},{7,3},{8,4},{9,5},{1... | collective-permute-start | bytes 417800 | tf_op jit(solution)/shard_map/ppermute | solution.py:39
  104.3 3.1 %assemble.2.refs_8_ = bf16[27,16,16,256]{3,2,1,0:T(8,128)(2,1)} custom-call(bf16[27,16,256]{2,1,0:T(8,128)(2,1)S(1)} %bitcast.19, bf16[27,16,256]{2,1,0:T(8,128)(2,1)S(1)} %bitcast.29, bf16[27,16,256]{2,1,0:T(8,128)(2,1)S(1)} %bitcast.28, bf16[27,16,256]{2,1,0:T(8,128)(2,1)S(1)} %bitcast.30, bf16[27,16,256]{2,1,0:T(8,128)(2,1)S(1)} %bitcast.31, ...), custom_call_target="tpu_custom_call" | custom-call | flops 1024 | bytes 1024 | tf_op jit(solution)/shard_map/assemble/pallas_call | solution.py:672
  107.8 5.0 %backward_halos.1 = (bf16[2,8,64,256]{3,2,1,0:T(8,128)(2,1)}, f32[1,256]{1,0:T(1,128)}) custom-call(s32[20]{0:T(128)S(1)} %get-tuple-element.81.table, f32[2,128,256]{2,1,0:T(8,128)S(1)} %get-tuple-element.117.partial, f32[1024,128]{1,0:T(8,128)S(1)} %get-tuple-element.73.mask, bf16[27,256,256]{2,1,0:T(8,128)(2,1)} %weight.5, ...), custom_call_target="tpu_custom_call", output_to_operand_aliasing={{0}: (4, {})} | custom-call | flops 1024 | bytes 1024 | tf_op jit(solution)/shard_map/backward_halos/pallas_call | solution.py:627
  112.8 3.1 %assemble.3 = bf16[27,16,16,256]{3,2,1,0:T(8,128)(2,1)} custom-call(bf16[27,16,256]{2,1,0:T(8,128)(2,1)S(1)} %bitcast.20, bf16[27,16,256]{2,1,0:T(8,128)(2,1)S(1)} %bitcast.22, bf16[27,16,256]{2,1,0:T(8,128)(2,1)S(1)} %bitcast.21, bf16[27,16,256]{2,1,0:T(8,128)(2,1)S(1)} %bitcast.23, ...), custom_call_target="tpu_custom_call", output_to_operand_aliasing={{}: (8, {})} | custom-call | flops 1024 | bytes 1024 | tf_op jit(solution)/shard_map/assemble/pallas_call | solution.py:672
  (64 shorter events, 19.7 us)
Async XLA Ops:
  1.7 7.8 %collective-permute-start = (bf16[272,256]{1,0:T(8,128)(2,1)S(1)}, bf16[272,256]{1,0:T(8,128)(2,1)S(1)}, u32[]{:S(2)}, u32[]{:S(2)}) collective-permute-start(bf16[272,256]{1,0:T(8,128)(2,1)S(1)} %rims.1.refs_0_), channel_id=1, source_target_pairs={{0,2},{1,3},{2,0},{3,1},{4,6},{5,7},{6,4},{7,5},{8,10},{9,11},{10,... | collective-permute-start | bytes 417800 | tf_op jit(solution)/shard_map/ppermute | solution.py:35
  4.8 10.0 %collective-permute-start.1 = (bf16[272,256]{1,0:T(8,128)(2,1)S(1)}, bf16[272,256]{1,0:T(8,128)(2,1)S(1)}, u32[]{:S(2)}, u32[]{:S(2)}) collective-permute-start(bf16[272,256]{1,0:T(8,128)(2,1)S(1)} %rims.1.refs_0_), channel_id=1, source_target_pairs={{0,1},{1,0},{2,3},{3,2},{4,5},{5,4},{6,7},{7,6},{8,9},{9,8},{10,11... | collective-permute-start | bytes 417800 | tf_op jit(solution)/shard_map/ppermute | solution.py:35
  14.8 16.7 %collective-permute-start.7 = (bf16[768,256]{1,0:T(8,128)(2,1)S(1)}, bf16[768,256]{1,0:T(8,128)(2,1)S(1)}, u32[]{:S(2)}, u32[]{:S(2)}) collective-permute-start(bf16[768,256]{1,0:T(8,128)(2,1)S(1)} %get-tuple-element.96.refs_0_.grad), channel_id=1, source_target_pairs={{0,2},{1,3},{2,0},{3,1},{4,6},{5,7},{6,4},{7,5},{8,10},{9,11},{10,... | collective-permute-start | bytes 1179656 | tf_op jit(solution)/shard_map/ppermute | solution.py:35
  16.6 14.9 %collective-permute-start.6 = (bf16[128,1024]{1,0:T(8,128)(2,1)S(1)}, bf16[128,1024]{1,0:T(8,128)(2,1)S(1)}, u32[]{:S(2)}, u32[]{:S(2)}) collective-permute-start(bf16[128,1024]{1,0:T(8,128)(2,1)S(1)} %get-tuple-element.95), channel_id=1, source_target_pairs={{0,2},{1,3},{2,0},{3,1},{4,6},{5,7},{6,4},{7,5},{8,10},{9,11},{10,... | collective-permute-start | bytes 786440 | tf_op jit(solution)/shard_map/ppermute | solution.py:35
  18.6 8.4 %collective-permute-start.3 = (bf16[256,256]{1,0:T(8,128)(2,1)S(1)}, bf16[256,256]{1,0:T(8,128)(2,1)S(1)}, u32[]{:S(2)}, u32[]{:S(2)}) collective-permute-start(bf16[256,256]{1,0:T(8,128)(2,1)S(1)} %get-tuple-element.92), channel_id=1, source_target_pairs={{0,4},{1,5},{2,6},{3,7},{4,8},{5,9},{6,10},{7,11},{8,12},{9,13},{1... | collective-permute-start | bytes 393224 | tf_op jit(solution)/shard_map/ppermute | solution.py:39
  20.2 10.9 %collective-permute-start.4 = (bf16[256,256]{1,0:T(8,128)(2,1)S(1)}, bf16[256,256]{1,0:T(8,128)(2,1)S(1)}, u32[]{:S(2)}, u32[]{:S(2)}) collective-permute-start(bf16[256,256]{1,0:T(8,128)(2,1)S(1)} %get-tuple-element.93), channel_id=1, source_target_pairs={{0,8},{1,9},{2,10},{3,11},{4,12},{5,13},{6,14},{7,15},{8,0},{9,1},... | collective-permute-start | bytes 393224 | tf_op jit(solution)/shard_map/ppermute | solution.py:39
  22.8 8.3 %collective-permute-start.5 = (bf16[256,256]{1,0:T(8,128)(2,1)S(1)}, bf16[256,256]{1,0:T(8,128)(2,1)S(1)}, u32[]{:S(2)}, u32[]{:S(2)}) collective-permute-start(bf16[256,256]{1,0:T(8,128)(2,1)S(1)} %get-tuple-element.94), channel_id=1, source_target_pairs={{0,12},{1,13},{2,14},{3,15},{4,0},{5,1},{6,2},{7,3},{8,4},{9,5},{1... | collective-permute-start | bytes 393224 | tf_op jit(solution)/shard_map/ppermute | solution.py:39
  27.0 9.8 %collective-permute-start.11 = (bf16[768,256]{1,0:T(8,128)(2,1)S(1)}, bf16[768,256]{1,0:T(8,128)(2,1)S(1)}, u32[]{:S(2)}, u32[]{:S(2)}) collective-permute-start(bf16[768,256]{1,0:T(8,128)(2,1)S(1)} %get-tuple-element.96.refs_0_.grad), channel_id=1, source_target_pairs={{0,1},{1,0},{2,3},{3,2},{4,5},{5,4},{6,7},{7,6},{8,9},{9,8},{10,11... | collective-permute-start | bytes 1179656 | tf_op jit(solution)/shard_map/ppermute | solution.py:35
  44.5 14.4 %collective-permute-start.17 = (bf16[432,256]{1,0:T(8,128)(2,1)S(1)}, bf16[432,256]{1,0:T(8,128)(2,1)S(1)}, u32[]{:S(2)}, u32[]{:S(2)}) collective-permute-start(bf16[432,256]{1,0:T(8,128)(2,1)S(1)} %get-tuple-element.122), channel_id=1, source_target_pairs={{0,12},{1,13},{2,14},{3,15},{4,0},{5,1},{6,2},{7,3},{8,4},{9,5},{1... | collective-permute-start | bytes 663560 | tf_op jit(solution)/shard_map/ppermute | solution.py:39
  48.6 20.1 %collective-permute-start.16 = (bf16[432,256]{1,0:T(8,128)(2,1)S(1)}, bf16[432,256]{1,0:T(8,128)(2,1)S(1)}, u32[]{:S(2)}, u32[]{:S(2)}) collective-permute-start(bf16[432,256]{1,0:T(8,128)(2,1)S(1)} %get-tuple-element.121), channel_id=1, source_target_pairs={{0,8},{1,9},{2,10},{3,11},{4,12},{5,13},{6,14},{7,15},{8,0},{9,1},... | collective-permute-start | bytes 663560 | tf_op jit(solution)/shard_map/ppermute | solution.py:39
  49.0 19.7 %collective-permute-start.15 = (bf16[432,256]{1,0:T(8,128)(2,1)S(1)}, bf16[432,256]{1,0:T(8,128)(2,1)S(1)}, u32[]{:S(2)}, u32[]{:S(2)}) collective-permute-start(bf16[432,256]{1,0:T(8,128)(2,1)S(1)} %get-tuple-element.120), channel_id=1, source_target_pairs={{0,4},{1,5},{2,6},{3,7},{4,8},{5,9},{6,10},{7,11},{8,12},{9,13},{1... | collective-permute-start | bytes 663560 | tf_op jit(solution)/shard_map/ppermute | solution.py:39
  68.8 10.3 %collective-permute-start.18 = (bf16[432,256]{1,0:T(8,128)(2,1)S(1)}, bf16[432,256]{1,0:T(8,128)(2,1)S(1)}, u32[]{:S(2)}, u32[]{:S(2)}) collective-permute-start(bf16[432,256]{1,0:T(8,128)(2,1)S(1)} %add_convert_fusion), channel_id=1, source_target_pairs={{0,4},{1,5},{2,6},{3,7},{4,8},{5,9},{6,10},{7,11},{8,12},{9,13},{1... | collective-permute-start | bytes 663560 | tf_op jit(solution)/shard_map/ppermute | solution.py:39
  68.9 10.8 %collective-permute-start.25 = (bf16[432,256]{1,0:T(8,128)(2,1)S(1)}, bf16[432,256]{1,0:T(8,128)(2,1)S(1)}, u32[]{:S(2)}, u32[]{:S(2)}) collective-permute-start(bf16[432,256]{1,0:T(8,128)(2,1)S(1)} %add_convert_fusion), channel_id=1, source_target_pairs={{0,2},{1,3},{2,0},{3,1},{4,6},{5,7},{6,4},{7,5},{8,10},{9,11},{10,... | collective-permute-start | bytes 663560 | tf_op jit(solution)/shard_map/ppermute | solution.py:35
  69.5 16.1 %collective-permute-start.23 = (bf16[432,256]{1,0:T(8,128)(2,1)S(1)}, bf16[432,256]{1,0:T(8,128)(2,1)S(1)}, u32[]{:S(2)}, u32[]{:S(2)}) collective-permute-start(bf16[432,256]{1,0:T(8,128)(2,1)S(1)} %add_convert_fusion), channel_id=1, source_target_pairs={{0,12},{1,13},{2,14},{3,15},{4,0},{5,1},{6,2},{7,3},{8,4},{9,5},{1... | collective-permute-start | bytes 663560 | tf_op jit(solution)/shard_map/ppermute | solution.py:39
  73.2 13.9 %collective-permute-start.32 = (bf16[432,256]{1,0:T(8,128)(2,1)S(1)}, bf16[432,256]{1,0:T(8,128)(2,1)S(1)}, u32[]{:S(2)}, u32[]{:S(2)}) collective-permute-start(bf16[432,256]{1,0:T(8,128)(2,1)S(1)} %add_convert_fusion), channel_id=1, source_target_pairs={{0,1},{1,0},{2,3},{3,2},{4,5},{5,4},{6,7},{7,6},{8,9},{9,8},{10,11... | collective-permute-start | bytes 663560 | tf_op jit(solution)/shard_map/ppermute | solution.py:35
  79.1 8.5 %collective-permute-start.19 = (bf16[432,256]{1,0:T(8,128)(2,1)S(1)}, bf16[432,256]{1,0:T(8,128)(2,1)S(1)}, u32[]{:S(2)}, u32[]{:S(2)}) collective-permute-start(bf16[432,256]{1,0:T(8,128)(2,1)S(1)} %collective-permute-done.18), channel_id=1, source_target_pairs={{0,2},{1,3},{2,0},{3,1},{4,6},{5,7},{6,4},{7,5},{8,10},{9,11},{10,... | collective-permute-start | bytes 663560 | tf_op jit(solution)/shard_map/ppermute | solution.py:35
  79.7 12.2 %collective-permute-start.26 = (bf16[432,256]{1,0:T(8,128)(2,1)S(1)}, bf16[432,256]{1,0:T(8,128)(2,1)S(1)}, u32[]{:S(2)}, u32[]{:S(2)}) collective-permute-start(bf16[432,256]{1,0:T(8,128)(2,1)S(1)} %add_convert_fusion), channel_id=1, source_target_pairs={{0,8},{1,9},{2,10},{3,11},{4,12},{5,13},{6,14},{7,15},{8,0},{9,1},... | collective-permute-start | bytes 663560 | tf_op jit(solution)/shard_map/ppermute | solution.py:39
  85.6 7.8 %collective-permute-start.24 = (bf16[432,256]{1,0:T(8,128)(2,1)S(1)}, bf16[432,256]{1,0:T(8,128)(2,1)S(1)}, u32[]{:S(2)}, u32[]{:S(2)}) collective-permute-start(bf16[432,256]{1,0:T(8,128)(2,1)S(1)} %collective-permute-done.23), channel_id=1, source_target_pairs={{0,2},{1,3},{2,0},{3,1},{4,6},{5,7},{6,4},{7,5},{8,10},{9,11},{10,... | collective-permute-start | bytes 663560 | tf_op jit(solution)/shard_map/ppermute | solution.py:35
  91.8 8.5 %collective-permute-start.27 = (bf16[432,256]{1,0:T(8,128)(2,1)S(1)}, bf16[432,256]{1,0:T(8,128)(2,1)S(1)}, u32[]{:S(2)}, u32[]{:S(2)}) collective-permute-start(bf16[432,256]{1,0:T(8,128)(2,1)S(1)} %collective-permute-done.26), channel_id=1, source_target_pairs={{0,2},{1,3},{2,0},{3,1},{4,6},{5,7},{6,4},{7,5},{8,10},{9,11},{10,... | collective-permute-start | bytes 663560 | tf_op jit(solution)/shard_map/ppermute | solution.py:35
  93.8 8.9 %collective-permute-start.21 = (bf16[272,256]{1,0:T(8,128)(2,1)S(1)}, bf16[272,256]{1,0:T(8,128)(2,1)S(1)}, u32[]{:S(2)}, u32[]{:S(2)}) collective-permute-start(bf16[272,256]{1,0:T(8,128)(2,1)S(1)} %get-tuple-element.129), channel_id=1, source_target_pairs={{0,8},{1,9},{2,10},{3,11},{4,12},{5,13},{6,14},{7,15},{8,0},{9,1},... | collective-permute-start | bytes 417800 | tf_op jit(solution)/shard_map/ppermute | solution.py:39
  94.0 18.8 %collective-permute-start.28 = (bf16[432,256]{1,0:T(8,128)(2,1)S(1)}, bf16[432,256]{1,0:T(8,128)(2,1)S(1)}, u32[]{:S(2)}, u32[]{:S(2)}) collective-permute-start(bf16[432,256]{1,0:T(8,128)(2,1)S(1)} %collective-permute-done.19), channel_id=1, source_target_pairs={{0,1},{1,0},{2,3},{3,2},{4,5},{5,4},{6,7},{7,6},{8,9},{9,8},{10,11... | collective-permute-start | bytes 663560 | tf_op jit(solution)/shard_map/ppermute | solution.py:35
  94.0 18.8 %collective-permute-start.30 = (bf16[432,256]{1,0:T(8,128)(2,1)S(1)}, bf16[432,256]{1,0:T(8,128)(2,1)S(1)}, u32[]{:S(2)}, u32[]{:S(2)}) collective-permute-start(bf16[432,256]{1,0:T(8,128)(2,1)S(1)} %collective-permute-done.26), channel_id=1, source_target_pairs={{0,1},{1,0},{2,3},{3,2},{4,5},{5,4},{6,7},{7,6},{8,9},{9,8},{10,11... | collective-permute-start | bytes 663560 | tf_op jit(solution)/shard_map/ppermute | solution.py:35
  100.3 12.5 %collective-permute-start.29 = (bf16[432,256]{1,0:T(8,128)(2,1)S(1)}, bf16[432,256]{1,0:T(8,128)(2,1)S(1)}, u32[]{:S(2)}, u32[]{:S(2)}) collective-permute-start(bf16[432,256]{1,0:T(8,128)(2,1)S(1)} %collective-permute-done.24), channel_id=1, source_target_pairs={{0,1},{1,0},{2,3},{3,2},{4,5},{5,4},{6,7},{7,6},{8,9},{9,8},{10,11... | collective-permute-start | bytes 663560 | tf_op jit(solution)/shard_map/ppermute | solution.py:35
  100.3 12.5 %collective-permute-start.31 = (bf16[432,256]{1,0:T(8,128)(2,1)S(1)}, bf16[432,256]{1,0:T(8,128)(2,1)S(1)}, u32[]{:S(2)}, u32[]{:S(2)}) collective-permute-start(bf16[432,256]{1,0:T(8,128)(2,1)S(1)} %collective-permute-done.27), channel_id=1, source_target_pairs={{0,1},{1,0},{2,3},{3,2},{4,5},{5,4},{6,7},{7,6},{8,9},{9,8},{10,11... | collective-permute-start | bytes 663560 | tf_op jit(solution)/shard_map/ppermute | solution.py:35
  (13 other events, 68.3 us)

commit v9 on v8

--- a/solution.py
+++ b/solution.py
@@ -546,7 +546,7 @@
     return results[:-1], results[-1]
 
 
-def backward_kernel(grad, parcel, mask, weight, grad_feats, partial, cols, total, near_weight, fetched):
+def backward_kernel(grad, parcel, mask, weight, grad_feats, partial, near_weight, cols, total, fetched):
     width = grad.shape[1]
     fetch_taps(weight, near_weight, fetched)
     valid = windows((128, width), 0)
@@ -582,12 +582,15 @@
     return pl.pallas_call(
         backward_kernel,
         in_specs=[WHOLE] * 3 + [FAR],
-        out_specs=(WHOLE, WHOLE),
-        out_shape=(jax.ShapeDtypeStruct((2, 8, 64, width), jnp.bfloat16), pltpu.VMEM((2, 128, width), jnp.float32)),
+        out_specs=(WHOLE,) * 3,
+        out_shape=(
+            jax.ShapeDtypeStruct((2, 8, 64, width), jnp.bfloat16),
+            pltpu.VMEM((2, 128, width), jnp.float32),
+            pltpu.VMEM(weight.shape, jnp.bfloat16),
+        ),
         scratch_shapes=[
             pltpu.VMEM((1024, 9 * width), jnp.bfloat16),
             pltpu.VMEM((1024, width), jnp.float32),
-            pltpu.VMEM(weight.shape, jnp.bfloat16),
             pltpu.SemaphoreType.DMA((weight.shape[0],)),
         ],
         compiler_params=params(16),
@@ -597,18 +600,16 @@
 
 
 def backward_halos_kernel(table, partial, mask, weight, done, *refs):
-    arrived, (grad_feats, bias_sum, planes, near_weight, fetched, sent) = refs[:-6], refs[-6:]
+    arrived, (grad_feats, bias_sum, planes, sent) = refs[:-4], refs[-4:]
     width = weight.shape[1]
-    fetch_taps(weight, near_weight, fetched)
     valid = windows((128, width), 0)
-    await_taps(0, weight.shape[0], weight, near_weight, fetched)
     for side in range(2):
         halo = jnp.concatenate([chosen(table, 2 * side + b, arrived) for b in range(2)], axis=0)
         total = partial[side]
         for at, moved in enumerate(shifts(halo, 0, valid, -1)):
             total += lax.dot_general(
                 moved,
-                near_weight[18 * (1 - side) + at],
+                weight[18 * (1 - side) + at],
                 (((1,), (1,)), ((), ())),
                 preferred_element_type=jnp.float32,
             )
@@ -626,28 +627,27 @@
     width = weight.shape[1]
     return pl.pallas_call(
         backward_halos_kernel,
-        in_specs=[SCALARS, WHOLE, WHOLE, FAR, FAR] + [WHOLE] * len(arrived),
+        in_specs=[SCALARS] + [WHOLE] * 3 + [FAR] + [WHOLE] * len(arrived),
         out_specs=(FAR, WHOLE),
         out_shape=(jax.ShapeDtypeStruct(done.shape, done.dtype), jax.ShapeDtypeStruct((1, width), jnp.float32)),
         scratch_shapes=[
             pltpu.VMEM((2, 2, 1, 64, width), jnp.bfloat16),
-            pltpu.VMEM(weight.shape, jnp.bfloat16),
-            pltpu.SemaphoreType.DMA((weight.shape[0],)),
             pltpu.SemaphoreType.DMA((2,)),
         ],
         input_output_aliases={4: 0},
         compiler_params=params(10),
         cost_estimate=cost(1024, 1024),
         name="backward_halos",
-    )(table, near(partial), near(mask), far(weight), done, *[near(x) for x in arrived])
-
-
-def assemble_kernel(outer, places, *refs):
-    parts, (out, done) = refs[: len(places)], refs[-2:]
+    )(table, near(partial), near(mask), near(weight), done, *[near(x) for x in arrived])
+
+
+def assemble_kernel(outer, places, parts, *refs):
+    out, done = refs[-2:]
     position = me()
+    blocks = [ref.at[index] for ref, count in zip(refs, parts) for index in range(count)]
     copies = []
-    for index, (ref, (steps, inner, core)) in enumerate(zip(parts, places)):
-        block = lax.rem(position // 4 - steps + outer, outer)
+    for index, (ref, (flip, inner, core)) in enumerate(zip(blocks, places)):
+        block = (position // 4) ^ flip
         quarter = 4 * ((position % 4) ^ (2 * inner + core))
         if outer == 4:
             copies.append((None, pltpu.make_async_copy(ref, out.at[:, quarter + block], done.at[index, 0])))
@@ -666,20 +666,20 @@
                 pl.when(condition)(act)
 
 
-def assemble(outer, places, parts, shape, given):
+def assemble(outer, places, stacks, shape, given):
     before = [] if given is None else [given]
     rows = units(outer)
     return pl.pallas_call(
-        functools.partial(assemble_kernel, outer, places),
-        in_specs=[WHOLE] * len(parts) + [FAR] * len(before),
+        functools.partial(assemble_kernel, outer, places, [x.shape[0] for x in stacks]),
+        in_specs=[WHOLE] * len(stacks) + [FAR] * len(before),
         out_specs=FAR,
         out_shape=jax.ShapeDtypeStruct(shape, jnp.bfloat16),
-        scratch_shapes=[pltpu.SemaphoreType.DMA((len(parts), rows))],
-        input_output_aliases={len(parts): 0} if before else {},
+        scratch_shapes=[pltpu.SemaphoreType.DMA((len(places), rows))],
+        input_output_aliases={len(stacks): 0} if before else {},
         compiler_params=params(),
         cost_estimate=cost(1024, 1024),
         name="assemble",
-    )(*[near(x.reshape(rows, 16, shape[-1])) for x in parts], *before)
+    )(*[near(x.reshape(x.shape[0], rows, 16, shape[-1])) for x in stacks], *before)
 
 
 def per_device(size, feats, voxmask, links, weight, bias, cotangent):
@@ -691,12 +691,13 @@
     inner, rows = lax.optimization_barrier((swap(parcel, size, 2), rows))
     parcels = [parcel, inner, swap(parcel, size, 1), swap(inner, size, 1)]
     out, grad, edge, bias_local = forward_inside(rows, mask, taps, bias.reshape(1, width), ends)
-    *parcels, grad = lax.optimization_barrier((*parcels, grad))
+    got_inner = swap(give_inner, size, 2)
+    *parcels, grad, got_inner = lax.optimization_barrier((*parcels, grad, got_inner))
     table, picks = route(parcels, outer)
 
-    *picks, give_inner, give_core = lax.optimization_barrier((*picks, give_inner, give_core))
+    *picks, give_core = lax.optimization_barrier((*picks, give_core))
     arrived = [rotate(pick, size, steps) if steps else pick for steps, pick in enumerate(picks)]
-    got_inner, grad_inner = swap(give_inner, size, 2), swap(grad, size, 2)
+    grad_inner = swap(grad, size, 2)
     *arrived, got_inner, grad_inner = lax.optimization_barrier((*arrived, got_inner, grad_inner))
     others = turn(got_inner, swap(give_core, size, 1), swap(got_inner, size, 1))
     grads = [grad, grad_inner, swap(grad, size, 1), swap(grad_inner, size, 1)]
@@ -709,27 +710,37 @@
 
     gives, stay = outer_terms(outer, turned, others, halos, parcels, terms)
     gots = [rotate(give, size, steps + 1) for steps, give in enumerate(gives)]
-    grad_feats, partial = backward(grad, to_inner, mask, weight)
+    grad_feats, partial, taps = backward(grad, to_inner, mask, weight)
     picks = repeat_route(table, parcels, outer)
     stay, partial, *picks = lax.optimization_barrier((stay, partial, *picks))
     part = (stay + sum(got.astype(jnp.float32) for got in gots)).astype(jnp.bfloat16)
 
-    blocks = {(0, 0): part, (0, 1): swap(part, size, 2)}
-    later, blocks[0, 1] = lax.optimization_barrier((part, blocks[0, 1]))
-    for steps in [k for k in range(1, outer) if k in (1, outer - 1)] + list(range(2, outer - 1)):
-        blocks[steps, 0] = rotate(part if steps in (1, outer - 1) else later, size, steps)
-        blocks[steps, 1] = swap(blocks[steps, 0], size, 2)
-    blocks[1, 1], *picks = lax.optimization_barrier((blocks[1, 1], *picks))
+    def stack(*blocks):
+        return jnp.concatenate([x.reshape(-1, *part.shape) for x in blocks])
+
+    def place_blocks(keys, blocks, given):
+        places = [(flip, bit, core) for core in range(2) for flip, bit in keys]
+        return assemble(outer, places, [blocks, swap(blocks, size, 1)], (27, 16, width // 16, width), given)
+
+    last = outer - 1
+    flips = list(range(1, last))
+    blocks = [part]
+    for flip in flips:
+        blocks.append(swap(blocks[flip & (flip - 1)], size, 4 * (flip & -flip)))
+    first_inner = swap(part, size, 2)
+    middle = stack(*blocks[1:])
+    farthest = swap(blocks[last & (last - 1)], size, 4)
+    middle, *picks = lax.optimization_barrier((middle, *picks))
+    middle_inner = swap(middle, size, 2)
     arrived = [rotate(pick, size, steps) if steps else pick for steps, pick in enumerate(picks)]
-    grad_feats, grad_bias = backward_halos(table, partial, mask, weight, grad_feats, arrived)
-
-    early = [(0, 0), (0, 1), (1, 0), (outer - 1, 0)]
-    grad_weight = None
-    for chosen_blocks in (early, [key for key in blocks if key not in early]):
-        places = [(steps, bit, core) for core in range(2) for steps, bit in chosen_blocks]
-        parts = [blocks[key] for key in chosen_blocks]
-        parts += [swap(x, size, 1) for x in parts]
-        grad_weight = assemble(outer, places, parts, (27, 16, width // 16, width), grad_weight)
+    grad_weight = place_blocks([(0, 0), (0, 1)] + [(flip, 0) for flip in flips], stack(part, first_inner, middle), None)
+    farthest_inner = swap(farthest, size, 2)
+    middle_inner, farthest_inner, grad_weight, *arrived = lax.optimization_barrier(
+        (middle_inner, farthest_inner, grad_weight, *arrived)
+    )
+    keys = [(flip, 1) for flip in flips] + [(last, 0), (last, 1)]
+    grad_weight = place_blocks(keys, stack(middle_inner, farthest, farthest_inner), grad_weight)
+    grad_feats, grad_bias = backward_halos(table, partial, mask, taps, grad_feats, arrived)
     return out, grad_feats, grad_weight.reshape(weight.shape), grad_bias.reshape(width)
 
 

time: 116 us -> 110 us (0.948); the launches traced: 116 us -> 109 us
  waiting for transfers between devices: 39.1 us -> 32.4 us
  Pallas kernels: 40.6 us -> 38.4 us
    ppermute x12 -> x9, waiting for transfers between devices: 34.9 us -> 14.9 us  [rotate(): lax.ppermute(x, 'zslab', [(i, (i + 4 * steps) % size) for i in range(size)])]
    ppermute x24 -> x20, waiting for transfers between devices: 4.18 us -> 17.5 us  [swap(): return lax.ppermute(x, 'zslab', [(i, i ^ bit) for i in range(size)])]
    ppermute x24 -> x20, starting transfers between devices: 13.1 us -> 18.2 us  [swap(): return lax.ppermute(x, 'zslab', [(i, i ^ bit) for i in range(size)])]
    ppermute x12 -> x9, starting transfers between devices: 22.2 us -> 18.1 us  [rotate(): lax.ppermute(x, 'zslab', [(i, (i + 4 * steps) % size) for i in range(size)])]
    pallas_call x3, Pallas kernels: 11.2 us -> 9 us  [the longest x2 6.28 us: assemble(): pl.pallas_call(functools.partial(assemble_kernel, outer, places, [x.shape...]
  transfers between devices with their start and end apart: 36 -> 29, of which waited for: 13 -> 11; matrix products, arithmetic and copies ran while one was open for 0% -> 0% of each run, Pallas kernels for 30% -> 30%
where the time goes in v9:
time: 110 us; the launch traced here: 109 us
  Pallas kernels  38.4 us (35%)
  starting transfers between devices  36.3 us (33%)
  waiting for transfers between devices  32.4 us (29%)
    ppermute x20, starting transfers between devices, swap(): return lax.ppermute(x, 'zslab', [(i, i ^ bit) for i in range(size)])  18.2 us
    ppermute x9, starting transfers between devices, rotate(): lax.ppermute(x, 'zslab', [(i, (i + 4 * steps) % size) for i in range(size)])  18.1 us
    ppermute x20, waiting for transfers between devices, swap(): return lax.ppermute(x, 'zslab', [(i, i ^ bit) for i in range(size)])  17.5 us
    ppermute x9, waiting for transfers between devices, rotate(): lax.ppermute(x, 'zslab', [(i, (i + 4 * steps) % size) for i in range(size)])  14.9 us
    pallas_call x1, Pallas kernels, backward(): pl.pallas_call(backward_kernel, in_specs=[WHOLE] * 3 + [FAR], out_specs=(...  8.95 us
    pallas_call x2, Pallas kernels, assemble(): pl.pallas_call(functools.partial(assemble_kernel, outer, places, [x.shape...  6.28 us
    pallas_call x1, Pallas kernels, prepare(): pl.pallas_call(prepare_kernel, in_specs=[FAR] * 4, out_specs=(WHOLE,) * 7...  4.77 us
    pallas_call x1, Pallas kernels, forward_inside(): pl.pallas_call(forward_kernel, in_specs=[WHOLE] * 5, out_specs=(WHOLE,) *...  4.66 us
  transfers between devices with their start and end apart: 29, of which 11 were waited for; matrix products, arithmetic and copies ran while one was open for 0% of the time, Pallas kernels for 30%

profile of v9, /device:TPU:0, one launch (start us, length us, event | category | flops | bytes accessed | tf_op | source)
XLA Modules:
  0.0 108.7 jit_solution(5847716220078018458)
XLA Ops:
  1.7 3.0 %collective-permute-start = (bf16[272,256]{1,0:T(8,128)(2,1)S(1)}, bf16[272,256]{1,0:T(8,128)(2,1)S(1)}, u32[]{:S(2)}, u32[]{:S(2)}) collective-permute-start(bf16[272,256]{1,0:T(8,128)(2,1)S(1)} %rims.1.refs_0_), channel_id=1, source_target_pairs={{0,2},{1,3},{2,0},{3,1},{4,6},{5,7},{6,4},{7,5},{8,10},{9,11},{10,... | collective-permute-start | bytes 417800 | tf_op jit(solution)/shard_map/ppermute | solution.py:35
  4.8 4.8 %prepare.1 = (f32[1024,128]{1,0:T(8,128)S(1)}, bf16[1024,256]{1,0:T(8,128)(2,1)S(1)}, bf16[128,1024]{1,0:T(8,128)(2,1)S(1)}, bf16[64,1024]{1,0:T(8,128)(2,1)S(1)...) custom-call(bf16[2,8,64,256]{3,2,1,0:T(8,128)(2,1)} %feats.3, ...), custom_call_target="tpu_custom_call" | custom-call | flops 1024 | bytes 1024 | tf_op jit(solution)/shard_map/prepare/pallas_call | solution.py:209
  10.2 4.7 %forward_inside.1 = (bf16[2,8,64,256]{3,2,1,0:T(8,128)(2,1)}, bf16[768,256]{1,0:T(8,128)(2,1)S(1)}, f32[2,128,256]{2,1,0:T(8,128)S(1)}, f32[1,256]{1,0:T(1,128)S(1)}) custom-call(bf16[1024,256]{1,0:T(8,128)(2,1)S(1)} %get-tuple-element.78.rows, f32[1024,128]{1,0:T(8,128)S(1)} %get-tuple-element.79.mask, bf16[27,256,256]{2,1,0:T(8,128)(2,1)S(1)} %get-tuple-element.80.weight, ...), custom_call_target="tpu_custom_call" | custom-call | flops 1024 | bytes 1024 | tf_op jit(solution)/shard_map/forward_inside/pallas_call | solution.py:379
  14.9 2.5 %collective-permute-done.3.inner = bf16[128,1024]{1,0:T(8,128)(2,1)S(1)} collective-permute-done((bf16[128,1024]{1,0:T(8,128)(2,1)S(1)}, bf16[128,1024]{1,0:T(8,128)(2,1)S(1)}, u32[]{:S(2)}, u32[]{:S(2)}) %collective-permute-start.3) | collective-permute-done | bytes 262176 | tf_op jit(solution)/shard_map/ppermute | solution.py:35
  19.4 1.8 %collective-permute-start.4 = (bf16[256,256]{1,0:T(8,128)(2,1)S(1)}, bf16[256,256]{1,0:T(8,128)(2,1)S(1)}, u32[]{:S(2)}, u32[]{:S(2)}) collective-permute-start(bf16[256,256]{1,0:T(8,128)(2,1)S(1)} %get-tuple-element.98), channel_id=1, source_target_pairs={{0,4},{1,5},{2,6},{3,7},{4,8},{5,9},{6,10},{7,11},{8,12},{9,13},{1... | collective-permute-start | bytes 393224 | tf_op jit(solution)/shard_map/ppermute | solution.py:39
  21.2 2.6 %collective-permute-start.5 = (bf16[256,256]{1,0:T(8,128)(2,1)S(1)}, bf16[256,256]{1,0:T(8,128)(2,1)S(1)}, u32[]{:S(2)}, u32[]{:S(2)}) collective-permute-start(bf16[256,256]{1,0:T(8,128)(2,1)S(1)} %get-tuple-element.99), channel_id=1, source_target_pairs={{0,8},{1,9},{2,10},{3,11},{4,12},{5,13},{6,14},{7,15},{8,0},{9,1},... | collective-permute-start | bytes 393224 | tf_op jit(solution)/shard_map/ppermute | solution.py:39
  25.2 2.6 %collective-permute-done.4.refs_1_ = bf16[256,256]{1,0:T(8,128)(2,1)S(1)} collective-permute-done((bf16[256,256]{1,0:T(8,128)(2,1)S(1)}, bf16[256,256]{1,0:T(8,128)(2,1)S(1)}, u32[]{:S(2)}, u32[]{:S(2)}) %collective-permute-start.4) | collective-permute-done | bytes 131104 | tf_op jit(solution)/shard_map/ppermute | solution.py:39
  27.8 3.7 %collective-permute-done.5.refs_2_ = bf16[256,256]{1,0:T(8,128)(2,1)S(1)} collective-permute-done((bf16[256,256]{1,0:T(8,128)(2,1)S(1)}, bf16[256,256]{1,0:T(8,128)(2,1)S(1)}, u32[]{:S(2)}, u32[]{:S(2)}) %collective-permute-start.5) | collective-permute-done | bytes 131104 | tf_op jit(solution)/shard_map/ppermute | solution.py:39
  32.0 1.9 %forward_edges.1 = (bf16[2,8,64,256]{3,2,1,0:T(8,128)(2,1)}, bf16[400,256]{1,0:T(8,128)(2,1)S(1)}, bf16[336,256]{1,0:T(8,128)(2,1)S(1)}, bf16[64,256]{1,0:T(8,128)(2,1)S(1)}) custom-call(s32[20]{0:T(128)S(1)} %get-tuple-element.88.table, f32[1024,128]{1,0:T(8,128)S(1)} %get-tuple-element.79.mask, ...), custom_call_target="tpu_custom_call", output_to_operand_aliasing={{0}: (6, {})} | custom-call | flops 1024 | bytes 1024 | tf_op jit(solution)/shard_map/forward_edges/pallas_call | solution.py:456
  37.5 2.9 %inner_terms.1.refs_4_ = f32[1728,256]{1,0:T(8,128)S(1)} custom-call(bf16[576,1024]{1,0:T(8,128)(2,1)S(1)} %get-tuple-element.108.mine, bf16[1728,1024]{1,0:T(8,128)(2,1)S(1)} %turn.1.others, bf16[768,256]{1,0:T(8,128)(2,1)S(1)} %get-tuple-element.102.refs_0_.grad, bf16[768,256]{1,0:T(8,128)(2,1)S(1)} %collective-permute-done.7.refs_1_, ...), custom_call_target="tpu_custom_call" | custom-call | flops 1024 | bytes 1024 | tf_op jit(solution)/shard_map/inner_terms/pallas_call | solution.py:414
  42.7 1.8 %outer_terms.1 = (bf16[432,256]{1,0:T(8,128)(2,1)S(1)}, bf16[432,256]{1,0:T(8,128)(2,1)S(1)}, bf16[432,256]{1,0:T(8,128)(2,1)S(1)}, f32[432,256]{1,0:T(8,128)S(1)}) custom-call(bf16[576,1024]{1,0:T(8,128)(2,1)S(1)} %get-tuple-element.108.mine, bf16[1728,1024]{1,0:T(8,128)(2,1)S(1)} %turn.1.others, bf16[64,256]{1,0:T(8,128)(2,1)S(1)} %get-tuple-element.111.halos, ...), custom_call_target="tpu_custom_call" | custom-call | flops 1024 | bytes 1024 | tf_op jit(solution)/shard_map/outer_terms/pallas_call | solution.py:533
  44.6 3.3 %collective-permute-start.15 = (bf16[432,256]{1,0:T(8,128)(2,1)S(1)}, bf16[432,256]{1,0:T(8,128)(2,1)S(1)}, u32[]{:S(2)}, u32[]{:S(2)}) collective-permute-start(bf16[432,256]{1,0:T(8,128)(2,1)S(1)} %get-tuple-element.127), channel_id=1, source_target_pairs={{0,4},{1,5},{2,6},{3,7},{4,8},{5,9},{6,10},{7,11},{8,12},{9,13},{1... | collective-permute-start | bytes 663560 | tf_op jit(solution)/shard_map/ppermute | solution.py:39
  50.3 9.0 %backward.1 = (bf16[2,8,64,256]{3,2,1,0:T(8,128)(2,1)}, f32[2,128,256]{2,1,0:T(8,128)S(1)}, bf16[27,256,256]{2,1,0:T(8,128)(2,1)S(1)}) custom-call(bf16[768,256]{1,0:T(8,128)(2,1)S(1)} %get-tuple-element.102.refs_0_.grad, bf16[400,256]{1,0:T(8,128)(2,1)S(1)} %get-tuple-element.112.refs_0_.parcel, f32[1024,128]{1,0:T(8,128)S(1)} %get-tuple-element.79.mask, ...), custom_call_target="tpu_custom_call" | custom-call | flops 1024 | bytes 1024 | tf_op jit(solution)/shard_map/backward/pallas_call | solution.py:582
  59.9 4.4 %collective-permute-done.16 = bf16[432,256]{1,0:T(8,128)(2,1)S(1)} collective-permute-done((bf16[432,256]{1,0:T(8,128)(2,1)S(1)}, bf16[432,256]{1,0:T(8,128)(2,1)S(1)}, u32[]{:S(2)}, u32[]{:S(2)}) %collective-permute-start.16) | collective-permute-done | bytes 221216 | tf_op jit(solution)/shard_map/ppermute | solution.py:39
  64.4 4.3 %collective-permute-start.19 = (bf16[432,256]{1,0:T(8,128)(2,1)S(1)}, bf16[432,256]{1,0:T(8,128)(2,1)S(1)}, u32[]{:S(2)}, u32[]{:S(2)}) collective-permute-start(bf16[432,256]{1,0:T(8,128)(2,1)S(1)} %add_convert_fusion), channel_id=1, source_target_pairs={{0,8},{1,9},{2,10},{3,11},{4,12},{5,13},{6,14},{7,15},{8,0},{9,1},... | collective-permute-start | bytes 663560 | tf_op jit(solution)/shard_map/ppermute | solution.py:35
  68.7 2.3 %collective-permute-start.18 = (bf16[432,256]{1,0:T(8,128)(2,1)S(1)}, bf16[432,256]{1,0:T(8,128)(2,1)S(1)}, u32[]{:S(2)}, u32[]{:S(2)}) collective-permute-start(bf16[432,256]{1,0:T(8,128)(2,1)S(1)} %add_convert_fusion), channel_id=1, source_target_pairs={{0,4},{1,5},{2,6},{3,7},{4,0},{5,1},{6,2},{7,3},{8,12},{9,13},{10,... | collective-permute-start | bytes 663560 | tf_op jit(solution)/shard_map/ppermute | solution.py:35
  72.1 6.9 %collective-permute-done.19 = bf16[432,256]{1,0:T(8,128)(2,1)S(1)} collective-permute-done((bf16[432,256]{1,0:T(8,128)(2,1)S(1)}, bf16[432,256]{1,0:T(8,128)(2,1)S(1)}, u32[]{:S(2)}, u32[]{:S(2)}) %collective-permute-start.19) | collective-permute-done | bytes 221216 | tf_op jit(solution)/shard_map/ppermute | solution.py:35
  79.3 1.8 %collective-permute-start.21 = (bf16[432,256]{1,0:T(8,128)(2,1)S(1)}, bf16[432,256]{1,0:T(8,128)(2,1)S(1)}, u32[]{:S(2)}, u32[]{:S(2)}) collective-permute-start(bf16[432,256]{1,0:T(8,128)(2,1)S(1)} %collective-permute-done.19), channel_id=1, source_target_pairs={{0,4},{1,5},{2,6},{3,7},{4,0},{5,1},{6,2},{7,3},{8,12},{9,13},{10,... | collective-permute-start | bytes 663560 | tf_op jit(solution)/shard_map/ppermute | solution.py:35
  82.3 4.9 %collective-permute-done.21 = bf16[432,256]{1,0:T(8,128)(2,1)S(1)} collective-permute-done((bf16[432,256]{1,0:T(8,128)(2,1)S(1)}, bf16[432,256]{1,0:T(8,128)(2,1)S(1)}, u32[]{:S(2)}, u32[]{:S(2)}) %collective-permute-start.21) | collective-permute-done | bytes 221216 | tf_op jit(solution)/shard_map/ppermute | solution.py:35
  90.1 3.5 %collective-permute-start.26 = (bf16[272,256]{1,0:T(8,128)(2,1)S(1)}, bf16[272,256]{1,0:T(8,128)(2,1)S(1)}, u32[]{:S(2)}, u32[]{:S(2)}) collective-permute-start(bf16[272,256]{1,0:T(8,128)(2,1)S(1)} %get-tuple-element.137), channel_id=1, source_target_pairs={{0,8},{1,9},{2,10},{3,11},{4,12},{5,13},{6,14},{7,15},{8,0},{9,1},... | collective-permute-start | bytes 417800 | tf_op jit(solution)/shard_map/ppermute | solution.py:39
  95.0 3.1 %assemble.2.refs_2_ = bf16[27,16,16,256]{3,2,1,0:T(8,128)(2,1)} custom-call(bf16[4,27,16,256]{3,2,1,0:T(8,128)(2,1)S(1)} %pad_maximum_fusion.refs_0_, bf16[4,27,16,256]{3,2,1,0:T(8,128)(2,1)S(1)} %bitcast.18), custom_call_target="tpu_custom_call" | custom-call | flops 1024 | bytes 1024 | tf_op jit(solution)/shard_map/assemble/pallas_call | solution.py:672
  98.2 4.2 %collective-permute-done.26.refs_2_ = bf16[272,256]{1,0:T(8,128)(2,1)S(1)} collective-permute-done((bf16[272,256]{1,0:T(8,128)(2,1)S(1)}, bf16[272,256]{1,0:T(8,128)(2,1)S(1)}, u32[]{:S(2)}, u32[]{:S(2)}) %collective-permute-start.26) | collective-permute-done | bytes 139296 | tf_op jit(solution)/shard_map/ppermute | solution.py:39
  102.5 2.7 %backward_halos.1 = (bf16[2,8,64,256]{3,2,1,0:T(8,128)(2,1)}, f32[1,256]{1,0:T(1,128)}) custom-call(s32[20]{0:T(128)S(1)} %get-tuple-element.88.table, f32[2,128,256]{2,1,0:T(8,128)S(1)} %get-tuple-element.123.partial, f32[1024,128]{1,0:T(8,128)S(1)} %get-tuple-element.79.mask, ...), custom_call_target="tpu_custom_call", output_to_operand_aliasing={{0}: (4, {})} | custom-call | flops 1024 | bytes 1024 | tf_op jit(solution)/shard_map/backward_halos/pallas_call | solution.py:628
  105.4 3.1 %assemble.3 = bf16[27,16,16,256]{3,2,1,0:T(8,128)(2,1)} custom-call(bf16[4,27,16,256]{3,2,1,0:T(8,128)(2,1)S(1)} %pad_maximum_fusion.2.refs_0_, bf16[4,27,16,256]{3,2,1,0:T(8,128)(2,1)S(1)} %bitcast.17, bf16[27,16,16,256]{3,2,1,0:T(8,128)(2,1)} %assemble.2.refs_2_), custom_call_target="tpu_custom_call", output_to_operand_aliasing={{}: (2, {})} | custom-call | flops 1024 | bytes 1024 | tf_op jit(solution)/shard_map/assemble/pallas_call | solution.py:672
  (55 shorter events, 21.7 us)
Async XLA Ops:
  1.7 8.0 %collective-permute-start = (bf16[272,256]{1,0:T(8,128)(2,1)S(1)}, bf16[272,256]{1,0:T(8,128)(2,1)S(1)}, u32[]{:S(2)}, u32[]{:S(2)}) collective-permute-start(bf16[272,256]{1,0:T(8,128)(2,1)S(1)} %rims.1.refs_0_), channel_id=1, source_target_pairs={{0,2},{1,3},{2,0},{3,1},{4,6},{5,7},{6,4},{7,5},{8,10},{9,11},{10,... | collective-permute-start | bytes 417800 | tf_op jit(solution)/shard_map/ppermute | solution.py:35
  9.6 7.8 %collective-permute-start.3 = (bf16[128,1024]{1,0:T(8,128)(2,1)S(1)}, bf16[128,1024]{1,0:T(8,128)(2,1)S(1)}, u32[]{:S(2)}, u32[]{:S(2)}) collective-permute-start(bf16[128,1024]{1,0:T(8,128)(2,1)S(1)} %get-tuple-element.83), channel_id=1, source_target_pairs={{0,2},{1,3},{2,0},{3,1},{4,6},{5,7},{6,4},{7,5},{8,10},{9,11},{10,... | collective-permute-start | bytes 786440 | tf_op jit(solution)/shard_map/ppermute | solution.py:35
  9.6 5.2 %collective-permute-start.1 = (bf16[272,256]{1,0:T(8,128)(2,1)S(1)}, bf16[272,256]{1,0:T(8,128)(2,1)S(1)}, u32[]{:S(2)}, u32[]{:S(2)}) collective-permute-start(bf16[272,256]{1,0:T(8,128)(2,1)S(1)} %rims.1.refs_0_), channel_id=1, source_target_pairs={{0,1},{1,0},{2,3},{3,2},{4,5},{5,4},{6,7},{7,6},{8,9},{9,8},{10,11... | collective-permute-start | bytes 417800 | tf_op jit(solution)/shard_map/ppermute | solution.py:35
  9.7 7.7 %collective-permute-start.2 = (bf16[272,256]{1,0:T(8,128)(2,1)S(1)}, bf16[272,256]{1,0:T(8,128)(2,1)S(1)}, u32[]{:S(2)}, u32[]{:S(2)}) collective-permute-start(bf16[272,256]{1,0:T(8,128)(2,1)S(1)} %collective-permute-done.refs_1_), channel_id=1, source_target_pairs={{0,1},{1,0},{2,3},{3,2},{4,5},{5,4},{6,7},{7,6},{8,9},{9,8},{10,11... | collective-permute-start | bytes 417800 | tf_op jit(solution)/shard_map/ppermute | solution.py:35
  17.4 14.1 %collective-permute-start.7 = (bf16[768,256]{1,0:T(8,128)(2,1)S(1)}, bf16[768,256]{1,0:T(8,128)(2,1)S(1)}, u32[]{:S(2)}, u32[]{:S(2)}) collective-permute-start(bf16[768,256]{1,0:T(8,128)(2,1)S(1)} %get-tuple-element.102.refs_0_.grad), channel_id=1, source_target_pairs={{0,2},{1,3},{2,0},{3,1},{4,6},{5,7},{6,4},{7,5},{8,10},{9,11},{10,... | collective-permute-start | bytes 1179656 | tf_op jit(solution)/shard_map/ppermute | solution.py:35
  19.4 8.4 %collective-permute-start.4 = (bf16[256,256]{1,0:T(8,128)(2,1)S(1)}, bf16[256,256]{1,0:T(8,128)(2,1)S(1)}, u32[]{:S(2)}, u32[]{:S(2)}) collective-permute-start(bf16[256,256]{1,0:T(8,128)(2,1)S(1)} %get-tuple-element.98), channel_id=1, source_target_pairs={{0,4},{1,5},{2,6},{3,7},{4,8},{5,9},{6,10},{7,11},{8,12},{9,13},{1... | collective-permute-start | bytes 393224 | tf_op jit(solution)/shard_map/ppermute | solution.py:39
  21.2 10.2 %collective-permute-start.5 = (bf16[256,256]{1,0:T(8,128)(2,1)S(1)}, bf16[256,256]{1,0:T(8,128)(2,1)S(1)}, u32[]{:S(2)}, u32[]{:S(2)}) collective-permute-start(bf16[256,256]{1,0:T(8,128)(2,1)S(1)} %get-tuple-element.99), channel_id=1, source_target_pairs={{0,8},{1,9},{2,10},{3,11},{4,12},{5,13},{6,14},{7,15},{8,0},{9,1},... | collective-permute-start | bytes 393224 | tf_op jit(solution)/shard_map/ppermute | solution.py:39
  23.8 7.7 %collective-permute-start.6 = (bf16[256,256]{1,0:T(8,128)(2,1)S(1)}, bf16[256,256]{1,0:T(8,128)(2,1)S(1)}, u32[]{:S(2)}, u32[]{:S(2)}) collective-permute-start(bf16[256,256]{1,0:T(8,128)(2,1)S(1)} %get-tuple-element.100), channel_id=1, source_target_pairs={{0,12},{1,13},{2,14},{3,15},{4,0},{5,1},{6,2},{7,3},{8,4},{9,5},{1... | collective-permute-start | bytes 393224 | tf_op jit(solution)/shard_map/ppermute | solution.py:39
  25.2 12.3 %collective-permute-start.11 = (bf16[768,256]{1,0:T(8,128)(2,1)S(1)}, bf16[768,256]{1,0:T(8,128)(2,1)S(1)}, u32[]{:S(2)}, u32[]{:S(2)}) collective-permute-start(bf16[768,256]{1,0:T(8,128)(2,1)S(1)} %get-tuple-element.102.refs_0_.grad), channel_id=1, source_target_pairs={{0,1},{1,0},{2,3},{3,2},{4,5},{5,4},{6,7},{7,6},{8,9},{9,8},{10,11... | collective-permute-start | bytes 1179656 | tf_op jit(solution)/shard_map/ppermute | solution.py:35
  31.5 5.9 %collective-permute-start.12 = (bf16[768,256]{1,0:T(8,128)(2,1)S(1)}, bf16[768,256]{1,0:T(8,128)(2,1)S(1)}, u32[]{:S(2)}, u32[]{:S(2)}) collective-permute-start(bf16[768,256]{1,0:T(8,128)(2,1)S(1)} %collective-permute-done.7.refs_1_), channel_id=1, source_target_pairs={{0,1},{1,0},{2,3},{3,2},{4,5},{5,4},{6,7},{7,6},{8,9},{9,8},{10,11... | collective-permute-start | bytes 1179656 | tf_op jit(solution)/shard_map/ppermute | solution.py:35
  34.0 7.1 %collective-permute-start.10 = (bf16[400,256]{1,0:T(8,128)(2,1)S(1)}, bf16[400,256]{1,0:T(8,128)(2,1)S(1)}, u32[]{:S(2)}, u32[]{:S(2)}) collective-permute-start(bf16[400,256]{1,0:T(8,128)(2,1)S(1)} %get-tuple-element.112.refs_0_.parcel), channel_id=1, source_target_pairs={{0,2},{1,3},{2,0},{3,1},{4,6},{5,7},{6,4},{7,5},{8,10},{9,11},{10,... | collective-permute-start | bytes 614408 | tf_op jit(solution)/shard_map/ppermute | solution.py:35
  44.6 15.3 %collective-permute-start.15 = (bf16[432,256]{1,0:T(8,128)(2,1)S(1)}, bf16[432,256]{1,0:T(8,128)(2,1)S(1)}, u32[]{:S(2)}, u32[]{:S(2)}) collective-permute-start(bf16[432,256]{1,0:T(8,128)(2,1)S(1)} %get-tuple-element.127), channel_id=1, source_target_pairs={{0,4},{1,5},{2,6},{3,7},{4,8},{5,9},{6,10},{7,11},{8,12},{9,13},{1... | collective-permute-start | bytes 663560 | tf_op jit(solution)/shard_map/ppermute | solution.py:39
  47.8 16.5 %collective-permute-start.16 = (bf16[432,256]{1,0:T(8,128)(2,1)S(1)}, bf16[432,256]{1,0:T(8,128)(2,1)S(1)}, u32[]{:S(2)}, u32[]{:S(2)}) collective-permute-start(bf16[432,256]{1,0:T(8,128)(2,1)S(1)} %get-tuple-element.128), channel_id=1, source_target_pairs={{0,8},{1,9},{2,10},{3,11},{4,12},{5,13},{6,14},{7,15},{8,0},{9,1},... | collective-permute-start | bytes 663560 | tf_op jit(solution)/shard_map/ppermute | solution.py:39
  49.5 14.9 %collective-permute-start.17 = (bf16[432,256]{1,0:T(8,128)(2,1)S(1)}, bf16[432,256]{1,0:T(8,128)(2,1)S(1)}, u32[]{:S(2)}, u32[]{:S(2)}) collective-permute-start(bf16[432,256]{1,0:T(8,128)(2,1)S(1)} %get-tuple-element.129), channel_id=1, source_target_pairs={{0,12},{1,13},{2,14},{3,15},{4,0},{5,1},{6,2},{7,3},{8,4},{9,5},{1... | collective-permute-start | bytes 663560 | tf_op jit(solution)/shard_map/ppermute | solution.py:39
  64.4 14.6 %collective-permute-start.19 = (bf16[432,256]{1,0:T(8,128)(2,1)S(1)}, bf16[432,256]{1,0:T(8,128)(2,1)S(1)}, u32[]{:S(2)}, u32[]{:S(2)}) collective-permute-start(bf16[432,256]{1,0:T(8,128)(2,1)S(1)} %add_convert_fusion), channel_id=1, source_target_pairs={{0,8},{1,9},{2,10},{3,11},{4,12},{5,13},{6,14},{7,15},{8,0},{9,1},... | collective-permute-start | bytes 663560 | tf_op jit(solution)/shard_map/ppermute | solution.py:35
  68.7 10.4 %collective-permute-start.18 = (bf16[432,256]{1,0:T(8,128)(2,1)S(1)}, bf16[432,256]{1,0:T(8,128)(2,1)S(1)}, u32[]{:S(2)}, u32[]{:S(2)}) collective-permute-start(bf16[432,256]{1,0:T(8,128)(2,1)S(1)} %add_convert_fusion), channel_id=1, source_target_pairs={{0,4},{1,5},{2,6},{3,7},{4,0},{5,1},{6,2},{7,3},{8,12},{9,13},{10,... | collective-permute-start | bytes 663560 | tf_op jit(solution)/shard_map/ppermute | solution.py:35
  71.0 8.1 %collective-permute-start.23 = (bf16[432,256]{1,0:T(8,128)(2,1)S(1)}, bf16[432,256]{1,0:T(8,128)(2,1)S(1)}, u32[]{:S(2)}, u32[]{:S(2)}) collective-permute-start(bf16[432,256]{1,0:T(8,128)(2,1)S(1)} %add_convert_fusion), channel_id=1, source_target_pairs={{0,2},{1,3},{2,0},{3,1},{4,6},{5,7},{6,4},{7,5},{8,10},{9,11},{10,... | collective-permute-start | bytes 663560 | tf_op jit(solution)/shard_map/ppermute | solution.py:35
  79.2 14.4 %collective-permute-start.24 = (bf16[4,432,256]{2,1,0:T(8,128)(2,1)S(1)}, bf16[4,432,256]{2,1,0:T(8,128)(2,1)S(1)}, u32[]{:S(2)}, u32[]{:S(2)}) collective-permute-start(bf16[4,432,256]{2,1,0:T(8,128)(2,1)S(1)} %pad_maximum_fusion.1), channel_id=1, source_target_pairs={{0,1},{1,0},{2,3},{3,2},{4,5},{5,4},{6,7},{7,6},{8,9},{9,8},{10,11... | collective-permute-start | bytes 2654216 | tf_op jit(solution)/shard_map/ppermute | solution.py:35
  79.3 7.9 %collective-permute-start.21 = (bf16[432,256]{1,0:T(8,128)(2,1)S(1)}, bf16[432,256]{1,0:T(8,128)(2,1)S(1)}, u32[]{:S(2)}, u32[]{:S(2)}) collective-permute-start(bf16[432,256]{1,0:T(8,128)(2,1)S(1)} %collective-permute-done.19), channel_id=1, source_target_pairs={{0,4},{1,5},{2,6},{3,7},{4,0},{5,1},{6,2},{7,3},{8,12},{9,13},{10,... | collective-permute-start | bytes 663560 | tf_op jit(solution)/shard_map/ppermute | solution.py:35
  81.1 21.2 %collective-permute-start.20 = (bf16[2,432,256]{2,1,0:T(8,128)(2,1)S(1)}, bf16[2,432,256]{2,1,0:T(8,128)(2,1)S(1)}, u32[]{:S(2)}, u32[]{:S(2)}) collective-permute-start(bf16[2,432,256]{2,1,0:T(8,128)(2,1)S(1)} %pad_maximum_fusion.4), channel_id=1, source_target_pairs={{0,2},{1,3},{2,0},{3,1},{4,6},{5,7},{6,4},{7,5},{8,10},{9,11},{10,... | collective-permute-start | bytes 1327112 | tf_op jit(solution)/shard_map/ppermute | solution.py:35
  87.2 15.2 %collective-permute-start.22 = (bf16[432,256]{1,0:T(8,128)(2,1)S(1)}, bf16[432,256]{1,0:T(8,128)(2,1)S(1)}, u32[]{:S(2)}, u32[]{:S(2)}) collective-permute-start(bf16[432,256]{1,0:T(8,128)(2,1)S(1)} %collective-permute-done.21), channel_id=1, source_target_pairs={{0,2},{1,3},{2,0},{3,1},{4,6},{5,7},{6,4},{7,5},{8,10},{9,11},{10,... | collective-permute-start | bytes 663560 | tf_op jit(solution)/shard_map/ppermute | solution.py:35
  88.3 9.8 %collective-permute-start.25 = (bf16[272,256]{1,0:T(8,128)(2,1)S(1)}, bf16[272,256]{1,0:T(8,128)(2,1)S(1)}, u32[]{:S(2)}, u32[]{:S(2)}) collective-permute-start(bf16[272,256]{1,0:T(8,128)(2,1)S(1)} %get-tuple-element.136), channel_id=1, source_target_pairs={{0,4},{1,5},{2,6},{3,7},{4,8},{5,9},{6,10},{7,11},{8,12},{9,13},{1... | collective-permute-start | bytes 417800 | tf_op jit(solution)/shard_map/ppermute | solution.py:39
  90.1 12.3 %collective-permute-start.26 = (bf16[272,256]{1,0:T(8,128)(2,1)S(1)}, bf16[272,256]{1,0:T(8,128)(2,1)S(1)}, u32[]{:S(2)}, u32[]{:S(2)}) collective-permute-start(bf16[272,256]{1,0:T(8,128)(2,1)S(1)} %get-tuple-element.137), channel_id=1, source_target_pairs={{0,8},{1,9},{2,10},{3,11},{4,12},{5,13},{6,14},{7,15},{8,0},{9,1},... | collective-permute-start | bytes 417800 | tf_op jit(solution)/shard_map/ppermute | solution.py:39
  93.6 8.7 %collective-permute-start.27 = (bf16[272,256]{1,0:T(8,128)(2,1)S(1)}, bf16[272,256]{1,0:T(8,128)(2,1)S(1)}, u32[]{:S(2)}, u32[]{:S(2)}) collective-permute-start(bf16[272,256]{1,0:T(8,128)(2,1)S(1)} %get-tuple-element.138), channel_id=1, source_target_pairs={{0,12},{1,13},{2,14},{3,15},{4,0},{5,1},{6,2},{7,3},{8,4},{9,5},{1... | collective-permute-start | bytes 417800 | tf_op jit(solution)/shard_map/ppermute | solution.py:39
  (6 other events, 22.3 us)

commit v10 on v9

--- a/solution.py
+++ b/solution.py
@@ -278,6 +278,7 @@
     copy.wait()
     for place in range(outer * 4):
         table[place] = 0
+        table[outer * 4 + 4 + place] = -1
     for plane in range(16):
         dev, side, brick = plane // 4, plane // 2 % 2, plane % 2
         dest = links[dev * 8, brick * 2 + side]
@@ -285,7 +286,9 @@
         @pl.when((dest >= 0) & ((dest // 2) % 4 == position % 4))
         def _():
             steps = lax.rem(dest // 8 - position // 4 + outer, outer)
-            table[steps * 4 + dest % 2 + (0 if side == 1 else 2)] = plane
+            slot = dest % 2 + (0 if side == 1 else 2)
+            table[steps * 4 + slot] = plane
+            table[outer * 4 + 4 + ((dest // 8) ^ (position // 4)) * 4 + slot] = plane
 
     for brick in range(2):
         for side in range(2):
@@ -302,7 +305,7 @@
         functools.partial(route_kernel, outer),
         in_specs=[WHOLE] * 4,
         out_specs=[SCALARS] + [WHOLE] * outer,
-        out_shape=[jax.ShapeDtypeStruct((outer * 4 + 4,), jnp.int32)]
+        out_shape=[jax.ShapeDtypeStruct((outer * 8 + 4,), jnp.int32)]
         + [pltpu.VMEM((256, width), jnp.bfloat16)] * outer,
         scratch_shapes=[
             pltpu.VMEM((32, 128), jnp.int32),
@@ -317,26 +320,64 @@
     return results[0], results[1:]
 
 
-def repeat_kernel(outer, table, *refs):
-    parcels, picks, planes = refs[:4], refs[4:-1], refs[-1]
-    copy_picks(outer, table, parcels, picks, planes)
+def deal_kernel(outer, table, *refs):
+    parcels, (give, keep, planes) = refs[:4], refs[4:]
+    for dev in range(4):
+        planes[256 * dev : 256 * dev + 256, :] = parcels[dev][:256, :]
+    for flip in range(outer):
+        target = (give if flip % 2 else keep).at[flip // 2]
+        for slot in range(4):
+            plane = table[outer * 4 + 4 + flip * 4 + slot]
+            rows = planes[aligned(jnp.maximum(plane, 0), 64), :]
+            target[64 * slot : 64 * slot + 64, :] = jnp.where(plane >= 0, rows.astype(jnp.float32), 0.0).astype(jnp.bfloat16)
     total = sum(read_extra(ref) for ref in parcels)
-    for ref in picks:
-        write_exact(total, ref)
-
-
-def repeat_route(table, parcels, outer):
+    for ref in (give, keep):
+        write_exact(total, ref.at[0])
+        for index in range(1, outer // 2):
+            ref[index, 256:272, :] = jnp.zeros((EXTRA, planes.shape[1]), jnp.bfloat16)
+
+
+def deal(table, parcels, outer):
     width = parcels[0].shape[1]
-    return pl.pallas_call(
-        functools.partial(repeat_kernel, outer),
+    shape = pltpu.VMEM((outer // 2, 256 + EXTRA, width), jnp.bfloat16)
+    return pl.pallas_call(
+        functools.partial(deal_kernel, outer),
         in_specs=[SCALARS] + [WHOLE] * 4,
-        out_specs=[WHOLE] * outer,
-        out_shape=[pltpu.VMEM((256 + EXTRA, width), jnp.bfloat16)] * outer,
+        out_specs=(WHOLE, WHOLE),
+        out_shape=(shape, shape),
         scratch_shapes=[pltpu.VMEM((1024, width), jnp.bfloat16)],
-        compiler_params=params(),
-        cost_estimate=cost(1024, 1024),
-        name="repeat_route",
+        compiler_params=params(8),
+        cost_estimate=cost(1024, 1024),
+        name="deal",
     )(table, *[near(x) for x in parcels])
+
+
+def merged(keep, got, index):
+    planes = keep[index, :256, :].astype(jnp.float32) + got[index, :256, :].astype(jnp.float32)
+    return planes
+
+
+def merge_kernel(kept, got, give, keep):
+    total = read_extra(kept.at[0]) + read_extra(got.at[0])
+    for index in range(kept.shape[0]):
+        target = (give if index % 2 else keep).at[index // 2]
+        target[:256, :] = merged(kept, got, index).astype(jnp.bfloat16)
+        target[256:272, :] = jnp.zeros((EXTRA, kept.shape[2]), jnp.bfloat16)
+    for ref in (give, keep):
+        write_exact(total, ref.at[0])
+
+
+def merge(kept, got):
+    shape = pltpu.VMEM((kept.shape[0] // 2, *kept.shape[1:]), jnp.bfloat16)
+    return pl.pallas_call(
+        merge_kernel,
+        in_specs=[WHOLE, WHOLE],
+        out_specs=(WHOLE, WHOLE),
+        out_shape=(shape, shape),
+        compiler_params=params(8),
+        cost_estimate=cost(1024, 1024),
+        name="merge",
+    )(near(kept), near(got))
 
 
 def chosen(table, slot, arrived):
@@ -599,52 +640,9 @@
     )(near(grad), near(parcel), near(mask), far(weight))
 
 
-def backward_halos_kernel(table, partial, mask, weight, done, *refs):
-    arrived, (grad_feats, bias_sum, planes, sent) = refs[:-4], refs[-4:]
-    width = weight.shape[1]
-    valid = windows((128, width), 0)
-    for side in range(2):
-        halo = jnp.concatenate([chosen(table, 2 * side + b, arrived) for b in range(2)], axis=0)
-        total = partial[side]
-        for at, moved in enumerate(shifts(halo, 0, valid, -1)):
-            total += lax.dot_general(
-                moved,
-                weight[18 * (1 - side) + at],
-                (((1,), (1,)), ((), ())),
-                preferred_element_type=jnp.float32,
-            )
-        rows = slice(896 * side, 896 * side + 128)
-        done_rows = jnp.where(wide(mask[rows, :]), total, 0.0).astype(jnp.bfloat16)
-        for b in range(2):
-            planes[side, b, 0] = done_rows[64 * b : 64 * b + 64]
-        pltpu.make_async_copy(planes.at[side], grad_feats.at[:, pl.ds(7 * side, 1)], sent.at[side]).start()
-    bias_sum[...] = sum(read_extra(ref) for ref in arrived)
-    for side in range(2):
-        pltpu.make_async_copy(planes.at[side], grad_feats.at[:, pl.ds(7 * side, 1)], sent.at[side]).wait()
-
-
-def backward_halos(table, partial, mask, weight, done, arrived):
-    width = weight.shape[1]
-    return pl.pallas_call(
-        backward_halos_kernel,
-        in_specs=[SCALARS] + [WHOLE] * 3 + [FAR] + [WHOLE] * len(arrived),
-        out_specs=(FAR, WHOLE),
-        out_shape=(jax.ShapeDtypeStruct(done.shape, done.dtype), jax.ShapeDtypeStruct((1, width), jnp.float32)),
-        scratch_shapes=[
-            pltpu.VMEM((2, 2, 1, 64, width), jnp.bfloat16),
-            pltpu.SemaphoreType.DMA((2,)),
-        ],
-        input_output_aliases={4: 0},
-        compiler_params=params(10),
-        cost_estimate=cost(1024, 1024),
-        name="backward_halos",
-    )(table, near(partial), near(mask), near(weight), done, *[near(x) for x in arrived])
-
-
-def assemble_kernel(outer, places, parts, *refs):
-    out, done = refs[-2:]
+def block_copies(outer, places, stacks, out, done):
     position = me()
-    blocks = [ref.at[index] for ref, count in zip(refs, parts) for index in range(count)]
+    blocks = [ref.at[index] for ref in stacks for index in range(ref.shape[0])]
     copies = []
     for index, (ref, (flip, inner, core)) in enumerate(zip(blocks, places)):
         block = (position // 4) ^ flip
@@ -657,29 +655,92 @@
             here = jnp.minimum(place, 107)
             target = out.at[here // 4, quarter + here % 4]
             copies.append((place < 108, pltpu.make_async_copy(ref.at[unit], target, done.at[index, unit])))
-    for wait in (False, True):
-        for condition, copy in copies:
-            act = copy.wait if wait else copy.start
-            if condition is None:
-                act()
-            else:
-                pl.when(condition)(act)
+    return copies
+
+
+def for_each(copies, wait):
+    for condition, copy in copies:
+        act = copy.wait if wait else copy.start
+        if condition is None:
+            act()
+        else:
+            pl.when(condition)(act)
+
+
+def assemble_kernel(outer, places, count, *refs):
+    out, done = refs[-2:]
+    copies = block_copies(outer, places, refs[:count], out, done)
+    for_each(copies, False)
+    for_each(copies, True)
+
+
+def in_units(stack, outer):
+    return near(stack.reshape(stack.shape[0], units(outer), 16, stack.shape[-1]))
 
 
 def assemble(outer, places, stacks, shape, given):
     before = [] if given is None else [given]
-    rows = units(outer)
-    return pl.pallas_call(
-        functools.partial(assemble_kernel, outer, places, [x.shape[0] for x in stacks]),
+    return pl.pallas_call(
+        functools.partial(assemble_kernel, outer, places, len(stacks)),
         in_specs=[WHOLE] * len(stacks) + [FAR] * len(before),
         out_specs=FAR,
         out_shape=jax.ShapeDtypeStruct(shape, jnp.bfloat16),
-        scratch_shapes=[pltpu.SemaphoreType.DMA((len(places), rows))],
+        scratch_shapes=[pltpu.SemaphoreType.DMA((len(places), units(outer)))],
         input_output_aliases={len(stacks): 0} if before else {},
         compiler_params=params(),
         cost_estimate=cost(1024, 1024),
         name="assemble",
-    )(*[near(x.reshape(x.shape[0], rows, 16, shape[-1])) for x in stacks], *before)
+    )(*[in_units(x, outer) for x in stacks], *before)
+
+
+def finish_kernel(outer, places, partial, mask, weight, kept, got, stack, feats_in, weight_in, *refs):
+    grad_feats, grad_weight, bias_sum, planes, sent, done = refs
+    copies = block_copies(outer, places, [stack], grad_weight, done)
+    for_each(copies, False)
+    width = weight.shape[1]
+    valid = windows((128, width), 0)
+    halos = merged(kept, got, 0)
+    for side in range(2):
+        total = partial[side]
+        for at, moved in enumerate(shifts(halos[128 * side : 128 * side + 128, :], 0, valid, -1)):
+            total += lax.dot_general(
+                moved,
+                weight[18 * (1 - side) + at],
+                (((1,), (1,)), ((), ())),
+                preferred_element_type=jnp.float32,
+            )
+        rows = slice(896 * side, 896 * side + 128)
+        done_rows = jnp.where(wide(mask[rows, :]), total, 0.0).astype(jnp.bfloat16)
+        for b in range(2):
+            planes[side, b, 0] = done_rows[64 * b : 64 * b + 64]
+        pltpu.make_async_copy(planes.at[side], grad_feats.at[:, pl.ds(7 * side, 1)], sent.at[side]).start()
+    bias_sum[...] = read_extra(kept.at[0]) + read_extra(got.at[0])
+    for side in range(2):
+        pltpu.make_async_copy(planes.at[side], grad_feats.at[:, pl.ds(7 * side, 1)], sent.at[side]).wait()
+    for_each(copies, True)
+
+
+def finish(outer, places, partial, mask, weight, kept, got, stack, grad_feats, grad_weight):
+    width = weight.shape[1]
+    return pl.pallas_call(
+        functools.partial(finish_kernel, outer, places),
+        in_specs=[WHOLE] * 6 + [FAR, FAR],
+        out_specs=(FAR, FAR, WHOLE),
+        out_shape=(
+            jax.ShapeDtypeStruct(grad_feats.shape, grad_feats.dtype),
+            jax.ShapeDtypeStruct(grad_weight.shape, grad_weight.dtype),
+            jax.ShapeDtypeStruct((1, width), jnp.float32),
+        ),
+        scratch_shapes=[
+            pltpu.VMEM((2, 2, 1, 64, width), jnp.bfloat16),
+            pltpu.SemaphoreType.DMA((2,)),
+            pltpu.SemaphoreType.DMA((len(places), units(outer))),
+        ],
+        input_output_aliases={6: 0, 7: 1},
+        compiler_params=params(10),
+        cost_estimate=cost(1024, 1024),
+        name="finish",
+    )(*[near(x) for x in (partial, mask, weight, kept, got)], in_units(stack, outer), grad_feats, grad_weight)
 
 
 def per_device(size, feats, voxmask, links, weight, bias, cotangent):
@@ -691,12 +752,13 @@
     inner, rows = lax.optimization_barrier((swap(parcel, size, 2), rows))
     parcels = [parcel, inner, swap(parcel, size, 1), swap(inner, size, 1)]
     out, grad, edge, bias_local = forward_inside(rows, mask, taps, bias.reshape(1, width), ends)
+    *parcels, grad = lax.optimization_barrier((*parcels, grad))
+    table, picks = route(parcels, outer)
+
+    *picks, give_core, grad = lax.optimization_barrier((*picks, give_core, grad))
+    arrived = [rotate(pick, size, steps) if steps else pick for steps, pick in enumerate(picks)]
     got_inner = swap(give_inner, size, 2)
-    *parcels, grad, got_inner = lax.optimization_barrier((*parcels, grad, got_inner))
-    table, picks = route(parcels, outer)
-
-    *picks, give_core = lax.optimization_barrier((*picks, give_core))
-    arrived = [rotate(pick, size, steps) if steps else pick for steps, pick in enumerate(picks)]
+    got_inner, grad = lax.optimization_barrier((got_inner, grad))
     grad_inner = swap(grad, size, 2)
     *arrived, got_inner, grad_inner = lax.optimization_barrier((*arrived, got_inner, grad_inner))
     others = turn(got_inner, swap(give_core, size, 1), swap(got_inner, size, 1))
@@ -710,16 +772,22 @@
 
     gives, stay = outer_terms(outer, turned, others, halos, parcels, terms)
     gots = [rotate(give, size, steps + 1) for steps, give in enumerate(gives)]
+    give, kept = deal(table, parcels, outer)
+    got = swap(give, size, 4)
     grad_feats, partial, taps = backward(grad, to_inner, mask, weight)
-    picks = repeat_route(table, parcels, outer)
-    stay, partial, *picks = lax.optimization_barrier((stay, partial, *picks))
+    bits = outer.bit_length() - 1
+    for bit in range(1, bits):
+        give, kept = merge(kept, got)
+        if bit < bits - 1:
+            got = swap(give, size, 4 << bit)
+    stay, partial, give, kept = lax.optimization_barrier((stay, partial, give, kept))
     part = (stay + sum(got.astype(jnp.float32) for got in gots)).astype(jnp.bfloat16)
 
     def stack(*blocks):
         return jnp.concatenate([x.reshape(-1, *part.shape) for x in blocks])
 
     def place_blocks(keys, blocks, given):
-        places = [(flip, bit, core) for core in range(2) for flip, bit in keys]
+        places = [(*key, core) for core in range(2) for key in keys]
         return assemble(outer, places, [blocks, swap(blocks, size, 1)], (27, 16, width // 16, width), given)
 
     last = outer - 1
@@ -730,17 +798,21 @@
     first_inner = swap(part, size, 2)
     middle = stack(*blocks[1:])
     farthest = swap(blocks[last & (last - 1)], size, 4)
-    middle, *picks = lax.optimization_barrier((middle, *picks))
+    middle, give = lax.optimization_barrier((middle, give))
     middle_inner = swap(middle, size, 2)
-    arrived = [rotate(pick, size, steps) if steps else pick for steps, pick in enumerate(picks)]
+    got = swap(give, size, 4 << (bits - 1))
     grad_weight = place_blocks([(0, 0), (0, 1)] + [(flip, 0) for flip in flips], stack(part, first_inner, middle), None)
     farthest_inner = swap(farthest, size, 2)
-    middle_inner, farthest_inner, grad_weight, *arrived = lax.optimization_barrier(
-        (middle_inner, farthest_inner, grad_weight, *arrived)
+    middle_inner, farthest_inner, grad_weight, got = lax.optimization_barrier(
+        (middle_inner, farthest_inner, grad_weight, got)
     )
     keys = [(flip, 1) for flip in flips] + [(last, 0), (last, 1)]
-    grad_weight = place_blocks(keys, stack(middle_inner, farthest, farthest_inner), grad_weight)
-    grad_feats, grad_bias = backward_halos(table, partial, mask, taps, grad_feats, arrived)
+    rest = stack(middle_inner, farthest, farthest_inner)
+    theirs = swap(rest, size, 1)
+    grad_feats, grad_weight, grad_bias = finish(
+        outer, [(*key, 0) for key in keys], partial, mask, taps, kept, got, rest, grad_feats, grad_weight
+    )
+    grad_weight = assemble(outer, [(*key, 1) for key in keys], [theirs], grad_weight.shape, grad_weight)
     return out, grad_feats, grad_weight.reshape(weight.shape), grad_bias.reshape(width)
 
 

time: 110 us -> 105 us (0.955); the launches traced: 109 us -> 105 us
  starting transfers between devices: 36.3 us -> 31.6 us
  waiting for transfers between devices: 32.4 us -> 33.8 us
    ppermute x9 -> x6, starting transfers between devices: 18.1 us -> 10.2 us  [rotate(): lax.ppermute(x, 'zslab', [(i, (i + 4 * steps) % size) for i in range(size)])]
    ppermute x20 -> x22, waiting for transfers between devices: 17.5 us -> 21 us  [swap(): return lax.ppermute(x, 'zslab', [(i, i ^ bit) for i in range(size)])]
    ppermute x20 -> x22, starting transfers between devices: 18.2 us -> 21.4 us  [swap(): return lax.ppermute(x, 'zslab', [(i, i ^ bit) for i in range(size)])]
    ppermute x9 -> x6, waiting for transfers between devices: 14.9 us -> 12.8 us  [rotate(): lax.ppermute(x, 'zslab', [(i, (i + 4 * steps) % size) for i in range(size)])]
    pallas_call x4 -> x5, Pallas kernels: 9.62 us -> 9.03 us  [the longest x2 5.03 us: assemble(): pl.pallas_call(functools.partial(assemble_kernel, outer, places, len(stac...]
  transfers between devices with their start and end apart: 29 -> 28, of which waited for: 11 -> 12; matrix products, arithmetic and copies ran while one was open for 0% -> 0% of each run, Pallas kernels for 30% -> 33%
where the time goes in v10:
time: 105 us
  Pallas kernels  37.8 us (36%)
  waiting for transfers between devices  33.8 us (32%)
  starting transfers between devices  31.6 us (30%)
    ppermute x22, starting transfers between devices, swap(): return lax.ppermute(x, 'zslab', [(i, i ^ bit) for i in range(size)])  21.4 us
    ppermute x22, waiting for transfers between devices, swap(): return lax.ppermute(x, 'zslab', [(i, i ^ bit) for i in range(size)])  21 us
    ppermute x6, waiting for transfers between devices, rotate(): lax.ppermute(x, 'zslab', [(i, (i + 4 * steps) % size) for i in range(size)])  12.8 us
    ppermute x6, starting transfers between devices, rotate(): lax.ppermute(x, 'zslab', [(i, (i + 4 * steps) % size) for i in range(size)])  10.2 us
    pallas_call x1, Pallas kernels, backward(): pl.pallas_call(backward_kernel, in_specs=[WHOLE] * 3 + [FAR], out_specs=(...  8.95 us
    pallas_call x2, Pallas kernels, assemble(): pl.pallas_call(functools.partial(assemble_kernel, outer, places, len(stac...  5.03 us
    pallas_call x1, Pallas kernels, prepare(): pl.pallas_call(prepare_kernel, in_specs=[FAR] * 4, out_specs=(WHOLE,) * 7...  4.77 us
    pallas_call x1, Pallas kernels, forward_inside(): pl.pallas_call(forward_kernel, in_specs=[WHOLE] * 5, out_specs=(WHOLE,) *...  4.66 us
  transfers between devices with their start and end apart: 28, of which 12 were waited for; matrix products, arithmetic and copies ran while one was open for 0% of the time, Pallas kernels for 33%

profile of v10, /device:TPU:0, one launch (start us, length us, event | category | flops | bytes accessed | tf_op | source)
XLA Modules:
  0.0 104.8 jit_solution(6644453026376235077)
XLA Ops:
  1.7 3.0 %collective-permute-start = (bf16[272,256]{1,0:T(8,128)(2,1)S(1)}, bf16[272,256]{1,0:T(8,128)(2,1)S(1)}, u32[]{:S(2)}, u32[]{:S(2)}) collective-permute-start(bf16[272,256]{1,0:T(8,128)(2,1)S(1)} %rims.1.refs_0_), channel_id=1, source_target_pairs={{0,2},{1,3},{2,0},{3,1},{4,6},{5,7},{6,4},{7,5},{8,10},{9,11},{10,... | collective-permute-start | bytes 417800 | tf_op jit(solution)/shard_map/ppermute | solution.py:35
  4.8 4.8 %prepare.1 = (f32[1024,128]{1,0:T(8,128)S(1)}, bf16[1024,256]{1,0:T(8,128)(2,1)S(1)}, bf16[128,1024]{1,0:T(8,128)(2,1)S(1)}, bf16[64,1024]{1,0:T(8,128)(2,1)S(1)...) custom-call(bf16[2,8,64,256]{3,2,1,0:T(8,128)(2,1)} %feats.3, ...), custom_call_target="tpu_custom_call" | custom-call | flops 1024 | bytes 1024 | tf_op jit(solution)/shard_map/prepare/pallas_call | solution.py:209
  10.2 4.7 %forward_inside.1 = (bf16[2,8,64,256]{3,2,1,0:T(8,128)(2,1)}, bf16[768,256]{1,0:T(8,128)(2,1)S(1)}, f32[2,128,256]{2,1,0:T(8,128)S(1)}, f32[1,256]{1,0:T(1,128)S(1)}) custom-call(bf16[1024,256]{1,0:T(8,128)(2,1)S(1)} %get-tuple-element.73.rows, f32[1024,128]{1,0:T(8,128)S(1)} %get-tuple-element.74.mask, bf16[27,256,256]{2,1,0:T(8,128)(2,1)S(1)} %get-tuple-element.75.weight, ...), custom_call_target="tpu_custom_call" | custom-call | flops 1024 | bytes 1024 | tf_op jit(solution)/shard_map/forward_inside/pallas_call | solution.py:420
  14.9 1.7 %route.1 = (s32[36]{0:T(128)S(1)}, bf16[256,256]{1,0:T(8,128)(2,1)S(1)}, bf16[256,256]{1,0:T(8,128)(2,1)S(1)}, bf16[256,256]{1,0:T(8,128)(2,1)S(1)}, bf16[256,256]{1,0:T(8,128)(2,1)S(1)}) custom-call(bf16[272,256]{1,0:T(8,128)(2,1)S(1)} %rims.1.refs_0_, bf16[272,256]{1,0:T(8,128)(2,1)S(1)} %collective-permute-done.refs_1_, ...), custom_call_target="tpu_custom_call" | custom-call | flops 1024 | bytes 1024 | tf_op jit(solution)/shard_map/route/pallas_call | solution.py:304
  20.2 2.6 %collective-permute-start.4 = (bf16[256,256]{1,0:T(8,128)(2,1)S(1)}, bf16[256,256]{1,0:T(8,128)(2,1)S(1)}, u32[]{:S(2)}, u32[]{:S(2)}) collective-permute-start(bf16[256,256]{1,0:T(8,128)(2,1)S(1)} %get-tuple-element.94), channel_id=1, source_target_pairs={{0,8},{1,9},{2,10},{3,11},{4,12},{5,13},{6,14},{7,15},{8,0},{9,1},... | collective-permute-start | bytes 393224 | tf_op jit(solution)/shard_map/ppermute | solution.py:39
  24.2 2.8 %collective-permute-done.3.refs_1_ = bf16[256,256]{1,0:T(8,128)(2,1)S(1)} collective-permute-done((bf16[256,256]{1,0:T(8,128)(2,1)S(1)}, bf16[256,256]{1,0:T(8,128)(2,1)S(1)}, u32[]{:S(2)}, u32[]{:S(2)}) %collective-permute-start.3) | collective-permute-done | bytes 131104 | tf_op jit(solution)/shard_map/ppermute | solution.py:39
  26.9 4.4 %collective-permute-done.4.refs_2_ = bf16[256,256]{1,0:T(8,128)(2,1)S(1)} collective-permute-done((bf16[256,256]{1,0:T(8,128)(2,1)S(1)}, bf16[256,256]{1,0:T(8,128)(2,1)S(1)}, u32[]{:S(2)}, u32[]{:S(2)}) %collective-permute-start.4) | collective-permute-done | bytes 131104 | tf_op jit(solution)/shard_map/ppermute | solution.py:39
  31.9 1.9 %forward_edges.1 = (bf16[2,8,64,256]{3,2,1,0:T(8,128)(2,1)}, bf16[400,256]{1,0:T(8,128)(2,1)S(1)}, bf16[336,256]{1,0:T(8,128)(2,1)S(1)}, bf16[64,256]{1,0:T(8,128)(2,1)S(1)}) custom-call(s32[36]{0:T(128)S(1)} %get-tuple-element.82.table, f32[1024,128]{1,0:T(8,128)S(1)} %get-tuple-element.74.mask, ...), custom_call_target="tpu_custom_call", output_to_operand_aliasing={{0}: (6, {})} | custom-call | flops 1024 | bytes 1024 | tf_op jit(solution)/shard_map/forward_edges/pallas_call | solution.py:497
  36.7 2.9 %inner_terms.1.refs_4_ = f32[1728,256]{1,0:T(8,128)S(1)} custom-call(bf16[576,1024]{1,0:T(8,128)(2,1)S(1)} %get-tuple-element.105.mine, bf16[1728,1024]{1,0:T(8,128)(2,1)S(1)} %turn.1.others, bf16[768,256]{1,0:T(8,128)(2,1)S(1)} %get-tuple-element.99.refs_0_.grad, bf16[768,256]{1,0:T(8,128)(2,1)S(1)} %collective-permute-done.7.refs_1_, ...), custom_call_target="tpu_custom_call" | custom-call | flops 1024 | bytes 1024 | tf_op jit(solution)/shard_map/inner_terms/pallas_call | solution.py:455
  43.3 3.3 %collective-permute-start.15 = (bf16[2,272,256]{2,1,0:T(8,128)(2,1)S(1)}, bf16[2,272,256]{2,1,0:T(8,128)(2,1)S(1)}, u32[]{:S(2)}, u32[]{:S(2)}) collective-permute-start(bf16[2,272,256]{2,1,0:T(8,128)(2,1)S(1)} %get-tuple-element.117), channel_id=1, source_target_pairs={{0,4},{1,5},{2,6},{3,7},{4,0},{5,1},{6,2},{7,3},{8,12},{9,13},{10,... | collective-permute-start | bytes 835592 | tf_op jit(solution)/shard_map/ppermute | solution.py:35
  46.6 1.8 %outer_terms.1 = (bf16[432,256]{1,0:T(8,128)(2,1)S(1)}, bf16[432,256]{1,0:T(8,128)(2,1)S(1)}, bf16[432,256]{1,0:T(8,128)(2,1)S(1)}, f32[432,256]{1,0:T(8,128)S(1)}) custom-call(bf16[576,1024]{1,0:T(8,128)(2,1)S(1)} %get-tuple-element.105.mine, bf16[1728,1024]{1,0:T(8,128)(2,1)S(1)} %turn.1.others, bf16[64,256]{1,0:T(8,128)(2,1)S(1)} %get-tuple-element.108.halos, ...), custom_call_target="tpu_custom_call" | custom-call | flops 1024 | bytes 1024 | tf_op jit(solution)/shard_map/outer_terms/pallas_call | solution.py:574
  48.5 1.8 %collective-permute-start.17 = (bf16[432,256]{1,0:T(8,128)(2,1)S(1)}, bf16[432,256]{1,0:T(8,128)(2,1)S(1)}, u32[]{:S(2)}, u32[]{:S(2)}) collective-permute-start(bf16[432,256]{1,0:T(8,128)(2,1)S(1)} %get-tuple-element.125), channel_id=1, source_target_pairs={{0,8},{1,9},{2,10},{3,11},{4,12},{5,13},{6,14},{7,15},{8,0},{9,1},... | collective-permute-start | bytes 663560 | tf_op jit(solution)/shard_map/ppermute | solution.py:39
  50.3 2.8 %collective-permute-start.18 = (bf16[432,256]{1,0:T(8,128)(2,1)S(1)}, bf16[432,256]{1,0:T(8,128)(2,1)S(1)}, u32[]{:S(2)}, u32[]{:S(2)}) collective-permute-start(bf16[432,256]{1,0:T(8,128)(2,1)S(1)} %get-tuple-element.126), channel_id=1, source_target_pairs={{0,12},{1,13},{2,14},{3,15},{4,0},{5,1},{6,2},{7,3},{8,4},{9,5},{1... | collective-permute-start | bytes 663560 | tf_op jit(solution)/shard_map/ppermute | solution.py:39
  53.1 9.0 %backward.1 = (bf16[2,8,64,256]{3,2,1,0:T(8,128)(2,1)}, f32[2,128,256]{2,1,0:T(8,128)S(1)}, bf16[27,256,256]{2,1,0:T(8,128)(2,1)S(1)}) custom-call(bf16[768,256]{1,0:T(8,128)(2,1)S(1)} %get-tuple-element.99.refs_0_.grad, bf16[400,256]{1,0:T(8,128)(2,1)S(1)} %get-tuple-element.109.refs_0_.parcel, f32[1024,128]{1,0:T(8,128)S(1)} %get-tuple-element.74.mask, ...), custom_call_target="tpu_custom_call" | custom-call | flops 1024 | bytes 1024 | tf_op jit(solution)/shard_map/backward/pallas_call | solution.py:623
  62.2 5.1 %collective-permute-done.17 = bf16[432,256]{1,0:T(8,128)(2,1)S(1)} collective-permute-done((bf16[432,256]{1,0:T(8,128)(2,1)S(1)}, bf16[432,256]{1,0:T(8,128)(2,1)S(1)}, u32[]{:S(2)}, u32[]{:S(2)}) %collective-permute-start.17) | collective-permute-done | bytes 221216 | tf_op jit(solution)/shard_map/ppermute | solution.py:39
  68.0 2.8 %collective-permute-start.20 = (bf16[432,256]{1,0:T(8,128)(2,1)S(1)}, bf16[432,256]{1,0:T(8,128)(2,1)S(1)}, u32[]{:S(2)}, u32[]{:S(2)}) collective-permute-start(bf16[432,256]{1,0:T(8,128)(2,1)S(1)} %add_convert_fusion), channel_id=1, source_target_pairs={{0,8},{1,9},{2,10},{3,11},{4,12},{5,13},{6,14},{7,15},{8,0},{9,1},... | collective-permute-start | bytes 663560 | tf_op jit(solution)/shard_map/ppermute | solution.py:35
  70.7 2.7 %collective-permute-start.19 = (bf16[432,256]{1,0:T(8,128)(2,1)S(1)}, bf16[432,256]{1,0:T(8,128)(2,1)S(1)}, u32[]{:S(2)}, u32[]{:S(2)}) collective-permute-start(bf16[432,256]{1,0:T(8,128)(2,1)S(1)} %add_convert_fusion), channel_id=1, source_target_pairs={{0,4},{1,5},{2,6},{3,7},{4,0},{5,1},{6,2},{7,3},{8,12},{9,13},{10,... | collective-permute-start | bytes 663560 | tf_op jit(solution)/shard_map/ppermute | solution.py:35
  73.9 6.8 %collective-permute-done.20 = bf16[432,256]{1,0:T(8,128)(2,1)S(1)} collective-permute-done((bf16[432,256]{1,0:T(8,128)(2,1)S(1)}, bf16[432,256]{1,0:T(8,128)(2,1)S(1)}, u32[]{:S(2)}, u32[]{:S(2)}) %collective-permute-start.20) | collective-permute-done | bytes 221216 | tf_op jit(solution)/shard_map/ppermute | solution.py:35
  82.8 6.0 %collective-permute-done.22 = bf16[432,256]{1,0:T(8,128)(2,1)S(1)} collective-permute-done((bf16[432,256]{1,0:T(8,128)(2,1)S(1)}, bf16[432,256]{1,0:T(8,128)(2,1)S(1)}, u32[]{:S(2)}, u32[]{:S(2)}) %collective-permute-start.22) | collective-permute-done | bytes 221216 | tf_op jit(solution)/shard_map/ppermute | solution.py:35
  89.3 3.2 %collective-permute-start.26 = (bf16[1,272,256]{2,1,0:T(8,128)(2,1)S(1)}, bf16[1,272,256]{2,1,0:T(8,128)(2,1)S(1)}, u32[]{:S(2)}, u32[]{:S(2)}) collective-permute-start(bf16[1,272,256]{2,1,0:T(8,128)(2,1)S(1)} %get-tuple-element.129), channel_id=1, source_target_pairs={{0,8},{1,9},{2,10},{3,11},{4,12},{5,13},{6,14},{7,15},{8,0},{9,1},... | collective-permute-start | bytes 417800 | tf_op jit(solution)/shard_map/ppermute | solution.py:35
  92.6 3.1 %assemble.2.weight_in = bf16[27,16,16,256]{3,2,1,0:T(8,128)(2,1)} custom-call(bf16[4,27,16,256]{3,2,1,0:T(8,128)(2,1)S(1)} %pad_maximum_fusion.refs_0_, bf16[4,27,16,256]{3,2,1,0:T(8,128)(2,1)S(1)} %bitcast.17), custom_call_target="tpu_custom_call" | custom-call | flops 1024 | bytes 1024 | tf_op jit(solution)/shard_map/assemble/pallas_call | solution.py:683
  95.7 2.9 %collective-permute-done.26.got = bf16[1,272,256]{2,1,0:T(8,128)(2,1)S(1)} collective-permute-done((bf16[1,272,256]{2,1,0:T(8,128)(2,1)S(1)}, bf16[1,272,256]{2,1,0:T(8,128)(2,1)S(1)}, u32[]{:S(2)}, u32[]{:S(2)}) %collective-permute-start.26) | collective-permute-done | bytes 139296 | tf_op jit(solution)/shard_map/ppermute | solution.py:35
  99.5 3.2 %finish.1 = (bf16[2,8,64,256]{3,2,1,0:T(8,128)(2,1)}, bf16[27,16,16,256]{3,2,1,0:T(8,128)(2,1)}, f32[1,256]{1,0:T(1,128)}) custom-call(f32[2,128,256]{2,1,0:T(8,128)S(1)} %get-tuple-element.120.partial, f32[1024,128]{1,0:T(8,128)S(1)} %get-tuple-element.74.mask, ...), custom_call_target="tpu_custom_call", output_to_operand_aliasing={{0}: (6, {}), {1}: (7, {})} | custom-call | flops 1024 | bytes 1024 | tf_op jit(solution)/shard_map/finish/pallas_call | solution.py:725
  102.8 1.9 %assemble.3 = bf16[27,16,16,256]{3,2,1,0:T(8,128)(2,1)} custom-call(bf16[4,27,16,256]{3,2,1,0:T(8,128)(2,1)S(1)} %bitcast.18, bf16[27,16,16,256]{3,2,1,0:T(8,128)(2,1)} %get-tuple-element.136.refs_1_), custom_call_target="tpu_custom_call", output_to_operand_aliasing={{}: (1, {})} | custom-call | flops 1024 | bytes 1024 | tf_op jit(solution)/shard_map/assemble/pallas_call | solution.py:683
  (54 shorter events, 18.6 us)
Async XLA Ops:
  1.7 8.0 %collective-permute-start = (bf16[272,256]{1,0:T(8,128)(2,1)S(1)}, bf16[272,256]{1,0:T(8,128)(2,1)S(1)}, u32[]{:S(2)}, u32[]{:S(2)}) collective-permute-start(bf16[272,256]{1,0:T(8,128)(2,1)S(1)} %rims.1.refs_0_), channel_id=1, source_target_pairs={{0,2},{1,3},{2,0},{3,1},{4,6},{5,7},{6,4},{7,5},{8,10},{9,11},{10,... | collective-permute-start | bytes 417800 | tf_op jit(solution)/shard_map/ppermute | solution.py:35
  9.6 7.8 %collective-permute-start.6 = (bf16[128,1024]{1,0:T(8,128)(2,1)S(1)}, bf16[128,1024]{1,0:T(8,128)(2,1)S(1)}, u32[]{:S(2)}, u32[]{:S(2)}) collective-permute-start(bf16[128,1024]{1,0:T(8,128)(2,1)S(1)} %get-tuple-element.96), channel_id=1, source_target_pairs={{0,2},{1,3},{2,0},{3,1},{4,6},{5,7},{6,4},{7,5},{8,10},{9,11},{10,... | collective-permute-start | bytes 786440 | tf_op jit(solution)/shard_map/ppermute | solution.py:35
  9.6 5.2 %collective-permute-start.1 = (bf16[272,256]{1,0:T(8,128)(2,1)S(1)}, bf16[272,256]{1,0:T(8,128)(2,1)S(1)}, u32[]{:S(2)}, u32[]{:S(2)}) collective-permute-start(bf16[272,256]{1,0:T(8,128)(2,1)S(1)} %rims.1.refs_0_), channel_id=1, source_target_pairs={{0,1},{1,0},{2,3},{3,2},{4,5},{5,4},{6,7},{7,6},{8,9},{9,8},{10,11... | collective-permute-start | bytes 417800 | tf_op jit(solution)/shard_map/ppermute | solution.py:35
  9.7 5.2 %collective-permute-start.2 = (bf16[272,256]{1,0:T(8,128)(2,1)S(1)}, bf16[272,256]{1,0:T(8,128)(2,1)S(1)}, u32[]{:S(2)}, u32[]{:S(2)}) collective-permute-start(bf16[272,256]{1,0:T(8,128)(2,1)S(1)} %collective-permute-done.refs_1_), channel_id=1, source_target_pairs={{0,1},{1,0},{2,3},{3,2},{4,5},{5,4},{6,7},{7,6},{8,9},{9,8},{10,11... | collective-permute-start | bytes 417800 | tf_op jit(solution)/shard_map/ppermute | solution.py:35
  17.4 14.0 %collective-permute-start.7 = (bf16[768,256]{1,0:T(8,128)(2,1)S(1)}, bf16[768,256]{1,0:T(8,128)(2,1)S(1)}, u32[]{:S(2)}, u32[]{:S(2)}) collective-permute-start(bf16[768,256]{1,0:T(8,128)(2,1)S(1)} %get-tuple-element.99.refs_0_.grad), channel_id=1, source_target_pairs={{0,2},{1,3},{2,0},{3,1},{4,6},{5,7},{6,4},{7,5},{8,10},{9,11},{10,... | collective-permute-start | bytes 1179656 | tf_op jit(solution)/shard_map/ppermute | solution.py:35
  18.6 8.3 %collective-permute-start.3 = (bf16[256,256]{1,0:T(8,128)(2,1)S(1)}, bf16[256,256]{1,0:T(8,128)(2,1)S(1)}, u32[]{:S(2)}, u32[]{:S(2)}) collective-permute-start(bf16[256,256]{1,0:T(8,128)(2,1)S(1)} %get-tuple-element.93), channel_id=1, source_target_pairs={{0,4},{1,5},{2,6},{3,7},{4,8},{5,9},{6,10},{7,11},{8,12},{9,13},{1... | collective-permute-start | bytes 393224 | tf_op jit(solution)/shard_map/ppermute | solution.py:39
  20.2 11.1 %collective-permute-start.4 = (bf16[256,256]{1,0:T(8,128)(2,1)S(1)}, bf16[256,256]{1,0:T(8,128)(2,1)S(1)}, u32[]{:S(2)}, u32[]{:S(2)}) collective-permute-start(bf16[256,256]{1,0:T(8,128)(2,1)S(1)} %get-tuple-element.94), channel_id=1, source_target_pairs={{0,8},{1,9},{2,10},{3,11},{4,12},{5,13},{6,14},{7,15},{8,0},{9,1},... | collective-permute-start | bytes 393224 | tf_op jit(solution)/shard_map/ppermute | solution.py:39
  22.8 8.5 %collective-permute-start.5 = (bf16[256,256]{1,0:T(8,128)(2,1)S(1)}, bf16[256,256]{1,0:T(8,128)(2,1)S(1)}, u32[]{:S(2)}, u32[]{:S(2)}) collective-permute-start(bf16[256,256]{1,0:T(8,128)(2,1)S(1)} %get-tuple-element.95), channel_id=1, source_target_pairs={{0,12},{1,13},{2,14},{3,15},{4,0},{5,1},{6,2},{7,3},{8,4},{9,5},{1... | collective-permute-start | bytes 393224 | tf_op jit(solution)/shard_map/ppermute | solution.py:39
  24.2 12.5 %collective-permute-start.11 = (bf16[768,256]{1,0:T(8,128)(2,1)S(1)}, bf16[768,256]{1,0:T(8,128)(2,1)S(1)}, u32[]{:S(2)}, u32[]{:S(2)}) collective-permute-start(bf16[768,256]{1,0:T(8,128)(2,1)S(1)} %get-tuple-element.99.refs_0_.grad), channel_id=1, source_target_pairs={{0,1},{1,0},{2,3},{3,2},{4,5},{5,4},{6,7},{7,6},{8,9},{9,8},{10,11... | collective-permute-start | bytes 1179656 | tf_op jit(solution)/shard_map/ppermute | solution.py:35
  31.3 5.4 %collective-permute-start.12 = (bf16[768,256]{1,0:T(8,128)(2,1)S(1)}, bf16[768,256]{1,0:T(8,128)(2,1)S(1)}, u32[]{:S(2)}, u32[]{:S(2)}) collective-permute-start(bf16[768,256]{1,0:T(8,128)(2,1)S(1)} %collective-permute-done.7.refs_1_), channel_id=1, source_target_pairs={{0,1},{1,0},{2,3},{3,2},{4,5},{5,4},{6,7},{7,6},{8,9},{9,8},{10,11... | collective-permute-start | bytes 1179656 | tf_op jit(solution)/shard_map/ppermute | solution.py:35
  31.4 4.4 %collective-permute-start.9 = (bf16[128,1024]{1,0:T(8,128)(2,1)S(1)}, bf16[128,1024]{1,0:T(8,128)(2,1)S(1)}, u32[]{:S(2)}, u32[]{:S(2)}) collective-permute-start(bf16[128,1024]{1,0:T(8,128)(2,1)S(1)} %collective-permute-done.6.inner), channel_id=1, source_target_pairs={{0,1},{1,0},{2,3},{3,2},{4,5},{5,4},{6,7},{7,6},{8,9},{9,8},{10,11... | collective-permute-start | bytes 786440 | tf_op jit(solution)/shard_map/ppermute | solution.py:35
  33.8 7.1 %collective-permute-start.10 = (bf16[400,256]{1,0:T(8,128)(2,1)S(1)}, bf16[400,256]{1,0:T(8,128)(2,1)S(1)}, u32[]{:S(2)}, u32[]{:S(2)}) collective-permute-start(bf16[400,256]{1,0:T(8,128)(2,1)S(1)} %get-tuple-element.109.refs_0_.parcel), channel_id=1, source_target_pairs={{0,2},{1,3},{2,0},{3,1},{4,6},{5,7},{6,4},{7,5},{8,10},{9,11},{10,... | collective-permute-start | bytes 614408 | tf_op jit(solution)/shard_map/ppermute | solution.py:35
  43.3 18.8 %collective-permute-start.15 = (bf16[2,272,256]{2,1,0:T(8,128)(2,1)S(1)}, bf16[2,272,256]{2,1,0:T(8,128)(2,1)S(1)}, u32[]{:S(2)}, u32[]{:S(2)}) collective-permute-start(bf16[2,272,256]{2,1,0:T(8,128)(2,1)S(1)} %get-tuple-element.117), channel_id=1, source_target_pairs={{0,4},{1,5},{2,6},{3,7},{4,0},{5,1},{6,2},{7,3},{8,12},{9,13},{10,... | collective-permute-start | bytes 835592 | tf_op jit(solution)/shard_map/ppermute | solution.py:35
  48.4 13.7 %collective-permute-start.16 = (bf16[432,256]{1,0:T(8,128)(2,1)S(1)}, bf16[432,256]{1,0:T(8,128)(2,1)S(1)}, u32[]{:S(2)}, u32[]{:S(2)}) collective-permute-start(bf16[432,256]{1,0:T(8,128)(2,1)S(1)} %get-tuple-element.124), channel_id=1, source_target_pairs={{0,4},{1,5},{2,6},{3,7},{4,8},{5,9},{6,10},{7,11},{8,12},{9,13},{1... | collective-permute-start | bytes 663560 | tf_op jit(solution)/shard_map/ppermute | solution.py:39
  48.5 18.7 %collective-permute-start.17 = (bf16[432,256]{1,0:T(8,128)(2,1)S(1)}, bf16[432,256]{1,0:T(8,128)(2,1)S(1)}, u32[]{:S(2)}, u32[]{:S(2)}) collective-permute-start(bf16[432,256]{1,0:T(8,128)(2,1)S(1)} %get-tuple-element.125), channel_id=1, source_target_pairs={{0,8},{1,9},{2,10},{3,11},{4,12},{5,13},{6,14},{7,15},{8,0},{9,1},... | collective-permute-start | bytes 663560 | tf_op jit(solution)/shard_map/ppermute | solution.py:39
  50.3 17.6 %collective-permute-start.18 = (bf16[432,256]{1,0:T(8,128)(2,1)S(1)}, bf16[432,256]{1,0:T(8,128)(2,1)S(1)}, u32[]{:S(2)}, u32[]{:S(2)}) collective-permute-start(bf16[432,256]{1,0:T(8,128)(2,1)S(1)} %get-tuple-element.126), channel_id=1, source_target_pairs={{0,12},{1,13},{2,14},{3,15},{4,0},{5,1},{6,2},{7,3},{8,4},{9,5},{1... | collective-permute-start | bytes 663560 | tf_op jit(solution)/shard_map/ppermute | solution.py:39
  68.0 12.8 %collective-permute-start.20 = (bf16[432,256]{1,0:T(8,128)(2,1)S(1)}, bf16[432,256]{1,0:T(8,128)(2,1)S(1)}, u32[]{:S(2)}, u32[]{:S(2)}) collective-permute-start(bf16[432,256]{1,0:T(8,128)(2,1)S(1)} %add_convert_fusion), channel_id=1, source_target_pairs={{0,8},{1,9},{2,10},{3,11},{4,12},{5,13},{6,14},{7,15},{8,0},{9,1},... | collective-permute-start | bytes 663560 | tf_op jit(solution)/shard_map/ppermute | solution.py:35
  70.7 10.0 %collective-permute-start.19 = (bf16[432,256]{1,0:T(8,128)(2,1)S(1)}, bf16[432,256]{1,0:T(8,128)(2,1)S(1)}, u32[]{:S(2)}, u32[]{:S(2)}) collective-permute-start(bf16[432,256]{1,0:T(8,128)(2,1)S(1)} %add_convert_fusion), channel_id=1, source_target_pairs={{0,4},{1,5},{2,6},{3,7},{4,0},{5,1},{6,2},{7,3},{8,12},{9,13},{10,... | collective-permute-start | bytes 663560 | tf_op jit(solution)/shard_map/ppermute | solution.py:35
  73.4 7.4 %collective-permute-start.24 = (bf16[432,256]{1,0:T(8,128)(2,1)S(1)}, bf16[432,256]{1,0:T(8,128)(2,1)S(1)}, u32[]{:S(2)}, u32[]{:S(2)}) collective-permute-start(bf16[432,256]{1,0:T(8,128)(2,1)S(1)} %add_convert_fusion), channel_id=1, source_target_pairs={{0,2},{1,3},{2,0},{3,1},{4,6},{5,7},{6,4},{7,5},{8,10},{9,11},{10,... | collective-permute-start | bytes 663560 | tf_op jit(solution)/shard_map/ppermute | solution.py:35
  80.9 11.7 %collective-permute-start.25 = (bf16[4,432,256]{2,1,0:T(8,128)(2,1)S(1)}, bf16[4,432,256]{2,1,0:T(8,128)(2,1)S(1)}, u32[]{:S(2)}, u32[]{:S(2)}) collective-permute-start(bf16[4,432,256]{2,1,0:T(8,128)(2,1)S(1)} %pad_maximum_fusion.1), channel_id=1, source_target_pairs={{0,1},{1,0},{2,3},{3,2},{4,5},{5,4},{6,7},{7,6},{8,9},{9,8},{10,11... | collective-permute-start | bytes 2654216 | tf_op jit(solution)/shard_map/ppermute | solution.py:35
  81.0 7.8 %collective-permute-start.22 = (bf16[432,256]{1,0:T(8,128)(2,1)S(1)}, bf16[432,256]{1,0:T(8,128)(2,1)S(1)}, u32[]{:S(2)}, u32[]{:S(2)}) collective-permute-start(bf16[432,256]{1,0:T(8,128)(2,1)S(1)} %collective-permute-done.20), channel_id=1, source_target_pairs={{0,4},{1,5},{2,6},{3,7},{4,0},{5,1},{6,2},{7,3},{8,12},{9,13},{10,... | collective-permute-start | bytes 663560 | tf_op jit(solution)/shard_map/ppermute | solution.py:35
  82.2 17.0 %collective-permute-start.21 = (bf16[2,432,256]{2,1,0:T(8,128)(2,1)S(1)}, bf16[2,432,256]{2,1,0:T(8,128)(2,1)S(1)}, u32[]{:S(2)}, u32[]{:S(2)}) collective-permute-start(bf16[2,432,256]{2,1,0:T(8,128)(2,1)S(1)} %pad_maximum_fusion.4), channel_id=1, source_target_pairs={{0,2},{1,3},{2,0},{3,1},{4,6},{5,7},{6,4},{7,5},{8,10},{9,11},{10,... | collective-permute-start | bytes 1327112 | tf_op jit(solution)/shard_map/ppermute | solution.py:35
  88.8 10.4 %collective-permute-start.23 = (bf16[432,256]{1,0:T(8,128)(2,1)S(1)}, bf16[432,256]{1,0:T(8,128)(2,1)S(1)}, u32[]{:S(2)}, u32[]{:S(2)}) collective-permute-start(bf16[432,256]{1,0:T(8,128)(2,1)S(1)} %collective-permute-done.22), channel_id=1, source_target_pairs={{0,2},{1,3},{2,0},{3,1},{4,6},{5,7},{6,4},{7,5},{8,10},{9,11},{10,... | collective-permute-start | bytes 663560 | tf_op jit(solution)/shard_map/ppermute | solution.py:35
  89.3 9.4 %collective-permute-start.26 = (bf16[1,272,256]{2,1,0:T(8,128)(2,1)S(1)}, bf16[1,272,256]{2,1,0:T(8,128)(2,1)S(1)}, u32[]{:S(2)}, u32[]{:S(2)}) collective-permute-start(bf16[1,272,256]{2,1,0:T(8,128)(2,1)S(1)} %get-tuple-element.129), channel_id=1, source_target_pairs={{0,8},{1,9},{2,10},{3,11},{4,12},{5,13},{6,14},{7,15},{8,0},{9,1},... | collective-permute-start | bytes 417800 | tf_op jit(solution)/shard_map/ppermute | solution.py:35
  (5 other events, 17.8 us)

commit v11 on v10

--- a/solution.py
+++ b/solution.py
@@ -33,10 +33,6 @@
 
 def swap(x, size, bit):
     return lax.ppermute(x, "zslab", [(i, i ^ bit) for i in range(size)])
-
-
-def rotate(x, size, steps):
-    return lax.ppermute(x, "zslab", [(i, (i + 4 * steps) % size) for i in range(size)])
 
 
 def me():
@@ -258,15 +254,6 @@
     )(near(inner), near(core), near(both_changed))
 
 
-def copy_picks(outer, table, parcels, picks, planes):
-    for dev in range(4):
-        planes[256 * dev : 256 * dev + 256, :] = parcels[dev][:256, :]
-    for steps in range(outer):
-        for slot in range(4):
-            start = pl.multiple_of(table[steps * 4 + slot] * 64, 64)
-            picks[steps][64 * slot : 64 * slot + 64, :] = planes[pl.ds(start, 64), :]
-
-
 def route_kernel(outer, *refs):
     position = me()
     parcels, (table, *picks), (codes, links, planes, done) = refs[:4], refs[4:-4], refs[-4:]
@@ -275,28 +262,28 @@
         codes[8 * dev : 8 * dev + 8, :] = row[:8, :].astype(jnp.int32)
     copy = pltpu.make_async_copy(codes, links, done)
     copy.start()
+    for dev in range(4):
+        planes[256 * dev : 256 * dev + 256, :] = parcels[dev][:256, :]
+    for place in range(outer * 4):
+        table[place] = -1
     copy.wait()
-    for place in range(outer * 4):
-        table[place] = 0
-        table[outer * 4 + 4 + place] = -1
     for plane in range(16):
         dev, side, brick = plane // 4, plane // 2 % 2, plane % 2
         dest = links[dev * 8, brick * 2 + side]
 
         @pl.when((dest >= 0) & ((dest // 2) % 4 == position % 4))
         def _():
-            steps = lax.rem(dest // 8 - position // 4 + outer, outer)
-            slot = dest % 2 + (0 if side == 1 else 2)
-            table[steps * 4 + slot] = plane
-            table[outer * 4 + 4 + ((dest // 8) ^ (position // 4)) * 4 + slot] = plane
+            flip = (dest // 8) ^ (position // 4)
+            table[flip * 4 + dest % 2 + (0 if side == 1 else 2)] = plane
 
     for brick in range(2):
         for side in range(2):
             dest = links[0, brick * 2 + side]
-            steps = lax.rem(position // 4 - dest // 8 + outer, outer)
-            table[outer * 4 + 2 * side + brick] = jnp.where(dest >= 0, steps, -1)
-
-    copy_picks(outer, table, parcels, picks, planes)
+            table[outer * 4 + 2 * side + brick] = jnp.where(dest >= 0, (dest // 8) ^ (position // 4), -1)
+    for flip in range(outer):
+        for slot in range(4):
+            plane = jnp.maximum(table[flip * 4 + slot], 0)
+            picks[flip][64 * slot : 64 * slot + 64, :] = planes[aligned(plane, 64), :]
 
 
 def route(parcels, outer):
@@ -305,7 +292,7 @@
         functools.partial(route_kernel, outer),
         in_specs=[WHOLE] * 4,
         out_specs=[SCALARS] + [WHOLE] * outer,
-        out_shape=[jax.ShapeDtypeStruct((outer * 8 + 4,), jnp.int32)]
+        out_shape=[jax.ShapeDtypeStruct((outer * 4 + 4,), jnp.int32)]
         + [pltpu.VMEM((256, width), jnp.bfloat16)] * outer,
         scratch_shapes=[
             pltpu.VMEM((32, 128), jnp.int32),
@@ -327,7 +314,7 @@
     for flip in range(outer):
         target = (give if flip % 2 else keep).at[flip // 2]
         for slot in range(4):
-            plane = table[outer * 4 + 4 + flip * 4 + slot]
+            plane = table[flip * 4 + slot]
             rows = planes[aligned(jnp.maximum(plane, 0), 64), :]
             target[64 * slot : 64 * slot + 64, :] = jnp.where(plane >= 0, rows.astype(jnp.float32), 0.0).astype(jnp.bfloat16)
     total = sum(read_extra(ref) for ref in parcels)
@@ -383,8 +370,8 @@
 def chosen(table, slot, arrived):
     rows = slice(64 * slot, 64 * slot + 64)
     plane = jnp.zeros((64, arrived[0].shape[1]), jnp.float32)
-    for steps, ref in enumerate(arrived):
-        plane = jnp.where(table[4 * len(arrived) + slot] == steps, ref[rows, :].astype(jnp.float32), plane)
+    for flip, ref in enumerate(arrived):
+        plane = jnp.where(table[4 * len(arrived) + slot] == flip, ref[rows, :].astype(jnp.float32), plane)
     return plane
 
 
@@ -557,13 +544,12 @@
         total[span, :] = inner[span, :] + jnp.dot(cols[...], facing, preferred_element_type=jnp.float32)
     if total.shape[0] > 3 * rows:
         total[3 * rows :, :] = jnp.zeros((total.shape[0] - 3 * rows, total.shape[1]), jnp.float32)
-    z = me() // 4
-    for steps in range(outer):
-        block = lax.rem(z + steps, outer)
+    for flip in range(outer):
+        block = (me() // 4) ^ flip
         for unit in range(units(outer)):
             piece = total[aligned(block + outer * unit, 16), :]
-            if steps:
-                gives[steps - 1][16 * unit : 16 * unit + 16, :] = piece.astype(jnp.bfloat16)
+            if flip:
+                gives[flip - 1][16 * unit : 16 * unit + 16, :] = piece.astype(jnp.bfloat16)
             else:
                 stay[16 * unit : 16 * unit + 16, :] = piece
 
@@ -756,7 +742,7 @@
     table, picks = route(parcels, outer)
 
     *picks, give_core, grad = lax.optimization_barrier((*picks, give_core, grad))
-    arrived = [rotate(pick, size, steps) if steps else pick for steps, pick in enumerate(picks)]
+    arrived = [swap(pick, size, 4 * flip) if flip else pick for flip, pick in enumerate(picks)]
     got_inner = swap(give_inner, size, 2)
     got_inner, grad = lax.optimization_barrier((got_inner, grad))
     grad_inner = swap(grad, size, 2)
@@ -771,8 +757,9 @@
     parcels = [to_inner, inner, swap(to_core, size, 1), swap(inner, size, 1)]
 
     gives, stay = outer_terms(outer, turned, others, halos, parcels, terms)
-    gots = [rotate(give, size, steps + 1) for steps, give in enumerate(gives)]
     give, kept = deal(table, parcels, outer)
+    give, *gives = lax.optimization_barrier((give, *gives))
+    gots = [swap(x, size, 4 * flip) for flip, x in enumerate(gives, 1)]
     got = swap(give, size, 4)
     grad_feats, partial, taps = backward(grad, to_inner, mask, weight)
     bits = outer.bit_length() - 1
@@ -796,23 +783,23 @@
     for flip in flips:
         blocks.append(swap(blocks[flip & (flip - 1)], size, 4 * (flip & -flip)))
     first_inner = swap(part, size, 2)
-    middle = stack(*blocks[1:])
+    near_inner = swap(first_inner, size, 4)
+    upper, give = lax.optimization_barrier((stack(*blocks[2:]), give))
+    upper_inner = swap(upper, size, 2)
     farthest = swap(blocks[last & (last - 1)], size, 4)
-    middle, give = lax.optimization_barrier((middle, give))
-    middle_inner = swap(middle, size, 2)
     got = swap(give, size, 4 << (bits - 1))
-    grad_weight = place_blocks([(0, 0), (0, 1)] + [(flip, 0) for flip in flips], stack(part, first_inner, middle), None)
+    farthest, got = lax.optimization_barrier((farthest, got))
     farthest_inner = swap(farthest, size, 2)
-    middle_inner, farthest_inner, grad_weight, got = lax.optimization_barrier(
-        (middle_inner, farthest_inner, grad_weight, got)
-    )
-    keys = [(flip, 1) for flip in flips] + [(last, 0), (last, 1)]
-    rest = stack(middle_inner, farthest, farthest_inner)
+    grad_weight = place_blocks([(0, 0), (0, 1)] + [(flip, 0) for flip in flips], stack(part, first_inner, *blocks[1:]), None)
+    keys = [(1, 1)] + [(flip, 1) for flip in flips[1:]] + [(last, 0)]
+    grad_weight = place_blocks(keys, stack(near_inner, upper_inner, farthest), grad_weight)
+    farthest_inner, grad_weight = lax.optimization_barrier((farthest_inner, grad_weight))
+    rest = stack(farthest_inner)
     theirs = swap(rest, size, 1)
     grad_feats, grad_weight, grad_bias = finish(
-        outer, [(*key, 0) for key in keys], partial, mask, taps, kept, got, rest, grad_feats, grad_weight
+        outer, [(last, 1, 0)], partial, mask, taps, kept, got, rest, grad_feats, grad_weight
     )
-    grad_weight = assemble(outer, [(*key, 1) for key in keys], [theirs], grad_weight.shape, grad_weight)
+    grad_weight = assemble(outer, [(last, 1, 1)], [theirs], grad_weight.shape, grad_weight)
     return out, grad_feats, grad_weight.reshape(weight.shape), grad_bias.reshape(width)
 
 

time: 105 us -> 111 us (1.057)
  waiting for transfers between devices: 33.8 us -> 46.2 us
  starting transfers between devices: 31.6 us -> 25 us
    ppermute x22 -> x30, waiting for transfers between devices: 21 us -> 46.2 us  [swap(): return lax.ppermute(x, 'zslab', [(i, i ^ bit) for i in range(size)])]
    ppermute x6 -> x0, waiting for transfers between devices: 12.8 us -> none  [rotate(): lax.ppermute(x, 'zslab', [(i, (i + 4 * steps) % size) for i in range(size)])]
    ppermute x6 -> x0, starting transfers between devices: 10.2 us -> none  [rotate(): lax.ppermute(x, 'zslab', [(i, (i + 4 * steps) % size) for i in range(size)])]
    ppermute x22 -> x30, starting transfers between devices: 21.4 us -> 25 us  [swap(): return lax.ppermute(x, 'zslab', [(i, i ^ bit) for i in range(size)])]
    pallas_call x2 -> x3, Pallas kernels: 5.03 us -> 6.6 us  [assemble(): pl.pallas_call(functools.partial(assemble_kernel, outer, places, len(stac...]
  transfers between devices with their start and end apart: 28 -> 30, of which waited for: 12 -> 13; matrix products, arithmetic and copies ran while one was open for 0% -> 0% of each run, Pallas kernels for 33% -> 31%
where the time goes in v11:
time: 111 us
  waiting for transfers between devices  46.2 us (42%)
  Pallas kernels  38.5 us (35%)
  starting transfers between devices  25 us (23%)
    ppermute x30, waiting for transfers between devices, swap(): return lax.ppermute(x, 'zslab', [(i, i ^ bit) for i in range(size)])  46.2 us
    ppermute x30, starting transfers between devices, swap(): return lax.ppermute(x, 'zslab', [(i, i ^ bit) for i in range(size)])  25 us
    pallas_call x1, Pallas kernels, backward(): pl.pallas_call(backward_kernel, in_specs=[WHOLE] * 3 + [FAR], out_specs=(...  9.12 us
    pallas_call x3, Pallas kernels, assemble(): pl.pallas_call(functools.partial(assemble_kernel, outer, places, len(stac...  6.6 us
    pallas_call x1, Pallas kernels, prepare(): pl.pallas_call(prepare_kernel, in_specs=[FAR] * 4, out_specs=(WHOLE,) * 7...  4.77 us
    pallas_call x1, Pallas kernels, forward_inside(): pl.pallas_call(forward_kernel, in_specs=[WHOLE] * 5, out_specs=(WHOLE,) *...  4.66 us
    pallas_call x1, Pallas kernels, inner_terms(): pl.pallas_call(inner_terms_kernel, in_specs=[WHOLE] * 6, out_specs=WHOLE,...  2.93 us
    pallas_call x1, Pallas kernels, finish(): pl.pallas_call(functools.partial(finish_kernel, outer, places), in_specs=...  2.4 us
  transfers between devices with their start and end apart: 30, of which 13 were waited for; matrix products, arithmetic and copies ran while one was open for 0% of the time, Pallas kernels for 31%

profile of v11, /device:TPU:0, one launch (start us, length us, event | category | flops | bytes accessed | tf_op | source)
XLA Modules:
  0.0 111.2 jit_solution(15108253054214647069)
XLA Ops:
  1.7 3.0 %collective-permute-start = (bf16[272,256]{1,0:T(8,128)(2,1)S(1)}, bf16[272,256]{1,0:T(8,128)(2,1)S(1)}, u32[]{:S(2)}, u32[]{:S(2)}) collective-permute-start(bf16[272,256]{1,0:T(8,128)(2,1)S(1)} %rims.1.refs_0_), channel_id=1, source_target_pairs={{0,2},{1,3},{2,0},{3,1},{4,6},{5,7},{6,4},{7,5},{8,10},{9,11},{10,... | collective-permute-start | bytes 417800 | tf_op jit(solution)/shard_map/ppermute | solution.py:35
  4.8 4.8 %prepare.1 = (f32[1024,128]{1,0:T(8,128)S(1)}, bf16[1024,256]{1,0:T(8,128)(2,1)S(1)}, bf16[128,1024]{1,0:T(8,128)(2,1)S(1)}, bf16[64,1024]{1,0:T(8,128)(2,1)S(1)...) custom-call(bf16[2,8,64,256]{3,2,1,0:T(8,128)(2,1)} %feats.3, ...), custom_call_target="tpu_custom_call" | custom-call | flops 1024 | bytes 1024 | tf_op jit(solution)/shard_map/prepare/pallas_call | solution.py:205
  10.2 4.7 %forward_inside.1 = (bf16[2,8,64,256]{3,2,1,0:T(8,128)(2,1)}, bf16[768,256]{1,0:T(8,128)(2,1)S(1)}, f32[2,128,256]{2,1,0:T(8,128)S(1)}, f32[1,256]{1,0:T(1,128)S(1)}) custom-call(bf16[1024,256]{1,0:T(8,128)(2,1)S(1)} %get-tuple-element.77.rows, f32[1024,128]{1,0:T(8,128)S(1)} %get-tuple-element.78.mask, bf16[27,256,256]{2,1,0:T(8,128)(2,1)S(1)} %get-tuple-element.79.weight, ...), custom_call_target="tpu_custom_call" | custom-call | flops 1024 | bytes 1024 | tf_op jit(solution)/shard_map/forward_inside/pallas_call | solution.py:407
  14.9 1.7 %route.1 = (s32[20]{0:T(128)S(1)}, bf16[256,256]{1,0:T(8,128)(2,1)S(1)}, bf16[256,256]{1,0:T(8,128)(2,1)S(1)}, bf16[256,256]{1,0:T(8,128)(2,1)S(1)}, bf16[256,256]{1,0:T(8,128)(2,1)S(1)}) custom-call(bf16[272,256]{1,0:T(8,128)(2,1)S(1)} %rims.1.refs_0_, bf16[272,256]{1,0:T(8,128)(2,1)S(1)} %collective-permute-done.refs_1_, ...), custom_call_target="tpu_custom_call" | custom-call | flops 1024 | bytes 1024 | tf_op jit(solution)/shard_map/route/pallas_call | solution.py:291
  18.6 1.6 %collective-permute-start.3 = (bf16[256,256]{1,0:T(8,128)(2,1)S(1)}, bf16[256,256]{1,0:T(8,128)(2,1)S(1)}, u32[]{:S(2)}, u32[]{:S(2)}) collective-permute-start(bf16[256,256]{1,0:T(8,128)(2,1)S(1)} %get-tuple-element.97), channel_id=1, source_target_pairs={{0,4},{1,5},{2,6},{3,7},{4,0},{5,1},{6,2},{7,3},{8,12},{9,13},{10,... | collective-permute-start | bytes 393224 | tf_op jit(solution)/shard_map/ppermute | solution.py:35
  20.2 2.6 %collective-permute-start.4 = (bf16[256,256]{1,0:T(8,128)(2,1)S(1)}, bf16[256,256]{1,0:T(8,128)(2,1)S(1)}, u32[]{:S(2)}, u32[]{:S(2)}) collective-permute-start(bf16[256,256]{1,0:T(8,128)(2,1)S(1)} %get-tuple-element.98), channel_id=1, source_target_pairs={{0,8},{1,9},{2,10},{3,11},{4,12},{5,13},{6,14},{7,15},{8,0},{9,1},... | collective-permute-start | bytes 393224 | tf_op jit(solution)/shard_map/ppermute | solution.py:35
  23.0 2.3 %collective-permute-done.3.refs_1_ = bf16[256,256]{1,0:T(8,128)(2,1)S(1)} collective-permute-done((bf16[256,256]{1,0:T(8,128)(2,1)S(1)}, bf16[256,256]{1,0:T(8,128)(2,1)S(1)}, u32[]{:S(2)}, u32[]{:S(2)}) %collective-permute-start.3) | collective-permute-done | bytes 131104 | tf_op jit(solution)/shard_map/ppermute | solution.py:35
  25.2 7.7 %collective-permute-done.4.refs_2_ = bf16[256,256]{1,0:T(8,128)(2,1)S(1)} collective-permute-done((bf16[256,256]{1,0:T(8,128)(2,1)S(1)}, bf16[256,256]{1,0:T(8,128)(2,1)S(1)}, u32[]{:S(2)}, u32[]{:S(2)}) %collective-permute-start.4) | collective-permute-done | bytes 131104 | tf_op jit(solution)/shard_map/ppermute | solution.py:35
  33.5 1.9 %forward_edges.1 = (bf16[2,8,64,256]{3,2,1,0:T(8,128)(2,1)}, bf16[400,256]{1,0:T(8,128)(2,1)S(1)}, bf16[336,256]{1,0:T(8,128)(2,1)S(1)}, bf16[64,256]{1,0:T(8,128)(2,1)S(1)}) custom-call(s32[20]{0:T(128)S(1)} %get-tuple-element.86.table, f32[1024,128]{1,0:T(8,128)S(1)} %get-tuple-element.78.mask, ...), custom_call_target="tpu_custom_call", output_to_operand_aliasing={{0}: (6, {})} | custom-call | flops 1024 | bytes 1024 | tf_op jit(solution)/shard_map/forward_edges/pallas_call | solution.py:484
  38.3 2.9 %inner_terms.1.refs_4_ = f32[1728,256]{1,0:T(8,128)S(1)} custom-call(bf16[576,1024]{1,0:T(8,128)(2,1)S(1)} %get-tuple-element.109.mine, bf16[1728,1024]{1,0:T(8,128)(2,1)S(1)} %turn.1.others, bf16[768,256]{1,0:T(8,128)(2,1)S(1)} %get-tuple-element.103.refs_0_.grad, bf16[768,256]{1,0:T(8,128)(2,1)S(1)} %collective-permute-done.7.refs_1_, ...), custom_call_target="tpu_custom_call" | custom-call | flops 1024 | bytes 1024 | tf_op jit(solution)/shard_map/inner_terms/pallas_call | solution.py:442
  45.0 1.7 %outer_terms.1 = (bf16[432,256]{1,0:T(8,128)(2,1)S(1)}, bf16[432,256]{1,0:T(8,128)(2,1)S(1)}, bf16[432,256]{1,0:T(8,128)(2,1)S(1)}, f32[432,256]{1,0:T(8,128)S(1)}) custom-call(bf16[576,1024]{1,0:T(8,128)(2,1)S(1)} %get-tuple-element.109.mine, bf16[1728,1024]{1,0:T(8,128)(2,1)S(1)} %turn.1.others, bf16[64,256]{1,0:T(8,128)(2,1)S(1)} %get-tuple-element.112.halos, ...), custom_call_target="tpu_custom_call" | custom-call | flops 1024 | bytes 1024 | tf_op jit(solution)/shard_map/outer_terms/pallas_call | solution.py:560
  46.6 2.0 %collective-permute-start.15 = (bf16[2,272,256]{2,1,0:T(8,128)(2,1)S(1)}, bf16[2,272,256]{2,1,0:T(8,128)(2,1)S(1)}, u32[]{:S(2)}, u32[]{:S(2)}) collective-permute-start(bf16[2,272,256]{2,1,0:T(8,128)(2,1)S(1)} %get-tuple-element.125), channel_id=1, source_target_pairs={{0,4},{1,5},{2,6},{3,7},{4,0},{5,1},{6,2},{7,3},{8,12},{9,13},{10,... | collective-permute-start | bytes 835592 | tf_op jit(solution)/shard_map/ppermute | solution.py:35
  48.7 2.9 %collective-permute-start.17 = (bf16[432,256]{1,0:T(8,128)(2,1)S(1)}, bf16[432,256]{1,0:T(8,128)(2,1)S(1)}, u32[]{:S(2)}, u32[]{:S(2)}) collective-permute-start(bf16[432,256]{1,0:T(8,128)(2,1)S(1)} %get-tuple-element.133), channel_id=1, source_target_pairs={{0,8},{1,9},{2,10},{3,11},{4,12},{5,13},{6,14},{7,15},{8,0},{9,1},... | collective-permute-start | bytes 663560 | tf_op jit(solution)/shard_map/ppermute | solution.py:35
  53.0 9.1 %backward.1 = (bf16[2,8,64,256]{3,2,1,0:T(8,128)(2,1)}, f32[2,128,256]{2,1,0:T(8,128)S(1)}, bf16[27,256,256]{2,1,0:T(8,128)(2,1)S(1)}) custom-call(bf16[768,256]{1,0:T(8,128)(2,1)S(1)} %get-tuple-element.103.refs_0_.grad, bf16[400,256]{1,0:T(8,128)(2,1)S(1)} %get-tuple-element.113.refs_0_.parcel, f32[1024,128]{1,0:T(8,128)S(1)} %get-tuple-element.78.mask, ...), custom_call_target="tpu_custom_call" | custom-call | flops 1024 | bytes 1024 | tf_op jit(solution)/shard_map/backward/pallas_call | solution.py:609
  62.2 2.9 %collective-permute-done.16 = bf16[432,256]{1,0:T(8,128)(2,1)S(1)} collective-permute-done((bf16[432,256]{1,0:T(8,128)(2,1)S(1)}, bf16[432,256]{1,0:T(8,128)(2,1)S(1)}, u32[]{:S(2)}, u32[]{:S(2)}) %collective-permute-start.16) | collective-permute-done | bytes 221216 | tf_op jit(solution)/shard_map/ppermute | solution.py:35
  65.1 6.9 %collective-permute-done.18 = bf16[432,256]{1,0:T(8,128)(2,1)S(1)} collective-permute-done((bf16[432,256]{1,0:T(8,128)(2,1)S(1)}, bf16[432,256]{1,0:T(8,128)(2,1)S(1)}, u32[]{:S(2)}, u32[]{:S(2)}) %collective-permute-start.18) | collective-permute-done | bytes 221216 | tf_op jit(solution)/shard_map/ppermute | solution.py:35
  74.7 8.7 %collective-permute-done.19 = bf16[432,256]{1,0:T(8,128)(2,1)S(1)} collective-permute-done((bf16[432,256]{1,0:T(8,128)(2,1)S(1)}, bf16[432,256]{1,0:T(8,128)(2,1)S(1)}, u32[]{:S(2)}, u32[]{:S(2)}) %collective-permute-start.19) | collective-permute-done | bytes 221216 | tf_op jit(solution)/shard_map/ppermute | solution.py:35
  84.0 3.0 %collective-permute-start.20 = (bf16[432,256]{1,0:T(8,128)(2,1)S(1)}, bf16[432,256]{1,0:T(8,128)(2,1)S(1)}, u32[]{:S(2)}, u32[]{:S(2)}) collective-permute-start(bf16[432,256]{1,0:T(8,128)(2,1)S(1)} %collective-permute-done.19), channel_id=1, source_target_pairs={{0,4},{1,5},{2,6},{3,7},{4,0},{5,1},{6,2},{7,3},{8,12},{9,13},{10,... | collective-permute-start | bytes 663560 | tf_op jit(solution)/shard_map/ppermute | solution.py:35
  87.2 5.6 %collective-permute-done.21.got = bf16[1,272,256]{2,1,0:T(8,128)(2,1)S(1)} collective-permute-done((bf16[1,272,256]{2,1,0:T(8,128)(2,1)S(1)}, bf16[1,272,256]{2,1,0:T(8,128)(2,1)S(1)}, u32[]{:S(2)}, u32[]{:S(2)}) %collective-permute-start.21) | collective-permute-done | bytes 139296 | tf_op jit(solution)/shard_map/ppermute | solution.py:35
  92.8 3.4 %collective-permute-done.20 = bf16[432,256]{1,0:T(8,128)(2,1)S(1)} collective-permute-done((bf16[432,256]{1,0:T(8,128)(2,1)S(1)}, bf16[432,256]{1,0:T(8,128)(2,1)S(1)}, u32[]{:S(2)}, u32[]{:S(2)}) %collective-permute-start.20) | collective-permute-done | bytes 221216 | tf_op jit(solution)/shard_map/ppermute | solution.py:35
  96.1 3.5 %collective-permute-done.24 = bf16[432,256]{1,0:T(8,128)(2,1)S(1)} collective-permute-done((bf16[432,256]{1,0:T(8,128)(2,1)S(1)}, bf16[432,256]{1,0:T(8,128)(2,1)S(1)}, u32[]{:S(2)}, u32[]{:S(2)}) %collective-permute-start.24) | collective-permute-done | bytes 221216 | tf_op jit(solution)/shard_map/ppermute | solution.py:35
  101.5 3.1 %assemble.3.refs_2_ = bf16[27,16,16,256]{3,2,1,0:T(8,128)(2,1)} custom-call(bf16[4,27,16,256]{3,2,1,0:T(8,128)(2,1)S(1)} %pad_maximum_fusion.refs_0_, bf16[4,27,16,256]{3,2,1,0:T(8,128)(2,1)S(1)} %bitcast.21), custom_call_target="tpu_custom_call" | custom-call | flops 1024 | bytes 1024 | tf_op jit(solution)/shard_map/assemble/pallas_call | solution.py:669
  104.7 2.5 %assemble.4.weight_in = bf16[27,16,16,256]{3,2,1,0:T(8,128)(2,1)} custom-call(bf16[3,27,16,256]{3,2,1,0:T(8,128)(2,1)S(1)} %pad_maximum_fusion.2.refs_0_, bf16[3,27,16,256]{3,2,1,0:T(8,128)(2,1)S(1)} %bitcast.22, bf16[27,16,16,256]{3,2,1,0:T(8,128)(2,1)} %assemble.3.refs_2_), custom_call_target="tpu_custom_call", output_to_operand_aliasing={{}: (2, {})} | custom-call | flops 1024 | bytes 1024 | tf_op jit(solution)/shard_map/assemble/pallas_call | solution.py:669
  107.6 2.4 %finish.1 = (bf16[2,8,64,256]{3,2,1,0:T(8,128)(2,1)}, bf16[27,16,16,256]{3,2,1,0:T(8,128)(2,1)}, f32[1,256]{1,0:T(1,128)}) custom-call(f32[2,128,256]{2,1,0:T(8,128)S(1)} %get-tuple-element.128.partial, f32[1024,128]{1,0:T(8,128)S(1)} %get-tuple-element.78.mask, ...), custom_call_target="tpu_custom_call", output_to_operand_aliasing={{0}: (6, {}), {1}: (7, {})} | custom-call | flops 1024 | bytes 1024 | tf_op jit(solution)/shard_map/finish/pallas_call | solution.py:711
  (58 shorter events, 19.3 us)
Async XLA Ops:
  1.7 8.0 %collective-permute-start = (bf16[272,256]{1,0:T(8,128)(2,1)S(1)}, bf16[272,256]{1,0:T(8,128)(2,1)S(1)}, u32[]{:S(2)}, u32[]{:S(2)}) collective-permute-start(bf16[272,256]{1,0:T(8,128)(2,1)S(1)} %rims.1.refs_0_), channel_id=1, source_target_pairs={{0,2},{1,3},{2,0},{3,1},{4,6},{5,7},{6,4},{7,5},{8,10},{9,11},{10,... | collective-permute-start | bytes 417800 | tf_op jit(solution)/shard_map/ppermute | solution.py:35
  9.6 7.8 %collective-permute-start.6 = (bf16[128,1024]{1,0:T(8,128)(2,1)S(1)}, bf16[128,1024]{1,0:T(8,128)(2,1)S(1)}, u32[]{:S(2)}, u32[]{:S(2)}) collective-permute-start(bf16[128,1024]{1,0:T(8,128)(2,1)S(1)} %get-tuple-element.100), channel_id=1, source_target_pairs={{0,2},{1,3},{2,0},{3,1},{4,6},{5,7},{6,4},{7,5},{8,10},{9,11},{10,... | collective-permute-start | bytes 786440 | tf_op jit(solution)/shard_map/ppermute | solution.py:35
  9.6 5.2 %collective-permute-start.1 = (bf16[272,256]{1,0:T(8,128)(2,1)S(1)}, bf16[272,256]{1,0:T(8,128)(2,1)S(1)}, u32[]{:S(2)}, u32[]{:S(2)}) collective-permute-start(bf16[272,256]{1,0:T(8,128)(2,1)S(1)} %rims.1.refs_0_), channel_id=1, source_target_pairs={{0,1},{1,0},{2,3},{3,2},{4,5},{5,4},{6,7},{7,6},{8,9},{9,8},{10,11... | collective-permute-start | bytes 417800 | tf_op jit(solution)/shard_map/ppermute | solution.py:35
  9.7 5.2 %collective-permute-start.2 = (bf16[272,256]{1,0:T(8,128)(2,1)S(1)}, bf16[272,256]{1,0:T(8,128)(2,1)S(1)}, u32[]{:S(2)}, u32[]{:S(2)}) collective-permute-start(bf16[272,256]{1,0:T(8,128)(2,1)S(1)} %collective-permute-done.refs_1_), channel_id=1, source_target_pairs={{0,1},{1,0},{2,3},{3,2},{4,5},{5,4},{6,7},{7,6},{8,9},{9,8},{10,11... | collective-permute-start | bytes 417800 | tf_op jit(solution)/shard_map/ppermute | solution.py:35
  17.4 15.6 %collective-permute-start.7 = (bf16[768,256]{1,0:T(8,128)(2,1)S(1)}, bf16[768,256]{1,0:T(8,128)(2,1)S(1)}, u32[]{:S(2)}, u32[]{:S(2)}) collective-permute-start(bf16[768,256]{1,0:T(8,128)(2,1)S(1)} %get-tuple-element.103.refs_0_.grad), channel_id=1, source_target_pairs={{0,2},{1,3},{2,0},{3,1},{4,6},{5,7},{6,4},{7,5},{8,10},{9,11},{10,... | collective-permute-start | bytes 1179656 | tf_op jit(solution)/shard_map/ppermute | solution.py:35
  18.6 6.7 %collective-permute-start.3 = (bf16[256,256]{1,0:T(8,128)(2,1)S(1)}, bf16[256,256]{1,0:T(8,128)(2,1)S(1)}, u32[]{:S(2)}, u32[]{:S(2)}) collective-permute-start(bf16[256,256]{1,0:T(8,128)(2,1)S(1)} %get-tuple-element.97), channel_id=1, source_target_pairs={{0,4},{1,5},{2,6},{3,7},{4,0},{5,1},{6,2},{7,3},{8,12},{9,13},{10,... | collective-permute-start | bytes 393224 | tf_op jit(solution)/shard_map/ppermute | solution.py:35
  20.2 12.8 %collective-permute-start.4 = (bf16[256,256]{1,0:T(8,128)(2,1)S(1)}, bf16[256,256]{1,0:T(8,128)(2,1)S(1)}, u32[]{:S(2)}, u32[]{:S(2)}) collective-permute-start(bf16[256,256]{1,0:T(8,128)(2,1)S(1)} %get-tuple-element.98), channel_id=1, source_target_pairs={{0,8},{1,9},{2,10},{3,11},{4,12},{5,13},{6,14},{7,15},{8,0},{9,1},... | collective-permute-start | bytes 393224 | tf_op jit(solution)/shard_map/ppermute | solution.py:35
  22.8 10.2 %collective-permute-start.5 = (bf16[256,256]{1,0:T(8,128)(2,1)S(1)}, bf16[256,256]{1,0:T(8,128)(2,1)S(1)}, u32[]{:S(2)}, u32[]{:S(2)}) collective-permute-start(bf16[256,256]{1,0:T(8,128)(2,1)S(1)} %get-tuple-element.99), channel_id=1, source_target_pairs={{0,12},{1,13},{2,14},{3,15},{4,8},{5,9},{6,10},{7,11},{8,4},{9,5},... | collective-permute-start | bytes 393224 | tf_op jit(solution)/shard_map/ppermute | solution.py:35
  23.0 15.3 %collective-permute-start.11 = (bf16[768,256]{1,0:T(8,128)(2,1)S(1)}, bf16[768,256]{1,0:T(8,128)(2,1)S(1)}, u32[]{:S(2)}, u32[]{:S(2)}) collective-permute-start(bf16[768,256]{1,0:T(8,128)(2,1)S(1)} %get-tuple-element.103.refs_0_.grad), channel_id=1, source_target_pairs={{0,1},{1,0},{2,3},{3,2},{4,5},{5,4},{6,7},{7,6},{8,9},{9,8},{10,11... | collective-permute-start | bytes 1179656 | tf_op jit(solution)/shard_map/ppermute | solution.py:35
  33.0 5.3 %collective-permute-start.12 = (bf16[768,256]{1,0:T(8,128)(2,1)S(1)}, bf16[768,256]{1,0:T(8,128)(2,1)S(1)}, u32[]{:S(2)}, u32[]{:S(2)}) collective-permute-start(bf16[768,256]{1,0:T(8,128)(2,1)S(1)} %collective-permute-done.7.refs_1_), channel_id=1, source_target_pairs={{0,1},{1,0},{2,3},{3,2},{4,5},{5,4},{6,7},{7,6},{8,9},{9,8},{10,11... | collective-permute-start | bytes 1179656 | tf_op jit(solution)/shard_map/ppermute | solution.py:35
  35.4 7.1 %collective-permute-start.10 = (bf16[400,256]{1,0:T(8,128)(2,1)S(1)}, bf16[400,256]{1,0:T(8,128)(2,1)S(1)}, u32[]{:S(2)}, u32[]{:S(2)}) collective-permute-start(bf16[400,256]{1,0:T(8,128)(2,1)S(1)} %get-tuple-element.113.refs_0_.parcel), channel_id=1, source_target_pairs={{0,2},{1,3},{2,0},{3,1},{4,6},{5,7},{6,4},{7,5},{8,10},{9,11},{10,... | collective-permute-start | bytes 614408 | tf_op jit(solution)/shard_map/ppermute | solution.py:35
  46.6 15.5 %collective-permute-start.15 = (bf16[2,272,256]{2,1,0:T(8,128)(2,1)S(1)}, bf16[2,272,256]{2,1,0:T(8,128)(2,1)S(1)}, u32[]{:S(2)}, u32[]{:S(2)}) collective-permute-start(bf16[2,272,256]{2,1,0:T(8,128)(2,1)S(1)} %get-tuple-element.125), channel_id=1, source_target_pairs={{0,4},{1,5},{2,6},{3,7},{4,0},{5,1},{6,2},{7,3},{8,12},{9,13},{10,... | collective-permute-start | bytes 835592 | tf_op jit(solution)/shard_map/ppermute | solution.py:35
  48.6 16.5 %collective-permute-start.16 = (bf16[432,256]{1,0:T(8,128)(2,1)S(1)}, bf16[432,256]{1,0:T(8,128)(2,1)S(1)}, u32[]{:S(2)}, u32[]{:S(2)}) collective-permute-start(bf16[432,256]{1,0:T(8,128)(2,1)S(1)} %get-tuple-element.132), channel_id=1, source_target_pairs={{0,4},{1,5},{2,6},{3,7},{4,0},{5,1},{6,2},{7,3},{8,12},{9,13},{10,... | collective-permute-start | bytes 663560 | tf_op jit(solution)/shard_map/ppermute | solution.py:35
  48.7 16.4 %collective-permute-start.17 = (bf16[432,256]{1,0:T(8,128)(2,1)S(1)}, bf16[432,256]{1,0:T(8,128)(2,1)S(1)}, u32[]{:S(2)}, u32[]{:S(2)}) collective-permute-start(bf16[432,256]{1,0:T(8,128)(2,1)S(1)} %get-tuple-element.133), channel_id=1, source_target_pairs={{0,8},{1,9},{2,10},{3,11},{4,12},{5,13},{6,14},{7,15},{8,0},{9,1},... | collective-permute-start | bytes 663560 | tf_op jit(solution)/shard_map/ppermute | solution.py:35
  51.6 20.4 %collective-permute-start.18 = (bf16[432,256]{1,0:T(8,128)(2,1)S(1)}, bf16[432,256]{1,0:T(8,128)(2,1)S(1)}, u32[]{:S(2)}, u32[]{:S(2)}) collective-permute-start(bf16[432,256]{1,0:T(8,128)(2,1)S(1)} %get-tuple-element.134), channel_id=1, source_target_pairs={{0,12},{1,13},{2,14},{3,15},{4,8},{5,9},{6,10},{7,11},{8,4},{9,5},... | collective-permute-start | bytes 663560 | tf_op jit(solution)/shard_map/ppermute | solution.py:35
  72.2 11.3 %collective-permute-start.19 = (bf16[432,256]{1,0:T(8,128)(2,1)S(1)}, bf16[432,256]{1,0:T(8,128)(2,1)S(1)}, u32[]{:S(2)}, u32[]{:S(2)}) collective-permute-start(bf16[432,256]{1,0:T(8,128)(2,1)S(1)} %add_convert_fusion), channel_id=1, source_target_pairs={{0,8},{1,9},{2,10},{3,11},{4,12},{5,13},{6,14},{7,15},{8,0},{9,1},... | collective-permute-start | bytes 663560 | tf_op jit(solution)/shard_map/ppermute | solution.py:35
  72.9 14.1 %collective-permute-start.23 = (bf16[432,256]{1,0:T(8,128)(2,1)S(1)}, bf16[432,256]{1,0:T(8,128)(2,1)S(1)}, u32[]{:S(2)}, u32[]{:S(2)}) collective-permute-start(bf16[432,256]{1,0:T(8,128)(2,1)S(1)} %add_convert_fusion), channel_id=1, source_target_pairs={{0,2},{1,3},{2,0},{3,1},{4,6},{5,7},{6,4},{7,5},{8,10},{9,11},{10,... | collective-permute-start | bytes 663560 | tf_op jit(solution)/shard_map/ppermute | solution.py:35
  73.4 13.6 %collective-permute-start.27 = (bf16[432,256]{1,0:T(8,128)(2,1)S(1)}, bf16[432,256]{1,0:T(8,128)(2,1)S(1)}, u32[]{:S(2)}, u32[]{:S(2)}) collective-permute-start(bf16[432,256]{1,0:T(8,128)(2,1)S(1)} %add_convert_fusion), channel_id=1, source_target_pairs={{0,4},{1,5},{2,6},{3,7},{4,0},{5,1},{6,2},{7,3},{8,12},{9,13},{10,... | collective-permute-start | bytes 663560 | tf_op jit(solution)/shard_map/ppermute | solution.py:35
  83.5 9.3 %collective-permute-start.21 = (bf16[1,272,256]{2,1,0:T(8,128)(2,1)S(1)}, bf16[1,272,256]{2,1,0:T(8,128)(2,1)S(1)}, u32[]{:S(2)}, u32[]{:S(2)}) collective-permute-start(bf16[1,272,256]{2,1,0:T(8,128)(2,1)S(1)} %get-tuple-element.136), channel_id=1, source_target_pairs={{0,8},{1,9},{2,10},{3,11},{4,12},{5,13},{6,14},{7,15},{8,0},{9,1},... | collective-permute-start | bytes 417800 | tf_op jit(solution)/shard_map/ppermute | solution.py:35
  83.5 16.2 %collective-permute-start.25 = (bf16[1,432,256]{2,1,0:T(8,128)(2,1)S(1)}, bf16[1,432,256]{2,1,0:T(8,128)(2,1)S(1)}, u32[]{:S(2)}, u32[]{:S(2)}) collective-permute-start(bf16[1,432,256]{2,1,0:T(8,128)(2,1)S(1)} %bitcast.30), channel_id=1, source_target_pairs={{0,2},{1,3},{2,0},{3,1},{4,6},{5,7},{6,4},{7,5},{8,10},{9,11},{10,... | collective-permute-start | bytes 663560 | tf_op jit(solution)/shard_map/ppermute | solution.py:35
  84.0 12.2 %collective-permute-start.20 = (bf16[432,256]{1,0:T(8,128)(2,1)S(1)}, bf16[432,256]{1,0:T(8,128)(2,1)S(1)}, u32[]{:S(2)}, u32[]{:S(2)}) collective-permute-start(bf16[432,256]{1,0:T(8,128)(2,1)S(1)} %collective-permute-done.19), channel_id=1, source_target_pairs={{0,4},{1,5},{2,6},{3,7},{4,0},{5,1},{6,2},{7,3},{8,12},{9,13},{10,... | collective-permute-start | bytes 663560 | tf_op jit(solution)/shard_map/ppermute | solution.py:35
  86.9 12.7 %collective-permute-start.24 = (bf16[432,256]{1,0:T(8,128)(2,1)S(1)}, bf16[432,256]{1,0:T(8,128)(2,1)S(1)}, u32[]{:S(2)}, u32[]{:S(2)}) collective-permute-start(bf16[432,256]{1,0:T(8,128)(2,1)S(1)} %collective-permute-done.23), channel_id=1, source_target_pairs={{0,4},{1,5},{2,6},{3,7},{4,0},{5,1},{6,2},{7,3},{8,12},{9,13},{10,... | collective-permute-start | bytes 663560 | tf_op jit(solution)/shard_map/ppermute | solution.py:35
  87.1 14.4 %collective-permute-start.28 = (bf16[4,432,256]{2,1,0:T(8,128)(2,1)S(1)}, bf16[4,432,256]{2,1,0:T(8,128)(2,1)S(1)}, u32[]{:S(2)}, u32[]{:S(2)}) collective-permute-start(bf16[4,432,256]{2,1,0:T(8,128)(2,1)S(1)} %pad_maximum_fusion.1), channel_id=1, source_target_pairs={{0,1},{1,0},{2,3},{3,2},{4,5},{5,4},{6,7},{7,6},{8,9},{9,8},{10,11... | collective-permute-start | bytes 2654216 | tf_op jit(solution)/shard_map/ppermute | solution.py:35
  99.8 7.8 %collective-permute-start.22 = (bf16[432,256]{1,0:T(8,128)(2,1)S(1)}, bf16[432,256]{1,0:T(8,128)(2,1)S(1)}, u32[]{:S(2)}, u32[]{:S(2)}) collective-permute-start(bf16[432,256]{1,0:T(8,128)(2,1)S(1)} %collective-permute-done.20), channel_id=1, source_target_pairs={{0,2},{1,3},{2,0},{3,1},{4,6},{5,7},{6,4},{7,5},{8,10},{9,11},{10,... | collective-permute-start | bytes 663560 | tf_op jit(solution)/shard_map/ppermute | solution.py:35
  (7 other events, 26.1 us)

commit v12 on v10

--- a/solution.py
+++ b/solution.py
@@ -146,9 +146,9 @@
     )(far(links), far(feats), far(voxmask))
 
 
-def fetch_taps(weight, near_weight, done):
-    for tap in range(weight.shape[0]):
-        pltpu.make_async_copy(weight.at[tap], near_weight.at[tap], done.at[tap]).start()
+def fetch_taps(weight, near_weight, done, skip=0):
+    for tap in range(near_weight.shape[0]):
+        pltpu.make_async_copy(weight.at[skip + tap], near_weight.at[tap], done.at[tap]).start()
 
 
 def await_taps(first, last, weight, near_weight, done):
@@ -176,15 +176,12 @@
 
 
 def prepare_kernel(
-    feats, voxmask, weight, cotangent, mask, rows, give_inner, give_core, turned, taps, slopes, planes, masks, flip, own, done, fetched
+    feats, voxmask, weight, mask, rows, give_inner, give_core, turned, taps, planes, masks, flip, own, done, fetched
 ):
-    count = weight.shape[0]
     pltpu.make_async_copy(voxmask, masks, done.at[8]).start()
     for z in range(8):
         pltpu.make_async_copy(feats.at[:, pl.ds(z, 1)], planes.at[:, pl.ds(z, 1)], done.at[z]).start()
     fetch_taps(weight, taps, fetched)
-    for z in range(8):
-        pltpu.make_async_copy(cotangent.at[:, pl.ds(z, 1)], slopes.at[:, pl.ds(z, 1)], fetched.at[count + z]).start()
     valid = windows((own.shape[0], 128), 1)
     pltpu.make_async_copy(voxmask, masks, done.at[8]).wait()
     for z in range(8):
@@ -198,26 +195,23 @@
     quarters(flip, own, give_inner, give_core)
     for z in range(8):
         turn_rows(own, slice(128 * z, 128 * z + 128), valid, turned, 0)
-    await_taps(0, count, weight, taps, fetched)
-    for z in range(8):
-        pltpu.make_async_copy(cotangent.at[:, pl.ds(z, 1)], slopes.at[:, pl.ds(z, 1)], fetched.at[count + z]).wait()
-
-
-def prepare(feats, voxmask, weight, cotangent):
+    await_taps(0, taps.shape[0], weight, taps, fetched)
+
+
+def prepare(feats, voxmask, weight):
     width = feats.shape[3]
     quarter = width // 4
     return pl.pallas_call(
         prepare_kernel,
-        in_specs=[FAR] * 4,
-        out_specs=(WHOLE,) * 7,
+        in_specs=[FAR] * 3,
+        out_specs=(WHOLE,) * 6,
         out_shape=(
             pltpu.VMEM((1024, 128), jnp.float32),
             pltpu.VMEM((1024, width), jnp.bfloat16),
             pltpu.VMEM((2 * quarter, 1024), jnp.bfloat16),
             pltpu.VMEM((quarter, 1024), jnp.bfloat16),
             pltpu.VMEM((9 * quarter, 1024), jnp.bfloat16),
-            pltpu.VMEM(weight.shape, jnp.bfloat16),
-            pltpu.VMEM(cotangent.shape, jnp.bfloat16),
+            pltpu.VMEM((18, width, width), jnp.bfloat16),
         ),
         scratch_shapes=[
             pltpu.VMEM(feats.shape, jnp.bfloat16),
@@ -225,12 +219,12 @@
             pltpu.VMEM((width, 1024), jnp.float32),
             pltpu.VMEM((quarter, 1024), jnp.float32),
             pltpu.SemaphoreType.DMA((9,)),
-            pltpu.SemaphoreType.DMA((weight.shape[0] + 8,)),
+            pltpu.SemaphoreType.DMA((18,)),
         ],
         compiler_params=params(12),
         cost_estimate=cost(1024, 1024),
         name="prepare",
-    )(far(feats), far(voxmask), far(weight), far(cotangent))
+    )(far(feats), far(voxmask), far(weight))
 
 
 def turn_kernel(inner, core, both_changed, turned):
@@ -388,20 +382,30 @@
     return plane
 
 
-def forward_kernel(rows, mask, weight, bias, slopes, out, grad, edge, bias_sum, cols, pre):
+def forward_kernel(rows, mask, first, weight, bias, cotangent, out, grad, edge, bias_sum, rest, slopes, cols, pre, done):
     width = rows.shape[1]
+    fetch_taps(weight, rest, done, 18)
+    copies = [
+        pltpu.make_async_copy(cotangent.at[:, pl.ds(z, 1)], slopes.at[:, pl.ds(z, 1)], done.at[9 + z]) for z in range(8)
+    ]
+    for copy in copies:
+        copy.start()
     valid = windows((128, width), 0)
     for z in range(8):
         span = slice(128 * z, 128 * z + 128)
         for place, moved in enumerate(shifts(rows[span, :].astype(jnp.float32), 0, valid)):
             cols[span, place * width : (place + 1) * width] = moved
 
-    def taps(a):
-        return weight[9 * a : 9 * a + 9].reshape(9 * width, width)
-
-    pre[...] = jnp.dot(cols[...], taps(1), preferred_element_type=jnp.float32) + bias[...]
-    pre[128:, :] += jnp.dot(cols[:896, :], taps(0), preferred_element_type=jnp.float32)
-    pre[:896, :] += jnp.dot(cols[128:, :], taps(2), preferred_element_type=jnp.float32)
+    def taps(ref, start):
+        return ref[start : start + 9].reshape(9 * width, width)
+
+    pre[...] = jnp.dot(cols[...], taps(first, 9), preferred_element_type=jnp.float32) + bias[...]
+    pre[128:, :] += jnp.dot(cols[:896, :], taps(first, 0), preferred_element_type=jnp.float32)
+    for tap in range(9):
+        pltpu.make_async_copy(weight.at[18 + tap], rest.at[tap], done.at[tap]).wait()
+    pre[:896, :] += jnp.dot(cols[128:, :], taps(rest, 0), preferred_element_type=jnp.float32)
+    for copy in copies:
+        copy.wait()
     for side in range(2):
         edge[side] = pre[896 * side : 896 * side + 128, :]
     total = jnp.zeros((1, width), jnp.float32)
@@ -415,26 +419,29 @@
     bias_sum[...] = total
 
 
-def forward_inside(rows, mask, weight, bias, cotangent):
+def forward_inside(rows, mask, first, weight, bias, cotangent):
     width = rows.shape[1]
     return pl.pallas_call(
         forward_kernel,
-        in_specs=[WHOLE] * 5,
-        out_specs=(WHOLE,) * 4,
+        in_specs=[WHOLE] * 3 + [FAR, WHOLE, FAR],
+        out_specs=(WHOLE,) * 6,
         out_shape=(
             jax.ShapeDtypeStruct(cotangent.shape, jnp.bfloat16),
             pltpu.VMEM((768, width), jnp.bfloat16),
             pltpu.VMEM((2, 128, width), jnp.float32),
             pltpu.VMEM((1, width), jnp.float32),
+            pltpu.VMEM((9, width, width), jnp.bfloat16),
+            pltpu.VMEM(cotangent.shape, jnp.bfloat16),
         ),
         scratch_shapes=[
             pltpu.VMEM((1024, 9 * width), jnp.bfloat16),
             pltpu.VMEM((1024, width), jnp.float32),
+            pltpu.SemaphoreType.DMA((17,)),
         ],
         compiler_params=params(12),
         cost_estimate=cost(1024, 1024),
         name="forward_inside",
-    )(near(rows), near(mask), near(weight), bias, near(cotangent))
+    )(near(rows), near(mask), near(first), far(weight), bias, far(cotangent))
 
 
 def inner_terms_kernel(mine, others, *refs):
@@ -463,7 +470,7 @@
     )(near(mine), near(others), *[near(x) for x in grads])
 
 
-def edge_kernel(table, mask, weight, edge, ends, inner, out_in, *refs):
+def edge_kernel(table, mask, first, rest, edge, ends, inner, out_in, *refs):
     arrived, (out, to_inner, to_core, own, planes, flip, done) = refs[:-7], refs[-7:]
     width = edge.shape[2]
     valid = windows((128, width), 0)
@@ -473,7 +480,7 @@
         halo = jnp.concatenate([chosen(table, 2 * side + b, arrived) for b in range(2)], axis=0)
         flip[:, rows] = halo.T
         cols = jnp.concatenate(shifts(halo, 0, valid), axis=1)
-        taps = weight[18 * side : 18 * side + 9].reshape(9 * width, width)
+        taps = (rest if side else first)[0:9].reshape(9 * width, width)
         pre = edge[side] + jnp.dot(cols, taps, preferred_element_type=jnp.float32)
         z = 7 * side
         keep = wide(mask[128 * z : 128 * z + 128, :])
@@ -491,12 +498,12 @@
         pltpu.make_async_copy(planes.at[side], out.at[:, pl.ds(7 * side, 1)], done.at[side]).wait()
 
 
-def forward_edges(table, mask, weight, edge, ends, inner, out, arrived):
+def forward_edges(table, mask, first, rest, edge, ends, inner, out, arrived):
     width = edge.shape[2]
     quarter = width // 4
     return pl.pallas_call(
         edge_kernel,
-        in_specs=[SCALARS] + [WHOLE] * 5 + [FAR] + [WHOLE] * len(arrived),
+        in_specs=[SCALARS] + [WHOLE] * 6 + [FAR] + [WHOLE] * len(arrived),
         out_specs=(FAR, WHOLE, WHOLE, WHOLE),
         out_shape=(
             jax.ShapeDtypeStruct(out.shape, out.dtype),
@@ -509,14 +516,15 @@
             pltpu.VMEM((width, 256), jnp.float32),
             pltpu.SemaphoreType.DMA((2,)),
         ],
-        input_output_aliases={6: 0},
+        input_output_aliases={7: 0},
         compiler_params=params(10),
         cost_estimate=cost(1024, 1024),
         name="forward_edges",
     )(
         table,
         near(mask),
-        near(weight),
+        near(first),
+        near(rest),
         near(edge),
         near(ends),
         near(inner),
@@ -748,10 +756,12 @@
     outer = size // 4
 
     parcel = rims(links, feats, voxmask)
-    mask, rows, give_inner, give_core, turned, taps, ends = prepare(feats, voxmask, weight, cotangent)
+    mask, rows, give_inner, give_core, turned, first = prepare(feats, voxmask, weight)
     inner, rows = lax.optimization_barrier((swap(parcel, size, 2), rows))
     parcels = [parcel, inner, swap(parcel, size, 1), swap(inner, size, 1)]
-    out, grad, edge, bias_local = forward_inside(rows, mask, taps, bias.reshape(1, width), ends)
+    out, grad, edge, bias_local, rest, ends = forward_inside(
+        rows, mask, first, weight, bias.reshape(1, width), cotangent
+    )
     *parcels, grad = lax.optimization_barrier((*parcels, grad))
     table, picks = route(parcels, outer)
 
@@ -764,15 +774,18 @@
     others = turn(got_inner, swap(give_core, size, 1), swap(got_inner, size, 1))
     grads = [grad, grad_inner, swap(grad, size, 1), swap(grad_inner, size, 1)]
 
-    out, to_inner, to_core, halos = forward_edges(table, mask, taps, edge, ends, bias_local, out, arrived)
+    out, to_inner, to_core, halos = forward_edges(
+        table, mask, first, rest, edge, ends, bias_local, out, arrived
+    )
     inner = swap(to_inner, size, 2)
     terms = inner_terms(turned, others, grads)
     inner, terms = lax.optimization_barrier((inner, terms))
     parcels = [to_inner, inner, swap(to_core, size, 1), swap(inner, size, 1)]
 
     gives, stay = outer_terms(outer, turned, others, halos, parcels, terms)
-    gots = [rotate(give, size, steps + 1) for steps, give in enumerate(gives)]
     give, kept = deal(table, parcels, outer)
+    give, *gives = lax.optimization_barrier((give, *gives))
+    gots = [rotate(x, size, steps) for steps, x in enumerate(gives, 1)]
     got = swap(give, size, 4)
     grad_feats, partial, taps = backward(grad, to_inner, mask, weight)
     bits = outer.bit_length() - 1

time: 105 us -> 108 us (1.029)
  waiting for transfers between devices: 33.8 us -> 38.2 us
  starting transfers between devices: 31.6 us -> 28.7 us
  Pallas kernels: 37.8 us -> 39.4 us
    ppermute x22, waiting for transfers between devices: 21 us -> 26.3 us  [swap(): return lax.ppermute(x, 'zslab', [(i, i ^ bit) for i in range(size)])]
    ppermute x22, starting transfers between devices: 21.4 us -> 18.6 us  [swap(): return lax.ppermute(x, 'zslab', [(i, i ^ bit) for i in range(size)])]
    pallas_call x3, Pallas kernels: 11.4 us -> 12.9 us  [the longest x1 6.99 us: forward_inside(): pl.pallas_call(forward_kernel, in_specs=[WHOLE] * 3 + [FAR, WHOLE, FAR],...]
  transfers between devices with their start and end apart: 28 -> 28, of which waited for: 12 -> 12; matrix products, arithmetic and copies ran while one was open for 0% -> 0% of each run, Pallas kernels for 33% -> 31%
where the time goes in v12:
time: 108 us
  Pallas kernels  39.4 us (36%)
  waiting for transfers between devices  38.2 us (35%)
  starting transfers between devices  28.7 us (27%)
    ppermute x22, waiting for transfers between devices, swap(): return lax.ppermute(x, 'zslab', [(i, i ^ bit) for i in range(size)])  26.3 us
    ppermute x22, starting transfers between devices, swap(): return lax.ppermute(x, 'zslab', [(i, i ^ bit) for i in range(size)])  18.6 us
    ppermute x6, waiting for transfers between devices, rotate(): lax.ppermute(x, 'zslab', [(i, (i + 4 * steps) % size) for i in range(size)])  11.9 us
    ppermute x6, starting transfers between devices, rotate(): lax.ppermute(x, 'zslab', [(i, (i + 4 * steps) % size) for i in range(size)])  10.1 us
    pallas_call x1, Pallas kernels, backward(): pl.pallas_call(backward_kernel, in_specs=[WHOLE] * 3 + [FAR], out_specs=(...  8.95 us
    pallas_call x1, Pallas kernels, forward_inside(): pl.pallas_call(forward_kernel, in_specs=[WHOLE] * 3 + [FAR, WHOLE, FAR],...  6.99 us
    pallas_call x2, Pallas kernels, assemble(): pl.pallas_call(functools.partial(assemble_kernel, outer, places, len(stac...  5.03 us
    pallas_call x1, Pallas kernels, prepare(): pl.pallas_call(prepare_kernel, in_specs=[FAR] * 3, out_specs=(WHOLE,) * 6...  3.93 us
  transfers between devices with their start and end apart: 28, of which 12 were waited for; matrix products, arithmetic and copies ran while one was open for 0% of the time, Pallas kernels for 31%

profile of v12, /device:TPU:0, one launch (start us, length us, event | category | flops | bytes accessed | tf_op | source)
XLA Modules:
  0.0 108.0 jit_solution(7087698203405337967)
XLA Ops:
  1.7 3.0 %collective-permute-start = (bf16[272,256]{1,0:T(8,128)(2,1)S(1)}, bf16[272,256]{1,0:T(8,128)(2,1)S(1)}, u32[]{:S(2)}, u32[]{:S(2)}) collective-permute-start(bf16[272,256]{1,0:T(8,128)(2,1)S(1)} %rims.1.refs_0_), channel_id=1, source_target_pairs={{0,2},{1,3},{2,0},{3,1},{4,6},{5,7},{6,4},{7,5},{8,10},{9,11},{10,... | collective-permute-start | bytes 417800 | tf_op jit(solution)/shard_map/ppermute | solution.py:35
  4.8 3.9 %prepare.1 = (f32[1024,128]{1,0:T(8,128)S(1)}, bf16[1024,256]{1,0:T(8,128)(2,1)S(1)}, bf16[128,1024]{1,0:T(8,128)(2,1)S(1)}, bf16[64,1024]{1,0:T(8,128)(2,1)S(1)...) custom-call(bf16[2,8,64,256]{3,2,1,0:T(8,128)(2,1)} %feats.3, s32[2,512]{1,0:T(2,128)} %voxmask.3, ...), custom_call_target="tpu_custom_call" | custom-call | flops 1024 | bytes 1024 | tf_op jit(solution)/shard_map/prepare/pallas_call | solution.py:204
  9.4 7.0 %forward_inside.1 = (bf16[2,8,64,256]{3,2,1,0:T(8,128)(2,1)}, bf16[768,256]{1,0:T(8,128)(2,1)S(1)}, f32[2,128,256]{2,1,0:T(8,128)S(1)}, f32[1,256]{1,0:T(1,128)S...) custom-call(bf16[1024,256]{1,0:T(8,128)(2,1)S(1)} %get-tuple-element.78.rows, ...), custom_call_target="tpu_custom_call" | custom-call | flops 1024 | bytes 1024 | tf_op jit(solution)/shard_map/forward_inside/pallas_call | solution.py:424
  18.1 2.0 %collective-permute-start.7 = (bf16[768,256]{1,0:T(8,128)(2,1)S(1)}, bf16[768,256]{1,0:T(8,128)(2,1)S(1)}, u32[]{:S(2)}, u32[]{:S(2)}) collective-permute-start(bf16[768,256]{1,0:T(8,128)(2,1)S(1)} %get-tuple-element.105.refs_0_.grad), channel_id=1, source_target_pairs={{0,2},{1,3},{2,0},{3,1},{4,6},{5,7},{6,4},{7,5},{8,10},{9,11},{10,... | collective-permute-start | bytes 1179656 | tf_op jit(solution)/shard_map/ppermute | solution.py:35
  21.7 2.6 %collective-permute-start.4 = (bf16[256,256]{1,0:T(8,128)(2,1)S(1)}, bf16[256,256]{1,0:T(8,128)(2,1)S(1)}, u32[]{:S(2)}, u32[]{:S(2)}) collective-permute-start(bf16[256,256]{1,0:T(8,128)(2,1)S(1)} %get-tuple-element.100), channel_id=1, source_target_pairs={{0,8},{1,9},{2,10},{3,11},{4,12},{5,13},{6,14},{7,15},{8,0},{9,1},... | collective-permute-start | bytes 393224 | tf_op jit(solution)/shard_map/ppermute | solution.py:39
  25.7 2.8 %collective-permute-done.3.refs_1_ = bf16[256,256]{1,0:T(8,128)(2,1)S(1)} collective-permute-done((bf16[256,256]{1,0:T(8,128)(2,1)S(1)}, bf16[256,256]{1,0:T(8,128)(2,1)S(1)}, u32[]{:S(2)}, u32[]{:S(2)}) %collective-permute-start.3) | collective-permute-done | bytes 131104 | tf_op jit(solution)/shard_map/ppermute | solution.py:39
  28.4 4.4 %collective-permute-done.4.refs_2_ = bf16[256,256]{1,0:T(8,128)(2,1)S(1)} collective-permute-done((bf16[256,256]{1,0:T(8,128)(2,1)S(1)}, bf16[256,256]{1,0:T(8,128)(2,1)S(1)}, u32[]{:S(2)}, u32[]{:S(2)}) %collective-permute-start.4) | collective-permute-done | bytes 131104 | tf_op jit(solution)/shard_map/ppermute | solution.py:39
  33.4 2.0 %forward_edges.1 = (bf16[2,8,64,256]{3,2,1,0:T(8,128)(2,1)}, bf16[400,256]{1,0:T(8,128)(2,1)S(1)}, bf16[336,256]{1,0:T(8,128)(2,1)S(1)}, bf16[64,256]{1,0:T(8,128)(2,1)S(1)}) custom-call(s32[36]{0:T(128)S(1)} %get-tuple-element.86.table, f32[1024,128]{1,0:T(8,128)S(1)} %get-tuple-element.79.mask, ...), custom_call_target="tpu_custom_call", output_to_operand_aliasing={{0}: (7, {})} | custom-call | flops 1024 | bytes 1024 | tf_op jit(solution)/shard_map/forward_edges/pallas_call | solution.py:504
  38.2 2.9 %inner_terms.1.refs_4_ = f32[1728,256]{1,0:T(8,128)S(1)} custom-call(bf16[576,1024]{1,0:T(8,128)(2,1)S(1)} %get-tuple-element.111.mine, bf16[1728,1024]{1,0:T(8,128)(2,1)S(1)} %turn.1.others, bf16[768,256]{1,0:T(8,128)(2,1)S(1)} %get-tuple-element.105.refs_0_.grad, bf16[768,256]{1,0:T(8,128)(2,1)S(1)} %collective-permute-done.7.refs_1_, ...), custom_call_target="tpu_custom_call" | custom-call | flops 1024 | bytes 1024 | tf_op jit(solution)/shard_map/inner_terms/pallas_call | solution.py:462
  44.9 1.8 %outer_terms.1 = (bf16[432,256]{1,0:T(8,128)(2,1)S(1)}, bf16[432,256]{1,0:T(8,128)(2,1)S(1)}, bf16[432,256]{1,0:T(8,128)(2,1)S(1)}, f32[432,256]{1,0:T(8,128)S(1)}) custom-call(bf16[576,1024]{1,0:T(8,128)(2,1)S(1)} %get-tuple-element.111.mine, bf16[1728,1024]{1,0:T(8,128)(2,1)S(1)} %turn.1.others, bf16[64,256]{1,0:T(8,128)(2,1)S(1)} %get-tuple-element.114.halos, ...), custom_call_target="tpu_custom_call" | custom-call | flops 1024 | bytes 1024 | tf_op jit(solution)/shard_map/outer_terms/pallas_call | solution.py:582
  46.7 3.3 %collective-permute-start.15 = (bf16[2,272,256]{2,1,0:T(8,128)(2,1)S(1)}, bf16[2,272,256]{2,1,0:T(8,128)(2,1)S(1)}, u32[]{:S(2)}, u32[]{:S(2)}) collective-permute-start(bf16[2,272,256]{2,1,0:T(8,128)(2,1)S(1)} %get-tuple-element.127), channel_id=1, source_target_pairs={{0,4},{1,5},{2,6},{3,7},{4,0},{5,1},{6,2},{7,3},{8,12},{9,13},{10,... | collective-permute-start | bytes 835592 | tf_op jit(solution)/shard_map/ppermute | solution.py:35
  51.8 2.9 %collective-permute-start.18 = (bf16[432,256]{1,0:T(8,128)(2,1)S(1)}, bf16[432,256]{1,0:T(8,128)(2,1)S(1)}, u32[]{:S(2)}, u32[]{:S(2)}) collective-permute-start(bf16[432,256]{1,0:T(8,128)(2,1)S(1)} %get-tuple-element.136), channel_id=1, source_target_pairs={{0,12},{1,13},{2,14},{3,15},{4,0},{5,1},{6,2},{7,3},{8,4},{9,5},{1... | collective-permute-start | bytes 663560 | tf_op jit(solution)/shard_map/ppermute | solution.py:39
  54.7 9.0 %backward.1 = (bf16[2,8,64,256]{3,2,1,0:T(8,128)(2,1)}, f32[2,128,256]{2,1,0:T(8,128)S(1)}, bf16[27,256,256]{2,1,0:T(8,128)(2,1)S(1)}) custom-call(bf16[768,256]{1,0:T(8,128)(2,1)S(1)} %get-tuple-element.105.refs_0_.grad, bf16[400,256]{1,0:T(8,128)(2,1)S(1)} %get-tuple-element.115.refs_0_.parcel, f32[1024,128]{1,0:T(8,128)S(1)} %get-tuple-element.79.mask, ...), custom_call_target="tpu_custom_call" | custom-call | flops 1024 | bytes 1024 | tf_op jit(solution)/shard_map/backward/pallas_call | solution.py:631
  63.6 2.8 %collective-permute-done.15.got = bf16[2,272,256]{2,1,0:T(8,128)(2,1)S(1)} collective-permute-done((bf16[2,272,256]{2,1,0:T(8,128)(2,1)S(1)}, bf16[2,272,256]{2,1,0:T(8,128)(2,1)S(1)}, u32[]{:S(2)}, u32[]{:S(2)}) %collective-permute-start.15) | collective-permute-done | bytes 278560 | tf_op jit(solution)/shard_map/ppermute | solution.py:35
  66.5 2.2 %collective-permute-done.17 = bf16[432,256]{1,0:T(8,128)(2,1)S(1)} collective-permute-done((bf16[432,256]{1,0:T(8,128)(2,1)S(1)}, bf16[432,256]{1,0:T(8,128)(2,1)S(1)}, u32[]{:S(2)}, u32[]{:S(2)}) %collective-permute-start.17) | collective-permute-done | bytes 221216 | tf_op jit(solution)/shard_map/ppermute | solution.py:39
  68.8 2.5 %collective-permute-done.18 = bf16[432,256]{1,0:T(8,128)(2,1)S(1)} collective-permute-done((bf16[432,256]{1,0:T(8,128)(2,1)S(1)}, bf16[432,256]{1,0:T(8,128)(2,1)S(1)}, u32[]{:S(2)}, u32[]{:S(2)}) %collective-permute-start.18) | collective-permute-done | bytes 221216 | tf_op jit(solution)/shard_map/ppermute | solution.py:39
  71.4 1.8 %collective-permute-start.20 = (bf16[432,256]{1,0:T(8,128)(2,1)S(1)}, bf16[432,256]{1,0:T(8,128)(2,1)S(1)}, u32[]{:S(2)}, u32[]{:S(2)}) collective-permute-start(bf16[432,256]{1,0:T(8,128)(2,1)S(1)} %add_convert_fusion), channel_id=1, source_target_pairs={{0,8},{1,9},{2,10},{3,11},{4,12},{5,13},{6,14},{7,15},{8,0},{9,1},... | collective-permute-start | bytes 663560 | tf_op jit(solution)/shard_map/ppermute | solution.py:35
  73.2 2.4 %collective-permute-start.19 = (bf16[432,256]{1,0:T(8,128)(2,1)S(1)}, bf16[432,256]{1,0:T(8,128)(2,1)S(1)}, u32[]{:S(2)}, u32[]{:S(2)}) collective-permute-start(bf16[432,256]{1,0:T(8,128)(2,1)S(1)} %add_convert_fusion), channel_id=1, source_target_pairs={{0,4},{1,5},{2,6},{3,7},{4,0},{5,1},{6,2},{7,3},{8,12},{9,13},{10,... | collective-permute-start | bytes 663560 | tf_op jit(solution)/shard_map/ppermute | solution.py:35
  76.1 8.2 %collective-permute-done.20 = bf16[432,256]{1,0:T(8,128)(2,1)S(1)} collective-permute-done((bf16[432,256]{1,0:T(8,128)(2,1)S(1)}, bf16[432,256]{1,0:T(8,128)(2,1)S(1)}, u32[]{:S(2)}, u32[]{:S(2)}) %collective-permute-start.20) | collective-permute-done | bytes 221216 | tf_op jit(solution)/shard_map/ppermute | solution.py:35
  85.9 6.5 %collective-permute-done.22 = bf16[432,256]{1,0:T(8,128)(2,1)S(1)} collective-permute-done((bf16[432,256]{1,0:T(8,128)(2,1)S(1)}, bf16[432,256]{1,0:T(8,128)(2,1)S(1)}, u32[]{:S(2)}, u32[]{:S(2)}) %collective-permute-start.22) | collective-permute-done | bytes 221216 | tf_op jit(solution)/shard_map/ppermute | solution.py:35
  94.3 3.1 %assemble.2.weight_in = bf16[27,16,16,256]{3,2,1,0:T(8,128)(2,1)} custom-call(bf16[4,27,16,256]{3,2,1,0:T(8,128)(2,1)S(1)} %pad_maximum_fusion.refs_0_, bf16[4,27,16,256]{3,2,1,0:T(8,128)(2,1)S(1)} %bitcast.17), custom_call_target="tpu_custom_call" | custom-call | flops 1024 | bytes 1024 | tf_op jit(solution)/shard_map/assemble/pallas_call | solution.py:691
  97.5 4.2 %collective-permute-done.26.got = bf16[1,272,256]{2,1,0:T(8,128)(2,1)S(1)} collective-permute-done((bf16[1,272,256]{2,1,0:T(8,128)(2,1)S(1)}, bf16[1,272,256]{2,1,0:T(8,128)(2,1)S(1)}, u32[]{:S(2)}, u32[]{:S(2)}) %collective-permute-start.26) | collective-permute-done | bytes 139296 | tf_op jit(solution)/shard_map/ppermute | solution.py:35
  102.7 3.2 %finish.1 = (bf16[2,8,64,256]{3,2,1,0:T(8,128)(2,1)}, bf16[27,16,16,256]{3,2,1,0:T(8,128)(2,1)}, f32[1,256]{1,0:T(1,128)}) custom-call(f32[2,128,256]{2,1,0:T(8,128)S(1)} %get-tuple-element.130.partial, f32[1024,128]{1,0:T(8,128)S(1)} %get-tuple-element.79.mask, ...), custom_call_target="tpu_custom_call", output_to_operand_aliasing={{0}: (6, {}), {1}: (7, {})} | custom-call | flops 1024 | bytes 1024 | tf_op jit(solution)/shard_map/finish/pallas_call | solution.py:733
  105.9 1.9 %assemble.3 = bf16[27,16,16,256]{3,2,1,0:T(8,128)(2,1)} custom-call(bf16[4,27,16,256]{3,2,1,0:T(8,128)(2,1)S(1)} %bitcast.18, bf16[27,16,16,256]{3,2,1,0:T(8,128)(2,1)} %get-tuple-element.146.refs_1_), custom_call_target="tpu_custom_call", output_to_operand_aliasing={{}: (1, {})} | custom-call | flops 1024 | bytes 1024 | tf_op jit(solution)/shard_map/assemble/pallas_call | solution.py:691
  (54 shorter events, 20.4 us)
Async XLA Ops:
  1.7 7.1 %collective-permute-start = (bf16[272,256]{1,0:T(8,128)(2,1)S(1)}, bf16[272,256]{1,0:T(8,128)(2,1)S(1)}, u32[]{:S(2)}, u32[]{:S(2)}) collective-permute-start(bf16[272,256]{1,0:T(8,128)(2,1)S(1)} %rims.1.refs_0_), channel_id=1, source_target_pairs={{0,2},{1,3},{2,0},{3,1},{4,6},{5,7},{6,4},{7,5},{8,10},{9,11},{10,... | collective-permute-start | bytes 417800 | tf_op jit(solution)/shard_map/ppermute | solution.py:35
  8.7 9.4 %collective-permute-start.6 = (bf16[128,1024]{1,0:T(8,128)(2,1)S(1)}, bf16[128,1024]{1,0:T(8,128)(2,1)S(1)}, u32[]{:S(2)}, u32[]{:S(2)}) collective-permute-start(bf16[128,1024]{1,0:T(8,128)(2,1)S(1)} %get-tuple-element.102), channel_id=1, source_target_pairs={{0,2},{1,3},{2,0},{3,1},{4,6},{5,7},{6,4},{7,5},{8,10},{9,11},{10,... | collective-permute-start | bytes 786440 | tf_op jit(solution)/shard_map/ppermute | solution.py:35
  8.8 7.6 %collective-permute-start.1 = (bf16[272,256]{1,0:T(8,128)(2,1)S(1)}, bf16[272,256]{1,0:T(8,128)(2,1)S(1)}, u32[]{:S(2)}, u32[]{:S(2)}) collective-permute-start(bf16[272,256]{1,0:T(8,128)(2,1)S(1)} %rims.1.refs_0_), channel_id=1, source_target_pairs={{0,1},{1,0},{2,3},{3,2},{4,5},{5,4},{6,7},{7,6},{8,9},{9,8},{10,11... | collective-permute-start | bytes 417800 | tf_op jit(solution)/shard_map/ppermute | solution.py:35
  8.9 7.5 %collective-permute-start.2 = (bf16[272,256]{1,0:T(8,128)(2,1)S(1)}, bf16[272,256]{1,0:T(8,128)(2,1)S(1)}, u32[]{:S(2)}, u32[]{:S(2)}) collective-permute-start(bf16[272,256]{1,0:T(8,128)(2,1)S(1)} %collective-permute-done.refs_1_), channel_id=1, source_target_pairs={{0,1},{1,0},{2,3},{3,2},{4,5},{5,4},{6,7},{7,6},{8,9},{9,8},{10,11... | collective-permute-start | bytes 417800 | tf_op jit(solution)/shard_map/ppermute | solution.py:35
  18.1 14.7 %collective-permute-start.7 = (bf16[768,256]{1,0:T(8,128)(2,1)S(1)}, bf16[768,256]{1,0:T(8,128)(2,1)S(1)}, u32[]{:S(2)}, u32[]{:S(2)}) collective-permute-start(bf16[768,256]{1,0:T(8,128)(2,1)S(1)} %get-tuple-element.105.refs_0_.grad), channel_id=1, source_target_pairs={{0,2},{1,3},{2,0},{3,1},{4,6},{5,7},{6,4},{7,5},{8,10},{9,11},{10,... | collective-permute-start | bytes 1179656 | tf_op jit(solution)/shard_map/ppermute | solution.py:35
  20.2 8.3 %collective-permute-start.3 = (bf16[256,256]{1,0:T(8,128)(2,1)S(1)}, bf16[256,256]{1,0:T(8,128)(2,1)S(1)}, u32[]{:S(2)}, u32[]{:S(2)}) collective-permute-start(bf16[256,256]{1,0:T(8,128)(2,1)S(1)} %get-tuple-element.99), channel_id=1, source_target_pairs={{0,4},{1,5},{2,6},{3,7},{4,8},{5,9},{6,10},{7,11},{8,12},{9,13},{1... | collective-permute-start | bytes 393224 | tf_op jit(solution)/shard_map/ppermute | solution.py:39
  21.7 11.1 %collective-permute-start.4 = (bf16[256,256]{1,0:T(8,128)(2,1)S(1)}, bf16[256,256]{1,0:T(8,128)(2,1)S(1)}, u32[]{:S(2)}, u32[]{:S(2)}) collective-permute-start(bf16[256,256]{1,0:T(8,128)(2,1)S(1)} %get-tuple-element.100), channel_id=1, source_target_pairs={{0,8},{1,9},{2,10},{3,11},{4,12},{5,13},{6,14},{7,15},{8,0},{9,1},... | collective-permute-start | bytes 393224 | tf_op jit(solution)/shard_map/ppermute | solution.py:39
  24.3 8.5 %collective-permute-start.5 = (bf16[256,256]{1,0:T(8,128)(2,1)S(1)}, bf16[256,256]{1,0:T(8,128)(2,1)S(1)}, u32[]{:S(2)}, u32[]{:S(2)}) collective-permute-start(bf16[256,256]{1,0:T(8,128)(2,1)S(1)} %get-tuple-element.101), channel_id=1, source_target_pairs={{0,12},{1,13},{2,14},{3,15},{4,0},{5,1},{6,2},{7,3},{8,4},{9,5},{1... | collective-permute-start | bytes 393224 | tf_op jit(solution)/shard_map/ppermute | solution.py:39
  25.7 12.5 %collective-permute-start.11 = (bf16[768,256]{1,0:T(8,128)(2,1)S(1)}, bf16[768,256]{1,0:T(8,128)(2,1)S(1)}, u32[]{:S(2)}, u32[]{:S(2)}) collective-permute-start(bf16[768,256]{1,0:T(8,128)(2,1)S(1)} %get-tuple-element.105.refs_0_.grad), channel_id=1, source_target_pairs={{0,1},{1,0},{2,3},{3,2},{4,5},{5,4},{6,7},{7,6},{8,9},{9,8},{10,11... | collective-permute-start | bytes 1179656 | tf_op jit(solution)/shard_map/ppermute | solution.py:35
  32.9 5.4 %collective-permute-start.12 = (bf16[768,256]{1,0:T(8,128)(2,1)S(1)}, bf16[768,256]{1,0:T(8,128)(2,1)S(1)}, u32[]{:S(2)}, u32[]{:S(2)}) collective-permute-start(bf16[768,256]{1,0:T(8,128)(2,1)S(1)} %collective-permute-done.7.refs_1_), channel_id=1, source_target_pairs={{0,1},{1,0},{2,3},{3,2},{4,5},{5,4},{6,7},{7,6},{8,9},{9,8},{10,11... | collective-permute-start | bytes 1179656 | tf_op jit(solution)/shard_map/ppermute | solution.py:35
  32.9 4.4 %collective-permute-start.9 = (bf16[128,1024]{1,0:T(8,128)(2,1)S(1)}, bf16[128,1024]{1,0:T(8,128)(2,1)S(1)}, u32[]{:S(2)}, u32[]{:S(2)}) collective-permute-start(bf16[128,1024]{1,0:T(8,128)(2,1)S(1)} %collective-permute-done.6.inner), channel_id=1, source_target_pairs={{0,1},{1,0},{2,3},{3,2},{4,5},{5,4},{6,7},{7,6},{8,9},{9,8},{10,11... | collective-permute-start | bytes 786440 | tf_op jit(solution)/shard_map/ppermute | solution.py:35
  35.4 7.1 %collective-permute-start.10 = (bf16[400,256]{1,0:T(8,128)(2,1)S(1)}, bf16[400,256]{1,0:T(8,128)(2,1)S(1)}, u32[]{:S(2)}, u32[]{:S(2)}) collective-permute-start(bf16[400,256]{1,0:T(8,128)(2,1)S(1)} %get-tuple-element.115.refs_0_.parcel), channel_id=1, source_target_pairs={{0,2},{1,3},{2,0},{3,1},{4,6},{5,7},{6,4},{7,5},{8,10},{9,11},{10,... | collective-permute-start | bytes 614408 | tf_op jit(solution)/shard_map/ppermute | solution.py:35
  46.7 19.7 %collective-permute-start.15 = (bf16[2,272,256]{2,1,0:T(8,128)(2,1)S(1)}, bf16[2,272,256]{2,1,0:T(8,128)(2,1)S(1)}, u32[]{:S(2)}, u32[]{:S(2)}) collective-permute-start(bf16[2,272,256]{2,1,0:T(8,128)(2,1)S(1)} %get-tuple-element.127), channel_id=1, source_target_pairs={{0,4},{1,5},{2,6},{3,7},{4,0},{5,1},{6,2},{7,3},{8,12},{9,13},{10,... | collective-permute-start | bytes 835592 | tf_op jit(solution)/shard_map/ppermute | solution.py:35
  50.0 16.5 %collective-permute-start.16 = (bf16[432,256]{1,0:T(8,128)(2,1)S(1)}, bf16[432,256]{1,0:T(8,128)(2,1)S(1)}, u32[]{:S(2)}, u32[]{:S(2)}) collective-permute-start(bf16[432,256]{1,0:T(8,128)(2,1)S(1)} %get-tuple-element.134), channel_id=1, source_target_pairs={{0,4},{1,5},{2,6},{3,7},{4,8},{5,9},{6,10},{7,11},{8,12},{9,13},{1... | collective-permute-start | bytes 663560 | tf_op jit(solution)/shard_map/ppermute | solution.py:39
  50.1 18.7 %collective-permute-start.17 = (bf16[432,256]{1,0:T(8,128)(2,1)S(1)}, bf16[432,256]{1,0:T(8,128)(2,1)S(1)}, u32[]{:S(2)}, u32[]{:S(2)}) collective-permute-start(bf16[432,256]{1,0:T(8,128)(2,1)S(1)} %get-tuple-element.135), channel_id=1, source_target_pairs={{0,8},{1,9},{2,10},{3,11},{4,12},{5,13},{6,14},{7,15},{8,0},{9,1},... | collective-permute-start | bytes 663560 | tf_op jit(solution)/shard_map/ppermute | solution.py:39
  51.8 19.5 %collective-permute-start.18 = (bf16[432,256]{1,0:T(8,128)(2,1)S(1)}, bf16[432,256]{1,0:T(8,128)(2,1)S(1)}, u32[]{:S(2)}, u32[]{:S(2)}) collective-permute-start(bf16[432,256]{1,0:T(8,128)(2,1)S(1)} %get-tuple-element.136), channel_id=1, source_target_pairs={{0,12},{1,13},{2,14},{3,15},{4,0},{5,1},{6,2},{7,3},{8,4},{9,5},{1... | collective-permute-start | bytes 663560 | tf_op jit(solution)/shard_map/ppermute | solution.py:39
  71.4 12.9 %collective-permute-start.20 = (bf16[432,256]{1,0:T(8,128)(2,1)S(1)}, bf16[432,256]{1,0:T(8,128)(2,1)S(1)}, u32[]{:S(2)}, u32[]{:S(2)}) collective-permute-start(bf16[432,256]{1,0:T(8,128)(2,1)S(1)} %add_convert_fusion), channel_id=1, source_target_pairs={{0,8},{1,9},{2,10},{3,11},{4,12},{5,13},{6,14},{7,15},{8,0},{9,1},... | collective-permute-start | bytes 663560 | tf_op jit(solution)/shard_map/ppermute | solution.py:35
  73.2 11.1 %collective-permute-start.19 = (bf16[432,256]{1,0:T(8,128)(2,1)S(1)}, bf16[432,256]{1,0:T(8,128)(2,1)S(1)}, u32[]{:S(2)}, u32[]{:S(2)}) collective-permute-start(bf16[432,256]{1,0:T(8,128)(2,1)S(1)} %add_convert_fusion), channel_id=1, source_target_pairs={{0,4},{1,5},{2,6},{3,7},{4,0},{5,1},{6,2},{7,3},{8,12},{9,13},{10,... | collective-permute-start | bytes 663560 | tf_op jit(solution)/shard_map/ppermute | solution.py:35
  75.6 8.7 %collective-permute-start.24 = (bf16[432,256]{1,0:T(8,128)(2,1)S(1)}, bf16[432,256]{1,0:T(8,128)(2,1)S(1)}, u32[]{:S(2)}, u32[]{:S(2)}) collective-permute-start(bf16[432,256]{1,0:T(8,128)(2,1)S(1)} %add_convert_fusion), channel_id=1, source_target_pairs={{0,2},{1,3},{2,0},{3,1},{4,6},{5,7},{6,4},{7,5},{8,10},{9,11},{10,... | collective-permute-start | bytes 663560 | tf_op jit(solution)/shard_map/ppermute | solution.py:35
  84.4 9.9 %collective-permute-start.25 = (bf16[4,432,256]{2,1,0:T(8,128)(2,1)S(1)}, bf16[4,432,256]{2,1,0:T(8,128)(2,1)S(1)}, u32[]{:S(2)}, u32[]{:S(2)}) collective-permute-start(bf16[4,432,256]{2,1,0:T(8,128)(2,1)S(1)} %pad_maximum_fusion.1), channel_id=1, source_target_pairs={{0,1},{1,0},{2,3},{3,2},{4,5},{5,4},{6,7},{7,6},{8,9},{9,8},{10,11... | collective-permute-start | bytes 2654216 | tf_op jit(solution)/shard_map/ppermute | solution.py:35
  84.5 7.8 %collective-permute-start.22 = (bf16[432,256]{1,0:T(8,128)(2,1)S(1)}, bf16[432,256]{1,0:T(8,128)(2,1)S(1)}, u32[]{:S(2)}, u32[]{:S(2)}) collective-permute-start(bf16[432,256]{1,0:T(8,128)(2,1)S(1)} %collective-permute-done.20), channel_id=1, source_target_pairs={{0,4},{1,5},{2,6},{3,7},{4,0},{5,1},{6,2},{7,3},{8,12},{9,13},{10,... | collective-permute-start | bytes 663560 | tf_op jit(solution)/shard_map/ppermute | solution.py:35
  85.4 17.0 %collective-permute-start.21 = (bf16[2,432,256]{2,1,0:T(8,128)(2,1)S(1)}, bf16[2,432,256]{2,1,0:T(8,128)(2,1)S(1)}, u32[]{:S(2)}, u32[]{:S(2)}) collective-permute-start(bf16[2,432,256]{2,1,0:T(8,128)(2,1)S(1)} %pad_maximum_fusion.4), channel_id=1, source_target_pairs={{0,2},{1,3},{2,0},{3,1},{4,6},{5,7},{6,4},{7,5},{8,10},{9,11},{10,... | collective-permute-start | bytes 1327112 | tf_op jit(solution)/shard_map/ppermute | solution.py:35
  92.4 10.0 %collective-permute-start.23 = (bf16[432,256]{1,0:T(8,128)(2,1)S(1)}, bf16[432,256]{1,0:T(8,128)(2,1)S(1)}, u32[]{:S(2)}, u32[]{:S(2)}) collective-permute-start(bf16[432,256]{1,0:T(8,128)(2,1)S(1)} %collective-permute-done.22), channel_id=1, source_target_pairs={{0,2},{1,3},{2,0},{3,1},{4,6},{5,7},{6,4},{7,5},{8,10},{9,11},{10,... | collective-permute-start | bytes 663560 | tf_op jit(solution)/shard_map/ppermute | solution.py:35
  92.9 8.8 %collective-permute-start.26 = (bf16[1,272,256]{2,1,0:T(8,128)(2,1)S(1)}, bf16[1,272,256]{2,1,0:T(8,128)(2,1)S(1)}, u32[]{:S(2)}, u32[]{:S(2)}) collective-permute-start(bf16[1,272,256]{2,1,0:T(8,128)(2,1)S(1)} %get-tuple-element.139), channel_id=1, source_target_pairs={{0,8},{1,9},{2,10},{3,11},{4,12},{5,13},{6,14},{7,15},{8,0},{9,1},... | collective-permute-start | bytes 417800 | tf_op jit(solution)/shard_map/ppermute | solution.py:35
  (5 other events, 16.9 us)

commit v13 on v10

--- a/solution.py
+++ b/solution.py
@@ -755,10 +755,9 @@
     *parcels, grad = lax.optimization_barrier((*parcels, grad))
     table, picks = route(parcels, outer)
 
-    *picks, give_core, grad = lax.optimization_barrier((*picks, give_core, grad))
+    got_inner = swap(give_inner, size, 2)
+    *picks, give_core, got_inner = lax.optimization_barrier((*picks, give_core, got_inner))
     arrived = [rotate(pick, size, steps) if steps else pick for steps, pick in enumerate(picks)]
-    got_inner = swap(give_inner, size, 2)
-    got_inner, grad = lax.optimization_barrier((got_inner, grad))
     grad_inner = swap(grad, size, 2)
     *arrived, got_inner, grad_inner = lax.optimization_barrier((*arrived, got_inner, grad_inner))
     others = turn(got_inner, swap(give_core, size, 1), swap(got_inner, size, 1))

time: 105 us -> 105 us (level)
  transfers between devices with their start and end apart: 28 -> 28, of which waited for: 12 -> 13; matrix products, arithmetic and copies ran while one was open for 0% -> 0% of each run, Pallas kernels for 33% -> 33%
where the time goes in v13:
time: 105 us
  Pallas kernels  37.8 us (36%)
  waiting for transfers between devices  33.6 us (32%)
  starting transfers between devices  31.7 us (30%)
    ppermute x22, starting transfers between devices, swap(): return lax.ppermute(x, 'zslab', [(i, i ^ bit) for i in range(size)])  21.6 us
    ppermute x22, waiting for transfers between devices, swap(): return lax.ppermute(x, 'zslab', [(i, i ^ bit) for i in range(size)])  21.2 us
    ppermute x6, waiting for transfers between devices, rotate(): lax.ppermute(x, 'zslab', [(i, (i + 4 * steps) % size) for i in range(size)])  12.4 us
    ppermute x6, starting transfers between devices, rotate(): lax.ppermute(x, 'zslab', [(i, (i + 4 * steps) % size) for i in range(size)])  10.1 us
    pallas_call x1, Pallas kernels, backward(): pl.pallas_call(backward_kernel, in_specs=[WHOLE] * 3 + [FAR], out_specs=(...  8.95 us
    pallas_call x2, Pallas kernels, assemble(): pl.pallas_call(functools.partial(assemble_kernel, outer, places, len(stac...  5.03 us
    pallas_call x1, Pallas kernels, prepare(): pl.pallas_call(prepare_kernel, in_specs=[FAR] * 4, out_specs=(WHOLE,) * 7...  4.77 us
    pallas_call x1, Pallas kernels, forward_inside(): pl.pallas_call(forward_kernel, in_specs=[WHOLE] * 5, out_specs=(WHOLE,) *...  4.66 us
  transfers between devices with their start and end apart: 28, of which 13 were waited for; matrix products, arithmetic and copies ran while one was open for 0% of the time, Pallas kernels for 33%

profile of v13, /device:TPU:0, one launch (start us, length us, event | category | flops | bytes accessed | tf_op | source)
XLA Modules:
  0.0 104.7 jit_solution(15641840641303365774)
XLA Ops:
  1.7 3.0 %collective-permute-start = (bf16[272,256]{1,0:T(8,128)(2,1)S(1)}, bf16[272,256]{1,0:T(8,128)(2,1)S(1)}, u32[]{:S(2)}, u32[]{:S(2)}) collective-permute-start(bf16[272,256]{1,0:T(8,128)(2,1)S(1)} %rims.1.refs_0_), channel_id=1, source_target_pairs={{0,2},{1,3},{2,0},{3,1},{4,6},{5,7},{6,4},{7,5},{8,10},{9,11},{10,... | collective-permute-start | bytes 417800 | tf_op jit(solution)/shard_map/ppermute | solution.py:35
  4.8 4.8 %prepare.1 = (f32[1024,128]{1,0:T(8,128)S(1)}, bf16[1024,256]{1,0:T(8,128)(2,1)S(1)}, bf16[128,1024]{1,0:T(8,128)(2,1)S(1)}, bf16[64,1024]{1,0:T(8,128)(2,1)S(1)...) custom-call(bf16[2,8,64,256]{3,2,1,0:T(8,128)(2,1)} %feats.3, ...), custom_call_target="tpu_custom_call" | custom-call | flops 1024 | bytes 1024 | tf_op jit(solution)/shard_map/prepare/pallas_call | solution.py:209
  10.2 4.7 %forward_inside.1 = (bf16[2,8,64,256]{3,2,1,0:T(8,128)(2,1)}, bf16[768,256]{1,0:T(8,128)(2,1)S(1)}, f32[2,128,256]{2,1,0:T(8,128)S(1)}, f32[1,256]{1,0:T(1,128)S(1)}) custom-call(bf16[1024,256]{1,0:T(8,128)(2,1)S(1)} %get-tuple-element.71.rows, f32[1024,128]{1,0:T(8,128)S(1)} %get-tuple-element.72.mask, bf16[27,256,256]{2,1,0:T(8,128)(2,1)S(1)} %get-tuple-element.73.weight, ...), custom_call_target="tpu_custom_call" | custom-call | flops 1024 | bytes 1024 | tf_op jit(solution)/shard_map/forward_inside/pallas_call | solution.py:420
  14.9 1.9 %collective-permute-start.7 = (bf16[768,256]{1,0:T(8,128)(2,1)S(1)}, bf16[768,256]{1,0:T(8,128)(2,1)S(1)}, u32[]{:S(2)}, u32[]{:S(2)}) collective-permute-start(bf16[768,256]{1,0:T(8,128)(2,1)S(1)} %get-tuple-element.95.refs_0_.grad), channel_id=1, source_target_pairs={{0,2},{1,3},{2,0},{3,1},{4,6},{5,7},{6,4},{7,5},{8,10},{9,11},{10,... | collective-permute-start | bytes 1179656 | tf_op jit(solution)/shard_map/ppermute | solution.py:35
  16.8 1.7 %route.1 = (s32[36]{0:T(128)S(1)}, bf16[256,256]{1,0:T(8,128)(2,1)S(1)}, bf16[256,256]{1,0:T(8,128)(2,1)S(1)}, bf16[256,256]{1,0:T(8,128)(2,1)S(1)}, bf16[256,256]{1,0:T(8,128)(2,1)S(1)}) custom-call(bf16[272,256]{1,0:T(8,128)(2,1)S(1)} %rims.1.refs_0_, bf16[272,256]{1,0:T(8,128)(2,1)S(1)} %collective-permute-done.refs_1_, ...), custom_call_target="tpu_custom_call" | custom-call | flops 1024 | bytes 1024 | tf_op jit(solution)/shard_map/route/pallas_call | solution.py:304
  20.7 2.6 %collective-permute-start.5 = (bf16[256,256]{1,0:T(8,128)(2,1)S(1)}, bf16[256,256]{1,0:T(8,128)(2,1)S(1)}, u32[]{:S(2)}, u32[]{:S(2)}) collective-permute-start(bf16[256,256]{1,0:T(8,128)(2,1)S(1)} %get-tuple-element.92), channel_id=1, source_target_pairs={{0,8},{1,9},{2,10},{3,11},{4,12},{5,13},{6,14},{7,15},{8,0},{9,1},... | collective-permute-start | bytes 393224 | tf_op jit(solution)/shard_map/ppermute | solution.py:39
  24.6 2.9 %collective-permute-done.4.refs_1_ = bf16[256,256]{1,0:T(8,128)(2,1)S(1)} collective-permute-done((bf16[256,256]{1,0:T(8,128)(2,1)S(1)}, bf16[256,256]{1,0:T(8,128)(2,1)S(1)}, u32[]{:S(2)}, u32[]{:S(2)}) %collective-permute-start.4) | collective-permute-done | bytes 131104 | tf_op jit(solution)/shard_map/ppermute | solution.py:39
  27.5 3.7 %collective-permute-done.5.refs_2_ = bf16[256,256]{1,0:T(8,128)(2,1)S(1)} collective-permute-done((bf16[256,256]{1,0:T(8,128)(2,1)S(1)}, bf16[256,256]{1,0:T(8,128)(2,1)S(1)}, u32[]{:S(2)}, u32[]{:S(2)}) %collective-permute-start.5) | collective-permute-done | bytes 131104 | tf_op jit(solution)/shard_map/ppermute | solution.py:39
  31.8 1.9 %forward_edges.1 = (bf16[2,8,64,256]{3,2,1,0:T(8,128)(2,1)}, bf16[400,256]{1,0:T(8,128)(2,1)S(1)}, bf16[336,256]{1,0:T(8,128)(2,1)S(1)}, bf16[64,256]{1,0:T(8,128)(2,1)S(1)}) custom-call(s32[36]{0:T(128)S(1)} %get-tuple-element.80.table, f32[1024,128]{1,0:T(8,128)S(1)} %get-tuple-element.72.mask, ...), custom_call_target="tpu_custom_call", output_to_operand_aliasing={{0}: (6, {})} | custom-call | flops 1024 | bytes 1024 | tf_op jit(solution)/shard_map/forward_edges/pallas_call | solution.py:497
  36.4 2.9 %inner_terms.1.refs_4_ = f32[1728,256]{1,0:T(8,128)S(1)} custom-call(bf16[576,1024]{1,0:T(8,128)(2,1)S(1)} %get-tuple-element.101.mine, bf16[1728,1024]{1,0:T(8,128)(2,1)S(1)} %turn.1.others, bf16[768,256]{1,0:T(8,128)(2,1)S(1)} %get-tuple-element.95.refs_0_.grad, bf16[768,256]{1,0:T(8,128)(2,1)S(1)} %collective-permute-done.7.refs_1_, ...), custom_call_target="tpu_custom_call" | custom-call | flops 1024 | bytes 1024 | tf_op jit(solution)/shard_map/inner_terms/pallas_call | solution.py:455
  43.2 3.3 %collective-permute-start.15 = (bf16[2,272,256]{2,1,0:T(8,128)(2,1)S(1)}, bf16[2,272,256]{2,1,0:T(8,128)(2,1)S(1)}, u32[]{:S(2)}, u32[]{:S(2)}) collective-permute-start(bf16[2,272,256]{2,1,0:T(8,128)(2,1)S(1)} %get-tuple-element.113), channel_id=1, source_target_pairs={{0,4},{1,5},{2,6},{3,7},{4,0},{5,1},{6,2},{7,3},{8,12},{9,13},{10,... | collective-permute-start | bytes 835592 | tf_op jit(solution)/shard_map/ppermute | solution.py:35
  46.5 1.8 %outer_terms.1 = (bf16[432,256]{1,0:T(8,128)(2,1)S(1)}, bf16[432,256]{1,0:T(8,128)(2,1)S(1)}, bf16[432,256]{1,0:T(8,128)(2,1)S(1)}, f32[432,256]{1,0:T(8,128)S(1)}) custom-call(bf16[576,1024]{1,0:T(8,128)(2,1)S(1)} %get-tuple-element.101.mine, bf16[1728,1024]{1,0:T(8,128)(2,1)S(1)} %turn.1.others, bf16[64,256]{1,0:T(8,128)(2,1)S(1)} %get-tuple-element.104.halos, ...), custom_call_target="tpu_custom_call" | custom-call | flops 1024 | bytes 1024 | tf_op jit(solution)/shard_map/outer_terms/pallas_call | solution.py:574
  50.1 2.8 %collective-permute-start.18 = (bf16[432,256]{1,0:T(8,128)(2,1)S(1)}, bf16[432,256]{1,0:T(8,128)(2,1)S(1)}, u32[]{:S(2)}, u32[]{:S(2)}) collective-permute-start(bf16[432,256]{1,0:T(8,128)(2,1)S(1)} %get-tuple-element.122), channel_id=1, source_target_pairs={{0,12},{1,13},{2,14},{3,15},{4,0},{5,1},{6,2},{7,3},{8,4},{9,5},{1... | collective-permute-start | bytes 663560 | tf_op jit(solution)/shard_map/ppermute | solution.py:39
  52.9 9.0 %backward.1 = (bf16[2,8,64,256]{3,2,1,0:T(8,128)(2,1)}, f32[2,128,256]{2,1,0:T(8,128)S(1)}, bf16[27,256,256]{2,1,0:T(8,128)(2,1)S(1)}) custom-call(bf16[768,256]{1,0:T(8,128)(2,1)S(1)} %get-tuple-element.95.refs_0_.grad, bf16[400,256]{1,0:T(8,128)(2,1)S(1)} %get-tuple-element.105.refs_0_.parcel, f32[1024,128]{1,0:T(8,128)S(1)} %get-tuple-element.72.mask, ...), custom_call_target="tpu_custom_call" | custom-call | flops 1024 | bytes 1024 | tf_op jit(solution)/shard_map/backward/pallas_call | solution.py:623
  62.0 5.1 %collective-permute-done.17 = bf16[432,256]{1,0:T(8,128)(2,1)S(1)} collective-permute-done((bf16[432,256]{1,0:T(8,128)(2,1)S(1)}, bf16[432,256]{1,0:T(8,128)(2,1)S(1)}, u32[]{:S(2)}, u32[]{:S(2)}) %collective-permute-start.17) | collective-permute-done | bytes 221216 | tf_op jit(solution)/shard_map/ppermute | solution.py:39
  67.8 2.8 %collective-permute-start.20 = (bf16[432,256]{1,0:T(8,128)(2,1)S(1)}, bf16[432,256]{1,0:T(8,128)(2,1)S(1)}, u32[]{:S(2)}, u32[]{:S(2)}) collective-permute-start(bf16[432,256]{1,0:T(8,128)(2,1)S(1)} %add_convert_fusion), channel_id=1, source_target_pairs={{0,8},{1,9},{2,10},{3,11},{4,12},{5,13},{6,14},{7,15},{8,0},{9,1},... | collective-permute-start | bytes 663560 | tf_op jit(solution)/shard_map/ppermute | solution.py:35
  70.6 2.6 %collective-permute-start.19 = (bf16[432,256]{1,0:T(8,128)(2,1)S(1)}, bf16[432,256]{1,0:T(8,128)(2,1)S(1)}, u32[]{:S(2)}, u32[]{:S(2)}) collective-permute-start(bf16[432,256]{1,0:T(8,128)(2,1)S(1)} %add_convert_fusion), channel_id=1, source_target_pairs={{0,4},{1,5},{2,6},{3,7},{4,0},{5,1},{6,2},{7,3},{8,12},{9,13},{10,... | collective-permute-start | bytes 663560 | tf_op jit(solution)/shard_map/ppermute | solution.py:35
  73.7 6.9 %collective-permute-done.20 = bf16[432,256]{1,0:T(8,128)(2,1)S(1)} collective-permute-done((bf16[432,256]{1,0:T(8,128)(2,1)S(1)}, bf16[432,256]{1,0:T(8,128)(2,1)S(1)}, u32[]{:S(2)}, u32[]{:S(2)}) %collective-permute-start.20) | collective-permute-done | bytes 221216 | tf_op jit(solution)/shard_map/ppermute | solution.py:35
  82.6 6.1 %collective-permute-done.22 = bf16[432,256]{1,0:T(8,128)(2,1)S(1)} collective-permute-done((bf16[432,256]{1,0:T(8,128)(2,1)S(1)}, bf16[432,256]{1,0:T(8,128)(2,1)S(1)}, u32[]{:S(2)}, u32[]{:S(2)}) %collective-permute-start.22) | collective-permute-done | bytes 221216 | tf_op jit(solution)/shard_map/ppermute | solution.py:35
  89.1 3.2 %collective-permute-start.26 = (bf16[1,272,256]{2,1,0:T(8,128)(2,1)S(1)}, bf16[1,272,256]{2,1,0:T(8,128)(2,1)S(1)}, u32[]{:S(2)}, u32[]{:S(2)}) collective-permute-start(bf16[1,272,256]{2,1,0:T(8,128)(2,1)S(1)} %get-tuple-element.125), channel_id=1, source_target_pairs={{0,8},{1,9},{2,10},{3,11},{4,12},{5,13},{6,14},{7,15},{8,0},{9,1},... | collective-permute-start | bytes 417800 | tf_op jit(solution)/shard_map/ppermute | solution.py:35
  92.4 3.1 %assemble.2.weight_in = bf16[27,16,16,256]{3,2,1,0:T(8,128)(2,1)} custom-call(bf16[4,27,16,256]{3,2,1,0:T(8,128)(2,1)S(1)} %pad_maximum_fusion.refs_0_, bf16[4,27,16,256]{3,2,1,0:T(8,128)(2,1)S(1)} %bitcast.17), custom_call_target="tpu_custom_call" | custom-call | flops 1024 | bytes 1024 | tf_op jit(solution)/shard_map/assemble/pallas_call | solution.py:683
  95.5 2.9 %collective-permute-done.26.got = bf16[1,272,256]{2,1,0:T(8,128)(2,1)S(1)} collective-permute-done((bf16[1,272,256]{2,1,0:T(8,128)(2,1)S(1)}, bf16[1,272,256]{2,1,0:T(8,128)(2,1)S(1)}, u32[]{:S(2)}, u32[]{:S(2)}) %collective-permute-start.26) | collective-permute-done | bytes 139296 | tf_op jit(solution)/shard_map/ppermute | solution.py:35
  99.4 3.2 %finish.1 = (bf16[2,8,64,256]{3,2,1,0:T(8,128)(2,1)}, bf16[27,16,16,256]{3,2,1,0:T(8,128)(2,1)}, f32[1,256]{1,0:T(1,128)}) custom-call(f32[2,128,256]{2,1,0:T(8,128)S(1)} %get-tuple-element.116.partial, f32[1024,128]{1,0:T(8,128)S(1)} %get-tuple-element.72.mask, ...), custom_call_target="tpu_custom_call", output_to_operand_aliasing={{0}: (6, {}), {1}: (7, {})} | custom-call | flops 1024 | bytes 1024 | tf_op jit(solution)/shard_map/finish/pallas_call | solution.py:725
  102.7 1.9 %assemble.3 = bf16[27,16,16,256]{3,2,1,0:T(8,128)(2,1)} custom-call(bf16[4,27,16,256]{3,2,1,0:T(8,128)(2,1)S(1)} %bitcast.18, bf16[27,16,16,256]{3,2,1,0:T(8,128)(2,1)} %get-tuple-element.132.refs_1_), custom_call_target="tpu_custom_call", output_to_operand_aliasing={{}: (1, {})} | custom-call | flops 1024 | bytes 1024 | tf_op jit(solution)/shard_map/assemble/pallas_call | solution.py:683
  (54 shorter events, 18.7 us)
Async XLA Ops:
  1.7 7.8 %collective-permute-start = (bf16[272,256]{1,0:T(8,128)(2,1)S(1)}, bf16[272,256]{1,0:T(8,128)(2,1)S(1)}, u32[]{:S(2)}, u32[]{:S(2)}) collective-permute-start(bf16[272,256]{1,0:T(8,128)(2,1)S(1)} %rims.1.refs_0_), channel_id=1, source_target_pairs={{0,2},{1,3},{2,0},{3,1},{4,6},{5,7},{6,4},{7,5},{8,10},{9,11},{10,... | collective-permute-start | bytes 417800 | tf_op jit(solution)/shard_map/ppermute | solution.py:35
  4.8 10.1 %collective-permute-start.1 = (bf16[272,256]{1,0:T(8,128)(2,1)S(1)}, bf16[272,256]{1,0:T(8,128)(2,1)S(1)}, u32[]{:S(2)}, u32[]{:S(2)}) collective-permute-start(bf16[272,256]{1,0:T(8,128)(2,1)S(1)} %rims.1.refs_0_), channel_id=1, source_target_pairs={{0,1},{1,0},{2,3},{3,2},{4,5},{5,4},{6,7},{7,6},{8,9},{9,8},{10,11... | collective-permute-start | bytes 417800 | tf_op jit(solution)/shard_map/ppermute | solution.py:35
  9.6 5.3 %collective-permute-start.2 = (bf16[272,256]{1,0:T(8,128)(2,1)S(1)}, bf16[272,256]{1,0:T(8,128)(2,1)S(1)}, u32[]{:S(2)}, u32[]{:S(2)}) collective-permute-start(bf16[272,256]{1,0:T(8,128)(2,1)S(1)} %collective-permute-done.refs_1_), channel_id=1, source_target_pairs={{0,1},{1,0},{2,3},{3,2},{4,5},{5,4},{6,7},{7,6},{8,9},{9,8},{10,11... | collective-permute-start | bytes 417800 | tf_op jit(solution)/shard_map/ppermute | solution.py:35
  10.1 9.0 %collective-permute-start.3 = (bf16[128,1024]{1,0:T(8,128)(2,1)S(1)}, bf16[128,1024]{1,0:T(8,128)(2,1)S(1)}, u32[]{:S(2)}, u32[]{:S(2)}) collective-permute-start(bf16[128,1024]{1,0:T(8,128)(2,1)S(1)} %get-tuple-element.89), channel_id=1, source_target_pairs={{0,2},{1,3},{2,0},{3,1},{4,6},{5,7},{6,4},{7,5},{8,10},{9,11},{10,... | collective-permute-start | bytes 786440 | tf_op jit(solution)/shard_map/ppermute | solution.py:35
  14.9 16.4 %collective-permute-start.7 = (bf16[768,256]{1,0:T(8,128)(2,1)S(1)}, bf16[768,256]{1,0:T(8,128)(2,1)S(1)}, u32[]{:S(2)}, u32[]{:S(2)}) collective-permute-start(bf16[768,256]{1,0:T(8,128)(2,1)S(1)} %get-tuple-element.95.refs_0_.grad), channel_id=1, source_target_pairs={{0,2},{1,3},{2,0},{3,1},{4,6},{5,7},{6,4},{7,5},{8,10},{9,11},{10,... | collective-permute-start | bytes 1179656 | tf_op jit(solution)/shard_map/ppermute | solution.py:35
  19.1 8.4 %collective-permute-start.4 = (bf16[256,256]{1,0:T(8,128)(2,1)S(1)}, bf16[256,256]{1,0:T(8,128)(2,1)S(1)}, u32[]{:S(2)}, u32[]{:S(2)}) collective-permute-start(bf16[256,256]{1,0:T(8,128)(2,1)S(1)} %get-tuple-element.91), channel_id=1, source_target_pairs={{0,4},{1,5},{2,6},{3,7},{4,8},{5,9},{6,10},{7,11},{8,12},{9,13},{1... | collective-permute-start | bytes 393224 | tf_op jit(solution)/shard_map/ppermute | solution.py:39
  20.7 10.6 %collective-permute-start.5 = (bf16[256,256]{1,0:T(8,128)(2,1)S(1)}, bf16[256,256]{1,0:T(8,128)(2,1)S(1)}, u32[]{:S(2)}, u32[]{:S(2)}) collective-permute-start(bf16[256,256]{1,0:T(8,128)(2,1)S(1)} %get-tuple-element.92), channel_id=1, source_target_pairs={{0,8},{1,9},{2,10},{3,11},{4,12},{5,13},{6,14},{7,15},{8,0},{9,1},... | collective-permute-start | bytes 393224 | tf_op jit(solution)/shard_map/ppermute | solution.py:39
  23.3 8.0 %collective-permute-start.6 = (bf16[256,256]{1,0:T(8,128)(2,1)S(1)}, bf16[256,256]{1,0:T(8,128)(2,1)S(1)}, u32[]{:S(2)}, u32[]{:S(2)}) collective-permute-start(bf16[256,256]{1,0:T(8,128)(2,1)S(1)} %get-tuple-element.93), channel_id=1, source_target_pairs={{0,12},{1,13},{2,14},{3,15},{4,0},{5,1},{6,2},{7,3},{8,4},{9,5},{1... | collective-permute-start | bytes 393224 | tf_op jit(solution)/shard_map/ppermute | solution.py:39
  24.6 11.8 %collective-permute-start.11 = (bf16[768,256]{1,0:T(8,128)(2,1)S(1)}, bf16[768,256]{1,0:T(8,128)(2,1)S(1)}, u32[]{:S(2)}, u32[]{:S(2)}) collective-permute-start(bf16[768,256]{1,0:T(8,128)(2,1)S(1)} %get-tuple-element.95.refs_0_.grad), channel_id=1, source_target_pairs={{0,1},{1,0},{2,3},{3,2},{4,5},{5,4},{6,7},{7,6},{8,9},{9,8},{10,11... | collective-permute-start | bytes 1179656 | tf_op jit(solution)/shard_map/ppermute | solution.py:35
  31.3 5.1 %collective-permute-start.12 = (bf16[768,256]{1,0:T(8,128)(2,1)S(1)}, bf16[768,256]{1,0:T(8,128)(2,1)S(1)}, u32[]{:S(2)}, u32[]{:S(2)}) collective-permute-start(bf16[768,256]{1,0:T(8,128)(2,1)S(1)} %collective-permute-done.7.refs_1_), channel_id=1, source_target_pairs={{0,1},{1,0},{2,3},{3,2},{4,5},{5,4},{6,7},{7,6},{8,9},{9,8},{10,11... | collective-permute-start | bytes 1179656 | tf_op jit(solution)/shard_map/ppermute | solution.py:35
  31.3 4.2 %collective-permute-start.9 = (bf16[128,1024]{1,0:T(8,128)(2,1)S(1)}, bf16[128,1024]{1,0:T(8,128)(2,1)S(1)}, u32[]{:S(2)}, u32[]{:S(2)}) collective-permute-start(bf16[128,1024]{1,0:T(8,128)(2,1)S(1)} %collective-permute-done.3.inner), channel_id=1, source_target_pairs={{0,1},{1,0},{2,3},{3,2},{4,5},{5,4},{6,7},{7,6},{8,9},{9,8},{10,11... | collective-permute-start | bytes 786440 | tf_op jit(solution)/shard_map/ppermute | solution.py:35
  33.7 7.1 %collective-permute-start.10 = (bf16[400,256]{1,0:T(8,128)(2,1)S(1)}, bf16[400,256]{1,0:T(8,128)(2,1)S(1)}, u32[]{:S(2)}, u32[]{:S(2)}) collective-permute-start(bf16[400,256]{1,0:T(8,128)(2,1)S(1)} %get-tuple-element.105.refs_0_.parcel), channel_id=1, source_target_pairs={{0,2},{1,3},{2,0},{3,1},{4,6},{5,7},{6,4},{7,5},{8,10},{9,11},{10,... | collective-permute-start | bytes 614408 | tf_op jit(solution)/shard_map/ppermute | solution.py:35
  43.2 18.7 %collective-permute-start.15 = (bf16[2,272,256]{2,1,0:T(8,128)(2,1)S(1)}, bf16[2,272,256]{2,1,0:T(8,128)(2,1)S(1)}, u32[]{:S(2)}, u32[]{:S(2)}) collective-permute-start(bf16[2,272,256]{2,1,0:T(8,128)(2,1)S(1)} %get-tuple-element.113), channel_id=1, source_target_pairs={{0,4},{1,5},{2,6},{3,7},{4,0},{5,1},{6,2},{7,3},{8,12},{9,13},{10,... | collective-permute-start | bytes 835592 | tf_op jit(solution)/shard_map/ppermute | solution.py:35
  48.3 13.7 %collective-permute-start.16 = (bf16[432,256]{1,0:T(8,128)(2,1)S(1)}, bf16[432,256]{1,0:T(8,128)(2,1)S(1)}, u32[]{:S(2)}, u32[]{:S(2)}) collective-permute-start(bf16[432,256]{1,0:T(8,128)(2,1)S(1)} %get-tuple-element.120), channel_id=1, source_target_pairs={{0,4},{1,5},{2,6},{3,7},{4,8},{5,9},{6,10},{7,11},{8,12},{9,13},{1... | collective-permute-start | bytes 663560 | tf_op jit(solution)/shard_map/ppermute | solution.py:39
  48.4 18.7 %collective-permute-start.17 = (bf16[432,256]{1,0:T(8,128)(2,1)S(1)}, bf16[432,256]{1,0:T(8,128)(2,1)S(1)}, u32[]{:S(2)}, u32[]{:S(2)}) collective-permute-start(bf16[432,256]{1,0:T(8,128)(2,1)S(1)} %get-tuple-element.121), channel_id=1, source_target_pairs={{0,8},{1,9},{2,10},{3,11},{4,12},{5,13},{6,14},{7,15},{8,0},{9,1},... | collective-permute-start | bytes 663560 | tf_op jit(solution)/shard_map/ppermute | solution.py:39
  50.1 17.7 %collective-permute-start.18 = (bf16[432,256]{1,0:T(8,128)(2,1)S(1)}, bf16[432,256]{1,0:T(8,128)(2,1)S(1)}, u32[]{:S(2)}, u32[]{:S(2)}) collective-permute-start(bf16[432,256]{1,0:T(8,128)(2,1)S(1)} %get-tuple-element.122), channel_id=1, source_target_pairs={{0,12},{1,13},{2,14},{3,15},{4,0},{5,1},{6,2},{7,3},{8,4},{9,5},{1... | collective-permute-start | bytes 663560 | tf_op jit(solution)/shard_map/ppermute | solution.py:39
  67.8 12.8 %collective-permute-start.20 = (bf16[432,256]{1,0:T(8,128)(2,1)S(1)}, bf16[432,256]{1,0:T(8,128)(2,1)S(1)}, u32[]{:S(2)}, u32[]{:S(2)}) collective-permute-start(bf16[432,256]{1,0:T(8,128)(2,1)S(1)} %add_convert_fusion), channel_id=1, source_target_pairs={{0,8},{1,9},{2,10},{3,11},{4,12},{5,13},{6,14},{7,15},{8,0},{9,1},... | collective-permute-start | bytes 663560 | tf_op jit(solution)/shard_map/ppermute | solution.py:35
  70.6 10.0 %collective-permute-start.19 = (bf16[432,256]{1,0:T(8,128)(2,1)S(1)}, bf16[432,256]{1,0:T(8,128)(2,1)S(1)}, u32[]{:S(2)}, u32[]{:S(2)}) collective-permute-start(bf16[432,256]{1,0:T(8,128)(2,1)S(1)} %add_convert_fusion), channel_id=1, source_target_pairs={{0,4},{1,5},{2,6},{3,7},{4,0},{5,1},{6,2},{7,3},{8,12},{9,13},{10,... | collective-permute-start | bytes 663560 | tf_op jit(solution)/shard_map/ppermute | solution.py:35
  73.2 7.5 %collective-permute-start.24 = (bf16[432,256]{1,0:T(8,128)(2,1)S(1)}, bf16[432,256]{1,0:T(8,128)(2,1)S(1)}, u32[]{:S(2)}, u32[]{:S(2)}) collective-permute-start(bf16[432,256]{1,0:T(8,128)(2,1)S(1)} %add_convert_fusion), channel_id=1, source_target_pairs={{0,2},{1,3},{2,0},{3,1},{4,6},{5,7},{6,4},{7,5},{8,10},{9,11},{10,... | collective-permute-start | bytes 663560 | tf_op jit(solution)/shard_map/ppermute | solution.py:35
  80.8 11.6 %collective-permute-start.25 = (bf16[4,432,256]{2,1,0:T(8,128)(2,1)S(1)}, bf16[4,432,256]{2,1,0:T(8,128)(2,1)S(1)}, u32[]{:S(2)}, u32[]{:S(2)}) collective-permute-start(bf16[4,432,256]{2,1,0:T(8,128)(2,1)S(1)} %pad_maximum_fusion.1), channel_id=1, source_target_pairs={{0,1},{1,0},{2,3},{3,2},{4,5},{5,4},{6,7},{7,6},{8,9},{9,8},{10,11... | collective-permute-start | bytes 2654216 | tf_op jit(solution)/shard_map/ppermute | solution.py:35
  80.8 7.8 %collective-permute-start.22 = (bf16[432,256]{1,0:T(8,128)(2,1)S(1)}, bf16[432,256]{1,0:T(8,128)(2,1)S(1)}, u32[]{:S(2)}, u32[]{:S(2)}) collective-permute-start(bf16[432,256]{1,0:T(8,128)(2,1)S(1)} %collective-permute-done.20), channel_id=1, source_target_pairs={{0,4},{1,5},{2,6},{3,7},{4,0},{5,1},{6,2},{7,3},{8,12},{9,13},{10,... | collective-permute-start | bytes 663560 | tf_op jit(solution)/shard_map/ppermute | solution.py:35
  82.1 17.0 %collective-permute-start.21 = (bf16[2,432,256]{2,1,0:T(8,128)(2,1)S(1)}, bf16[2,432,256]{2,1,0:T(8,128)(2,1)S(1)}, u32[]{:S(2)}, u32[]{:S(2)}) collective-permute-start(bf16[2,432,256]{2,1,0:T(8,128)(2,1)S(1)} %pad_maximum_fusion.4), channel_id=1, source_target_pairs={{0,2},{1,3},{2,0},{3,1},{4,6},{5,7},{6,4},{7,5},{8,10},{9,11},{10,... | collective-permute-start | bytes 1327112 | tf_op jit(solution)/shard_map/ppermute | solution.py:35
  88.7 10.4 %collective-permute-start.23 = (bf16[432,256]{1,0:T(8,128)(2,1)S(1)}, bf16[432,256]{1,0:T(8,128)(2,1)S(1)}, u32[]{:S(2)}, u32[]{:S(2)}) collective-permute-start(bf16[432,256]{1,0:T(8,128)(2,1)S(1)} %collective-permute-done.22), channel_id=1, source_target_pairs={{0,2},{1,3},{2,0},{3,1},{4,6},{5,7},{6,4},{7,5},{8,10},{9,11},{10,... | collective-permute-start | bytes 663560 | tf_op jit(solution)/shard_map/ppermute | solution.py:35
  89.1 9.4 %collective-permute-start.26 = (bf16[1,272,256]{2,1,0:T(8,128)(2,1)S(1)}, bf16[1,272,256]{2,1,0:T(8,128)(2,1)S(1)}, u32[]{:S(2)}, u32[]{:S(2)}) collective-permute-start(bf16[1,272,256]{2,1,0:T(8,128)(2,1)S(1)} %get-tuple-element.125), channel_id=1, source_target_pairs={{0,8},{1,9},{2,10},{3,11},{4,12},{5,13},{6,14},{7,15},{8,0},{9,1},... | collective-permute-start | bytes 417800 | tf_op jit(solution)/shard_map/ppermute | solution.py:35
  (5 other events, 17.8 us)
